TPU v7x, 32 devices: a whole 2x2x4 slice. The times are simulated.
32 devices in a mesh: grp: 2 (over y), row: 16 (over z, x, core).
Axes of the slice: x: 2, y: 2, z: 4, core: 2. Of those that a mesh axis runs over, the one named last changes fastest.
Arguments:
- features: float32 [128, 32, 512], P(('grp', 'row')), parts along dimension 0, may hold values from -6 to 6
- cotangent: float32 [128, 32, 512], P(('grp', 'row')), parts along dimension 0, may hold values from -8 to 8
- kernel: float32 [7, 7, 512], replicated, may hold values from -0.875 to 0.875
- norm_gain: float32 [512], replicated, may hold values from 0.1 to 1.9
- norm_bias: float32 [512], replicated, may hold values from -3 to 3
- in_weight: float32 [512, 2048], P('row'), may hold values from -0.25 to 0.25
- in_bias: float32 [2048], replicated, may hold values from -3 to 3
- out_weight: float32 [512, 2048], P('row'), may hold values from -0.125 to 0.125
- layer_scale: float32 [512], replicated, may hold values from 0.3 to 1.5
Outputs:
- output: float32 [128, 32, 512], P(('grp', 'row')), parts along dimension 0
- input_grad: float32 [128, 32, 512], P(('grp', 'row')), parts along dimension 0
- in_weight_grad: float32 [1024, 2048], P(('grp', 'row')), parts along dimension 0
- out_weight_grad: float32 [1024, 2048], P(('grp', 'row')), parts along dimension 0
- kernel_grad: float32 [14, 7, 512], P('grp'), parts along dimension 0
- gain_grad: float32 [1024], P('grp'), parts along dimension 0
- bias_grad: float32 [1024], P('grp'), parts along dimension 0
- in_bias_grad: float32 [4096], P('grp'), parts along dimension 0
- scale_grad: float32 [1024], P('grp'), parts along dimension 0
There are 2 independent parts, one for each index of `grp`. A program takes and returns all parts, laid end to end along the dimension named above; an argument that names none is the same for every part. Nothing has to cross between parts.
All inputs are finite; a program needn't handle non-finite values.
Results may differ from a plain program's by a relative error of at most 0.0071.
Values may be sent and summed in bfloat16 or wider, within the bound.
No kernel may reach another device: no remote copies, remote signals or barrier semaphores. Data moves between devices by JAX's collectives and lax.ppermute only.
A program may use at most 64 MiB of HBM per device.

v0:
```python
import math

import jax
import jax.numpy as jnp
from jax import lax
from jax.sharding import PartitionSpec as P


def extended(block, sides, width):
    for axis, dim in sides:
        count = lax.axis_size(axis)
        forward = [(i, i + 1) for i in range(count - 1)]
        backward = [(target, source) for source, target in forward]
        low = lax.ppermute(
            lax.slice_in_dim(block, block.shape[dim] - width, None, axis=dim), axis, forward
        )
        high = lax.ppermute(lax.slice_in_dim(block, 0, width, axis=dim), axis, backward)
        block = jnp.concatenate([low, block, high], axis=dim)
    return block


def conv_taps(padded, kernel, row_count, col_count):
    running = jnp.zeros((row_count, col_count, padded.shape[2]), jnp.float32)
    for tap_row in range(7):
        for tap_col in range(7):
            running = (
                running
                + padded[tap_row : tap_row + row_count, tap_col : tap_col + col_count]
                * kernel[tap_row, tap_col]
            )
    return running


def contract_last(left, right):
    return lax.dot_general(
        left, right, (((1,), (1,)), ((), ())), preferred_element_type=jnp.float32
    )


def contract_first(left, right):
    return lax.dot_general(
        left, right, (((0,), (0,)), ((), ())), preferred_element_type=jnp.float32
    )


def per_device(
    features, cotangent, kernel, norm_gain, norm_bias, in_weight, in_bias, out_weight, layer_scale
):
    row_count, col_count, channels = features.shape
    hidden_count = in_weight.shape[1]
    norm_scale = 1.0 / math.sqrt(row_count * col_count * lax.axis_size("row"))
    rimmed = extended(features, (("row", 0),), 3)
    padded = jnp.pad(rimmed, ((0, 0), (3, 3), (0, 0)))
    convolved = conv_taps(padded, kernel, row_count, col_count).reshape(-1, channels)
    average = jnp.mean(convolved, axis=1, keepdims=True)
    centred = convolved - average
    inv_std = lax.rsqrt(jnp.mean(centred * centred, axis=1, keepdims=True) + 1e-06)
    normed = centred * inv_std
    normed_out = (normed * norm_gain + norm_bias).astype(jnp.bfloat16)
    in_narrow = in_weight.astype(jnp.bfloat16)
    out_narrow = out_weight.astype(jnp.bfloat16)

    def fold_rows(left, piece):
        return jnp.dot(left, piece, preferred_element_type=jnp.float32)

    def map_rows(left, piece):
        return contract_last(left, piece)

    preact = fold_rows(normed_out, lax.all_gather(in_narrow, "row", axis=0, tiled=True)) + in_bias
    cdf_value = 0.5 * (1.0 + jax.scipy.special.erf(preact * 0.7071067811865476))
    activated = (preact * cdf_value).astype(jnp.bfloat16)
    mixed = map_rows(activated, lax.all_gather(out_narrow, "row", axis=0, tiled=True))
    flat_input = features.reshape(-1, channels)
    flat_cotan = cotangent.reshape(-1, channels)
    output = (flat_input + layer_scale * mixed).reshape(row_count, col_count, channels)
    scale_term = jnp.sum(flat_cotan * mixed, axis=0)
    branch_grad = (layer_scale * flat_cotan).astype(jnp.bfloat16)
    act_grad = fold_rows(branch_grad, lax.all_gather(out_narrow, "row", axis=0, tiled=True))
    gelu_slope = cdf_value + preact * jnp.exp(-0.5 * preact * preact) * 0.3989422804014327
    hidden_grad = act_grad * gelu_slope
    in_bias_term = jnp.sum(hidden_grad, axis=0)
    hidden_narrow = hidden_grad.astype(jnp.bfloat16)
    out_grad = map_rows(hidden_narrow, lax.all_gather(in_narrow, "row", axis=0, tiled=True))
    gain_term = jnp.sum(out_grad * normed, axis=0)
    bias_term = jnp.sum(out_grad, axis=0)
    normed_grad = out_grad * norm_gain
    conv_grad = inv_std * (
        normed_grad
        - jnp.mean(normed_grad, axis=1, keepdims=True)
        - normed * jnp.mean(normed_grad * normed, axis=1, keepdims=True)
    )
    grad_pairs = lax.psum_scatter(
        jnp.concatenate(
            [
                norm_scale * contract_first(normed_out, hidden_narrow),
                norm_scale * contract_first(branch_grad, activated),
            ],
            axis=1,
        ),
        "row",
        scatter_dimension=0,
        tiled=True,
    )
    in_weight_grad = grad_pairs[:, :hidden_count]
    out_weight_grad = grad_pairs[:, hidden_count:]
    conv_grid = conv_grad.reshape(row_count, col_count, channels)
    grad_rimmed = extended(conv_grid, (("row", 0),), 3)
    grad_padded = jnp.pad(grad_rimmed, ((0, 0), (3, 3), (0, 0)))
    input_grad = cotangent
    kernel_rows = []
    for tap_row in range(7):
        tap_list = []
        for tap_col in range(7):
            input_grad = (
                input_grad
                + kernel[tap_row, tap_col]
                * grad_padded[
                    6 - tap_row : 6 - tap_row + row_count, 6 - tap_col : 6 - tap_col + col_count
                ]
            )
            tap_list.append(
                jnp.sum(
                    padded[tap_row : tap_row + row_count, tap_col : tap_col + col_count]
                    * conv_grid,
                    axis=(0, 1),
                )
            )
        kernel_rows.append(jnp.stack(tap_list))
    kernel_term = norm_scale * jnp.stack(kernel_rows)
    small_sums = lax.psum(
        (
            kernel_term,
            norm_scale * gain_term,
            norm_scale * bias_term,
            norm_scale * in_bias_term,
            norm_scale * scale_term,
        ),
        "row",
    )
    return (
        output,
        input_grad,
        in_weight_grad,
        out_weight_grad,
        small_sums[0],
        small_sums[1],
        small_sums[2],
        small_sums[3],
        small_sums[4],
    )


def solution(mesh):
    return jax.shard_map(
        per_device,
        mesh=mesh,
        in_specs=(
            P(("grp", "row"), None, None),
            P(("grp", "row"), None, None),
            P(),
            P(),
            P(),
            P("row", None),
            P(),
            P("row", None),
            P(),
        ),
        out_specs=(
            P(("grp", "row"), None, None),
            P(("grp", "row"), None, None),
            P(("grp", "row"), None),
            P(("grp", "row"), None),
            P("grp", None, None),
            P("grp"),
            P("grp"),
            P("grp"),
            P("grp"),
        ),
        check_vma=False,
    )
```

profile of v0, /device:TPU:1, one launch (start us, length us, event | category | flops | bytes accessed | tf_op | source)
XLA Modules:
  0.0 310.6 jit_solution(13903080589390694371)
XLA Ops:
  7.2 1.7 convert_element_type.22
  9.0 1.6 convert_element_type.24
  11.7 4.5 %collective-permute-start = (f32[3,32,512]{2,1,0:T(8,128)S(1)}, f32[3,32,512]{2,1,0:T(8,128)S(1)}, u32[]{:S(2)}, u32[]{:S(2)}) collective-permute-start(f32[3,32,512]{2,1,0:T(8,128)S(1)} %get-tuple-element.87), channel_id=1, source_target_pairs={{0,1},{1,2},{2,3},{3,4},{4,5},{5,6},{6,7},{7,8},{8,9},{9,10},{10,1... | collective-permute-start | bytes 589832 | tf_op jit(solution)/shard_map/ppermute | solution.py:14
  16.2 1.9 collective-permute-start.1
  18.2 1.2 fusion.74
  23.3 1.2 select_maximum_fusion.2
  24.6 2.0 fusion.70
  27.3 27.6 %all-gather.3.cloned.1.call-done = bf16[512,2048]{1,0:T(8,128)(2,1)} async-done(((bf16[32,2048]{1,0:T(8,128)(2,1)}), bf16[512,2048]{1,0:T(8,128)(2,1)}) %all-gather.3.cloned.1.call-update) | async-done | bytes 2097168 | tf_op jit(solution)/shard_map/all_gather | solution.py:69
  54.8 2.1 multiply_convert_fusion
  57.0 40.8 %all-gather.5.cloned.1.call-done = bf16[512,2048]{1,0:T(8,128)(2,1)} async-done(((bf16[32,2048]{1,0:T(8,128)(2,1)}), bf16[512,2048]{1,0:T(8,128)(2,1)}) %all-gather.5.cloned.1.call-update) | async-done | bytes 2097168 | tf_op jit(solution)/shard_map/all_gather | solution.py:72
  97.8 3.9 %fusion.65 = (f32[512]{0:T(512)}, bf16[128,512]{1,0:T(8,128)(2,1)S(1)}, f32[128,512]{1,0:T(8,128)}) fusion(f32[4,32,512]{2,1,0:T(8,128)S(1)} %copy-done.8, f32[512]{0:T(512)} %param.17, f32[4,32,512]{2,1,0:T(8,128)S(1)} %copy-done, bf16[128,2048]{1,0:T(8,128)(2,1)S(1)} %get-tuple-element.138, bf16[512,2048]{1,0:T(8,128)(2,1)} %all-gather.5.cloned.1.call-done), kind=kOutput, calls=%fused_computation.133 | convolution fusion | flops 268828160 | bytes 3543040 | tf_op jit(solution)/shard_map/dot_general | solution.py:35
  102.4 1.4 fusion.77
  104.5 3.8 %pad_maximum_fusion = f32[512,4096]{1,0:T(8,128)} fusion(f32[512,2048]{1,0:T(8,128)S(1)} %convolution_multiply_fusion, f32[512,2048]{1,0:T(8,128)S(1)} %convolution_multiply_fusion.1), kind=kLoop, calls=%fused_computation | loop fusion | flops 2097152 | bytes 16777216 | tf_op jit(solution)/shard_map/concatenate | solution.py:93
  108.4 1.5 copy-done.1
  109.9 2.7 multiply_reduce_fusion
  112.5 1.3 multiply_reduce_fusion.1
  113.9 2.3 collective-permute-start.2
  116.3 2.1 collective-permute-start.3
  120.7 57.3 %all-reduce.2 = (f32[512]{0:T(512)}, f32[512]{0:T(512)}, f32[2048]{0:T(1024)}, f32[512]{0:T(512)}) all-reduce(f32[512]{0:T(512)S(1)} %get-tuple-element.144, f32[512]{0:T(512)S(1)} %get-tuple-element.143, f32[2048]{0:T(1024)S(1)} %broadcast_multiply_fusion.1, ...), channel_id=1, replica_groups=mesh['grp'=2,'row'=16] {'row'}, use_global_device_ids=true, to_apply=%region_56.57 | all-reduce | flops 3584 | bytes 28672 | tf_op jit(solution)/shard_map/psum | solution.py:130
  178.3 2.6 fusion.17
  180.9 31.0 %reduce-scatter.2.cloned.1.call-done = f32[32,4096]{1,0:T(8,128)} async-done(((f32[512,4096]{1,0:T(8,128)}), f32[32,4096]{1,0:T(8,128)}) %reduce-scatter.2.cloned.1.call-update) | async-done | bytes 524304 | tf_op jit(solution)/shard_map/reduce_scatter | solution.py:92
  211.8 1.9 fusion.71
  213.7 88.9 %all-reduce.5.cloned.1.call-done = f32[7,7,512]{2,1,0:T(8,128)} async-done(((f32[7,7,512]{2,1,0:T(8,128)}), f32[7,7,512]{2,1,0:T(8,128)}) %all-reduce.5.cloned.1.call-update) | async-done | bytes 100368 | tf_op jit(solution)/shard_map/psum | solution.py:130
  302.6 1.6 copy.27
  (174 shorter events, 9.1 us)
Async XLA Ops:
  7.2 47.6 %all-gather.3.cloned.1.call-start = ((), (), s32[]{:S(2)}) async-start(), calls=%async_computation.1 | async-start | bytes 2228224 | tf_op jit(solution)/shard_map/all_gather | solution.py:69
  8.9 88.9 %all-gather.5.cloned.1.call-start = ((), (), s32[]{:S(2)}) async-start(), calls=%async_computation.2 | async-start | bytes 2228224 | tf_op jit(solution)/shard_map/all_gather | solution.py:72
  10.6 201.2 %reduce-scatter.2.cloned.1.call-start = ((), (), s32[]{:S(2)}) async-start(), calls=%async_computation.3 | async-start | bytes 8912896 | tf_op jit(solution)/shard_map/reduce_scatter | solution.py:92
  11.7 9.9 %collective-permute-start = (f32[3,32,512]{2,1,0:T(8,128)S(1)}, f32[3,32,512]{2,1,0:T(8,128)S(1)}, u32[]{:S(2)}, u32[]{:S(2)}) collective-permute-start(f32[3,32,512]{2,1,0:T(8,128)S(1)} %get-tuple-element.87), channel_id=1, source_target_pairs={{0,1},{1,2},{2,3},{3,4},{4,5},{5,6},{6,7},{7,8},{8,9},{9,10},{10,1... | collective-permute-start | bytes 589832 | tf_op jit(solution)/shard_map/ppermute | solution.py:14
  16.2 7.0 %collective-permute-start.1 = (f32[3,32,512]{2,1,0:T(8,128)S(1)}, f32[3,32,512]{2,1,0:T(8,128)S(1)}, u32[]{:S(2)}, u32[]{:S(2)}) collective-permute-start(f32[3,32,512]{2,1,0:T(8,128)S(1)} %get-tuple-element.88), channel_id=1, source_target_pairs={{1,0},{2,1},{3,2},{4,3},{5,4},{6,5},{7,6},{8,7},{9,8},{10,9},{11,1... | collective-permute-start | bytes 589832 | tf_op jit(solution)/shard_map/ppermute | solution.py:17
  26.7 71.0 %copy-start.8 = (f32[4,32,512]{2,1,0:T(8,128)S(1)}, f32[4,32,512]{2,1,0:T(8,128)}, u32[]{:S(2)}) copy-start(f32[4,32,512]{2,1,0:T(8,128)} %param.10) | copy-start | bytes 786436
  26.9 70.9 %copy-start.60 = (f32[128]{0:T(128)}, f32[128]{0:T(128)S(1)}, u32[]{:S(2)}) copy-start(f32[128]{0:T(128)S(1)} %div.15) | copy-start | bytes 1540
  27.1 70.7 %copy-start.61 = (f32[128]{0:T(128)}, f32[128]{0:T(128)S(1)}, u32[]{:S(2)}) copy-start(f32[128]{0:T(128)S(1)} %rsqrt.12) | copy-start | bytes 1540
  108.3 194.2 %all-reduce.5.cloned.1.call-start = ((), (), s32[]{:S(2)}) async-start(), calls=%async_computation.4 | async-start | bytes 229376 | tf_op jit(solution)/shard_map/psum | solution.py:130
  113.9 64.1 %collective-permute-start.2 = (f32[3,32,512]{2,1,0:T(8,128)S(1)}, f32[3,32,512]{2,1,0:T(8,128)S(1)}, u32[]{:S(2)}, u32[]{:S(2)}) collective-permute-start(f32[3,32,512]{2,1,0:T(8,128)S(1)} %bitcast.203), channel_id=1, source_target_pairs={{0,1},{1,2},{2,3},{3,4},{4,5},{5,6},{6,7},{7,8},{8,9},{9,10},{10,1... | collective-permute-start | bytes 589832 | tf_op jit(solution)/shard_map/ppermute | solution.py:14
  116.3 61.7 %collective-permute-start.3 = (f32[3,32,512]{2,1,0:T(8,128)S(1)}, f32[3,32,512]{2,1,0:T(8,128)S(1)}, u32[]{:S(2)}, u32[]{:S(2)}) collective-permute-start(f32[3,32,512]{2,1,0:T(8,128)S(1)} %bitcast.202), channel_id=1, source_target_pairs={{1,0},{2,1},{3,2},{4,3},{5,4},{6,5},{7,6},{8,7},{9,8},{10,9},{11,1... | collective-permute-start | bytes 589832 | tf_op jit(solution)/shard_map/ppermute | solution.py:17
  118.8 59.3 %copy-start.12 = (f32[1,1,512]{2,1,0:T(1,128)S(1)}, f32[1,1,512]{2,1,0:T(1,128)}, u32[]{:S(2)}) copy-start(f32[1,1,512]{2,1,0:T(1,128)} %copy-done.11) | copy-start | bytes 6148
  118.8 59.3 %copy-start.14 = (f32[1,1,512]{2,1,0:T(1,128)S(1)}, f32[1,1,512]{2,1,0:T(1,128)}, u32[]{:S(2)}) copy-start(f32[1,1,512]{2,1,0:T(1,128)} %copy-done.13) | copy-start | bytes 6148
  118.8 59.3 %copy-start.16 = (f32[1,1,512]{2,1,0:T(1,128)S(1)}, f32[1,1,512]{2,1,0:T(1,128)}, u32[]{:S(2)}) copy-start(f32[1,1,512]{2,1,0:T(1,128)} %copy-done.15) | copy-start | bytes 6148
  118.8 59.3 %copy-start.18 = (f32[1,1,512]{2,1,0:T(1,128)S(1)}, f32[1,1,512]{2,1,0:T(1,128)}, u32[]{:S(2)}) copy-start(f32[1,1,512]{2,1,0:T(1,128)} %copy-done.17) | copy-start | bytes 6148
  118.9 59.3 %copy-start.20 = (f32[1,1,512]{2,1,0:T(1,128)S(1)}, f32[1,1,512]{2,1,0:T(1,128)}, u32[]{:S(2)}) copy-start(f32[1,1,512]{2,1,0:T(1,128)} %copy-done.19) | copy-start | bytes 6148
  118.9 59.3 %copy-start.22 = (f32[1,1,512]{2,1,0:T(1,128)S(1)}, f32[1,1,512]{2,1,0:T(1,128)}, u32[]{:S(2)}) copy-start(f32[1,1,512]{2,1,0:T(1,128)} %copy-done.21) | copy-start | bytes 6148
  118.9 59.3 %copy-start.24 = (f32[1,1,512]{2,1,0:T(1,128)S(1)}, f32[1,1,512]{2,1,0:T(1,128)}, u32[]{:S(2)}) copy-start(f32[1,1,512]{2,1,0:T(1,128)} %copy-done.23) | copy-start | bytes 6148
  118.9 59.3 %copy-start.26 = (f32[1,1,512]{2,1,0:T(1,128)S(1)}, f32[1,1,512]{2,1,0:T(1,128)}, u32[]{:S(2)}) copy-start(f32[1,1,512]{2,1,0:T(1,128)} %copy-done.25) | copy-start | bytes 6148
  118.9 59.3 %copy-start.28 = (f32[1,1,512]{2,1,0:T(1,128)S(1)}, f32[1,1,512]{2,1,0:T(1,128)}, u32[]{:S(2)}) copy-start(f32[1,1,512]{2,1,0:T(1,128)} %copy-done.27) | copy-start | bytes 6148
  118.9 59.3 %copy-start.30 = (f32[1,1,512]{2,1,0:T(1,128)S(1)}, f32[1,1,512]{2,1,0:T(1,128)}, u32[]{:S(2)}) copy-start(f32[1,1,512]{2,1,0:T(1,128)} %copy-done.29) | copy-start | bytes 6148
  118.9 59.3 %copy-start.32 = (f32[1,1,512]{2,1,0:T(1,128)S(1)}, f32[1,1,512]{2,1,0:T(1,128)}, u32[]{:S(2)}) copy-start(f32[1,1,512]{2,1,0:T(1,128)} %copy-done.31) | copy-start | bytes 6148
  118.9 59.3 %copy-start.34 = (f32[1,1,512]{2,1,0:T(1,128)S(1)}, f32[1,1,512]{2,1,0:T(1,128)}, u32[]{:S(2)}) copy-start(f32[1,1,512]{2,1,0:T(1,128)} %copy-done.33) | copy-start | bytes 6148
  118.9 59.3 %copy-start.36 = (f32[1,1,512]{2,1,0:T(1,128)S(1)}, f32[1,1,512]{2,1,0:T(1,128)}, u32[]{:S(2)}) copy-start(f32[1,1,512]{2,1,0:T(1,128)} %copy-done.35) | copy-start | bytes 6148
  (47 other events, 820.0 us)
Sparse Core Ops, SparseCore 0:
  10.8 44.0 all-gather.2
  57.6 40.1 all-gather.4
  108.4 103.3 reduce-scatter.1
  215.7 86.8 all-reduce.4
where the time goes:
time: 312 us; the launch traced here: 311 us
  waiting for transfers between devices  189 us (61%)
  blocking collectives  57.3 us (18%)
  other arithmetic  16.1 us (5%)
  between operations  14.9 us (5%)
  matrix products  11.5 us (4%)
  starting transfers between devices  11.1 us (4%)
  local copies, waits for them, and re-layouts  10.9 us (3%)
    psum x1, waiting for transfers between devices, per_device(): lax.psum((kernel_term, norm_scale * gain_term, norm_scale * bias_term, no...  88.9 us
    psum x1, blocking collectives, per_device(): lax.psum((kernel_term, norm_scale * gain_term, norm_scale * bias_term, no...  57.3 us
    all_gather x1, waiting for transfers between devices, per_device(): lax.all_gather(out_narrow, 'row', axis=0, tiled=True)  40.8 us
    reduce_scatter x1, waiting for transfers between devices, per_device(): lax.psum_scatter(jnp.concatenate([norm_scale * contract_first(normed_out,...  31 us
    all_gather x1, waiting for transfers between devices, per_device(): lax.all_gather(in_narrow, 'row', axis=0, tiled=True)  27.6 us
    ppermute x2, starting transfers between devices, extended(): lax.ppermute(lax.slice_in_dim(block, block.shape[dim] - width, None, axis...  6.84 us
    dot_general x2, matrix products, contract_last(): lax.dot_general(left, right, (((1,), (1,)), ((), ())), preferred_element_...  6.52 us
  transfers between devices with their start and end apart: 8, of which 5 were waited for; matrix products, arithmetic and copies ran while one was open for 7% of the time, Pallas kernels for 0%

commit v1 on v0

v1 whole, which is shorter than its diff:
```python
import itertools
import math

import jax
import jax.numpy as jnp
from jax import lax
from jax.sharding import PartitionSpec as P

NARROW = jnp.bfloat16
WIDE = jnp.float32


def swap(value, bit):
    count = lax.axis_size("row")
    return lax.ppermute(value, "row", [(i, i ^ bit) for i in range(count)])


def shift(value, step):
    count = lax.axis_size("row")
    pairs = [(i, i + step) for i in range(count) if 0 <= i + step < count]
    return lax.ppermute(value, "row", pairs)


def conv_taps(padded, kernel, row_count, col_count):
    running = jnp.zeros((row_count, col_count, padded.shape[2]), jnp.float32)
    for tap_row in range(7):
        for tap_col in range(7):
            running = (
                running
                + padded[tap_row : tap_row + row_count, tap_col : tap_col + col_count]
                * kernel[tap_row, tap_col]
            )
    return running


def rimmed(block, low, high):
    joined = jnp.concatenate([low.astype(WIDE), block, high.astype(WIDE)], axis=0)
    return jnp.pad(joined, ((0, 0), (3, 3), (0, 0)))


def dot(left, right, dims):
    return lax.dot_general(left, right, (dims, ((), ())), preferred_element_type=WIDE)


def flipped(blocks, axis, bit_set):
    return jnp.where(bit_set == 1, jnp.flip(blocks, axis), blocks)


def canonical(blocks, me, bit_count):
    tail = blocks.shape[1:]
    blocks = blocks.reshape((2,) * bit_count + tail)
    for place in range(bit_count):
        blocks = flipped(blocks, bit_count - 1 - place, (me >> place) & 1)
    return blocks.reshape((2**bit_count,) + tail)


def per_device(
    features, cotangent, kernel, norm_gain, norm_bias, in_weight, in_bias, out_weight, layer_scale
):
    row_count, col_count, channels = features.shape
    own_rows, hidden_count = in_weight.shape
    pixels = row_count * col_count
    count = lax.axis_size("row")
    bit_count = count.bit_length() - 1
    me = lax.axis_index("row")
    far = count // 2
    core_bit = me & 1
    far_bit = me >> (bit_count - 1)
    quarter = hidden_count // 4
    mine = 2 * far_bit + core_bit
    norm_scale = 1.0 / math.sqrt(pixels * count)
    peers = list(range(1, count // 4))

    both = jnp.stack([in_weight, out_weight]).astype(NARROW)
    both = both.reshape(2, own_rows, 2, 2, quarter)
    keep = lax.dynamic_index_in_dim(both, core_bit, 3, keepdims=False)
    give = lax.dynamic_index_in_dim(both, 1 - core_bit, 3, keepdims=False)
    got = swap(give, 1)
    pair = jnp.stack([keep, got])
    stay = lax.dynamic_index_in_dim(pair, far_bit, 3, keepdims=False)
    leave = lax.dynamic_index_in_dim(pair, 1 - far_bit, 3, keepdims=False)
    got = swap(leave, far)
    block = jnp.stack([stay, got])

    narrow_rim = features.astype(NARROW)
    low = shift(narrow_rim[row_count - 3 :], 1)
    high = shift(narrow_rim[:3], -1)

    flat_input = features.reshape(-1, channels)
    flat_cotan = cotangent.reshape(-1, channels)
    branch_grad = (layer_scale * flat_cotan).astype(NARROW)

    def group_gather(value):
        two = jnp.stack([value, swap(value, far)])
        four = jnp.stack([two, swap(two, 1)])
        return four.reshape(-1, channels)

    branch_all = group_gather(branch_grad)
    gathered = [block] + [swap(block, 2 * p) for p in peers]
    weights = jnp.stack(gathered)
    weights = jnp.moveaxis(weights, 0, 1).reshape(count, 2, own_rows, quarter)
    weights = canonical(weights, me, bit_count)
    weights = jnp.moveaxis(weights, 1, 0).reshape(2, channels, quarter)
    in_narrow, out_narrow = weights[0], weights[1]

    padded = rimmed(features, low, high)
    convolved = conv_taps(padded, kernel, row_count, col_count).reshape(-1, channels)
    average = jnp.mean(convolved, axis=1, keepdims=True)
    centred = convolved - average
    inv_std = lax.rsqrt(jnp.mean(centred * centred, axis=1, keepdims=True) + 1e-06)
    normed = centred * inv_std
    normed_out = (normed * norm_gain + norm_bias).astype(NARROW)
    normed_all = group_gather(normed_out)

    bias_part = lax.dynamic_slice_in_dim(in_bias, mine * quarter, quarter)
    preact = dot(normed_all, in_narrow, ((1,), (0,))) + bias_part
    cdf_value = 0.5 * (1.0 + jax.scipy.special.erf(preact * 0.7071067811865476))
    activated = (preact * cdf_value).astype(NARROW)
    act_grad = dot(branch_all, out_narrow, ((1,), (0,)))
    gelu_slope = cdf_value + preact * jnp.exp(-0.5 * preact * preact) * 0.3989422804014327
    hidden_grad = act_grad * gelu_slope
    in_bias_part = jnp.sum(hidden_grad, axis=0)
    hidden_narrow = hidden_grad.astype(NARROW)

    def group_sum(partial):
        partial = partial.reshape(2, 2, pixels, channels)
        got = swap(partial[1].astype(NARROW), 1)
        half = partial[0] + got.astype(WIDE)
        got = swap(half[1].astype(NARROW), far)
        return half[0] + got.astype(WIDE)

    out_grad = group_sum(dot(hidden_narrow, in_narrow, ((1,), (1,))))
    mixed = group_sum(dot(activated, out_narrow, ((1,), (1,))))
    output = (flat_input + layer_scale * mixed).reshape(row_count, col_count, channels)
    scale_term = jnp.sum(flat_cotan * mixed, axis=0)

    grads = norm_scale * jnp.stack(
        [
            dot(normed_all, hidden_narrow, ((0,), (0,))),
            dot(branch_all, activated, ((0,), (0,))),
        ]
    )
    grads = jnp.moveaxis(grads.reshape(2, count, own_rows, quarter), 1, 0)
    grads = canonical(grads, me, bit_count)
    grads = grads.reshape(2, count // 4, 2, 2, own_rows, quarter)
    total = grads[:, 0]
    for p in peers:
        total = total + swap(grads[:, p].astype(NARROW), 2 * p).astype(WIDE)
    got = swap(total[1].astype(NARROW), far).astype(WIDE)
    halves = flipped(jnp.stack([total[0], got]), 0, far_bit)
    got = swap(halves[:, 1].astype(NARROW), 1).astype(WIDE)
    quarters = flipped(jnp.stack([halves[:, 0], got], axis=1), 1, core_bit)
    final = jnp.transpose(quarters, (2, 3, 0, 1, 4)).reshape(2, own_rows, hidden_count)
    in_weight_grad, out_weight_grad = final[0], final[1]

    gain_term = jnp.sum(out_grad * normed, axis=0)
    bias_term = jnp.sum(out_grad, axis=0)
    normed_grad = out_grad * norm_gain
    conv_grad = inv_std * (
        normed_grad
        - jnp.mean(normed_grad, axis=1, keepdims=True)
        - normed * jnp.mean(normed_grad * normed, axis=1, keepdims=True)
    )
    conv_grid = conv_grad.reshape(row_count, col_count, channels)
    narrow_grid = conv_grid.astype(NARROW)
    grad_low = shift(narrow_grid[row_count - 3 :], 1)
    grad_high = shift(narrow_grid[:3], -1)

    kernel_rows = []
    for tap_row in range(7):
        for tap_col in range(7):
            kernel_rows.append(
                jnp.sum(
                    padded[tap_row : tap_row + row_count, tap_col : tap_col + col_count]
                    * conv_grid,
                    axis=(0, 1),
                )
            )
    in_bias_term = lax.dynamic_update_slice_in_dim(
        jnp.zeros((hidden_count,), WIDE), in_bias_part, mine * quarter, 0
    )
    small = jnp.concatenate(
        [
            jnp.concatenate(kernel_rows),
            gain_term,
            bias_term,
            scale_term,
            in_bias_term,
        ]
    )
    small = norm_scale * small
    lengths = (49 * channels, channels, channels, channels, hidden_count)
    small = small.reshape(2, -1, 128)
    stay = lax.dynamic_index_in_dim(small, core_bit, 0, keepdims=False)
    leave = lax.dynamic_index_in_dim(small, 1 - core_bit, 0, keepdims=False)
    half = stay + swap(leave, 1)
    for place in range(1, bit_count):
        half = half + swap(half, 1 << place)
    small = flipped(jnp.stack([half, swap(half, 1)]), 0, core_bit).reshape(-1)
    ends = list(itertools.accumulate(lengths))
    parts = [small[end - size : end] for end, size in zip(ends, lengths)]

    grad_padded = rimmed(conv_grid, grad_low, grad_high)
    input_grad = cotangent
    for tap_row in range(7):
        for tap_col in range(7):
            input_grad = (
                input_grad
                + kernel[tap_row, tap_col]
                * grad_padded[
                    6 - tap_row : 6 - tap_row + row_count, 6 - tap_col : 6 - tap_col + col_count
                ]
            )
    return (
        output,
        input_grad,
        in_weight_grad,
        out_weight_grad,
        parts[0].reshape(7, 7, channels),
        parts[1],
        parts[2],
        parts[4],
        parts[3],
    )


def solution(mesh):
    return jax.shard_map(
        per_device,
        mesh=mesh,
        in_specs=(
            P(("grp", "row"), None, None),
            P(("grp", "row"), None, None),
            P(),
            P(),
            P(),
            P("row", None),
            P(),
            P("row", None),
            P(),
        ),
        out_specs=(
            P(("grp", "row"), None, None),
            P(("grp", "row"), None, None),
            P(("grp", "row"), None),
            P(("grp", "row"), None),
            P("grp", None, None),
            P("grp"),
            P("grp"),
            P("grp"),
            P("grp"),
        ),
        check_vma=False,
    )
```

time: 312 us -> 143 us (0.46)
  waiting for transfers between devices: 189 us -> 59.6 us
  blocking collectives: 57.3 us -> 0 us
  starting transfers between devices: 11.1 us -> 34.3 us
  between operations: 14.9 us -> 3.03 us
  other arithmetic: 16.1 us -> 22.8 us
  local copies, waits for them, and re-layouts: 10.9 us -> 17.1 us
  matrix products: 11.5 us -> 5.99 us
    psum x1 -> x0, waiting for transfers between devices: 88.9 us -> none  [per_device(): lax.psum((kernel_term, norm_scale * gain_term, norm_scale * bias_term, no...]
    all_gather x2 -> x0, waiting for transfers between devices: 68.4 us -> none  [the longest x1 40.8 us: per_device(): lax.all_gather(out_narrow, 'row', axis=0, tiled=True)]
    ppermute x4 -> x27, waiting for transfers between devices: 0.61 us -> 59.6 us  [the longest x23 53.9 us: swap(): return lax.ppermute(value, 'row', [(i, i ^ bit) for i in range(count)])]
    psum x1 -> x0, blocking collectives: 57.3 us -> none  [per_device(): lax.psum((kernel_term, norm_scale * gain_term, norm_scale * bias_term, no...]
    reduce_scatter x1 -> x0, waiting for transfers between devices: 31 us -> none  [per_device(): lax.psum_scatter(jnp.concatenate([norm_scale * contract_first(normed_out,...]
    ppermute x4 -> x27, starting transfers between devices: 10.9 us -> 34.3 us  [the longest x23 23.5 us: swap(): return lax.ppermute(value, 'row', [(i, i ^ bit) for i in range(count)])]
    another operation x0 -> x12, other arithmetic: none -> 6.07 us  [the longest x4 1.99 us: group_gather(): four = jnp.stack([two, swap(two, 1)])]
    dot_general x6, matrix products: 11.5 us -> 5.99 us  [dot(): lax.dot_general(left, right, (dims, ((), ())), preferred_element_type=WIDE)]
  transfers between devices with their start and end apart: 8 -> 27, of which waited for: 5 -> 16; matrix products, arithmetic and copies ran while one was open for 7% -> 19% of each run, Pallas kernels for 0% -> 0%
where the time goes in v1:
time: 143 us
  waiting for transfers between devices  59.6 us (42%)
  starting transfers between devices  34.3 us (24%)
  other arithmetic  22.8 us (16%)
  local copies, waits for them, and re-layouts  17.1 us (12%)
  matrix products  5.99 us (4%)
  between operations  3.03 us (2%)
    ppermute x23, waiting for transfers between devices, swap(): return lax.ppermute(value, 'row', [(i, i ^ bit) for i in range(count)])  53.9 us
    ppermute x23, starting transfers between devices, swap(): return lax.ppermute(value, 'row', [(i, i ^ bit) for i in range(count)])  23.5 us
    ppermute x4, starting transfers between devices, shift(): return lax.ppermute(value, 'row', pairs)  10.8 us
    dot_general x6, matrix products, dot(): lax.dot_general(left, right, (dims, ((), ())), preferred_element_type=WIDE)  5.99 us
    ppermute x4, waiting for transfers between devices, shift(): return lax.ppermute(value, 'row', pairs)  5.73 us
    add x1, other arithmetic, per_device(): input_grad + kernel[tap_row, tap_col] * grad_padded[6 - tap_row:6 - tap_r...  3.38 us
    reduce_sum x1, other arithmetic, per_device(): average = jnp.mean(convolved, axis=1, keepdims=True)  3.13 us
    select_n x10, other arithmetic, flipped(): return jnp.where(bit_set == 1, jnp.flip(blocks, axis), blocks)  2.94 us
  transfers between devices with their start and end apart: 27, of which 16 were waited for; matrix products, arithmetic and copies ran while one was open for 19% of the time, Pallas kernels for 0%

profile of v1, /device:TPU:1, one launch (start us, length us, event | category | flops | bytes accessed | tf_op | source)
XLA Modules:
  0.0 142.9 jit_solution(15039575033589399121)
XLA Ops:
  3.8 4.5 %collective-permute-start = (bf16[3,32,512]{2,1,0:T(8,128)(2,1)S(1)}, bf16[3,32,512]{2,1,0:T(8,128)(2,1)S(1)}, u32[]{:S(2)}, u32[]{:S(2)}) collective-permute-start(bf16[3,32,512]{2,1,0:T(8,128)(2,1)S(1)} %get-tuple-element.90), channel_id=1, source_target_pairs={{0,1},{1,2},{2,3},{3,4},{4,5},{5,6},{6,7},{7,8},{8,9},{9,10},{10,1... | collective-permute-start | bytes 294920 | tf_op jit(solution)/shard_map/ppermute | solution.py:21
  8.3 1.9 %collective-permute-start.1 = (bf16[3,32,512]{2,1,0:T(8,128)(2,1)S(1)}, bf16[3,32,512]{2,1,0:T(8,128)(2,1)S(1)}, u32[]{:S(2)}, u32[]{:S(2)}) collective-permute-start(bf16[3,32,512]{2,1,0:T(8,128)(2,1)S(1)} %get-tuple-element.91), channel_id=1, source_target_pairs={{1,0},{2,1},{3,2},{4,3},{5,4},{6,5},{7,6},{8,7},{9,8},{10,9},{11,1... | collective-permute-start | bytes 294920 | tf_op jit(solution)/shard_map/ppermute | solution.py:21
  12.0 2.3 %collective-permute-done.1 = bf16[3,32,512]{2,1,0:T(8,128)(2,1)S(1)} collective-permute-done((bf16[3,32,512]{2,1,0:T(8,128)(2,1)S(1)}, bf16[3,32,512]{2,1,0:T(8,128)(2,1)S(1)}, u32[]{:S(2)}, u32[]{:S(2)}) %collective-permute-start.1) | collective-permute-done | bytes 98336 | tf_op jit(solution)/shard_map/ppermute | solution.py:21
  14.4 3.1 %fusion.98 = (f32[4,32]{1,0:T(4,128)S(1)}, f32[4,32,512]{2,1,0:T(8,128)S(1)}) fusion(f32[512]{0:T(512)} %bitcast.49, f32[10,38,512]{2,1,0:T(8,128)S(1)} %select_maximum_fusion.2, f32[512]{0:T(512)} %bitcast.48, f32[512]{0:T(512)S(1)} %bitcast.308, f32[512]{0:T(512)S(1)} %bitcast.310, f32[3,32,512]{2,1,0:T(8,128)S(1)} %convert_element_type.114, ...), kind=kLoop, calls=%fused_computation.341 | loop fusion | flops 6815616 | bytes 12028416 | tf_op jit(solution)/shard_map/reduce_sum | solution.py:108
  18.5 2.4 %collective-permute-start.2 = (bf16[128,512]{1,0:T(8,128)(2,1)S(1)}, bf16[128,512]{1,0:T(8,128)(2,1)S(1)}, u32[]{:S(2)}, u32[]{:S(2)}) collective-permute-start(bf16[128,512]{1,0:T(8,128)(2,1)S(1)} %add_convert_fusion), channel_id=1, source_target_pairs={{0,8},{1,9},{2,10},{3,11},{4,12},{5,13},{6,14},{7,15},{8,0},{9,1},... | collective-permute-start | bytes 393224 | tf_op jit(solution)/shard_map/ppermute | solution.py:15
  21.1 9.4 %collective-permute-done.2 = bf16[128,512]{1,0:T(8,128)(2,1)S(1)} collective-permute-done((bf16[128,512]{1,0:T(8,128)(2,1)S(1)}, bf16[128,512]{1,0:T(8,128)(2,1)S(1)}, u32[]{:S(2)}, u32[]{:S(2)}) %collective-permute-start.2) | collective-permute-done | bytes 131104 | tf_op jit(solution)/shard_map/ppermute | solution.py:15
  30.8 2.3 %collective-permute-done.5 = bf16[2,2,32,512]{3,2,1,0:T(8,128)(2,1)S(1)} collective-permute-done((bf16[2,2,32,512]{3,2,1,0:T(8,128)(2,1)S(1)}, bf16[2,2,32,512]{3,2,1,0:T(8,128)(2,1)S(1)}, u32[]{:S(2)}, u32[]{:S(2)}) %collective-permute-start.5) | collective-permute-done | bytes 131104 | tf_op jit(solution)/shard_map/ppermute | solution.py:15
  33.9 1.9 %collective-permute-start.8 = (bf16[2,2,2,32,512]{4,3,2,1,0:T(8,128)(2,1)S(1)}, bf16[2,2,2,32,512]{4,3,2,1,0:T(8,128)(2,1)}, u32[]{:S(2)}, u32[]{:S(2)}) collective-permute-start(bf16[2,2,2,32,512]{4,3,2,1,0:T(8,128)(2,1)S(1)} %get-tuple-element.81), channel_id=1, source_target_pairs={{0,6},{1,7},{2,4},{3,5},{4,2},{5,3},{6,0},{7,1},{8,14},{9,15},{10,... | collective-permute-start | bytes 786440 | tf_op jit(solution)/shard_map/ppermute | solution.py:15
  36.6 4.0 %collective-permute-done.6 = bf16[2,2,2,32,512]{4,3,2,1,0:T(8,128)(2,1)S(1)} collective-permute-done((bf16[2,2,2,32,512]{4,3,2,1,0:T(8,128)(2,1)S(1)}, bf16[2,2,2,32,512]{4,3,2,1,0:T(8,128)(2,1)S(1)}, u32[]{:S(2)}, u32[]{:S(2)}) %collective-permute-start.6) | collective-permute-done | bytes 262176 | tf_op jit(solution)/shard_map/ppermute | solution.py:15
  41.6 5.6 %collective-permute-done.8 = bf16[2,2,2,32,512]{4,3,2,1,0:T(8,128)(2,1)} collective-permute-done((bf16[2,2,2,32,512]{4,3,2,1,0:T(8,128)(2,1)S(1)}, bf16[2,2,2,32,512]{4,3,2,1,0:T(8,128)(2,1)}, u32[]{:S(2)}, u32[]{:S(2)}) %collective-permute-start.8) | collective-permute-done | bytes 262176 | tf_op jit(solution)/shard_map/ppermute | solution.py:15
  54.6 2.4 %collective-permute-start.10 = (bf16[128,512]{1,0:T(8,128)(2,1)S(1)}, bf16[128,512]{1,0:T(8,128)(2,1)S(1)}, u32[]{:S(2)}, u32[]{:S(2)}) collective-permute-start(bf16[128,512]{1,0:T(8,128)(2,1)S(1)} %fusion.86), channel_id=1, source_target_pairs={{0,8},{1,9},{2,10},{3,11},{4,12},{5,13},{6,14},{7,15},{8,0},{9,1},... | collective-permute-start | bytes 393224 | tf_op jit(solution)/shard_map/ppermute | solution.py:15
  57.0 6.1 %collective-permute-done.10 = bf16[128,512]{1,0:T(8,128)(2,1)S(1)} collective-permute-done((bf16[128,512]{1,0:T(8,128)(2,1)S(1)}, bf16[128,512]{1,0:T(8,128)(2,1)S(1)}, u32[]{:S(2)}, u32[]{:S(2)}) %collective-permute-start.10) | collective-permute-done | bytes 131104 | tf_op jit(solution)/shard_map/ppermute | solution.py:15
  64.5 4.7 %collective-permute-done.11 = bf16[128,512]{1,0:T(8,128)(2,1)S(1)} collective-permute-done((bf16[128,512]{1,0:T(8,128)(2,1)S(1)}, bf16[128,512]{1,0:T(8,128)(2,1)S(1)}, u32[]{:S(2)}, u32[]{:S(2)}) %collective-permute-start.11) | collective-permute-done | bytes 131104 | tf_op jit(solution)/shard_map/ppermute | solution.py:15
  70.0 5.1 %collective-permute-start.12 = (bf16[2,128,512]{2,1,0:T(8,128)(2,1)}, bf16[2,128,512]{2,1,0:T(8,128)(2,1)}, u32[]{:S(2)}, u32[]{:S(2)}) collective-permute-start(bf16[2,128,512]{2,1,0:T(8,128)(2,1)} %get-tuple-element.79), channel_id=1, source_target_pairs={{0,1},{1,0},{2,3},{3,2},{4,5},{5,4},{6,7},{7,6},{8,9},{9,8},{10,11... | collective-permute-start | bytes 786440 | tf_op jit(solution)/shard_map/ppermute | solution.py:15
  77.7 2.7 %fusion.107 = (f32[512]{0:T(512)}, bf16[512,512]{1,0:T(8,128)(2,1)S(1)}) fusion(f32[512,512]{1,0:T(8,128)} %get-tuple-element.145, bf16[512,512]{1,0:T(8,128)(2,1)S(1)} %bitcast.279, bf16[512,512]{1,0:T(8,128)(2,1)} %bitcast.287), kind=kOutput, calls=%fused_computation.350 | convolution fusion | flops 271318528 | bytes 2623488 | tf_op jit(solution)/shard_map/dot_general | solution.py:42
  87.0 2.3 %collective-permute-start.19 = (bf16[2,2,2,32,512]{4,3,2,1,0:T(8,128)(2,1)}, bf16[2,2,2,32,512]{4,3,2,1,0:T(8,128)(2,1)}, u32[]{:S(2)}, u32[]{:S(2)}) collective-permute-start(bf16[2,2,2,32,512]{4,3,2,1,0:T(8,128)(2,1)} %get-tuple-element.69), channel_id=1, source_target_pairs={{0,6},{1,7},{2,4},{3,5},{4,2},{5,3},{6,0},{7,1},{8,14},{9,15},{10,... | collective-permute-start | bytes 786440 | tf_op jit(solution)/shard_map/ppermute | solution.py:15
  92.7 1.8 %collective-permute-done.17 = bf16[2,2,2,32,512]{4,3,2,1,0:T(8,128)(2,1)} collective-permute-done((bf16[2,2,2,32,512]{4,3,2,1,0:T(8,128)(2,1)}, bf16[2,2,2,32,512]{4,3,2,1,0:T(8,128)(2,1)}, u32[]{:S(2)}, u32[]{:S(2)}) %collective-permute-start.17) | collective-permute-done | bytes 262176 | tf_op jit(solution)/shard_map/ppermute | solution.py:15
  94.5 9.3 %collective-permute-done.19 = bf16[2,2,2,32,512]{4,3,2,1,0:T(8,128)(2,1)} collective-permute-done((bf16[2,2,2,32,512]{4,3,2,1,0:T(8,128)(2,1)}, bf16[2,2,2,32,512]{4,3,2,1,0:T(8,128)(2,1)}, u32[]{:S(2)}, u32[]{:S(2)}) %collective-permute-start.19) | collective-permute-done | bytes 262176 | tf_op jit(solution)/shard_map/ppermute | solution.py:15
  109.8 2.6 %collective-permute-done.20 = bf16[2,2,32,512]{3,2,1,0:T(8,128)(2,1)S(1)} collective-permute-done((bf16[2,2,32,512]{3,2,1,0:T(8,128)(2,1)S(1)}, bf16[2,2,32,512]{3,2,1,0:T(8,128)(2,1)S(1)}, u32[]{:S(2)}, u32[]{:S(2)}) %collective-permute-start.20) | collective-permute-done | bytes 131104 | tf_op jit(solution)/shard_map/ppermute | solution.py:15
  116.9 2.5 %collective-permute-start.15 = (bf16[3,32,512]{2,1,0:T(8,128)(2,1)S(1)}, bf16[3,32,512]{2,1,0:T(8,128)(2,1)S(1)}, u32[]{:S(2)}, u32[]{:S(2)}) collective-permute-start(bf16[3,32,512]{2,1,0:T(8,128)(2,1)S(1)} %get-tuple-element.89), channel_id=1, source_target_pairs={{0,1},{1,2},{2,3},{3,4},{4,5},{5,6},{6,7},{7,8},{8,9},{9,10},{10,1... | collective-permute-start | bytes 294920 | tf_op jit(solution)/shard_map/ppermute | solution.py:21
  119.3 1.9 %collective-permute-start.16 = (bf16[3,32,512]{2,1,0:T(8,128)(2,1)S(1)}, bf16[3,32,512]{2,1,0:T(8,128)(2,1)S(1)}, u32[]{:S(2)}, u32[]{:S(2)}) collective-permute-start(bf16[3,32,512]{2,1,0:T(8,128)(2,1)S(1)} %get-tuple-element.88), channel_id=1, source_target_pairs={{1,0},{2,1},{3,2},{4,3},{5,4},{6,5},{7,6},{8,7},{9,8},{10,9},{11,1... | collective-permute-start | bytes 294920 | tf_op jit(solution)/shard_map/ppermute | solution.py:21
  122.0 3.5 %collective-permute-done.16 = bf16[3,32,512]{2,1,0:T(8,128)(2,1)S(1)} collective-permute-done((bf16[3,32,512]{2,1,0:T(8,128)(2,1)S(1)}, bf16[3,32,512]{2,1,0:T(8,128)(2,1)S(1)}, u32[]{:S(2)}, u32[]{:S(2)}) %collective-permute-start.16) | collective-permute-done | bytes 98336 | tf_op jit(solution)/shard_map/ppermute | solution.py:21
  126.0 3.4 %fusion.22 = f32[4,32,512]{2,1,0:T(8,128)} fusion(f32[4,32,512]{2,1,0:T(8,128)S(1)} %bitcast.268, f32[3,32,512]{2,1,0:T(8,128)S(1)} %convert_element_type.130, f32[3,32,512]{2,1,0:T(8,128)S(1)} %convert_element_type.131, f32[10,38,512]{2,1,0:T(8,128)S(1)} %select_maximum_fusion, f32[4,32,512]{2,1,0:T(8,128)S(1)} %copy-done.6, f32[512]{0:T(512)} %bitcast.49, ...), kind=kLoop, calls=%fused_computation.76 | loop fusion | flops 6815744 | bytes 12290048 | tf_op jit(solution)/shard_map/add | solution.py:208
  134.7 3.7 %collective-permute-done.25 = f32[112,128]{1,0:T(8,128)S(1)} collective-permute-done((f32[112,128]{1,0:T(8,128)S(1)}, f32[112,128]{1,0:T(8,128)S(1)}, u32[]{:S(2)}, u32[]{:S(2)}) %collective-permute-start.25) | collective-permute-done | bytes 57376 | tf_op jit(solution)/shard_map/ppermute | solution.py:15
  (381 shorter events, 50.6 us)
Async XLA Ops:
  3.6 17.2 %collective-permute-start.4 = (bf16[2,32,2,512]{3,1,2,0:T(8,128)(2,1)S(1)}, bf16[2,32,2,512]{3,1,2,0:T(8,128)(2,1)S(1)}, u32[]{:S(2)}, u32[]{:S(2)}) collective-permute-start(bf16[2,32,2,512]{3,1,2,0:T(8,128)(2,1)S(1)} %bitcast.300), channel_id=1, source_target_pairs={{0,1},{1,0},{2,3},{3,2},{4,5},{5,4},{6,7},{7,6},{8,9},{9,8},{10,11... | collective-permute-start | bytes 393224 | tf_op jit(solution)/shard_map/ppermute | solution.py:15
  3.8 8.1 %collective-permute-start = (bf16[3,32,512]{2,1,0:T(8,128)(2,1)S(1)}, bf16[3,32,512]{2,1,0:T(8,128)(2,1)S(1)}, u32[]{:S(2)}, u32[]{:S(2)}) collective-permute-start(bf16[3,32,512]{2,1,0:T(8,128)(2,1)S(1)} %get-tuple-element.90), channel_id=1, source_target_pairs={{0,1},{1,2},{2,3},{3,4},{4,5},{5,6},{6,7},{7,8},{8,9},{9,10},{10,1... | collective-permute-start | bytes 294920 | tf_op jit(solution)/shard_map/ppermute | solution.py:21
  8.3 5.9 %collective-permute-start.1 = (bf16[3,32,512]{2,1,0:T(8,128)(2,1)S(1)}, bf16[3,32,512]{2,1,0:T(8,128)(2,1)S(1)}, u32[]{:S(2)}, u32[]{:S(2)}) collective-permute-start(bf16[3,32,512]{2,1,0:T(8,128)(2,1)S(1)} %get-tuple-element.91), channel_id=1, source_target_pairs={{1,0},{2,1},{3,2},{4,3},{5,4},{6,5},{7,6},{8,7},{9,8},{10,9},{11,1... | collective-permute-start | bytes 294920 | tf_op jit(solution)/shard_map/ppermute | solution.py:21
  18.5 12.1 %collective-permute-start.2 = (bf16[128,512]{1,0:T(8,128)(2,1)S(1)}, bf16[128,512]{1,0:T(8,128)(2,1)S(1)}, u32[]{:S(2)}, u32[]{:S(2)}) collective-permute-start(bf16[128,512]{1,0:T(8,128)(2,1)S(1)} %add_convert_fusion), channel_id=1, source_target_pairs={{0,8},{1,9},{2,10},{3,11},{4,12},{5,13},{6,14},{7,15},{8,0},{9,1},... | collective-permute-start | bytes 393224 | tf_op jit(solution)/shard_map/ppermute | solution.py:15
  20.9 12.2 %collective-permute-start.5 = (bf16[2,2,32,512]{3,2,1,0:T(8,128)(2,1)S(1)}, bf16[2,2,32,512]{3,2,1,0:T(8,128)(2,1)S(1)}, u32[]{:S(2)}, u32[]{:S(2)}) collective-permute-start(bf16[2,2,32,512]{3,2,1,0:T(8,128)(2,1)S(1)} %get-tuple-element.83), channel_id=1, source_target_pairs={{0,8},{1,9},{2,10},{3,11},{4,12},{5,13},{6,14},{7,15},{8,0},{9,1},... | collective-permute-start | bytes 393224 | tf_op jit(solution)/shard_map/ppermute | solution.py:15
  30.6 6.0 %collective-permute-start.3 = (bf16[2,128,512]{2,1,0:T(8,128)(2,1)S(1)}, bf16[2,128,512]{2,1,0:T(8,128)(2,1)S(1)}, u32[]{:S(2)}, u32[]{:S(2)}) collective-permute-start(bf16[2,128,512]{2,1,0:T(8,128)(2,1)S(1)} %get-tuple-element.87), channel_id=1, source_target_pairs={{0,1},{1,0},{2,3},{3,2},{4,5},{5,4},{6,7},{7,6},{8,9},{9,8},{10,11... | collective-permute-start | bytes 786440 | tf_op jit(solution)/shard_map/ppermute | solution.py:15
  33.1 7.6 %collective-permute-start.6 = (bf16[2,2,2,32,512]{4,3,2,1,0:T(8,128)(2,1)S(1)}, bf16[2,2,2,32,512]{4,3,2,1,0:T(8,128)(2,1)S(1)}, u32[]{:S(2)}, u32[]{:S(2)}) collective-permute-start(bf16[2,2,2,32,512]{4,3,2,1,0:T(8,128)(2,1)S(1)} %get-tuple-element.81), channel_id=1, source_target_pairs={{0,2},{1,3},{2,0},{3,1},{4,6},{5,7},{6,4},{7,5},{8,10},{9,11},{10,... | collective-permute-start | bytes 786440 | tf_op jit(solution)/shard_map/ppermute | solution.py:15
  33.7 8.0 %collective-permute-start.7 = (bf16[2,2,2,32,512]{4,3,2,1,0:T(8,128)(2,1)S(1)}, bf16[2,2,2,32,512]{4,3,2,1,0:T(8,128)(2,1)S(1)}, u32[]{:S(2)}, u32[]{:S(2)}) collective-permute-start(bf16[2,2,2,32,512]{4,3,2,1,0:T(8,128)(2,1)S(1)} %get-tuple-element.81), channel_id=1, source_target_pairs={{0,4},{1,5},{2,6},{3,7},{4,0},{5,1},{6,2},{7,3},{8,12},{9,13},{10,... | collective-permute-start | bytes 786440 | tf_op jit(solution)/shard_map/ppermute | solution.py:15
  33.9 13.3 %collective-permute-start.8 = (bf16[2,2,2,32,512]{4,3,2,1,0:T(8,128)(2,1)S(1)}, bf16[2,2,2,32,512]{4,3,2,1,0:T(8,128)(2,1)}, u32[]{:S(2)}, u32[]{:S(2)}) collective-permute-start(bf16[2,2,2,32,512]{4,3,2,1,0:T(8,128)(2,1)S(1)} %get-tuple-element.81), channel_id=1, source_target_pairs={{0,6},{1,7},{2,4},{3,5},{4,2},{5,3},{6,0},{7,1},{8,14},{9,15},{10,... | collective-permute-start | bytes 786440 | tf_op jit(solution)/shard_map/ppermute | solution.py:15
  54.6 8.5 %collective-permute-start.10 = (bf16[128,512]{1,0:T(8,128)(2,1)S(1)}, bf16[128,512]{1,0:T(8,128)(2,1)S(1)}, u32[]{:S(2)}, u32[]{:S(2)}) collective-permute-start(bf16[128,512]{1,0:T(8,128)(2,1)S(1)} %fusion.86), channel_id=1, source_target_pairs={{0,8},{1,9},{2,10},{3,11},{4,12},{5,13},{6,14},{7,15},{8,0},{9,1},... | collective-permute-start | bytes 393224 | tf_op jit(solution)/shard_map/ppermute | solution.py:15
  64.5 4.7 %collective-permute-start.11 = (bf16[128,512]{1,0:T(8,128)(2,1)S(1)}, bf16[128,512]{1,0:T(8,128)(2,1)S(1)}, u32[]{:S(2)}, u32[]{:S(2)}) collective-permute-start(bf16[128,512]{1,0:T(8,128)(2,1)S(1)} %get-tuple-element.77), channel_id=1, source_target_pairs={{0,8},{1,9},{2,10},{3,11},{4,12},{5,13},{6,14},{7,15},{8,0},{9,1},... | collective-permute-start | bytes 393224 | tf_op jit(solution)/shard_map/ppermute | solution.py:15
  70.0 6.6 %collective-permute-start.12 = (bf16[2,128,512]{2,1,0:T(8,128)(2,1)}, bf16[2,128,512]{2,1,0:T(8,128)(2,1)}, u32[]{:S(2)}, u32[]{:S(2)}) collective-permute-start(bf16[2,128,512]{2,1,0:T(8,128)(2,1)} %get-tuple-element.79), channel_id=1, source_target_pairs={{0,1},{1,0},{2,3},{3,2},{4,5},{5,4},{6,7},{7,6},{8,9},{9,8},{10,11... | collective-permute-start | bytes 786440 | tf_op jit(solution)/shard_map/ppermute | solution.py:15
  82.6 8.7 %collective-permute-start.13 = (bf16[2,128,512]{2,1,0:T(8,128)(2,1)}, bf16[2,128,512]{2,1,0:T(8,128)(2,1)}, u32[]{:S(2)}, u32[]{:S(2)}) collective-permute-start(bf16[2,128,512]{2,1,0:T(8,128)(2,1)} %bitcast.294), channel_id=1, source_target_pairs={{0,1},{1,0},{2,3},{3,2},{4,5},{5,4},{6,7},{7,6},{8,9},{9,8},{10,11... | collective-permute-start | bytes 786440 | tf_op jit(solution)/shard_map/ppermute | solution.py:15
  86.6 7.8 %collective-permute-start.17 = (bf16[2,2,2,32,512]{4,3,2,1,0:T(8,128)(2,1)}, bf16[2,2,2,32,512]{4,3,2,1,0:T(8,128)(2,1)}, u32[]{:S(2)}, u32[]{:S(2)}) collective-permute-start(bf16[2,2,2,32,512]{4,3,2,1,0:T(8,128)(2,1)} %get-tuple-element.68), channel_id=1, source_target_pairs={{0,2},{1,3},{2,0},{3,1},{4,6},{5,7},{6,4},{7,5},{8,10},{9,11},{10,... | collective-permute-start | bytes 786440 | tf_op jit(solution)/shard_map/ppermute | solution.py:15
  87.0 7.5 %collective-permute-start.18 = (bf16[2,2,2,32,512]{4,3,2,1,0:T(8,128)(2,1)}, bf16[2,2,2,32,512]{4,3,2,1,0:T(8,128)(2,1)}, u32[]{:S(2)}, u32[]{:S(2)}) collective-permute-start(bf16[2,2,2,32,512]{4,3,2,1,0:T(8,128)(2,1)} %get-tuple-element.70), channel_id=1, source_target_pairs={{0,4},{1,5},{2,6},{3,7},{4,0},{5,1},{6,2},{7,3},{8,12},{9,13},{10,... | collective-permute-start | bytes 786440 | tf_op jit(solution)/shard_map/ppermute | solution.py:15
  87.0 16.8 %collective-permute-start.19 = (bf16[2,2,2,32,512]{4,3,2,1,0:T(8,128)(2,1)}, bf16[2,2,2,32,512]{4,3,2,1,0:T(8,128)(2,1)}, u32[]{:S(2)}, u32[]{:S(2)}) collective-permute-start(bf16[2,2,2,32,512]{4,3,2,1,0:T(8,128)(2,1)} %get-tuple-element.69), channel_id=1, source_target_pairs={{0,6},{1,7},{2,4},{3,5},{4,2},{5,3},{6,0},{7,1},{8,14},{9,15},{10,... | collective-permute-start | bytes 786440 | tf_op jit(solution)/shard_map/ppermute | solution.py:15
  92.6 12.9 %collective-permute-start.14 = (bf16[128,512]{1,0:T(8,128)(2,1)S(1)}, bf16[128,512]{1,0:T(8,128)(2,1)S(1)}, u32[]{:S(2)}, u32[]{:S(2)}) collective-permute-start(bf16[128,512]{1,0:T(8,128)(2,1)S(1)} %fusion.87), channel_id=1, source_target_pairs={{0,8},{1,9},{2,10},{3,11},{4,12},{5,13},{6,14},{7,15},{8,0},{9,1},... | collective-permute-start | bytes 393224 | tf_op jit(solution)/shard_map/ppermute | solution.py:15
  105.1 7.2 %collective-permute-start.20 = (bf16[2,2,32,512]{3,2,1,0:T(8,128)(2,1)S(1)}, bf16[2,2,32,512]{3,2,1,0:T(8,128)(2,1)S(1)}, u32[]{:S(2)}, u32[]{:S(2)}) collective-permute-start(bf16[2,2,32,512]{3,2,1,0:T(8,128)(2,1)S(1)} %fusion.88), channel_id=1, source_target_pairs={{0,8},{1,9},{2,10},{3,11},{4,12},{5,13},{6,14},{7,15},{8,0},{9,1},... | collective-permute-start | bytes 393224 | tf_op jit(solution)/shard_map/ppermute | solution.py:15
  108.2 13.1 %collective-permute-start.22 = (f32[112,128]{1,0:T(8,128)S(1)}, f32[112,128]{1,0:T(8,128)S(1)}, u32[]{:S(2)}, u32[]{:S(2)}) collective-permute-start(f32[112,128]{1,0:T(8,128)S(1)} %dynamic-slice_bitcast_fusion), channel_id=1, source_target_pairs={{0,1},{1,0},{2,3},{3,2},{4,5},{5,4},{6,7},{7,6},{8,9},{9,8},{10,11... | collective-permute-start | bytes 172040 | tf_op jit(solution)/shard_map/ppermute | solution.py:15
  115.4 14.1 %collective-permute-start.21 = (bf16[2,2,32,512]{3,0,2,1:T(2,128)(2,1)S(1)}, bf16[2,2,32,512]{3,0,2,1:T(2,128)(2,1)S(1)}, u32[]{:S(2)}, u32[]{:S(2)}) collective-permute-start(bf16[2,2,32,512]{3,0,2,1:T(2,128)(2,1)S(1)} %fusion.89), channel_id=1, source_target_pairs={{0,1},{1,0},{2,3},{3,2},{4,5},{5,4},{6,7},{7,6},{8,9},{9,8},{10,11... | collective-permute-start | bytes 393224 | tf_op jit(solution)/shard_map/ppermute | solution.py:15
  116.9 5.1 %collective-permute-start.15 = (bf16[3,32,512]{2,1,0:T(8,128)(2,1)S(1)}, bf16[3,32,512]{2,1,0:T(8,128)(2,1)S(1)}, u32[]{:S(2)}, u32[]{:S(2)}) collective-permute-start(bf16[3,32,512]{2,1,0:T(8,128)(2,1)S(1)} %get-tuple-element.89), channel_id=1, source_target_pairs={{0,1},{1,2},{2,3},{3,4},{4,5},{5,6},{6,7},{7,8},{8,9},{9,10},{10,1... | collective-permute-start | bytes 294920 | tf_op jit(solution)/shard_map/ppermute | solution.py:21
  119.3 6.1 %collective-permute-start.16 = (bf16[3,32,512]{2,1,0:T(8,128)(2,1)S(1)}, bf16[3,32,512]{2,1,0:T(8,128)(2,1)S(1)}, u32[]{:S(2)}, u32[]{:S(2)}) collective-permute-start(bf16[3,32,512]{2,1,0:T(8,128)(2,1)S(1)} %get-tuple-element.88), channel_id=1, source_target_pairs={{1,0},{2,1},{3,2},{4,3},{5,4},{6,5},{7,6},{8,7},{9,8},{10,9},{11,1... | collective-permute-start | bytes 294920 | tf_op jit(solution)/shard_map/ppermute | solution.py:21
  121.3 8.1 %collective-permute-start.23 = (f32[112,128]{1,0:T(8,128)S(1)}, f32[112,128]{1,0:T(8,128)S(1)}, u32[]{:S(2)}, u32[]{:S(2)}) collective-permute-start(f32[112,128]{1,0:T(8,128)S(1)} %bitcast_add_fusion.1), channel_id=1, source_target_pairs={{0,2},{1,3},{2,0},{3,1},{4,6},{5,7},{6,4},{7,5},{8,10},{9,11},{10,... | collective-permute-start | bytes 172040 | tf_op jit(solution)/shard_map/ppermute | solution.py:15
  132.5 5.9 %collective-permute-start.25 = (f32[112,128]{1,0:T(8,128)S(1)}, f32[112,128]{1,0:T(8,128)S(1)}, u32[]{:S(2)}, u32[]{:S(2)}) collective-permute-start(f32[112,128]{1,0:T(8,128)S(1)} %add.529), channel_id=1, source_target_pairs={{0,8},{1,9},{2,10},{3,11},{4,12},{5,13},{6,14},{7,15},{8,0},{9,1},... | collective-permute-start | bytes 172040 | tf_op jit(solution)/shard_map/ppermute | solution.py:15
  (98 other events, 798.1 us)

commit v2 on v0

v2 whole, which is shorter than its diff:
```python
import functools
import math

import jax
import jax.numpy as jnp
from jax import lax
from jax.experimental import pallas as pl
from jax.experimental.pallas import tpu as pltpu
from jax.sharding import PartitionSpec as P

NARROW = jnp.bfloat16
WIDE = jnp.float32
TAPS = 7
RIM = 3
EDGE = 8
LANES = 128
SMALL_ROWS = 28


def swap(value, bit):
    count = lax.axis_size("row")
    return lax.ppermute(value, "row", [(i, i ^ bit) for i in range(count)])


def shift(value, step):
    count = lax.axis_size("row")
    pairs = [(i, i + step) for i in range(count) if 0 <= i + step < count]
    return lax.ppermute(value, "row", pairs)


def shaped(shape, dtype=WIDE):
    return jax.ShapeDtypeStruct(shape, dtype)


def run(body, outs, *operands, scratch=(), mib=16, flops=0):
    size = sum(math.prod(x.shape) * x.dtype.itemsize for x in (*operands, *outs))
    return pl.pallas_call(
        body,
        out_shape=outs,
        scratch_shapes=scratch,
        compiler_params=pltpu.CompilerParams(vmem_limit_bytes=mib * 2**20),
        cost_estimate=pl.CostEstimate(flops=flops, bytes_accessed=size, transcendentals=0),
    )(*operands)


def place():
    me = lax.axis_index("row")
    half = lax.axis_size("row") // 2
    return me, lax.rem(me, 2), lax.div(me, half)


def dot(left, right, dims):
    return lax.dot_general(left, right, (dims, ((), ())), preferred_element_type=WIDE)


def split_body(inw, outw, cotan, scale, feats, own, core, far, both, branch, first, last):
    _, core_bit, far_bit = place()
    quarter = own.shape[-1]
    rows = feats.shape[0]
    for target, c, z in (
        (own, core_bit, far_bit),
        (core, 1 - core_bit, far_bit),
        (far, core_bit, 1 - far_bit),
        (both, 1 - core_bit, 1 - far_bit),
    ):
        lanes = pl.ds(pl.multiple_of((2 * z + c) * quarter, quarter), quarter)
        target[0] = inw[:, lanes].astype(NARROW)
        target[1] = outw[:, lanes].astype(NARROW)
    branch[...] = (scale[...] * cotan[...]).astype(NARROW)
    first[...] = feats[:RIM].astype(NARROW)
    last[...] = feats[rows - RIM :].astype(NARROW)


def fill(padded, block, low, high):
    rows, cols, _ = block.shape
    padded[:, :EDGE, :] = jnp.zeros_like(padded[:, :EDGE, :])
    padded[:, EDGE + cols :, :] = jnp.zeros_like(padded[:, EDGE + cols :, :])
    inner = slice(EDGE, EDGE + cols)
    padded[:RIM, inner, :] = low[...].astype(WIDE)
    padded[RIM : RIM + rows, inner, :] = block[...]
    padded[RIM + rows :, inner, :] = high[...].astype(WIDE)


def taps_sum(padded, kernel, lanes, rows, cols, mirrored, start):
    total = list(start)
    for tap_col in range(TAPS):
        for row in range(rows + TAPS - 1):
            line = padded[row, pl.ds(EDGE - RIM + tap_col, cols), lanes]
            for out in range(rows):
                tap_row = row - out
                if 0 <= tap_row < TAPS:
                    if mirrored:
                        tap = kernel[TAPS - 1 - tap_row, pl.ds(TAPS - 1 - tap_col, 1), lanes]
                    else:
                        tap = kernel[tap_row, pl.ds(tap_col, 1), lanes]
                    total[out] = total[out] + line * tap
    return total


def conv_body(feats, low, high, kernel, gain, bias, normed, inv, narrow, padded, result):
    rows, cols, channels = feats.shape
    fill(padded, feats, low, high)

    @pl.loop(0, channels // LANES)
    def _(step):
        lanes = pl.ds(pl.multiple_of(step * LANES, LANES), LANES)
        zero = [jnp.zeros((cols, LANES), WIDE)] * rows
        total = taps_sum(padded, kernel, lanes, rows, cols, False, zero)
        for row in range(rows):
            result[pl.ds(row * cols, cols), lanes] = total[row]

    value = result[...]
    centred = value - jnp.mean(value, axis=1, keepdims=True)
    spread = lax.rsqrt(jnp.mean(centred * centred, axis=1, keepdims=True) + 1e-06)
    value = centred * spread
    normed[...] = value
    inv[...] = jnp.broadcast_to(spread, inv.shape)
    narrow[...] = (value * gain[...] + bias[...]).astype(NARROW)


def hidden_body(copied, *refs):
    count = lax.axis_size("row")
    me, _, far_bit = place()
    mine = 2 * far_bit + lax.rem(me, 2)
    normed, branch, in_bias = refs[:2], refs[2:4], refs[4]
    outs = 5 + (count // 2 if copied else 1)
    pieces = refs[5:outs]
    keep, send, active, hidden, out_narrow, bias_part, in_narrow = refs[outs:]
    half = normed[0].shape[0]
    if copied:
        own = pieces[0].shape[2]
        for pattern in range(count // 4):
            for z in range(2):
                piece = pieces[2 * pattern + z]
                for c in range(2):
                    device = jnp.bitwise_xor(me, z * (count // 2) + 2 * pattern + c)
                    rows = pl.ds(pl.multiple_of(device * own, own), own)
                    in_narrow[rows, :] = piece[c, 0]
                    out_narrow[rows, :] = piece[c, 1]
    else:
        in_narrow[...] = pieces[0][0]
        out_narrow[...] = pieces[0][1]
    bias_row = in_bias[pl.ds(mine, 1), :]
    total = jnp.zeros_like(bias_row)
    for side in (1, 0):
        preact = dot(normed[side][...], in_narrow[...], ((1,), (0,))) + bias_row
        act_grad = dot(branch[side][...], out_narrow[...], ((1,), (0,)))
        cdf = 0.5 * (1.0 + lax.erf(preact * 0.7071067811865476))
        rows = pl.ds(side * half, half)
        active[rows, :] = (preact * cdf).astype(NARROW)
        slope = cdf + preact * jnp.exp(-0.5 * preact * preact) * 0.3989422804014327
        grad = act_grad * slope
        total = total + jnp.sum(grad, axis=0, keepdims=True)
        narrow = grad.astype(NARROW)
        hidden[rows, :] = narrow
        out_grad = dot(narrow, in_narrow[...], ((1,), (1,)))
        if side:
            send[...] = out_grad.astype(NARROW)
        else:
            keep[...] = out_grad
    bias_part[...] = total


def weight_body(copied, norm_scale, *refs):
    count = lax.axis_size("row")
    me, _, _ = place()
    normed, branch = refs[:2], refs[2:4]
    active, hidden, out_narrow, scale = refs[4:8]
    outs = refs[8:-1]
    holder = refs[-1]
    half = normed[0].shape[0]
    first, second = pl.ds(0, half), pl.ds(half, half)
    for which, (left, right) in enumerate(((normed, hidden), (branch, active))):
        grad = dot(left[0][...], right[first, :], ((0,), (0,)))
        grad = grad + dot(left[1][...], right[second, :], ((0,), (0,)))
        holder[which] = norm_scale * grad
    if copied:
        own = outs[0].shape[3]
        for pattern in range(count // 4):
            for z in range(2):
                for c in range(2):
                    device = jnp.bitwise_xor(me, z * (count // 2) + 2 * pattern + c)
                    rows = pl.ds(pl.multiple_of(device * own, own), own)
                    for which in range(2):
                        target = outs[pattern]
                        target[z, c, which] = holder[which, rows, :].astype(target.dtype)
        rest = outs[count // 4 :]
    else:
        outs[0][...] = holder[...]
        rest = outs[1:]
    mixed_keep, mixed_send, scale_part = rest
    total = jnp.zeros_like(scale_part)
    for side, rows in enumerate((first, second)):
        mixed = dot(active[rows, :], out_narrow[...], ((1,), (1,)))
        total = total + jnp.sum(mixed * branch[side][...].astype(WIDE), axis=0, keepdims=True)
        if side:
            mixed_send[...] = mixed.astype(NARROW)
        else:
            mixed_keep[...] = mixed
    scale_part[...] = total / scale[...]


def fold_body(kept, got, stay, leave):
    size = stay.shape[0]
    stay[...] = kept[:size] + got[:size].astype(WIDE)
    leave[...] = (kept[size:] + got[size:].astype(WIDE)).astype(NARROW)


def norm_grad_body(kept, got, normed, inv, gain, grad, first, last, gain_part, bias_part):
    out_grad = kept[...] + got[...].astype(WIDE)
    value = normed[...]
    product = out_grad * value
    gain_part[...] = jnp.sum(product, axis=0, keepdims=True)
    bias_part[...] = jnp.sum(out_grad, axis=0, keepdims=True)
    normed_grad = out_grad * gain[...]
    mean = jnp.mean(normed_grad, axis=1, keepdims=True)
    along = jnp.mean(normed_grad * value, axis=1, keepdims=True)
    result = inv[:, :1] * (normed_grad - mean - value * along)
    grad[...] = result
    pixels = result.shape[0]
    rim = first.shape[0]
    first[...] = result[:rim].astype(NARROW)
    last[...] = result[pixels - rim :].astype(NARROW)


def kernel_grad_body(
    norm_scale, feats, low, high, grad, gain, bias, scale, in_bias, stay, leave, padded, small
):
    rows, cols, channels = feats.shape
    _, core_bit, far_bit = place()
    fill(padded, feats, low, high)

    def put(row, lanes, value):
        small[row // SMALL_ROWS, pl.ds(row % SMALL_ROWS, 1), lanes] = norm_scale * value

    @pl.loop(0, channels // LANES)
    def _(step):
        lanes = pl.ds(pl.multiple_of(step * LANES, LANES), LANES)
        own = [grad[pl.ds(row * cols, cols), lanes] for row in range(rows)]
        for tap_col in range(TAPS):
            totals = [jnp.zeros((8, LANES), WIDE)] * TAPS
            for row in range(rows + TAPS - 1):
                line = padded[row, pl.ds(EDGE - RIM + tap_col, cols), lanes]
                for out in range(rows):
                    tap_row = row - out
                    if 0 <= tap_row < TAPS:
                        product = line * own[out]
                        for part in range(cols // 8):
                            totals[tap_row] = totals[tap_row] + product[8 * part : 8 * part + 8]
            for tap_row in range(TAPS):
                value = jnp.sum(totals[tap_row], axis=0, keepdims=True)
                put(TAPS * tap_row + tap_col, lanes, value)

    everything = slice(None)
    row = TAPS * TAPS
    put(row, everything, gain[...])
    put(row + 1, everything, bias[...])
    put(row + 2, everything, scale[...])
    mine = 2 * far_bit + core_bit
    for part in range(4):
        own_part = jnp.where(mine == part, 1.0, 0.0)
        put(row + 3 + part, everything, own_part * in_bias[...])
    stay[...] = small[core_bit]
    leave[...] = small[1 - core_bit]


def input_grad_body(grad, low, high, kernel, cotan, result, padded):
    rows, cols, channels = grad.shape
    fill(padded, grad, low, high)

    @pl.loop(0, channels // LANES)
    def _(step):
        lanes = pl.ds(pl.multiple_of(step * LANES, LANES), LANES)
        start = [cotan[row, :, lanes] for row in range(rows)]
        total = taps_sum(padded, kernel, lanes, rows, cols, True, start)
        for row in range(rows):
            result[row, :, lanes] = total[row]


def output_body(feats, scale, kept, got, result):
    result[...] = feats[...] + scale[...] * (kept[...] + got[...].astype(WIDE))


def total_body(*refs):
    own, others, (stay, near, leave) = refs[0], refs[1:-3], refs[-3:]
    total = own[...]
    for other in others:
        total = total + other[...].astype(WIDE)
    stay[...] = total[0, 0]
    near[...] = total[0, 1].astype(NARROW)
    leave[...] = total[1].astype(NARROW)


def owner_body(stay, near, far, both, in_grad, out_grad):
    _, c, z = place()
    quarter = stay.shape[-1]
    for value, core, side in (
        (stay, c, z),
        (near, 1 - c, z),
        (far, c, 1 - z),
        (both, 1 - c, 1 - z),
    ):
        lanes = pl.ds(pl.multiple_of((2 * side + core) * quarter, quarter), quarter)
        in_grad[:, lanes] = value[0].astype(WIDE)
        out_grad[:, lanes] = value[1].astype(WIDE)


def small_body(mine, other, kernel_grad, gain, bias, scale, in_bias, held):
    _, core_bit, _ = place()
    held[core_bit] = mine[...]
    held[1 - core_bit] = other[...]

    def take(row):
        return held[row // SMALL_ROWS, pl.ds(row % SMALL_ROWS, 1), :]

    for tap_row in range(TAPS):
        for tap_col in range(TAPS):
            kernel_grad[tap_row, pl.ds(tap_col, 1), :] = take(TAPS * tap_row + tap_col)
    row = TAPS * TAPS
    gain[...] = take(row)
    bias[...] = take(row + 1)
    scale[...] = take(row + 2)
    quarter = take(row).shape[1]
    for part in range(4):
        in_bias[:, pl.ds(part * quarter, quarter)] = take(row + 3 + part)


def flipped(blocks, axis, bit_set):
    return jnp.where(bit_set == 1, jnp.flip(blocks, axis), blocks)


def canonical(blocks, me, bit_count):
    tail = blocks.shape[1:]
    blocks = blocks.reshape((2,) * bit_count + tail)
    for spot in range(bit_count):
        blocks = flipped(blocks, bit_count - 1 - spot, (me >> spot) & 1)
    return blocks.reshape((2**bit_count,) + tail)


def per_device(
    features, cotangent, kernel, norm_gain, norm_bias, in_weight, in_bias, out_weight, layer_scale
):
    row_count, col_count, channels = features.shape
    own_rows, hidden_count = in_weight.shape
    pixels = row_count * col_count
    count = lax.axis_size("row")
    bit_count = count.bit_length() - 1
    me = lax.axis_index("row")
    far = count // 2
    quarter = hidden_count // 4
    norm_scale = 1.0 / math.sqrt(pixels * count)
    patterns = count // 4
    copied = own_rows % 16 == 0
    flat_features = features.reshape(pixels, channels)
    flat_cotan = cotangent.reshape(pixels, channels)
    gain_row = norm_gain.reshape(1, channels)
    bias_row = norm_bias.reshape(1, channels)
    scale_row = layer_scale.reshape(1, channels)
    rim = (RIM, col_count, channels)
    padded = pltpu.VMEM((row_count + 2 * RIM, col_count + 2 * EDGE, channels), WIDE)
    conv_flops = 2 * TAPS * TAPS * pixels * channels

    piece = shaped((2, own_rows, quarter), NARROW)
    own, core, beyond, both, branch, first, last = run(
        split_body,
        (piece,) * 4 + (shaped((pixels, channels), NARROW), shaped(rim, NARROW), shaped(rim, NARROW)),
        in_weight,
        out_weight,
        flat_cotan,
        scale_row,
        features,
    )
    low = shift(last, 1)
    high = shift(first, -1)
    near = jnp.stack([own, swap(core, 1)])
    got = swap(jnp.stack([beyond, both]), far)
    distant = jnp.stack([got[0], swap(got[1], 1)])
    pieces = [near, distant]
    for p in range(1, patterns):
        pieces += [swap(near, 2 * p), swap(distant, 2 * p)]

    def group_gather(value):
        two = jnp.concatenate([value, swap(value, far)])
        return two, swap(two, 1)

    branch_all = group_gather(branch)
    normed, inv, normed_out = run(
        conv_body,
        (
            shaped((pixels, channels)),
            shaped((pixels, LANES)),
            shaped((pixels, channels), NARROW),
        ),
        features,
        low,
        high,
        kernel,
        gain_row,
        bias_row,
        scratch=(padded, pltpu.VMEM((pixels, channels), WIDE)),
        flops=conv_flops,
    )
    normed_all = group_gather(normed_out)

    if not copied:
        stacked = jnp.stack(pieces).reshape(patterns, 2, 2, 2, own_rows, quarter)
        stacked = jnp.moveaxis(stacked, 0, 1).reshape(count, 2, own_rows, quarter)
        stacked = jnp.moveaxis(canonical(stacked, me, bit_count), 1, 0)
        pieces = [stacked.reshape(2, channels, quarter)]
    group = 4 * pixels
    out_keep, out_send, active, hidden, out_narrow, in_bias_part = run(
        functools.partial(hidden_body, copied),
        (
            shaped((2 * pixels, channels)),
            shaped((2 * pixels, channels), NARROW),
            shaped((group, quarter), NARROW),
            shaped((group, quarter), NARROW),
            shaped((channels, quarter), NARROW),
            shaped((1, quarter)),
        ),
        *normed_all,
        *branch_all,
        in_bias.reshape(4, quarter),
        *pieces,
        scratch=(pltpu.VMEM((channels, quarter), NARROW),),
        mib=24,
        flops=6 * group * channels * quarter,
    )
    half = (shaped((pixels, channels)), shaped((pixels, channels), NARROW))
    out_stay, out_leave = run(fold_body, half, out_keep, swap(out_send, 1))
    out_got = swap(out_leave, far)

    grads = (2, 2, 2, own_rows, quarter)
    if copied:
        grad_shapes = (shaped(grads),) + (shaped(grads, NARROW),) * (patterns - 1)
    else:
        grad_shapes = (shaped((2, channels, quarter)),)
    *grad_parts, mixed_keep, mixed_send, scale_part = run(
        functools.partial(weight_body, copied, norm_scale),
        grad_shapes
        + (
            shaped((2 * pixels, channels)),
            shaped((2 * pixels, channels), NARROW),
            shaped((1, channels)),
        ),
        *normed_all,
        *branch_all,
        active,
        hidden,
        out_narrow,
        scale_row,
        scratch=(pltpu.VMEM((2, channels, quarter), WIDE),),
        mib=24,
        flops=6 * group * channels * quarter,
    )
    if not copied:
        parts = grad_parts[0].reshape(2, count, own_rows, quarter)
        parts = canonical(jnp.moveaxis(parts, 1, 0), me, bit_count)
        parts = parts.reshape(2, patterns, 2, 2, own_rows, quarter)
        grad_parts = [parts[:, 0]] + [parts[:, p].astype(NARROW) for p in range(1, patterns)]
    arrived = [swap(grad_parts[p], 2 * p) for p in range(1, patterns)]
    mixed_stay, mixed_leave = run(fold_body, half, mixed_keep, swap(mixed_send, 1))
    mixed_got = swap(mixed_leave, far)

    flat_rim = shaped((RIM * col_count, channels), NARROW)
    conv_grad, first, last, gain_part, bias_part = run(
        norm_grad_body,
        (
            shaped((pixels, channels)),
            flat_rim,
            flat_rim,
            shaped((1, channels)),
            shaped((1, channels)),
        ),
        out_stay,
        out_got,
        normed,
        inv,
        gain_row,
    )
    grad_low = shift(last, 1).reshape(rim)
    grad_high = shift(first, -1).reshape(rim)
    small = shaped((SMALL_ROWS, channels))
    stay, leave = run(
        functools.partial(kernel_grad_body, norm_scale),
        (small, small),
        features,
        low,
        high,
        conv_grad,
        gain_part,
        bias_part,
        scale_part,
        in_bias_part,
        scratch=(padded, pltpu.VMEM((2, SMALL_ROWS, channels), WIDE)),
        flops=conv_flops,
    )
    sums = stay + swap(leave, 1)
    for spot in range(1, bit_count):
        sums = sums + swap(sums, 1 << spot)

    input_grad = run(
        input_grad_body,
        (shaped(features.shape),),
        conv_grad.reshape(features.shape),
        grad_low,
        grad_high,
        kernel,
        cotangent,
        scratch=(padded,),
        flops=conv_flops,
    )[0]
    output = run(
        output_body,
        (shaped((pixels, channels)),),
        flat_features,
        scale_row,
        mixed_stay,
        mixed_got,
    )[0].reshape(features.shape)

    quarters = (2, own_rows, quarter)
    stay, near, leave = run(
        total_body,
        (shaped(quarters), shaped(quarters, NARROW), shaped((2,) + quarters, NARROW)),
        grad_parts[0],
        *arrived,
    )
    near_got = swap(near, 1)
    far_got = swap(leave, far)
    both_got = swap(far_got[1], 1)
    in_weight_grad, out_weight_grad = run(
        owner_body,
        (shaped((own_rows, hidden_count)),) * 2,
        stay,
        near_got,
        far_got[0],
        both_got,
    )
    kernel_grad, gain_grad, bias_grad, scale_grad, in_bias_grad = run(
        small_body,
        (
            shaped(kernel.shape),
            shaped((1, channels)),
            shaped((1, channels)),
            shaped((1, channels)),
            shaped((1, hidden_count)),
        ),
        sums,
        swap(sums, 1),
        scratch=(pltpu.VMEM((2, SMALL_ROWS, channels), WIDE),),
    )
    return (
        output,
        input_grad,
        in_weight_grad,
        out_weight_grad,
        kernel_grad,
        gain_grad.reshape(channels),
        bias_grad.reshape(channels),
        in_bias_grad.reshape(hidden_count),
        scale_grad.reshape(channels),
    )


def solution(mesh):
    return jax.shard_map(
        per_device,
        mesh=mesh,
        in_specs=(
            P(("grp", "row"), None, None),
            P(("grp", "row"), None, None),
            P(),
            P(),
            P(),
            P("row", None),
            P(),
            P("row", None),
            P(),
        ),
        out_specs=(
            P(("grp", "row"), None, None),
            P(("grp", "row"), None, None),
            P(("grp", "row"), None),
            P(("grp", "row"), None),
            P("grp", None, None),
            P("grp"),
            P("grp"),
            P("grp"),
            P("grp"),
        ),
        check_vma=False,
    )
```

time: 312 us -> 94 us (0.30)
  waiting for transfers between devices: 189 us -> 24 us
  blocking collectives: 57.3 us -> 0 us
  starting transfers between devices: 11.1 us -> 51.2 us
  other arithmetic: 16.1 us -> 0.09 us
  between operations: 14.9 us -> 0.92 us
  Pallas kernels: 0 us -> 12.3 us
  matrix products: 11.5 us -> 0 us
  local copies, waits for them, and re-layouts: 10.9 us -> 4.64 us
    psum x1 -> x0, waiting for transfers between devices: 88.9 us -> none  [per_device(): lax.psum((kernel_term, norm_scale * gain_term, norm_scale * bias_term, no...]
    all_gather x2 -> x0, waiting for transfers between devices: 68.4 us -> none  [the longest x1 40.8 us: per_device(): lax.all_gather(out_narrow, 'row', axis=0, tiled=True)]
    psum x1 -> x0, blocking collectives: 57.3 us -> none  [per_device(): lax.psum((kernel_term, norm_scale * gain_term, norm_scale * bias_term, no...]
    ppermute x4 -> x32, starting transfers between devices: 10.9 us -> 51.2 us  [the longest x28 39.8 us: swap(): return lax.ppermute(value, 'row', [(i, i ^ bit) for i in range(count)])]
    reduce_scatter x1 -> x0, waiting for transfers between devices: 31 us -> none  [per_device(): lax.psum_scatter(jnp.concatenate([norm_scale * contract_first(normed_out,...]
    ppermute x4 -> x32, waiting for transfers between devices: 0.61 us -> 24 us  [the longest x28 24 us: swap(): return lax.ppermute(value, 'row', [(i, i ^ bit) for i in range(count)])]
    pallas_call x0 -> x13, Pallas kernels: none -> 12.3 us  [run(): pl.pallas_call(body, out_shape=outs, scratch_shapes=scratch, compiler_par...]
    dot_general x6 -> x0, matrix products: 11.5 us -> none  [the longest x2 6.52 us: contract_last(): lax.dot_general(left, right, (((1,), (1,)), ((), ())), preferred_element_...]
  transfers between devices with their start and end apart: 8 -> 32, of which waited for: 5 -> 8; matrix products, arithmetic and copies ran while one was open for 7% -> 0% of each run, Pallas kernels for 0% -> 11%
where the time goes in v2:
time: 94 us; the launch traced here: 93.1 us
  starting transfers between devices  51.2 us (54%)
  waiting for transfers between devices  24 us (26%)
  Pallas kernels  12.3 us (13%)
  local copies, waits for them, and re-layouts  4.64 us (5%)
    ppermute x28, starting transfers between devices, swap(): return lax.ppermute(value, 'row', [(i, i ^ bit) for i in range(count)])  39.8 us
    ppermute x28, waiting for transfers between devices, swap(): return lax.ppermute(value, 'row', [(i, i ^ bit) for i in range(count)])  24 us
    pallas_call x13, Pallas kernels, run(): pl.pallas_call(body, out_shape=outs, scratch_shapes=scratch, compiler_par...  12.3 us
    ppermute x4, starting transfers between devices, shift(): return lax.ppermute(value, 'row', pairs)  11.4 us
    unnamed x24, local copies, waits for them, and re-layouts  4.59 us
  transfers between devices with their start and end apart: 32, of which 8 were waited for; matrix products, arithmetic and copies ran while one was open for 0% of the time, Pallas kernels for 11%

profile of v2, /device:TPU:1, one launch (start us, length us, event | category | flops | bytes accessed | tf_op | source)
XLA Modules:
  0.0 93.1 jit_solution(2736279087523725235)
XLA Ops:
  5.2 4.5 %collective-permute-start = (bf16[3,32,512]{2,1,0:T(8,128)(2,1)S(1)}, bf16[3,32,512]{2,1,0:T(8,128)(2,1)S(1)}, u32[]{:S(2)}, u32[]{:S(2)}) collective-permute-start(bf16[3,32,512]{2,1,0:T(8,128)(2,1)S(1)} %get-tuple-element.53), channel_id=1, source_target_pairs={{0,1},{1,2},{2,3},{3,4},{4,5},{5,6},{6,7},{7,8},{8,9},{9,10},{10,1... | collective-permute-start | bytes 294920 | tf_op jit(solution)/shard_map/ppermute | solution.py:28
  9.7 1.9 %collective-permute-start.1 = (bf16[3,32,512]{2,1,0:T(8,128)(2,1)S(1)}, bf16[3,32,512]{2,1,0:T(8,128)(2,1)S(1)}, u32[]{:S(2)}, u32[]{:S(2)}) collective-permute-start(bf16[3,32,512]{2,1,0:T(8,128)(2,1)S(1)} %get-tuple-element.54), channel_id=1, source_target_pairs={{1,0},{2,1},{3,2},{4,3},{5,4},{6,5},{7,6},{8,7},{9,8},{10,9},{11,1... | collective-permute-start | bytes 294920 | tf_op jit(solution)/shard_map/ppermute | solution.py:28
  11.7 2.4 %collective-permute-start.7 = (bf16[2,2,32,512]{3,2,1,0:T(8,128)(2,1)S(1)}, bf16[2,2,32,512]{3,2,1,0:T(8,128)(2,1)S(1)}, u32[]{:S(2)}, u32[]{:S(2)}) collective-permute-start(bf16[2,2,32,512]{3,2,1,0:T(8,128)(2,1)S(1)} %pad_maximum_fusion.1), channel_id=1, source_target_pairs={{0,8},{1,9},{2,10},{3,11},{4,12},{5,13},{6,14},{7,15},{8,0},{9,1},... | collective-permute-start | bytes 393224 | tf_op jit(solution)/shard_map/ppermute | solution.py:22
  14.1 1.8 %collective-permute-start.6 = (bf16[2,32,512]{2,1,0:T(8,128)(2,1)S(1)}, bf16[2,32,512]{2,1,0:T(8,128)(2,1)S(1)}, u32[]{:S(2)}, u32[]{:S(2)}) collective-permute-start(bf16[2,32,512]{2,1,0:T(8,128)(2,1)S(1)} %get-tuple-element.58), channel_id=1, source_target_pairs={{0,1},{1,0},{2,3},{3,2},{4,5},{5,4},{6,7},{7,6},{8,9},{9,8},{10,11... | collective-permute-start | bytes 196616 | tf_op jit(solution)/shard_map/ppermute | solution.py:22
  16.9 1.6 %collective-permute-start.11 = (bf16[2,2,32,512]{3,2,1,0:T(8,128)(2,1)S(1)}, bf16[2,2,32,512]{3,2,1,0:T(8,128)(2,1)S(1)}, u32[]{:S(2)}, u32[]{:S(2)}) collective-permute-start(bf16[2,2,32,512]{3,2,1,0:T(8,128)(2,1)S(1)} %pad_maximum_fusion.refs_5_), channel_id=1, source_target_pairs={{0,4},{1,5},{2,6},{3,7},{4,0},{5,1},{6,2},{7,3},{8,12},{9,13},{10,... | collective-permute-start | bytes 393224 | tf_op jit(solution)/shard_map/ppermute | solution.py:22
  19.8 2.4 %shard_map.161 = (f32[128,512]{1,0:T(8,128)S(1)}, f32[128,128]{1,0:T(8,128)S(1)}, bf16[128,512]{1,0:T(8,128)(2,1)S(1)}) custom-call(f32[4,32,512]{2,1,0:T(8,128)S(1)} %copy-done.1, bf16[3,32,512]{2,1,0:T(8,128)(2,1)S(1)} %collective-permute-done.low, bf16[3,32,512]{2,1,0:T(8,128)(2,1)S(1)} %collective-permute-done.1.high, f32[7,7,512]{2,1,0:T(8,128)S(1)} %copy-done.4, ...), custom_call_target="tpu_custom_call" | custom-call | flops 6422528 | bytes 1021952 | tf_op jit(solution)/shard_map/pallas_call | solution.py:37
  22.2 2.5 %collective-permute-start.2 = (bf16[128,512]{1,0:T(8,128)(2,1)S(1)}, bf16[128,512]{1,0:T(8,128)(2,1)S(1)}, u32[]{:S(2)}, u32[]{:S(2)}) collective-permute-start(bf16[128,512]{1,0:T(8,128)(2,1)S(1)} %get-tuple-element.55), channel_id=1, source_target_pairs={{0,8},{1,9},{2,10},{3,11},{4,12},{5,13},{6,14},{7,15},{8,0},{9,1},... | collective-permute-start | bytes 393224 | tf_op jit(solution)/shard_map/ppermute | solution.py:22
  25.4 4.1 %collective-permute-start.8 = (bf16[2,32,512]{2,1,0:T(8,128)(2,1)S(1)}, bf16[2,32,512]{2,1,0:T(8,128)(2,1)S(1)}, u32[]{:S(2)}, u32[]{:S(2)}) collective-permute-start(bf16[2,32,512]{2,1,0:T(8,128)(2,1)S(1)} %get-tuple-element.100), channel_id=1, source_target_pairs={{0,1},{1,0},{2,3},{3,2},{4,5},{5,4},{6,7},{7,6},{8,9},{9,8},{10,11... | collective-permute-start | bytes 196616 | tf_op jit(solution)/shard_map/ppermute | solution.py:22
  29.5 4.7 %collective-permute-start.5 = (bf16[256,512]{1,0:T(8,128)(2,1)S(1)}, bf16[256,512]{1,0:T(8,128)(2,1)S(1)}, u32[]{:S(2)}, u32[]{:S(2)}) collective-permute-start(bf16[256,512]{1,0:T(8,128)(2,1)S(1)} %constant_dynamic-update-slice_fusion.2.refs_2_), channel_id=1, source_target_pairs={{0,1},{1,0},{2,3},{3,2},{4,5},{5,4},{6,7},{7,6},{8,9},{9,8},{10,11... | collective-permute-start | bytes 786440 | tf_op jit(solution)/shard_map/ppermute | solution.py:22
  35.2 1.9 %collective-permute-start.14 = (bf16[2,2,32,512]{3,2,1,0:T(8,128)(2,1)S(1)}, bf16[2,2,32,512]{3,2,1,0:T(8,128)(2,1)S(1)}, u32[]{:S(2)}, u32[]{:S(2)}) collective-permute-start(bf16[2,2,32,512]{3,2,1,0:T(8,128)(2,1)S(1)} %pad_maximum_fusion.2.refs_6_), channel_id=1, source_target_pairs={{0,6},{1,7},{2,4},{3,5},{4,2},{5,3},{6,0},{7,1},{8,14},{9,15},{10,... | collective-permute-start | bytes 393224 | tf_op jit(solution)/shard_map/ppermute | solution.py:22
  37.1 1.9 %collective-permute-done.10.refs_8_ = bf16[2,2,32,512]{3,2,1,0:T(8,128)(2,1)S(1)} collective-permute-done((bf16[2,2,32,512]{3,2,1,0:T(8,128)(2,1)S(1)}, bf16[2,2,32,512]{3,2,1,0:T(8,128)(2,1)S(1)}, u32[]{:S(2)}, u32[]{:S(2)}) %collective-permute-start.10) | collective-permute-done | bytes 131104 | tf_op jit(solution)/shard_map/ppermute | solution.py:22
  39.4 3.3 %collective-permute-done.14.refs_12_ = bf16[2,2,32,512]{3,2,1,0:T(8,128)(2,1)S(1)} collective-permute-done((bf16[2,2,32,512]{3,2,1,0:T(8,128)(2,1)S(1)}, bf16[2,2,32,512]{3,2,1,0:T(8,128)(2,1)S(1)}, u32[]{:S(2)}, u32[]{:S(2)}) %collective-permute-start.14) | collective-permute-done | bytes 131104 | tf_op jit(solution)/shard_map/ppermute | solution.py:22
  44.1 1.7 %collective-permute-start.17 = (bf16[256,512]{1,0:T(8,128)(2,1)S(1)}, bf16[256,512]{1,0:T(8,128)(2,1)S(1)}, u32[]{:S(2)}, u32[]{:S(2)}) collective-permute-start(bf16[256,512]{1,0:T(8,128)(2,1)S(1)} %get-tuple-element.69), channel_id=1, source_target_pairs={{0,1},{1,0},{2,3},{3,2},{4,5},{5,4},{6,7},{7,6},{8,9},{9,8},{10,11... | collective-permute-start | bytes 786440 | tf_op jit(solution)/shard_map/ppermute | solution.py:22
  47.7 1.9 %collective-permute-start.23 = (bf16[2,2,2,32,512]{4,3,2,1,0:T(8,128)(2,1)S(1)}, bf16[2,2,2,32,512]{4,3,2,1,0:T(8,128)(2,1)S(1)}, u32[]{:S(2)}, u32[]{:S(2)}) collective-permute-start(bf16[2,2,2,32,512]{4,3,2,1,0:T(8,128)(2,1)S(1)} %get-tuple-element.80), channel_id=1, source_target_pairs={{0,6},{1,7},{2,4},{3,5},{4,2},{5,3},{6,0},{7,1},{8,14},{9,15},{10,... | collective-permute-start | bytes 786440 | tf_op jit(solution)/shard_map/ppermute | solution.py:22
  51.8 9.8 %collective-permute-done.18.got = bf16[128,512]{1,0:T(8,128)(2,1)S(1)} collective-permute-done((bf16[128,512]{1,0:T(8,128)(2,1)S(1)}, bf16[128,512]{1,0:T(8,128)(2,1)S(1)}, u32[]{:S(2)}, u32[]{:S(2)}) %collective-permute-start.18) | collective-permute-done | bytes 131104 | tf_op jit(solution)/shard_map/ppermute | solution.py:22
  61.8 1.7 %shard_map.171 = (f32[28,512]{1,0:T(8,128)S(1)}, f32[28,512]{1,0:T(8,128)S(1)}) custom-call(f32[4,32,512]{2,1,0:T(8,128)S(1)} %copy-done.1, bf16[3,32,512]{2,1,0:T(8,128)(2,1)S(1)} %collective-permute-done.low, bf16[3,32,512]{2,1,0:T(8,128)(2,1)S(1)} %collective-permute-done.1.high, f32[128,512]{1,0:T(8,128)S(1)} %get-tuple-element.74.grad, ...), custom_call_target="tpu_custom_call" | custom-call | flops 6422528 | bytes 843776 | tf_op jit(solution)/shard_map/pallas_call | solution.py:37
  64.8 3.2 %collective-permute-start.25 = (bf16[2,2,32,512]{3,2,1,0:T(8,128)(2,1)S(1)}, bf16[2,2,32,512]{3,2,1,0:T(8,128)(2,1)S(1)}, u32[]{:S(2)}, u32[]{:S(2)}) collective-permute-start(bf16[2,2,32,512]{3,2,1,0:T(8,128)(2,1)S(1)} %get-tuple-element.83), channel_id=1, source_target_pairs={{0,8},{1,9},{2,10},{3,11},{4,12},{5,13},{6,14},{7,15},{8,0},{9,1},... | collective-permute-start | bytes 393224 | tf_op jit(solution)/shard_map/ppermute | solution.py:22
  68.8 2.7 %collective-permute-done.28 = f32[28,512]{1,0:T(8,128)S(1)} collective-permute-done((f32[28,512]{1,0:T(8,128)S(1)}, f32[28,512]{1,0:T(8,128)S(1)}, u32[]{:S(2)}, u32[]{:S(2)}) %collective-permute-start.28) | collective-permute-done | bytes 57376 | tf_op jit(solution)/shard_map/ppermute | solution.py:22
  73.6 1.7 %collective-permute-start.16 = (bf16[128,512]{1,0:T(8,128)(2,1)S(1)}, bf16[128,512]{1,0:T(8,128)(2,1)S(1)}, u32[]{:S(2)}, u32[]{:S(2)}) collective-permute-start(bf16[128,512]{1,0:T(8,128)(2,1)S(1)} %get-tuple-element.67), channel_id=1, source_target_pairs={{0,8},{1,9},{2,10},{3,11},{4,12},{5,13},{6,14},{7,15},{8,0},{9,1},... | collective-permute-start | bytes 393224 | tf_op jit(solution)/shard_map/ppermute | solution.py:22
  75.2 3.0 %collective-permute-start.19 = (bf16[96,512]{1,0:T(8,128)(2,1)S(1)}, bf16[96,512]{1,0:T(8,128)(2,1)S(1)}, u32[]{:S(2)}, u32[]{:S(2)}) collective-permute-start(bf16[96,512]{1,0:T(8,128)(2,1)S(1)} %get-tuple-element.75), channel_id=1, source_target_pairs={{0,1},{1,2},{2,3},{3,4},{4,5},{5,6},{6,7},{7,8},{8,9},{9,10},{10,1... | collective-permute-start | bytes 294920 | tf_op jit(solution)/shard_map/ppermute | solution.py:28
  78.3 1.9 %collective-permute-start.20 = (bf16[96,512]{1,0:T(8,128)(2,1)S(1)}, bf16[96,512]{1,0:T(8,128)(2,1)S(1)}, u32[]{:S(2)}, u32[]{:S(2)}) collective-permute-start(bf16[96,512]{1,0:T(8,128)(2,1)S(1)} %get-tuple-element.76), channel_id=1, source_target_pairs={{1,0},{2,1},{3,2},{4,3},{5,4},{6,5},{7,6},{8,7},{9,8},{10,9},{11,1... | collective-permute-start | bytes 294920 | tf_op jit(solution)/shard_map/ppermute | solution.py:28
  81.1 4.3 %collective-permute-done.30 = f32[28,512]{1,0:T(8,128)S(1)} collective-permute-done((f32[28,512]{1,0:T(8,128)S(1)}, f32[28,512]{1,0:T(8,128)S(1)}, u32[]{:S(2)}, u32[]{:S(2)}) %collective-permute-start.30) | collective-permute-done | bytes 57376 | tf_op jit(solution)/shard_map/ppermute | solution.py:22
  85.3 2.5 %collective-permute-start.26 = (bf16[2,32,512]{2,1,0:T(8,128)(2,1)S(1)}, bf16[2,32,512]{2,1,0:T(8,128)(2,1)S(1)}, u32[]{:S(2)}, u32[]{:S(2)}) collective-permute-start(bf16[2,32,512]{2,1,0:T(8,128)(2,1)S(1)} %get-tuple-element.97), channel_id=1, source_target_pairs={{0,1},{1,0},{2,3},{3,2},{4,5},{5,4},{6,7},{7,6},{8,9},{9,8},{10,11... | collective-permute-start | bytes 196616 | tf_op jit(solution)/shard_map/ppermute | solution.py:22
  89.6 2.8 %shard_map.168 = f32[4,32,512]{2,1,0:T(8,128)} custom-call(f32[4,32,512]{2,1,0:T(8,128)S(1)} %bitcast.26, bf16[3,32,512]{2,1,0:T(8,128)(2,1)S(1)} %bitcast.27, bf16[3,32,512]{2,1,0:T(8,128)(2,1)S(1)} %bitcast.28, f32[7,7,512]{2,1,0:T(8,128)S(1)} %copy-done.4, f32[4,32,512]{2,1,0:T(8,128)S(1)} %copy-done.3), custom_call_target="tpu_custom_call" | custom-call | flops 6422528 | bytes 1083392 | tf_op jit(solution)/shard_map/pallas_call | solution.py:37
  (89 shorter events, 22.0 us)
Async XLA Ops:
  5.2 13.3 %collective-permute-start = (bf16[3,32,512]{2,1,0:T(8,128)(2,1)S(1)}, bf16[3,32,512]{2,1,0:T(8,128)(2,1)S(1)}, u32[]{:S(2)}, u32[]{:S(2)}) collective-permute-start(bf16[3,32,512]{2,1,0:T(8,128)(2,1)S(1)} %get-tuple-element.53), channel_id=1, source_target_pairs={{0,1},{1,2},{2,3},{3,4},{4,5},{5,6},{6,7},{7,8},{8,9},{9,10},{10,1... | collective-permute-start | bytes 294920 | tf_op jit(solution)/shard_map/ppermute | solution.py:28
  9.7 9.0 %collective-permute-start.1 = (bf16[3,32,512]{2,1,0:T(8,128)(2,1)S(1)}, bf16[3,32,512]{2,1,0:T(8,128)(2,1)S(1)}, u32[]{:S(2)}, u32[]{:S(2)}) collective-permute-start(bf16[3,32,512]{2,1,0:T(8,128)(2,1)S(1)} %get-tuple-element.54), channel_id=1, source_target_pairs={{1,0},{2,1},{3,2},{4,3},{5,4},{6,5},{7,6},{8,7},{9,8},{10,9},{11,1... | collective-permute-start | bytes 294920 | tf_op jit(solution)/shard_map/ppermute | solution.py:28
  11.7 10.6 %collective-permute-start.7 = (bf16[2,2,32,512]{3,2,1,0:T(8,128)(2,1)S(1)}, bf16[2,2,32,512]{3,2,1,0:T(8,128)(2,1)S(1)}, u32[]{:S(2)}, u32[]{:S(2)}) collective-permute-start(bf16[2,2,32,512]{3,2,1,0:T(8,128)(2,1)S(1)} %pad_maximum_fusion.1), channel_id=1, source_target_pairs={{0,8},{1,9},{2,10},{3,11},{4,12},{5,13},{6,14},{7,15},{8,0},{9,1},... | collective-permute-start | bytes 393224 | tf_op jit(solution)/shard_map/ppermute | solution.py:22
  14.0 11.4 %collective-permute-start.4 = (bf16[128,512]{1,0:T(8,128)(2,1)S(1)}, bf16[128,512]{1,0:T(8,128)(2,1)S(1)}, u32[]{:S(2)}, u32[]{:S(2)}) collective-permute-start(bf16[128,512]{1,0:T(8,128)(2,1)S(1)} %get-tuple-element.56), channel_id=1, source_target_pairs={{0,8},{1,9},{2,10},{3,11},{4,12},{5,13},{6,14},{7,15},{8,0},{9,1},... | collective-permute-start | bytes 393224 | tf_op jit(solution)/shard_map/ppermute | solution.py:22
  16.9 17.5 %collective-permute-start.11 = (bf16[2,2,32,512]{3,2,1,0:T(8,128)(2,1)S(1)}, bf16[2,2,32,512]{3,2,1,0:T(8,128)(2,1)S(1)}, u32[]{:S(2)}, u32[]{:S(2)}) collective-permute-start(bf16[2,2,32,512]{3,2,1,0:T(8,128)(2,1)S(1)} %pad_maximum_fusion.refs_5_), channel_id=1, source_target_pairs={{0,4},{1,5},{2,6},{3,7},{4,0},{5,1},{6,2},{7,3},{8,12},{9,13},{10,... | collective-permute-start | bytes 393224 | tf_op jit(solution)/shard_map/ppermute | solution.py:22
  18.5 16.7 %collective-permute-start.13 = (bf16[2,2,32,512]{3,2,1,0:T(8,128)(2,1)S(1)}, bf16[2,2,32,512]{3,2,1,0:T(8,128)(2,1)S(1)}, u32[]{:S(2)}, u32[]{:S(2)}) collective-permute-start(bf16[2,2,32,512]{3,2,1,0:T(8,128)(2,1)S(1)} %pad_maximum_fusion.refs_5_), channel_id=1, source_target_pairs={{0,6},{1,7},{2,4},{3,5},{4,2},{5,3},{6,0},{7,1},{8,14},{9,15},{10,... | collective-permute-start | bytes 393224 | tf_op jit(solution)/shard_map/ppermute | solution.py:22
  18.7 16.5 %collective-permute-start.9 = (bf16[2,2,32,512]{3,2,1,0:T(8,128)(2,1)S(1)}, bf16[2,2,32,512]{3,2,1,0:T(8,128)(2,1)S(1)}, u32[]{:S(2)}, u32[]{:S(2)}) collective-permute-start(bf16[2,2,32,512]{3,2,1,0:T(8,128)(2,1)S(1)} %pad_maximum_fusion.refs_5_), channel_id=1, source_target_pairs={{0,2},{1,3},{2,0},{3,1},{4,6},{5,7},{6,4},{7,5},{8,10},{9,11},{10,... | collective-permute-start | bytes 393224 | tf_op jit(solution)/shard_map/ppermute | solution.py:22
  22.2 7.3 %collective-permute-start.2 = (bf16[128,512]{1,0:T(8,128)(2,1)S(1)}, bf16[128,512]{1,0:T(8,128)(2,1)S(1)}, u32[]{:S(2)}, u32[]{:S(2)}) collective-permute-start(bf16[128,512]{1,0:T(8,128)(2,1)S(1)} %get-tuple-element.55), channel_id=1, source_target_pairs={{0,8},{1,9},{2,10},{3,11},{4,12},{5,13},{6,14},{7,15},{8,0},{9,1},... | collective-permute-start | bytes 393224 | tf_op jit(solution)/shard_map/ppermute | solution.py:22
  25.4 8.8 %collective-permute-start.8 = (bf16[2,32,512]{2,1,0:T(8,128)(2,1)S(1)}, bf16[2,32,512]{2,1,0:T(8,128)(2,1)S(1)}, u32[]{:S(2)}, u32[]{:S(2)}) collective-permute-start(bf16[2,32,512]{2,1,0:T(8,128)(2,1)S(1)} %get-tuple-element.100), channel_id=1, source_target_pairs={{0,1},{1,0},{2,3},{3,2},{4,5},{5,4},{6,7},{7,6},{8,9},{9,8},{10,11... | collective-permute-start | bytes 196616 | tf_op jit(solution)/shard_map/ppermute | solution.py:22
  29.5 13.2 %collective-permute-start.5 = (bf16[256,512]{1,0:T(8,128)(2,1)S(1)}, bf16[256,512]{1,0:T(8,128)(2,1)S(1)}, u32[]{:S(2)}, u32[]{:S(2)}) collective-permute-start(bf16[256,512]{1,0:T(8,128)(2,1)S(1)} %constant_dynamic-update-slice_fusion.2.refs_2_), channel_id=1, source_target_pairs={{0,1},{1,0},{2,3},{3,2},{4,5},{5,4},{6,7},{7,6},{8,9},{9,8},{10,11... | collective-permute-start | bytes 786440 | tf_op jit(solution)/shard_map/ppermute | solution.py:22
  34.3 8.5 %collective-permute-start.3 = (bf16[256,512]{1,0:T(8,128)(2,1)S(1)}, bf16[256,512]{1,0:T(8,128)(2,1)S(1)}, u32[]{:S(2)}, u32[]{:S(2)}) collective-permute-start(bf16[256,512]{1,0:T(8,128)(2,1)S(1)} %constant_dynamic-update-slice_fusion.refs_0_), channel_id=1, source_target_pairs={{0,1},{1,0},{2,3},{3,2},{4,5},{5,4},{6,7},{7,6},{8,9},{9,8},{10,11... | collective-permute-start | bytes 786440 | tf_op jit(solution)/shard_map/ppermute | solution.py:22
  35.2 7.6 %collective-permute-start.14 = (bf16[2,2,32,512]{3,2,1,0:T(8,128)(2,1)S(1)}, bf16[2,2,32,512]{3,2,1,0:T(8,128)(2,1)S(1)}, u32[]{:S(2)}, u32[]{:S(2)}) collective-permute-start(bf16[2,2,32,512]{3,2,1,0:T(8,128)(2,1)S(1)} %pad_maximum_fusion.2.refs_6_), channel_id=1, source_target_pairs={{0,6},{1,7},{2,4},{3,5},{4,2},{5,3},{6,0},{7,1},{8,14},{9,15},{10,... | collective-permute-start | bytes 393224 | tf_op jit(solution)/shard_map/ppermute | solution.py:22
  44.1 5.6 %collective-permute-start.17 = (bf16[256,512]{1,0:T(8,128)(2,1)S(1)}, bf16[256,512]{1,0:T(8,128)(2,1)S(1)}, u32[]{:S(2)}, u32[]{:S(2)}) collective-permute-start(bf16[256,512]{1,0:T(8,128)(2,1)S(1)} %get-tuple-element.69), channel_id=1, source_target_pairs={{0,1},{1,0},{2,3},{3,2},{4,5},{5,4},{6,7},{7,6},{8,9},{9,8},{10,11... | collective-permute-start | bytes 786440 | tf_op jit(solution)/shard_map/ppermute | solution.py:22
  46.9 17.7 %collective-permute-start.21 = (bf16[2,2,2,32,512]{4,3,2,1,0:T(8,128)(2,1)S(1)}, bf16[2,2,2,32,512]{4,3,2,1,0:T(8,128)(2,1)S(1)}, u32[]{:S(2)}, u32[]{:S(2)}) collective-permute-start(bf16[2,2,2,32,512]{4,3,2,1,0:T(8,128)(2,1)S(1)} %get-tuple-element.78), channel_id=1, source_target_pairs={{0,2},{1,3},{2,0},{3,1},{4,6},{5,7},{6,4},{7,5},{8,10},{9,11},{10,... | collective-permute-start | bytes 786440 | tf_op jit(solution)/shard_map/ppermute | solution.py:22
  47.7 17.0 %collective-permute-start.22 = (bf16[2,2,2,32,512]{4,3,2,1,0:T(8,128)(2,1)S(1)}, bf16[2,2,2,32,512]{4,3,2,1,0:T(8,128)(2,1)S(1)}, u32[]{:S(2)}, u32[]{:S(2)}) collective-permute-start(bf16[2,2,2,32,512]{4,3,2,1,0:T(8,128)(2,1)S(1)} %get-tuple-element.79), channel_id=1, source_target_pairs={{0,4},{1,5},{2,6},{3,7},{4,0},{5,1},{6,2},{7,3},{8,12},{9,13},{10,... | collective-permute-start | bytes 786440 | tf_op jit(solution)/shard_map/ppermute | solution.py:22
  47.7 17.0 %collective-permute-start.23 = (bf16[2,2,2,32,512]{4,3,2,1,0:T(8,128)(2,1)S(1)}, bf16[2,2,2,32,512]{4,3,2,1,0:T(8,128)(2,1)S(1)}, u32[]{:S(2)}, u32[]{:S(2)}) collective-permute-start(bf16[2,2,2,32,512]{4,3,2,1,0:T(8,128)(2,1)S(1)} %get-tuple-element.80), channel_id=1, source_target_pairs={{0,6},{1,7},{2,4},{3,5},{4,2},{5,3},{6,0},{7,1},{8,14},{9,15},{10,... | collective-permute-start | bytes 786440 | tf_op jit(solution)/shard_map/ppermute | solution.py:22
  49.7 11.9 %collective-permute-start.18 = (bf16[128,512]{1,0:T(8,128)(2,1)S(1)}, bf16[128,512]{1,0:T(8,128)(2,1)S(1)}, u32[]{:S(2)}, u32[]{:S(2)}) collective-permute-start(bf16[128,512]{1,0:T(8,128)(2,1)S(1)} %get-tuple-element.71), channel_id=1, source_target_pairs={{0,8},{1,9},{2,10},{3,11},{4,12},{5,13},{6,14},{7,15},{8,0},{9,1},... | collective-permute-start | bytes 393224 | tf_op jit(solution)/shard_map/ppermute | solution.py:22
  50.6 22.9 %collective-permute-start.15 = (bf16[256,512]{1,0:T(8,128)(2,1)S(1)}, bf16[256,512]{1,0:T(8,128)(2,1)S(1)}, u32[]{:S(2)}, u32[]{:S(2)}) collective-permute-start(bf16[256,512]{1,0:T(8,128)(2,1)S(1)} %get-tuple-element.65), channel_id=1, source_target_pairs={{0,1},{1,0},{2,3},{3,2},{4,5},{5,4},{6,7},{7,6},{8,9},{9,8},{10,11... | collective-permute-start | bytes 786440 | tf_op jit(solution)/shard_map/ppermute | solution.py:22
  64.8 15.4 %collective-permute-start.25 = (bf16[2,2,32,512]{3,2,1,0:T(8,128)(2,1)S(1)}, bf16[2,2,32,512]{3,2,1,0:T(8,128)(2,1)S(1)}, u32[]{:S(2)}, u32[]{:S(2)}) collective-permute-start(bf16[2,2,32,512]{3,2,1,0:T(8,128)(2,1)S(1)} %get-tuple-element.83), channel_id=1, source_target_pairs={{0,8},{1,9},{2,10},{3,11},{4,12},{5,13},{6,14},{7,15},{8,0},{9,1},... | collective-permute-start | bytes 393224 | tf_op jit(solution)/shard_map/ppermute | solution.py:22
  71.5 6.8 %collective-permute-start.29 = (f32[28,512]{1,0:T(8,128)S(1)}, f32[28,512]{1,0:T(8,128)S(1)}, u32[]{:S(2)}, u32[]{:S(2)}) collective-permute-start(f32[28,512]{1,0:T(8,128)S(1)} %add.13), channel_id=1, source_target_pairs={{0,4},{1,5},{2,6},{3,7},{4,0},{5,1},{6,2},{7,3},{8,12},{9,13},{10,... | collective-permute-start | bytes 172040 | tf_op jit(solution)/shard_map/ppermute | solution.py:22
  72.0 16.6 %collective-permute-start.24 = (bf16[2,32,512]{2,1,0:T(8,128)(2,1)S(1)}, bf16[2,32,512]{2,1,0:T(8,128)(2,1)S(1)}, u32[]{:S(2)}, u32[]{:S(2)}) collective-permute-start(bf16[2,32,512]{2,1,0:T(8,128)(2,1)S(1)} %get-tuple-element.82), channel_id=1, source_target_pairs={{0,1},{1,0},{2,3},{3,2},{4,5},{5,4},{6,7},{7,6},{8,9},{9,8},{10,11... | collective-permute-start | bytes 196616 | tf_op jit(solution)/shard_map/ppermute | solution.py:22
  73.6 14.2 %collective-permute-start.16 = (bf16[128,512]{1,0:T(8,128)(2,1)S(1)}, bf16[128,512]{1,0:T(8,128)(2,1)S(1)}, u32[]{:S(2)}, u32[]{:S(2)}) collective-permute-start(bf16[128,512]{1,0:T(8,128)(2,1)S(1)} %get-tuple-element.67), channel_id=1, source_target_pairs={{0,8},{1,9},{2,10},{3,11},{4,12},{5,13},{6,14},{7,15},{8,0},{9,1},... | collective-permute-start | bytes 393224 | tf_op jit(solution)/shard_map/ppermute | solution.py:22
  75.2 14.3 %collective-permute-start.19 = (bf16[96,512]{1,0:T(8,128)(2,1)S(1)}, bf16[96,512]{1,0:T(8,128)(2,1)S(1)}, u32[]{:S(2)}, u32[]{:S(2)}) collective-permute-start(bf16[96,512]{1,0:T(8,128)(2,1)S(1)} %get-tuple-element.75), channel_id=1, source_target_pairs={{0,1},{1,2},{2,3},{3,4},{4,5},{5,6},{6,7},{7,8},{8,9},{9,10},{10,1... | collective-permute-start | bytes 294920 | tf_op jit(solution)/shard_map/ppermute | solution.py:28
  78.3 11.2 %collective-permute-start.20 = (bf16[96,512]{1,0:T(8,128)(2,1)S(1)}, bf16[96,512]{1,0:T(8,128)(2,1)S(1)}, u32[]{:S(2)}, u32[]{:S(2)}) collective-permute-start(bf16[96,512]{1,0:T(8,128)(2,1)S(1)} %get-tuple-element.76), channel_id=1, source_target_pairs={{1,0},{2,1},{3,2},{4,3},{5,4},{6,5},{7,6},{8,7},{9,8},{10,9},{11,1... | collective-permute-start | bytes 294920 | tf_op jit(solution)/shard_map/ppermute | solution.py:28
  (19 other events, 55.3 us)

commit v3 on v2

--- a/solution.py
+++ b/solution.py
@@ -32,43 +32,82 @@
     return jax.ShapeDtypeStruct(shape, dtype)
 
 
-def run(body, outs, *operands, scratch=(), mib=16, flops=0):
-    size = sum(math.prod(x.shape) * x.dtype.itemsize for x in (*operands, *outs))
+def swap_group(value):
+    return lax.ppermute(value, "grp", [(0, 1), (1, 0)])
+
+
+def run(body, outs, *operands, scratch=(), mib=16, order=0, apart=False):
+    extra = {"in_specs": [pl.BlockSpec(memory_space=pltpu.HBM)] * len(operands)} if apart else {}
     return pl.pallas_call(
         body,
         out_shape=outs,
+        **extra,
         scratch_shapes=scratch,
         compiler_params=pltpu.CompilerParams(vmem_limit_bytes=mib * 2**20),
-        cost_estimate=pl.CostEstimate(flops=flops, bytes_accessed=size, transcendentals=0),
+        cost_estimate=pl.CostEstimate(flops=order * 10**9, bytes_accessed=0, transcendentals=0),
     )(*operands)
 
 
 def place():
     me = lax.axis_index("row")
-    half = lax.axis_size("row") // 2
-    return me, lax.rem(me, 2), lax.div(me, half)
+    return me, lax.rem(me, 2), lax.rem(lax.div(me, 2), 2)
 
 
 def dot(left, right, dims):
     return lax.dot_general(left, right, (dims, ((), ())), preferred_element_type=WIDE)
 
 
-def split_body(inw, outw, cotan, scale, feats, own, core, far, both, branch, first, last):
-    _, core_bit, far_bit = place()
+def split_body(*refs):
+    sources, outs, held, sems = refs[:5], refs[5:10], refs[10:15], refs[15]
+    own, core, branch, first, last = outs
+    copies = [
+        pltpu.make_async_copy(source, copy, sems.at[k])
+        for k, (source, copy) in enumerate(zip(sources, held))
+    ]
+    for copy in copies:
+        copy.start()
+    inw, outw, feats, cotan, scale = held
+    _, c, x = place()
     quarter = own.shape[-1]
     rows = feats.shape[0]
-    for target, c, z in (
-        (own, core_bit, far_bit),
-        (core, 1 - core_bit, far_bit),
-        (far, core_bit, 1 - far_bit),
-        (both, 1 - core_bit, 1 - far_bit),
+    copies[0].wait()
+    copies[1].wait()
+    for target, part in (
+        (own.at[0], 2 * x + c),
+        (own.at[1], 2 * (1 - x) + c),
+        (core.at[0], 2 * x + 1 - c),
+        (core.at[1], 2 * (1 - x) + 1 - c),
     ):
-        lanes = pl.ds(pl.multiple_of((2 * z + c) * quarter, quarter), quarter)
+        lanes = pl.ds(pl.multiple_of(part * quarter, quarter), quarter)
         target[0] = inw[:, lanes].astype(NARROW)
         target[1] = outw[:, lanes].astype(NARROW)
-    branch[...] = (scale[...] * cotan[...]).astype(NARROW)
+    copies[2].wait()
     first[...] = feats[:RIM].astype(NARROW)
     last[...] = feats[rows - RIM :].astype(NARROW)
+    copies[3].wait()
+    copies[4].wait()
+    branch[...] = (scale[...] * cotan[...]).astype(NARROW)
+
+
+def join_body(mine, other, *targets):
+    which = lax.axis_index("grp")
+    for side in range(2):
+        full, sent = targets[2 * side : 2 * side + 2]
+        full[:, 0] = mine[side]
+        full[:, 1] = other[side]
+        sent[...] = full[which]
+
+
+def acts_body(normed, normed_got, branch, branch_got, acts):
+    pixels = normed.shape[0]
+    for which, (mine, got) in enumerate(((normed, normed_got), (branch, branch_got))):
+        acts[which, :pixels] = mine[...]
+        acts[which, pixels:] = got[...]
+
+
+def stack_body(*refs):
+    for place_in, ref in enumerate(refs[:-1]):
+        refs[-1][place_in] = ref[...]
 
 
 def fill(padded, block, low, high):
@@ -119,32 +158,38 @@
 
 
 def hidden_body(copied, *refs):
-    count = lax.axis_size("row")
-    me, _, far_bit = place()
-    mine = 2 * far_bit + lax.rem(me, 2)
-    normed, branch, in_bias = refs[:2], refs[2:4], refs[4]
-    outs = 5 + (count // 2 if copied else 1)
-    pieces = refs[5:outs]
-    keep, send, active, hidden, out_narrow, bias_part, in_narrow = refs[outs:]
-    half = normed[0].shape[0]
+    patterns = lax.axis_size("row") // 4
+    me, _, _ = place()
+    mine = lax.rem(me, 4)
+    acts, in_bias = refs[:2], refs[2]
+    pieces = refs[3:-7]
+    keep, send, active, hidden, out_narrow, bias_part, weights = refs[-7:]
+    half = acts[0].shape[1]
     if copied:
         own = pieces[0].shape[2]
-        for pattern in range(count // 4):
-            for z in range(2):
-                piece = pieces[2 * pattern + z]
+        group = lax.axis_index("grp")
+        for side in range(2):
+            full, near, here, there = pieces[4 * side : 4 * side + 4]
+            for pattern in range(patterns):
                 for c in range(2):
-                    device = jnp.bitwise_xor(me, z * (count // 2) + 2 * pattern + c)
+                    device = jnp.bitwise_xor(me, 4 * pattern + 2 * side + c)
                     rows = pl.ds(pl.multiple_of(device * own, own), own)
-                    in_narrow[rows, :] = piece[c, 0]
-                    out_narrow[rows, :] = piece[c, 1]
+                    if pattern < 2:
+                        source = near if pattern else full
+                        weights[0, rows, :] = source[0, c]
+                        weights[1, rows, :] = source[1, c]
+                    else:
+                        weights[group, rows, :] = here[pattern - 2, c]
+                        weights[1 - group, rows, :] = there[pattern - 2, c]
     else:
-        in_narrow[...] = pieces[0][0]
-        out_narrow[...] = pieces[0][1]
+        weights[...] = pieces[0][...]
+    in_narrow = weights.at[0]
+    out_narrow[...] = weights[1]
     bias_row = in_bias[pl.ds(mine, 1), :]
     total = jnp.zeros_like(bias_row)
     for side in (1, 0):
-        preact = dot(normed[side][...], in_narrow[...], ((1,), (0,))) + bias_row
-        act_grad = dot(branch[side][...], out_narrow[...], ((1,), (0,)))
+        preact = dot(acts[side][0], in_narrow[...], ((1,), (0,))) + bias_row
+        act_grad = dot(acts[side][1], out_narrow[...], ((1,), (0,)))
         cdf = 0.5 * (1.0 + lax.erf(preact * 0.7071067811865476))
         rows = pl.ds(side * half, half)
         active[rows, :] = (preact * cdf).astype(NARROW)
@@ -161,43 +206,37 @@
     bias_part[...] = total
 
 
-def weight_body(copied, norm_scale, *refs):
-    count = lax.axis_size("row")
-    me, _, _ = place()
-    normed, branch = refs[:2], refs[2:4]
-    active, hidden, out_narrow, scale = refs[4:8]
-    outs = refs[8:-1]
-    holder = refs[-1]
-    half = normed[0].shape[0]
+def weight_body(norm_scale, *refs):
+    acts = refs[:2]
+    active, hidden, out_narrow, scale = refs[2:6]
+    holder, mixed_keep, mixed_send, scale_part = refs[6:]
+    half = acts[0].shape[1]
     first, second = pl.ds(0, half), pl.ds(half, half)
-    for which, (left, right) in enumerate(((normed, hidden), (branch, active))):
-        grad = dot(left[0][...], right[first, :], ((0,), (0,)))
-        grad = grad + dot(left[1][...], right[second, :], ((0,), (0,)))
+    for which, right in enumerate((hidden, active)):
+        grad = dot(acts[0][which], right[first, :], ((0,), (0,)))
+        grad = grad + dot(acts[1][which], right[second, :], ((0,), (0,)))
         holder[which] = norm_scale * grad
-    if copied:
-        own = outs[0].shape[3]
-        for pattern in range(count // 4):
-            for z in range(2):
-                for c in range(2):
-                    device = jnp.bitwise_xor(me, z * (count // 2) + 2 * pattern + c)
-                    rows = pl.ds(pl.multiple_of(device * own, own), own)
-                    for which in range(2):
-                        target = outs[pattern]
-                        target[z, c, which] = holder[which, rows, :].astype(target.dtype)
-        rest = outs[count // 4 :]
-    else:
-        outs[0][...] = holder[...]
-        rest = outs[1:]
-    mixed_keep, mixed_send, scale_part = rest
     total = jnp.zeros_like(scale_part)
     for side, rows in enumerate((first, second)):
         mixed = dot(active[rows, :], out_narrow[...], ((1,), (1,)))
-        total = total + jnp.sum(mixed * branch[side][...].astype(WIDE), axis=0, keepdims=True)
+        total = total + jnp.sum(mixed * acts[side][1].astype(WIDE), axis=0, keepdims=True)
         if side:
             mixed_send[...] = mixed.astype(NARROW)
         else:
             mixed_keep[...] = mixed
     scale_part[...] = total / scale[...]
+
+
+def owners_body(holder, after, *targets):
+    del after
+    me, _, _ = place()
+    own = targets[0].shape[2]
+    for pattern, target in enumerate(targets):
+        for c in range(2):
+            device = jnp.bitwise_xor(me, 2 * pattern + c)
+            rows = pl.ds(pl.multiple_of(device * own, own), own)
+            for which in range(2):
+                target[c, which] = holder[which, rows, :].astype(target.dtype)
 
 
 def fold_body(kept, got, stay, leave):
@@ -227,7 +266,7 @@
     norm_scale, feats, low, high, grad, gain, bias, scale, in_bias, stay, leave, padded, small
 ):
     rows, cols, channels = feats.shape
-    _, core_bit, far_bit = place()
+    me, core_bit, _ = place()
     fill(padded, feats, low, high)
 
     def put(row, lanes, value):
@@ -256,7 +295,7 @@
     put(row, everything, gain[...])
     put(row + 1, everything, bias[...])
     put(row + 2, everything, scale[...])
-    mine = 2 * far_bit + core_bit
+    mine = lax.rem(me, 4)
     for part in range(4):
         own_part = jnp.where(mine == part, 1.0, 0.0)
         put(row + 3 + part, everything, own_part * in_bias[...])
@@ -281,26 +320,27 @@
     result[...] = feats[...] + scale[...] * (kept[...] + got[...].astype(WIDE))
 
 
-def total_body(*refs):
-    own, others, (stay, near, leave) = refs[0], refs[1:-3], refs[-3:]
-    total = own[...]
-    for other in others:
-        total = total + other[...].astype(WIDE)
-    stay[...] = total[0, 0]
-    near[...] = total[0, 1].astype(NARROW)
-    leave[...] = total[1].astype(NARROW)
-
-
-def owner_body(stay, near, far, both, in_grad, out_grad):
-    _, c, z = place()
+def total_body(turns, *refs):
+    stay, leave = refs[-2:]
+    for side in range(2):
+        total = jnp.zeros(stay.shape[1:], WIDE)
+        for part, turn in zip(refs, turns):
+            if turn % 2 == side:
+                total = total + part[...].astype(WIDE)
+        stay[side] = total[0]
+        leave[side] = total[1].astype(NARROW)
+
+
+def owner_body(stay, got, in_grad, out_grad):
+    _, c, x = place()
     quarter = stay.shape[-1]
-    for value, core, side in (
-        (stay, c, z),
-        (near, 1 - c, z),
-        (far, c, 1 - z),
-        (both, 1 - c, 1 - z),
+    for value, part in (
+        (stay[0], 2 * x + c),
+        (stay[1], 2 * (1 - x) + c),
+        (got[0], 2 * x + 1 - c),
+        (got[1], 2 * (1 - x) + 1 - c),
     ):
-        lanes = pl.ds(pl.multiple_of((2 * side + core) * quarter, quarter), quarter)
+        lanes = pl.ds(pl.multiple_of(part * quarter, quarter), quarter)
         in_grad[:, lanes] = value[0].astype(WIDE)
         out_grad[:, lanes] = value[1].astype(WIDE)
 
@@ -346,7 +386,7 @@
     count = lax.axis_size("row")
     bit_count = count.bit_length() - 1
     me = lax.axis_index("row")
-    far = count // 2
+    group_index = lax.axis_index("grp")
     quarter = hidden_count // 4
     norm_scale = 1.0 / math.sqrt(pixels * count)
     patterns = count // 4
@@ -358,32 +398,43 @@
     scale_row = layer_scale.reshape(1, channels)
     rim = (RIM, col_count, channels)
     padded = pltpu.VMEM((row_count + 2 * RIM, col_count + 2 * EDGE, channels), WIDE)
-    conv_flops = 2 * TAPS * TAPS * pixels * channels
-
-    piece = shaped((2, own_rows, quarter), NARROW)
-    own, core, beyond, both, branch, first, last = run(
+
+    piece = (2, own_rows, quarter)
+    sources = (in_weight, out_weight, features, flat_cotan, scale_row)
+    own, core, branch, first, last = run(
         split_body,
-        (piece,) * 4 + (shaped((pixels, channels), NARROW), shaped(rim, NARROW), shaped(rim, NARROW)),
-        in_weight,
-        out_weight,
-        flat_cotan,
-        scale_row,
-        features,
+        (
+            shaped((2,) + piece, NARROW),
+            shaped((2,) + piece, NARROW),
+            shaped((pixels, channels), NARROW),
+            shaped(rim, NARROW),
+            shaped(rim, NARROW),
+        ),
+        *sources,
+        scratch=tuple(pltpu.VMEM(x.shape, x.dtype) for x in sources)
+        + (pltpu.SemaphoreType.DMA((len(sources),)),),
+        mib=60,
+        apart=True,
+    )
+
+    full_shape = shaped((2, 2, own_rows, quarter), NARROW)
+    joined = run(
+        join_body,
+        (full_shape, shaped(piece, NARROW)) * 2,
+        own,
+        swap(core, 1),
     )
     low = shift(last, 1)
     high = shift(first, -1)
-    near = jnp.stack([own, swap(core, 1)])
-    got = swap(jnp.stack([beyond, both]), far)
-    distant = jnp.stack([got[0], swap(got[1], 1)])
-    pieces = [near, distant]
-    for p in range(1, patterns):
-        pieces += [swap(near, 2 * p), swap(distant, 2 * p)]
-
-    def group_gather(value):
-        two = jnp.concatenate([value, swap(value, far)])
-        return two, swap(two, 1)
-
-    branch_all = group_gather(branch)
+    pieces = []
+    for side in range(2):
+        full, sent = joined[2 * side : 2 * side + 2]
+        here = [swap(sent, 4 * p + 2 * side) for p in range(2, patterns)]
+        here = run(stack_body, (shaped((patterns - 2,) + piece, NARROW),), *here, order=8)[0]
+        near = swap(full, 4 + 2 * side)
+        pieces += [swap(full, 2) if side else full, near, here, swap_group(here)]
+
+    branch_got = swap(branch, 2)
     normed, inv, normed_out = run(
         conv_body,
         (
@@ -398,15 +449,31 @@
         gain_row,
         bias_row,
         scratch=(padded, pltpu.VMEM((pixels, channels), WIDE)),
-        flops=conv_flops,
-    )
-    normed_all = group_gather(normed_out)
+    )
+    group_shape = (2, 2 * pixels, channels)
+    acts = run(
+        acts_body,
+        (shaped(group_shape, NARROW),),
+        normed_out,
+        swap(normed_out, 2),
+        branch,
+        branch_got,
+    )[0]
+    acts_got = swap(acts, 1)
 
     if not copied:
-        stacked = jnp.stack(pieces).reshape(patterns, 2, 2, 2, own_rows, quarter)
-        stacked = jnp.moveaxis(stacked, 0, 1).reshape(count, 2, own_rows, quarter)
-        stacked = jnp.moveaxis(canonical(stacked, me, bit_count), 1, 0)
-        pieces = [stacked.reshape(2, channels, quarter)]
+        lines = []
+        for pattern in range(patterns):
+            for side in range(2):
+                full, near, here, there = pieces[4 * side : 4 * side + 4]
+                if pattern < 2:
+                    lines.append(near if pattern else full)
+                else:
+                    pair = jnp.stack([here[pattern - 2], there[pattern - 2]])
+                    lines.append(flipped(pair, 0, group_index))
+        lines = jnp.moveaxis(jnp.stack(lines), 1, 2).reshape(count, 2, own_rows, quarter)
+        lines = jnp.moveaxis(canonical(lines, me, bit_count), 1, 0)
+        pieces = [lines.reshape(2, channels, quarter)]
     group = 4 * pixels
     out_keep, out_send, active, hidden, out_narrow, in_bias_part = run(
         functools.partial(hidden_body, copied),
@@ -418,50 +485,44 @@
             shaped((channels, quarter), NARROW),
             shaped((1, quarter)),
         ),
-        *normed_all,
-        *branch_all,
+        acts,
+        acts_got,
         in_bias.reshape(4, quarter),
         *pieces,
-        scratch=(pltpu.VMEM((channels, quarter), NARROW),),
+        scratch=(pltpu.VMEM((2, channels, quarter), NARROW),),
         mib=24,
-        flops=6 * group * channels * quarter,
     )
     half = (shaped((pixels, channels)), shaped((pixels, channels), NARROW))
     out_stay, out_leave = run(fold_body, half, out_keep, swap(out_send, 1))
-    out_got = swap(out_leave, far)
-
-    grads = (2, 2, 2, own_rows, quarter)
-    if copied:
-        grad_shapes = (shaped(grads),) + (shaped(grads, NARROW),) * (patterns - 1)
-    else:
-        grad_shapes = (shaped((2, channels, quarter)),)
-    *grad_parts, mixed_keep, mixed_send, scale_part = run(
-        functools.partial(weight_body, copied, norm_scale),
-        grad_shapes
-        + (
+    out_got = swap(out_leave, 2)
+
+    owned = (2, 2, own_rows, quarter)
+    holder, mixed_keep, mixed_send, scale_part = run(
+        functools.partial(weight_body, norm_scale),
+        (
+            shaped((2, channels, quarter)),
             shaped((2 * pixels, channels)),
             shaped((2 * pixels, channels), NARROW),
             shaped((1, channels)),
         ),
-        *normed_all,
-        *branch_all,
+        acts,
+        acts_got,
         active,
         hidden,
         out_narrow,
         scale_row,
-        scratch=(pltpu.VMEM((2, channels, quarter), WIDE),),
         mib=24,
-        flops=6 * group * channels * quarter,
-    )
-    if not copied:
-        parts = grad_parts[0].reshape(2, count, own_rows, quarter)
+    )
+    kinds = (WIDE,) + (NARROW,) * (2 * patterns - 1)
+    if copied:
+        parts = run(owners_body, tuple(shaped(owned, kind) for kind in kinds), holder, out_leave)
+    else:
+        parts = holder.reshape(2, count, own_rows, quarter)
         parts = canonical(jnp.moveaxis(parts, 1, 0), me, bit_count)
-        parts = parts.reshape(2, patterns, 2, 2, own_rows, quarter)
-        grad_parts = [parts[:, 0]] + [parts[:, p].astype(NARROW) for p in range(1, patterns)]
-    arrived = [swap(grad_parts[p], 2 * p) for p in range(1, patterns)]
-    mixed_stay, mixed_leave = run(fold_body, half, mixed_keep, swap(mixed_send, 1))
-    mixed_got = swap(mixed_leave, far)
-
+        parts = parts.reshape(2 * patterns, 2, 2, own_rows, quarter)
+        parts = [parts[p].astype(kind) for p, kind in enumerate(kinds)]
+    turns = (*range(4, 2 * patterns), 2, 3, 1, 0)
+    parts = [swap(parts[p], 2 * p) if p else parts[p] for p in turns]
     flat_rim = shaped((RIM * col_count, channels), NARROW)
     conv_grad, first, last, gain_part, bias_part = run(
         norm_grad_body,
@@ -493,11 +554,14 @@
         scale_part,
         in_bias_part,
         scratch=(padded, pltpu.VMEM((2, SMALL_ROWS, channels), WIDE)),
-        flops=conv_flops,
     )
     sums = stay + swap(leave, 1)
     for spot in range(1, bit_count):
         sums = sums + swap(sums, 1 << spot)
+        if spot == 1:
+            sums, mixed_send = lax.optimization_barrier((sums, mixed_send))
+    mixed_stay, mixed_leave = run(fold_body, half, mixed_keep, swap(mixed_send, 1))
+    mixed_got = swap(mixed_leave, 2)
 
     input_grad = run(
         input_grad_body,
@@ -508,7 +572,6 @@
         kernel,
         cotangent,
         scratch=(padded,),
-        flops=conv_flops,
     )[0]
     output = run(
         output_body,
@@ -519,23 +582,14 @@
         mixed_got,
     )[0].reshape(features.shape)
 
-    quarters = (2, own_rows, quarter)
-    stay, near, leave = run(
-        total_body,
-        (shaped(quarters), shaped(quarters, NARROW), shaped((2,) + quarters, NARROW)),
-        grad_parts[0],
-        *arrived,
-    )
-    near_got = swap(near, 1)
-    far_got = swap(leave, far)
-    both_got = swap(far_got[1], 1)
+    stay, leave = run(
+        functools.partial(total_body, turns),
+        (shaped((2,) + piece), shaped((2,) + piece, NARROW)),
+        *parts,
+        order=20,
+    )
     in_weight_grad, out_weight_grad = run(
-        owner_body,
-        (shaped((own_rows, hidden_count)),) * 2,
-        stay,
-        near_got,
-        far_got[0],
-        both_got,
+        owner_body, (shaped((own_rows, hidden_count)),) * 2, stay, swap(leave, 1)
     )
     kernel_grad, gain_grad, bias_grad, scale_grad, in_bias_grad = run(
         small_body,

time: 94 us -> 92.6 us (0.985)
  waiting for transfers between devices: 24 us -> 21 us
  Pallas kernels: 12.3 us -> 14.4 us
    ppermute x28, waiting for transfers between devices: 24 us -> 15.8 us  [swap(): return lax.ppermute(value, 'row', [(i, i ^ bit) for i in range(count)])]
    ppermute x4, waiting for transfers between devices: 0.01 us -> 3.9 us  [shift(): return lax.ppermute(value, 'row', pairs)]
    ppermute x0 -> x2, starting transfers between devices: none -> 2.61 us  [swap_group(): return lax.ppermute(value, 'grp', [(0, 1), (1, 0)])]
    pallas_call x13 -> x18, Pallas kernels: 12.3 us -> 14.4 us  [run(): pl.pallas_call(body, out_shape=outs, **extra, scratch_shapes=scratch, com...]
    ppermute x28, starting transfers between devices: 39.8 us -> 37.8 us  [swap(): return lax.ppermute(value, 'row', [(i, i ^ bit) for i in range(count)])]
    ppermute x0 -> x2, waiting for transfers between devices: none -> 1.23 us  [swap_group(): return lax.ppermute(value, 'grp', [(0, 1), (1, 0)])]
  transfers between devices with their start and end apart: 32 -> 34, of which waited for: 8 -> 8; matrix products, arithmetic and copies ran while one was open for 0% -> 0% of each run, Pallas kernels for 11% -> 11%
where the time goes in v3:
time: 92.6 us; the launch traced here: 92.2 us
  starting transfers between devices  51.7 us (56%)
  waiting for transfers between devices  21 us (23%)
  Pallas kernels  14.4 us (16%)
  local copies, waits for them, and re-layouts  4.15 us (4%)
  between operations  0.96 us (1%)
    ppermute x28, starting transfers between devices, swap(): return lax.ppermute(value, 'row', [(i, i ^ bit) for i in range(count)])  37.8 us
    ppermute x28, waiting for transfers between devices, swap(): return lax.ppermute(value, 'row', [(i, i ^ bit) for i in range(count)])  15.8 us
    pallas_call x18, Pallas kernels, run(): pl.pallas_call(body, out_shape=outs, **extra, scratch_shapes=scratch, com...  14.4 us
    ppermute x4, starting transfers between devices, shift(): return lax.ppermute(value, 'row', pairs)  11.4 us
    unnamed x24, local copies, waits for them, and re-layouts  4.14 us
    ppermute x4, waiting for transfers between devices, shift(): return lax.ppermute(value, 'row', pairs)  3.9 us
    ppermute x2, starting transfers between devices, swap_group(): return lax.ppermute(value, 'grp', [(0, 1), (1, 0)])  2.61 us
  transfers between devices with their start and end apart: 34, of which 8 were waited for; matrix products, arithmetic and copies ran while one was open for 0% of the time, Pallas kernels for 11%

profile of v3, /device:TPU:1, one launch (start us, length us, event | category | flops | bytes accessed | tf_op | source)
XLA Modules:
  0.0 92.2 jit_solution(13718751703841249543)
XLA Ops:
  0.6 2.0 %shard_map.160 = (bf16[2,2,32,512]{3,2,1,0:T(8,128)(2,1)}, bf16[2,2,32,512]{3,2,1,0:T(8,128)(2,1)}, bf16[128,512]{1,0:T(8,128)(2,1)}, bf16[3,32,512]{2,1,0:T(8,128)(2,1)}, bf16[3,32,512]{2,1,0:T(8,128)(2,1)}) custom-call(f32[32,2048]{1,0:T(8,128)} %refs_0_.1, f32[32,2048]{1,0:T(8,128)} %refs_1_.1, f32[4,32,512]{2,1,0:T(8,128)} %feats.3, ...), custom_call_target="tpu_custom_call" | custom-call | tf_op jit(solution)/shard_map/pallas_call | solution.py:41
  2.8 4.5 %collective-permute-start = (bf16[3,32,512]{2,1,0:T(8,128)(2,1)}, bf16[3,32,512]{2,1,0:T(8,128)(2,1)S(1)}, u32[]{:S(2)}, u32[]{:S(2)}) collective-permute-start(bf16[3,32,512]{2,1,0:T(8,128)(2,1)} %get-tuple-element.61), channel_id=1, source_target_pairs={{0,1},{1,2},{2,3},{3,4},{4,5},{5,6},{6,7},{7,8},{8,9},{9,10},{10,1... | collective-permute-start | bytes 294920 | tf_op jit(solution)/shard_map/ppermute | solution.py:28
  7.3 1.9 %collective-permute-start.1 = (bf16[3,32,512]{2,1,0:T(8,128)(2,1)}, bf16[3,32,512]{2,1,0:T(8,128)(2,1)S(1)}, u32[]{:S(2)}, u32[]{:S(2)}) collective-permute-start(bf16[3,32,512]{2,1,0:T(8,128)(2,1)} %get-tuple-element.62), channel_id=1, source_target_pairs={{1,0},{2,1},{3,2},{4,3},{5,4},{6,5},{7,6},{8,7},{9,8},{10,9},{11,1... | collective-permute-start | bytes 294920 | tf_op jit(solution)/shard_map/ppermute | solution.py:28
  10.2 3.4 %collective-permute-start.12 = (bf16[2,32,512]{2,1,0:T(8,128)(2,1)S(1)}, bf16[2,32,512]{2,1,0:T(8,128)(2,1)S(1)}, u32[]{:S(2)}, u32[]{:S(2)}) collective-permute-start(bf16[2,32,512]{2,1,0:T(8,128)(2,1)S(1)} %get-tuple-element.70), channel_id=1, source_target_pairs={{0,10},{1,11},{2,8},{3,9},{4,14},{5,15},{6,12},{7,13},{8,2},{9,3},... | collective-permute-start | bytes 196616 | tf_op jit(solution)/shard_map/ppermute | solution.py:22
  19.0 2.4 %shard_map.161 = (f32[128,512]{1,0:T(8,128)S(1)}, f32[128,128]{1,0:T(8,128)S(1)}, bf16[128,512]{1,0:T(8,128)(2,1)S(1)}) custom-call(f32[4,32,512]{2,1,0:T(8,128)S(1)} %copy-done, bf16[3,32,512]{2,1,0:T(8,128)(2,1)S(1)} %collective-permute-done.low, bf16[3,32,512]{2,1,0:T(8,128)(2,1)S(1)} %collective-permute-done.1.high, f32[7,7,512]{2,1,0:T(8,128)S(1)} %copy-done.3, ...), custom_call_target="tpu_custom_call" | custom-call | tf_op jit(solution)/shard_map/pallas_call | solution.py:41
  21.7 3.0 %collective-permute-start.7 = (bf16[2,32,512]{2,1,0:T(8,128)(2,1)S(1)}, bf16[2,32,512]{2,1,0:T(8,128)(2,1)S(1)}, u32[]{:S(2)}, u32[]{:S(2)}) collective-permute-start(bf16[2,32,512]{2,1,0:T(8,128)(2,1)S(1)} %get-tuple-element.68), channel_id=1, source_target_pairs={{0,8},{1,9},{2,10},{3,11},{4,12},{5,13},{6,14},{7,15},{8,0},{9,1},... | collective-permute-start | bytes 196616 | tf_op jit(solution)/shard_map/ppermute | solution.py:22
  26.3 2.5 %collective-permute-start.6 = (bf16[2,2,32,512]{3,2,1,0:T(8,128)(2,1)S(1)}, bf16[2,2,32,512]{3,2,1,0:T(8,128)(2,1)S(1)}, u32[]{:S(2)}, u32[]{:S(2)}) collective-permute-start(bf16[2,2,32,512]{3,2,1,0:T(8,128)(2,1)S(1)} %get-tuple-element.67.refs_3_), channel_id=1, source_target_pairs={{0,4},{1,5},{2,6},{3,7},{4,0},{5,1},{6,2},{7,3},{8,12},{9,13},{10,... | collective-permute-start | bytes 393224 | tf_op jit(solution)/shard_map/ppermute | solution.py:22
  30.1 2.4 %collective-permute-start.4 = (bf16[2,256,512]{2,1,0:T(8,128)(2,1)S(1)}, bf16[2,256,512]{2,1,0:T(8,128)(2,1)S(1)}, u32[]{:S(2)}, u32[]{:S(2)}) collective-permute-start(bf16[2,256,512]{2,1,0:T(8,128)(2,1)S(1)} %shard_map.162.refs_0_), channel_id=1, source_target_pairs={{0,1},{1,0},{2,3},{3,2},{4,5},{5,4},{6,7},{7,6},{8,9},{9,8},{10,11... | collective-permute-start | bytes 1572872 | tf_op jit(solution)/shard_map/ppermute | solution.py:22
  36.5 1.4 %shard_map.166 = (f32[256,512]{1,0:T(8,128)S(1)}, bf16[256,512]{1,0:T(8,128)(2,1)S(1)}, bf16[512,512]{1,0:T(8,128)(2,1)S(1)}, bf16[512,512]{1,0:T(8,128)(2,1)S(1...) custom-call(bf16[2,256,512]{2,1,0:T(8,128)(2,1)S(1)} %shard_map.162.refs_0_, ...), custom_call_target="tpu_custom_call" | custom-call | tf_op jit(solution)/shard_map/pallas_call | solution.py:41
  37.9 2.8 %collective-permute-start.15 = (bf16[256,512]{1,0:T(8,128)(2,1)S(1)}, bf16[256,512]{1,0:T(8,128)(2,1)S(1)}, u32[]{:S(2)}, u32[]{:S(2)}) collective-permute-start(bf16[256,512]{1,0:T(8,128)(2,1)S(1)} %get-tuple-element.76), channel_id=1, source_target_pairs={{0,1},{1,0},{2,3},{3,2},{4,5},{5,4},{6,7},{7,6},{8,9},{9,8},{10,11... | collective-permute-start | bytes 786440 | tf_op jit(solution)/shard_map/ppermute | solution.py:22
  44.4 2.4 %collective-permute-start.24 = (bf16[2,2,32,512]{3,2,1,0:T(8,128)(2,1)S(1)}, bf16[2,2,32,512]{3,2,1,0:T(8,128)(2,1)S(1)}, u32[]{:S(2)}, u32[]{:S(2)}) collective-permute-start(bf16[2,2,32,512]{3,2,1,0:T(8,128)(2,1)S(1)} %get-tuple-element.96), channel_id=1, source_target_pairs={{0,10},{1,11},{2,8},{3,9},{4,14},{5,15},{6,12},{7,13},{8,2},{9,3},... | collective-permute-start | bytes 393224 | tf_op jit(solution)/shard_map/ppermute | solution.py:22
  47.0 1.7 %shard_map.170 = (f32[28,512]{1,0:T(8,128)S(1)}, f32[28,512]{1,0:T(8,128)S(1)}) custom-call(f32[4,32,512]{2,1,0:T(8,128)S(1)} %copy-done.1, bf16[3,32,512]{2,1,0:T(8,128)(2,1)S(1)} %collective-permute-done.low, bf16[3,32,512]{2,1,0:T(8,128)(2,1)S(1)} %collective-permute-done.1.high, f32[128,512]{1,0:T(8,128)S(1)} %get-tuple-element.81.grad, ...), custom_call_target="tpu_custom_call" | custom-call | tf_op jit(solution)/shard_map/pallas_call | solution.py:41
  51.0 2.7 %collective-permute-start.25 = (bf16[2,2,32,512]{3,2,1,0:T(8,128)(2,1)S(1)}, bf16[2,2,32,512]{3,2,1,0:T(8,128)(2,1)S(1)}, u32[]{:S(2)}, u32[]{:S(2)}) collective-permute-start(bf16[2,2,32,512]{3,2,1,0:T(8,128)(2,1)S(1)} %get-tuple-element.97), channel_id=1, source_target_pairs={{0,12},{1,13},{2,14},{3,15},{4,8},{5,9},{6,10},{7,11},{8,4},{9,5},... | collective-permute-start | bytes 393224 | tf_op jit(solution)/shard_map/ppermute | solution.py:22
  53.6 1.8 %collective-permute-start.26 = (bf16[2,2,32,512]{3,2,1,0:T(8,128)(2,1)S(1)}, bf16[2,2,32,512]{3,2,1,0:T(8,128)(2,1)S(1)}, u32[]{:S(2)}, u32[]{:S(2)}) collective-permute-start(bf16[2,2,32,512]{3,2,1,0:T(8,128)(2,1)S(1)} %get-tuple-element.98), channel_id=1, source_target_pairs={{0,14},{1,15},{2,12},{3,13},{4,10},{5,11},{6,8},{7,9},{8,6},{9,7},... | collective-permute-start | bytes 393224 | tf_op jit(solution)/shard_map/ppermute | solution.py:22
  55.4 9.3 %collective-permute-done.24.refs_1_ = bf16[2,2,32,512]{3,2,1,0:T(8,128)(2,1)S(1)} collective-permute-done((bf16[2,2,32,512]{3,2,1,0:T(8,128)(2,1)S(1)}, bf16[2,2,32,512]{3,2,1,0:T(8,128)(2,1)S(1)}, u32[]{:S(2)}, u32[]{:S(2)}) %collective-permute-start.24) | collective-permute-done | bytes 131104 | tf_op jit(solution)/shard_map/ppermute | solution.py:22
  64.8 2.7 %collective-permute-start.31 = (f32[28,512]{1,0:T(8,128)S(1)}, f32[28,512]{1,0:T(8,128)S(1)}, u32[]{:S(2)}, u32[]{:S(2)}) collective-permute-start(f32[28,512]{1,0:T(8,128)S(1)} %add.13), channel_id=1, source_target_pairs={{0,4},{1,5},{2,6},{3,7},{4,0},{5,1},{6,2},{7,3},{8,12},{9,13},{10,... | collective-permute-start | bytes 172040 | tf_op jit(solution)/shard_map/ppermute | solution.py:22
  67.5 1.5 %collective-permute-start.19 = (bf16[256,512]{1,0:T(8,128)(2,1)S(1)}, bf16[256,512]{1,0:T(8,128)(2,1)S(1)}, u32[]{:S(2)}, u32[]{:S(2)}) collective-permute-start(bf16[256,512]{1,0:T(8,128)(2,1)S(1)} %get-tuple-element.89), channel_id=1, source_target_pairs={{0,1},{1,0},{2,3},{3,2},{4,5},{5,4},{6,7},{7,6},{8,9},{9,8},{10,11... | collective-permute-start | bytes 786440 | tf_op jit(solution)/shard_map/ppermute | solution.py:22
  70.1 2.0 %collective-permute-done.29.refs_6_ = bf16[2,2,32,512]{3,2,1,0:T(8,128)(2,1)S(1)} collective-permute-done((bf16[2,2,32,512]{3,2,1,0:T(8,128)(2,1)S(1)}, bf16[2,2,32,512]{3,2,1,0:T(8,128)(2,1)S(1)}, u32[]{:S(2)}, u32[]{:S(2)}) %collective-permute-start.29) | collective-permute-done | bytes 131104 | tf_op jit(solution)/shard_map/ppermute | solution.py:22
  72.2 1.5 %collective-permute-start.30 = (bf16[2,2,32,512]{3,2,1,0:T(8,128)(2,1)S(1)}, bf16[2,2,32,512]{3,2,1,0:T(8,128)(2,1)S(1)}, u32[]{:S(2)}, u32[]{:S(2)}) collective-permute-start(bf16[2,2,32,512]{3,2,1,0:T(8,128)(2,1)S(1)} %get-tuple-element.104), channel_id=1, source_target_pairs={{0,1},{1,0},{2,3},{3,2},{4,5},{5,4},{6,7},{7,6},{8,9},{9,8},{10,11... | collective-permute-start | bytes 393224 | tf_op jit(solution)/shard_map/ppermute | solution.py:22
  73.8 4.3 %collective-permute-start.32 = (f32[28,512]{1,0:T(8,128)S(1)}, f32[28,512]{1,0:T(8,128)S(1)}, u32[]{:S(2)}, u32[]{:S(2)}) collective-permute-start(f32[28,512]{1,0:T(8,128)S(1)} %add.14), channel_id=1, source_target_pairs={{0,8},{1,9},{2,10},{3,11},{4,12},{5,13},{6,14},{7,15},{8,0},{9,1},... | collective-permute-start | bytes 172040 | tf_op jit(solution)/shard_map/ppermute | solution.py:22
  78.1 3.1 %collective-permute-start.21 = (bf16[96,512]{1,0:T(8,128)(2,1)S(1)}, bf16[96,512]{1,0:T(8,128)(2,1)S(1)}, u32[]{:S(2)}, u32[]{:S(2)}) collective-permute-start(bf16[96,512]{1,0:T(8,128)(2,1)S(1)} %get-tuple-element.92), channel_id=1, source_target_pairs={{0,1},{1,2},{2,3},{3,4},{4,5},{5,6},{6,7},{7,8},{8,9},{9,10},{10,1... | collective-permute-start | bytes 294920 | tf_op jit(solution)/shard_map/ppermute | solution.py:28
  81.2 1.9 %collective-permute-start.22 = (bf16[96,512]{1,0:T(8,128)(2,1)S(1)}, bf16[96,512]{1,0:T(8,128)(2,1)S(1)}, u32[]{:S(2)}, u32[]{:S(2)}) collective-permute-start(bf16[96,512]{1,0:T(8,128)(2,1)S(1)} %get-tuple-element.93), channel_id=1, source_target_pairs={{1,0},{2,1},{3,2},{4,3},{5,4},{6,5},{7,6},{8,7},{9,8},{10,9},{11,1... | collective-permute-start | bytes 294920 | tf_op jit(solution)/shard_map/ppermute | solution.py:28
  83.2 3.9 %collective-permute-done.22 = bf16[96,512]{1,0:T(8,128)(2,1)S(1)} collective-permute-done((bf16[96,512]{1,0:T(8,128)(2,1)S(1)}, bf16[96,512]{1,0:T(8,128)(2,1)S(1)}, u32[]{:S(2)}, u32[]{:S(2)}) %collective-permute-start.22) | collective-permute-done | bytes 98336 | tf_op jit(solution)/shard_map/ppermute | solution.py:28
  87.1 2.9 %shard_map.173 = f32[4,32,512]{2,1,0:T(8,128)} custom-call(f32[4,32,512]{2,1,0:T(8,128)S(1)} %bitcast.15, bf16[3,32,512]{2,1,0:T(8,128)(2,1)S(1)} %bitcast.16, bf16[3,32,512]{2,1,0:T(8,128)(2,1)S(1)} %bitcast.17, f32[7,7,512]{2,1,0:T(8,128)S(1)} %copy-done.4, f32[4,32,512]{2,1,0:T(8,128)S(1)} %copy-done.2), custom_call_target="tpu_custom_call" | custom-call | tf_op jit(solution)/shard_map/pallas_call | solution.py:41
  (91 shorter events, 23.5 us)
Async XLA Ops:
  2.7 6.5 %collective-permute-start.5 = (bf16[2,2,32,512]{3,2,1,0:T(8,128)(2,1)}, bf16[2,2,32,512]{3,2,1,0:T(8,128)(2,1)S(1)}, u32[]{:S(2)}, u32[]{:S(2)}) collective-permute-start(bf16[2,2,32,512]{3,2,1,0:T(8,128)(2,1)} %get-tuple-element.66), channel_id=1, source_target_pairs={{0,1},{1,0},{2,3},{3,2},{4,5},{5,4},{6,7},{7,6},{8,9},{9,8},{10,11... | collective-permute-start | bytes 393224 | tf_op jit(solution)/shard_map/ppermute | solution.py:22
  2.8 13.0 %collective-permute-start = (bf16[3,32,512]{2,1,0:T(8,128)(2,1)}, bf16[3,32,512]{2,1,0:T(8,128)(2,1)S(1)}, u32[]{:S(2)}, u32[]{:S(2)}) collective-permute-start(bf16[3,32,512]{2,1,0:T(8,128)(2,1)} %get-tuple-element.61), channel_id=1, source_target_pairs={{0,1},{1,2},{2,3},{3,4},{4,5},{5,6},{6,7},{7,8},{8,9},{9,10},{10,1... | collective-permute-start | bytes 294920 | tf_op jit(solution)/shard_map/ppermute | solution.py:28
  7.3 8.5 %collective-permute-start.1 = (bf16[3,32,512]{2,1,0:T(8,128)(2,1)}, bf16[3,32,512]{2,1,0:T(8,128)(2,1)S(1)}, u32[]{:S(2)}, u32[]{:S(2)}) collective-permute-start(bf16[3,32,512]{2,1,0:T(8,128)(2,1)} %get-tuple-element.62), channel_id=1, source_target_pairs={{1,0},{2,1},{3,2},{4,3},{5,4},{6,5},{7,6},{8,7},{9,8},{10,9},{11,1... | collective-permute-start | bytes 294920 | tf_op jit(solution)/shard_map/ppermute | solution.py:28
  10.2 14.5 %collective-permute-start.12 = (bf16[2,32,512]{2,1,0:T(8,128)(2,1)S(1)}, bf16[2,32,512]{2,1,0:T(8,128)(2,1)S(1)}, u32[]{:S(2)}, u32[]{:S(2)}) collective-permute-start(bf16[2,32,512]{2,1,0:T(8,128)(2,1)S(1)} %get-tuple-element.70), channel_id=1, source_target_pairs={{0,10},{1,11},{2,8},{3,9},{4,14},{5,15},{6,12},{7,13},{8,2},{9,3},... | collective-permute-start | bytes 196616 | tf_op jit(solution)/shard_map/ppermute | solution.py:22
  13.5 12.5 %collective-permute-start.13 = (bf16[2,32,512]{2,1,0:T(8,128)(2,1)S(1)}, bf16[2,32,512]{2,1,0:T(8,128)(2,1)S(1)}, u32[]{:S(2)}, u32[]{:S(2)}) collective-permute-start(bf16[2,32,512]{2,1,0:T(8,128)(2,1)S(1)} %get-tuple-element.70), channel_id=1, source_target_pairs={{0,14},{1,15},{2,12},{3,13},{4,10},{5,11},{6,8},{7,9},{8,6},{9,7},... | collective-permute-start | bytes 196616 | tf_op jit(solution)/shard_map/ppermute | solution.py:22
  14.5 11.6 %collective-permute-start.3 = (bf16[128,512]{1,0:T(8,128)(2,1)}, bf16[128,512]{1,0:T(8,128)(2,1)S(1)}, u32[]{:S(2)}, u32[]{:S(2)}) collective-permute-start(bf16[128,512]{1,0:T(8,128)(2,1)} %get-tuple-element.64.branch), channel_id=1, source_target_pairs={{0,2},{1,3},{2,0},{3,1},{4,6},{5,7},{6,4},{7,5},{8,10},{9,11},{10,... | collective-permute-start | bytes 393224 | tf_op jit(solution)/shard_map/ppermute | solution.py:22
  21.7 7.1 %collective-permute-start.7 = (bf16[2,32,512]{2,1,0:T(8,128)(2,1)S(1)}, bf16[2,32,512]{2,1,0:T(8,128)(2,1)S(1)}, u32[]{:S(2)}, u32[]{:S(2)}) collective-permute-start(bf16[2,32,512]{2,1,0:T(8,128)(2,1)S(1)} %get-tuple-element.68), channel_id=1, source_target_pairs={{0,8},{1,9},{2,10},{3,11},{4,12},{5,13},{6,14},{7,15},{8,0},{9,1},... | collective-permute-start | bytes 196616 | tf_op jit(solution)/shard_map/ppermute | solution.py:22
  26.0 6.6 %collective-permute-start.10 = (bf16[2,2,32,512]{3,2,1,0:T(8,128)(2,1)S(1)}, bf16[2,2,32,512]{3,2,1,0:T(8,128)(2,1)S(1)}, u32[]{:S(2)}, u32[]{:S(2)}) collective-permute-start(bf16[2,2,32,512]{3,2,1,0:T(8,128)(2,1)S(1)} %get-tuple-element.69), channel_id=1, source_target_pairs={{0,2},{1,3},{2,0},{3,1},{4,6},{5,7},{6,4},{7,5},{8,10},{9,11},{10,... | collective-permute-start | bytes 393224 | tf_op jit(solution)/shard_map/ppermute | solution.py:22
  26.1 7.8 %collective-permute-start.11 = (bf16[2,2,32,512]{3,2,1,0:T(8,128)(2,1)S(1)}, bf16[2,2,32,512]{3,2,1,0:T(8,128)(2,1)S(1)}, u32[]{:S(2)}, u32[]{:S(2)}) collective-permute-start(bf16[2,2,32,512]{3,2,1,0:T(8,128)(2,1)S(1)} %get-tuple-element.69), channel_id=1, source_target_pairs={{0,6},{1,7},{2,4},{3,5},{4,2},{5,3},{6,0},{7,1},{8,14},{9,15},{10,... | collective-permute-start | bytes 393224 | tf_op jit(solution)/shard_map/ppermute | solution.py:22
  26.3 9.0 %collective-permute-start.6 = (bf16[2,2,32,512]{3,2,1,0:T(8,128)(2,1)S(1)}, bf16[2,2,32,512]{3,2,1,0:T(8,128)(2,1)S(1)}, u32[]{:S(2)}, u32[]{:S(2)}) collective-permute-start(bf16[2,2,32,512]{3,2,1,0:T(8,128)(2,1)S(1)} %get-tuple-element.67.refs_3_), channel_id=1, source_target_pairs={{0,4},{1,5},{2,6},{3,7},{4,0},{5,1},{6,2},{7,3},{8,12},{9,13},{10,... | collective-permute-start | bytes 393224 | tf_op jit(solution)/shard_map/ppermute | solution.py:22
  28.8 6.4 %collective-permute-start.14 = (bf16[2,2,32,512]{3,2,1,0:T(8,128)(2,1)S(1)}, bf16[2,2,32,512]{3,2,1,0:T(8,128)(2,1)S(1)}, u32[]{:S(2)}, u32[]{:S(2)}) collective-permute-start(bf16[2,2,32,512]{3,2,1,0:T(8,128)(2,1)S(1)} %shard_map.165.refs_9_), channel_id=1, source_target_pairs={{0,16},{16,0},{1,17},{17,1},{2,18},{18,2},{3,19},{19,3},{4,20},{20... | collective-permute-start | bytes 393224 | tf_op jit(solution)/shard_map/ppermute | solution.py:36
  30.1 6.4 %collective-permute-start.4 = (bf16[2,256,512]{2,1,0:T(8,128)(2,1)S(1)}, bf16[2,256,512]{2,1,0:T(8,128)(2,1)S(1)}, u32[]{:S(2)}, u32[]{:S(2)}) collective-permute-start(bf16[2,256,512]{2,1,0:T(8,128)(2,1)S(1)} %shard_map.162.refs_0_), channel_id=1, source_target_pairs={{0,1},{1,0},{2,3},{3,2},{4,5},{5,4},{6,7},{7,6},{8,9},{9,8},{10,11... | collective-permute-start | bytes 1572872 | tf_op jit(solution)/shard_map/ppermute | solution.py:22
  43.1 12.2 %collective-permute-start.23 = (bf16[2,2,32,512]{3,2,1,0:T(8,128)(2,1)S(1)}, bf16[2,2,32,512]{3,2,1,0:T(8,128)(2,1)S(1)}, u32[]{:S(2)}, u32[]{:S(2)}) collective-permute-start(bf16[2,2,32,512]{3,2,1,0:T(8,128)(2,1)S(1)} %get-tuple-element.95), channel_id=1, source_target_pairs={{0,8},{1,9},{2,10},{3,11},{4,12},{5,13},{6,14},{7,15},{8,0},{9,1},... | collective-permute-start | bytes 393224 | tf_op jit(solution)/shard_map/ppermute | solution.py:22
  44.4 20.4 %collective-permute-start.24 = (bf16[2,2,32,512]{3,2,1,0:T(8,128)(2,1)S(1)}, bf16[2,2,32,512]{3,2,1,0:T(8,128)(2,1)S(1)}, u32[]{:S(2)}, u32[]{:S(2)}) collective-permute-start(bf16[2,2,32,512]{3,2,1,0:T(8,128)(2,1)S(1)} %get-tuple-element.96), channel_id=1, source_target_pairs={{0,10},{1,11},{2,8},{3,9},{4,14},{5,15},{6,12},{7,13},{8,2},{9,3},... | collective-permute-start | bytes 393224 | tf_op jit(solution)/shard_map/ppermute | solution.py:22
  50.9 13.8 %collective-permute-start.18 = (f32[28,512]{1,0:T(8,128)S(1)}, f32[28,512]{1,0:T(8,128)S(1)}, u32[]{:S(2)}, u32[]{:S(2)}) collective-permute-start(f32[28,512]{1,0:T(8,128)S(1)} %add.12), channel_id=1, source_target_pairs={{0,2},{1,3},{2,0},{3,1},{4,6},{5,7},{6,4},{7,5},{8,10},{9,11},{10,... | collective-permute-start | bytes 172040 | tf_op jit(solution)/shard_map/ppermute | solution.py:22
  51.0 13.8 %collective-permute-start.25 = (bf16[2,2,32,512]{3,2,1,0:T(8,128)(2,1)S(1)}, bf16[2,2,32,512]{3,2,1,0:T(8,128)(2,1)S(1)}, u32[]{:S(2)}, u32[]{:S(2)}) collective-permute-start(bf16[2,2,32,512]{3,2,1,0:T(8,128)(2,1)S(1)} %get-tuple-element.97), channel_id=1, source_target_pairs={{0,12},{1,13},{2,14},{3,15},{4,8},{5,9},{6,10},{7,11},{8,4},{9,5},... | collective-permute-start | bytes 393224 | tf_op jit(solution)/shard_map/ppermute | solution.py:22
  53.6 13.9 %collective-permute-start.26 = (bf16[2,2,32,512]{3,2,1,0:T(8,128)(2,1)S(1)}, bf16[2,2,32,512]{3,2,1,0:T(8,128)(2,1)S(1)}, u32[]{:S(2)}, u32[]{:S(2)}) collective-permute-start(bf16[2,2,32,512]{3,2,1,0:T(8,128)(2,1)S(1)} %get-tuple-element.98), channel_id=1, source_target_pairs={{0,14},{1,15},{2,12},{3,13},{4,10},{5,11},{6,8},{7,9},{8,6},{9,7},... | collective-permute-start | bytes 393224 | tf_op jit(solution)/shard_map/ppermute | solution.py:22
  55.4 13.6 %collective-permute-start.27 = (bf16[2,2,32,512]{3,2,1,0:T(8,128)(2,1)S(1)}, bf16[2,2,32,512]{3,2,1,0:T(8,128)(2,1)S(1)}, u32[]{:S(2)}, u32[]{:S(2)}) collective-permute-start(bf16[2,2,32,512]{3,2,1,0:T(8,128)(2,1)S(1)} %get-tuple-element.99), channel_id=1, source_target_pairs={{0,4},{1,5},{2,6},{3,7},{4,0},{5,1},{6,2},{7,3},{8,12},{9,13},{10,... | collective-permute-start | bytes 393224 | tf_op jit(solution)/shard_map/ppermute | solution.py:22
  64.7 7.3 %collective-permute-start.29 = (bf16[2,2,32,512]{3,2,1,0:T(8,128)(2,1)S(1)}, bf16[2,2,32,512]{3,2,1,0:T(8,128)(2,1)S(1)}, u32[]{:S(2)}, u32[]{:S(2)}) collective-permute-start(bf16[2,2,32,512]{3,2,1,0:T(8,128)(2,1)S(1)} %get-tuple-element.101), channel_id=1, source_target_pairs={{0,2},{1,3},{2,0},{3,1},{4,6},{5,7},{6,4},{7,5},{8,10},{9,11},{10,... | collective-permute-start | bytes 393224 | tf_op jit(solution)/shard_map/ppermute | solution.py:22
  64.8 9.0 %collective-permute-start.31 = (f32[28,512]{1,0:T(8,128)S(1)}, f32[28,512]{1,0:T(8,128)S(1)}, u32[]{:S(2)}, u32[]{:S(2)}) collective-permute-start(f32[28,512]{1,0:T(8,128)S(1)} %add.13), channel_id=1, source_target_pairs={{0,4},{1,5},{2,6},{3,7},{4,0},{5,1},{6,2},{7,3},{8,12},{9,13},{10,... | collective-permute-start | bytes 172040 | tf_op jit(solution)/shard_map/ppermute | solution.py:22
  72.2 17.8 %collective-permute-start.30 = (bf16[2,2,32,512]{3,2,1,0:T(8,128)(2,1)S(1)}, bf16[2,2,32,512]{3,2,1,0:T(8,128)(2,1)S(1)}, u32[]{:S(2)}, u32[]{:S(2)}) collective-permute-start(bf16[2,2,32,512]{3,2,1,0:T(8,128)(2,1)S(1)} %get-tuple-element.104), channel_id=1, source_target_pairs={{0,1},{1,0},{2,3},{3,2},{4,5},{5,4},{6,7},{7,6},{8,9},{9,8},{10,11... | collective-permute-start | bytes 393224 | tf_op jit(solution)/shard_map/ppermute | solution.py:22
  73.7 17.8 %collective-permute-start.20 = (bf16[128,512]{1,0:T(8,128)(2,1)S(1)}, bf16[128,512]{1,0:T(8,128)(2,1)S(1)}, u32[]{:S(2)}, u32[]{:S(2)}) collective-permute-start(bf16[128,512]{1,0:T(8,128)(2,1)S(1)} %get-tuple-element.91), channel_id=1, source_target_pairs={{0,2},{1,3},{2,0},{3,1},{4,6},{5,7},{6,4},{7,5},{8,10},{9,11},{10,... | collective-permute-start | bytes 393224 | tf_op jit(solution)/shard_map/ppermute | solution.py:22
  73.8 9.3 %collective-permute-start.32 = (f32[28,512]{1,0:T(8,128)S(1)}, f32[28,512]{1,0:T(8,128)S(1)}, u32[]{:S(2)}, u32[]{:S(2)}) collective-permute-start(f32[28,512]{1,0:T(8,128)S(1)} %add.14), channel_id=1, source_target_pairs={{0,8},{1,9},{2,10},{3,11},{4,12},{5,13},{6,14},{7,15},{8,0},{9,1},... | collective-permute-start | bytes 172040 | tf_op jit(solution)/shard_map/ppermute | solution.py:22
  83.1 7.7 %collective-permute-start.33 = (f32[28,512]{1,0:T(8,128)S(1)}, f32[28,512]{1,0:T(8,128)S(1)}, u32[]{:S(2)}, u32[]{:S(2)}) collective-permute-start(f32[28,512]{1,0:T(8,128)S(1)} %add.15.mine), channel_id=1, source_target_pairs={{0,1},{1,0},{2,3},{3,2},{4,5},{5,4},{6,7},{7,6},{8,9},{9,8},{10,11... | collective-permute-start | bytes 172040 | tf_op jit(solution)/shard_map/ppermute | solution.py:22
  (22 other events, 107.9 us)

commit v4 on v3

v4 whole, which is shorter than its diff:
```python
import functools
import math

import jax
import jax.numpy as jnp
from jax import lax
from jax.experimental import pallas as pl
from jax.experimental.pallas import tpu as pltpu
from jax.sharding import PartitionSpec as P

NARROW = jnp.bfloat16
WIDE = jnp.float32
TAPS = 7
RIM = 3
EDGE = 8
LANES = 128
SMALL_ROWS = 28


def swap(value, bit):
    count = lax.axis_size("row")
    return lax.ppermute(value, "row", [(i, i ^ bit) for i in range(count)])


def swap_rim(value):
    count = lax.axis_size("row")
    pairs = [(i, i + 1) for i in range(1, count - 1, 2)]
    return lax.ppermute(value, "row", pairs + [(j, i) for i, j in pairs])


def shaped(shape, dtype=WIDE):
    return jax.ShapeDtypeStruct(shape, dtype)


def swap_group(value):
    return lax.ppermute(value, "grp", [(0, 1), (1, 0)])


def run(body, outs, *operands, scratch=(), mib=16, order=0, apart=False):
    extra = {}
    if apart:
        extra = {"in_specs": [pl.BlockSpec(memory_space=pltpu.HBM)] * len(operands)}
        operands = [pltpu.with_memory_space_constraint(x, pltpu.HBM) for x in operands]
    return pl.pallas_call(
        body,
        out_shape=outs,
        **extra,
        scratch_shapes=scratch,
        compiler_params=pltpu.CompilerParams(vmem_limit_bytes=mib * 2**20),
        cost_estimate=pl.CostEstimate(flops=order * 10**9, bytes_accessed=0, transcendentals=0),
    )(*operands)


def place():
    me = lax.axis_index("row")
    return me, lax.rem(me, 2), lax.rem(lax.div(me, 2), 2)


def dot(left, right, dims):
    return lax.dot_general(left, right, (dims, ((), ())), preferred_element_type=WIDE)


def split_body(*refs):
    inw_hbm, outw_hbm, in_bias_hbm = refs[:3]
    own, core, outer, branch, bias_part = refs[9:14]
    inw, outw, in_bias, sems = refs[20:]
    feats, cotan, scale = refs[14:17]
    pairs = list(zip(refs[3:9], refs[14:20]))
    pairs += [(inw_hbm, inw), (outw_hbm, outw), (in_bias_hbm, in_bias)]
    copies = [pltpu.make_async_copy(a, b, sems.at[k]) for k, (a, b) in enumerate(pairs)]
    for copy in copies[6:] + copies[:6]:
        copy.start()
    me, c, x = place()
    even = c == 0
    quarter = own.shape[-1]
    rows, cols, channels = feats.shape
    own_rows = inw.shape[0]
    copies[6].wait()
    copies[7].wait()
    for side in range(2):
        for part, near in ((2 * jnp.bitwise_xor(x, side) + c, True), (2 * jnp.bitwise_xor(x, side) + 1 - c, False)):
            lanes = pl.ds(pl.multiple_of(part * quarter, quarter), quarter)
            for which, source in enumerate((inw, outw)):
                value = source[:, lanes].astype(NARROW)
                if near:
                    own[side, which] = value
                else:
                    core[pl.ds((2 * side + which) * own_rows, own_rows), :] = value
    copies[0].wait()
    first = feats[:RIM].astype(NARROW).reshape(RIM * cols, channels)
    last = feats[rows - RIM :].astype(NARROW).reshape(RIM * cols, channels)
    core[4 * own_rows :, :] = jnp.where(even, last, first)
    outer[...] = jnp.where(even, first, last)
    copies[1].wait()
    copies[2].wait()
    branch[...] = (scale[...] * cotan[...].reshape(branch.shape)).astype(NARROW)
    copies[8].wait()
    lanes = pl.ds(pl.multiple_of(lax.rem(me, 4) * quarter, quarter), quarter)
    bias_part[...] = in_bias[:, lanes]
    for copy in copies[3:6]:
        copy.wait()


def join_body(mine, other, *targets):
    group = lax.axis_index("grp")
    for side in range(2):
        full, sent = targets[2 * side : 2 * side + 2]
        own_rows = mine.shape[2]
        for which in range(2):
            full[which, 0] = mine[side, which]
            full[which, 1] = other[pl.ds((2 * side + which) * own_rows, own_rows), :]
        sent[...] = full[group]


def acts_body(mine, got, acts):
    pixels = mine.shape[1]
    acts[:, :pixels] = mine[...]
    acts[:, pixels:] = got[...]


def stack_body(*refs):
    for place_in, ref in enumerate(refs[:-1]):
        refs[-1][place_in] = ref[...]


def fill(padded, block, inner, outer):
    rows, cols, channels = block.shape
    _, c, _ = place()
    padded[:, :EDGE, :] = jnp.zeros_like(padded[:, :EDGE, :])
    padded[:, EDGE + cols :, :] = jnp.zeros_like(padded[:, EDGE + cols :, :])
    middle = slice(EDGE, EDGE + cols)
    inner = inner.astype(WIDE).reshape(RIM, cols, channels)
    outer = outer.astype(WIDE).reshape(RIM, cols, channels)
    padded[:RIM, middle, :] = jnp.where(c == 0, outer, inner)
    padded[RIM : RIM + rows, middle, :] = block
    padded[RIM + rows :, middle, :] = jnp.where(c == 0, inner, outer)


def taps_sum(padded, kernel, lanes, rows, cols, mirrored, start):
    total = list(start)
    for tap_col in range(TAPS):
        for row in range(rows + TAPS - 1):
            line = padded[row, pl.ds(EDGE - RIM + tap_col, cols), lanes]
            for out in range(rows):
                tap_row = row - out
                if 0 <= tap_row < TAPS:
                    if mirrored:
                        tap = kernel[TAPS - 1 - tap_row, pl.ds(TAPS - 1 - tap_col, 1), lanes]
                    else:
                        tap = kernel[tap_row, pl.ds(tap_col, 1), lanes]
                    total[out] = total[out] + line * tap
    return total


def conv_body(
    feats, core_got, outer, kernel, gain, bias, branch, normed, inv, acts, padded, result
):
    rows, cols, channels = feats.shape
    start = core_got.shape[0] - RIM * cols
    fill(padded, feats[...], core_got[start:, :], outer[...])

    @pl.loop(0, channels // LANES)
    def _(step):
        lanes = pl.ds(pl.multiple_of(step * LANES, LANES), LANES)
        zero = [jnp.zeros((cols, LANES), WIDE)] * rows
        total = taps_sum(padded, kernel, lanes, rows, cols, False, zero)
        for row in range(rows):
            result[pl.ds(row * cols, cols), lanes] = total[row]

    value = result[...]
    centred = value - jnp.mean(value, axis=1, keepdims=True)
    spread = lax.rsqrt(jnp.mean(centred * centred, axis=1, keepdims=True) + 1e-06)
    value = centred * spread
    normed[...] = value
    inv[...] = jnp.broadcast_to(spread, inv.shape)
    acts[0] = (value * gain[...] + bias[...]).astype(NARROW)
    acts[1] = branch[...]


def hidden_body(copied, *refs):
    patterns = lax.axis_size("row") // 4
    me, _, _ = place()
    acts, in_bias = refs[:2], refs[2]
    scale = refs[3]
    pieces = refs[4:-7]
    keep, send, active, hidden, scale_part, bias_part, weights = refs[-7:]
    half = acts[0].shape[1]
    if copied:
        own = pieces[0].shape[2]
        group = lax.axis_index("grp")
        for side in range(2):
            full, near, here, there = pieces[4 * side : 4 * side + 4]
            for pattern in range(patterns):
                for c in range(2):
                    device = jnp.bitwise_xor(me, 4 * pattern + 2 * side + c)
                    rows = pl.ds(pl.multiple_of(device * own, own), own)
                    if pattern < 2:
                        source = near if pattern else full
                        weights[0, rows, :] = source[0, c]
                        weights[1, rows, :] = source[1, c]
                    else:
                        weights[group, rows, :] = here[pattern - 2, c]
                        weights[1 - group, rows, :] = there[pattern - 2, c]
    else:
        weights[...] = pieces[0][...]
    in_narrow = weights.at[0]
    out_narrow = weights.at[1]
    bias_row = in_bias[...]
    total = jnp.zeros_like(bias_row)
    scale_total = jnp.zeros_like(scale_part)
    for side in (1, 0):
        preact = dot(acts[side][0], in_narrow[...], ((1,), (0,))) + bias_row
        act_grad = dot(acts[side][1], out_narrow[...], ((1,), (0,)))
        cdf = 0.5 * (1.0 + lax.erf(preact * 0.7071067811865476))
        rows = pl.ds(side * half, half)
        activated = (preact * cdf).astype(NARROW)
        active[rows, :] = activated
        slope = cdf + preact * jnp.exp(-0.5 * preact * preact) * 0.3989422804014327
        grad = act_grad * slope
        total = total + jnp.sum(grad, axis=0, keepdims=True)
        narrow = grad.astype(NARROW)
        hidden[rows, :] = narrow
        out_grad = dot(narrow, in_narrow[...], ((1,), (1,)))
        mixed = dot(activated, out_narrow[...], ((1,), (1,)))
        scale_total = scale_total + jnp.sum(
            mixed * acts[side][1].astype(WIDE), axis=0, keepdims=True
        )
        if side:
            send[0] = out_grad.astype(NARROW)
            send[1] = mixed.astype(NARROW)
        else:
            keep[0] = out_grad
            keep[1] = mixed
    bias_part[...] = total
    scale_part[...] = scale_total / scale[...]


def weight_body(norm_scale, *refs):
    acts, (active, hidden, holder) = refs[:2], refs[2:]
    half = acts[0].shape[1]
    first, second = pl.ds(0, half), pl.ds(half, half)
    for which, right in enumerate((hidden, active)):
        grad = dot(acts[0][which], right[first, :], ((0,), (0,)))
        grad = grad + dot(acts[1][which], right[second, :], ((0,), (0,)))
        holder[which] = norm_scale * grad


def owners_body(turns, holder, after, *targets):
    del after
    me, _, _ = place()
    own = targets[0].shape[2]
    for pattern, target in zip(turns, targets):
        for c in range(2):
            device = jnp.bitwise_xor(me, 2 * pattern + c)
            rows = pl.ds(pl.multiple_of(device * own, own), own)
            for which in range(2):
                target[c, which] = holder[which, rows, :].astype(target.dtype)


def fold_body(kept, got, stay, leave, mixed_stay, mixed_leave):
    size = stay.shape[0]
    for which, (near, away) in enumerate(((stay, leave), (mixed_stay, mixed_leave))):
        near[...] = kept[which, :size] + got[which, :size].astype(WIDE)
        away[...] = (kept[which, size:] + got[which, size:].astype(WIDE)).astype(NARROW)


def conv_grad_body(norm_scale, *refs):
    kept, got, normed, inv, gain, feats, core_got, outer, scale, in_bias = refs[:10]
    grad, rim_out, stay, leave, padded, small = refs[10:]
    rows, cols, channels = feats.shape
    me, c, _ = place()
    out_grad = kept[...] + got[...].astype(WIDE)
    value = normed[...]
    normed_grad = out_grad * gain[...]
    mean = jnp.mean(normed_grad, axis=1, keepdims=True)
    along = jnp.mean(normed_grad * value, axis=1, keepdims=True)
    result = inv[:, :1] * (normed_grad - mean - value * along)
    grad[...] = result
    pixels = rows * cols
    rim = RIM * cols
    rim_out[...] = jnp.where(c == 0, result[:rim], result[pixels - rim :]).astype(NARROW)
    leave[:rim, :] = jnp.where(c == 0, result[pixels - rim :], result[:rim])
    fill(padded, feats[...], core_got[core_got.shape[0] - rim :, :], outer[...])

    def put(row, lanes, total):
        small[row // SMALL_ROWS, pl.ds(row % SMALL_ROWS, 1), lanes] = norm_scale * total

    @pl.loop(0, channels // LANES)
    def _(step):
        lanes = pl.ds(pl.multiple_of(step * LANES, LANES), LANES)
        own = [grad[pl.ds(row * cols, cols), lanes] for row in range(rows)]
        for tap_col in range(TAPS):
            totals = [jnp.zeros((8, LANES), WIDE)] * TAPS
            for row in range(rows + TAPS - 1):
                line = padded[row, pl.ds(EDGE - RIM + tap_col, cols), lanes]
                for out in range(rows):
                    tap_row = row - out
                    if 0 <= tap_row < TAPS:
                        product = line * own[out]
                        for part in range(cols // 8):
                            totals[tap_row] = totals[tap_row] + product[8 * part : 8 * part + 8]
            for tap_row in range(TAPS):
                total = jnp.sum(totals[tap_row], axis=0, keepdims=True)
                put(TAPS * tap_row + tap_col, lanes, total)

    everything = slice(None)
    row = TAPS * TAPS
    put(row, everything, jnp.sum(out_grad * value, axis=0, keepdims=True))
    put(row + 1, everything, jnp.sum(out_grad, axis=0, keepdims=True))
    put(row + 2, everything, scale[...])
    for part in range(4):
        own_part = jnp.where(lax.rem(me, 4) == part, 1.0, 0.0)
        put(row + 3 + part, everything, own_part * in_bias[...])
    stay[...] = small[c]
    leave[rim:, :] = small[1 - c]


def input_grad_body(grad, core_got, outer, kernel, cotan, result, padded):
    rows, cols, channels = cotan.shape
    fill(padded, grad[...].reshape(cotan.shape), core_got[: RIM * cols, :], outer[...])

    @pl.loop(0, channels // LANES)
    def _(step):
        lanes = pl.ds(pl.multiple_of(step * LANES, LANES), LANES)
        start = [cotan[row, :, lanes] for row in range(rows)]
        total = taps_sum(padded, kernel, lanes, rows, cols, True, start)
        for row in range(rows):
            result[row, :, lanes] = total[row]


def output_body(feats, scale, kept, got, result):
    mixed = kept[...] + got[...].astype(WIDE)
    result[...] = feats[...] + (scale[...] * mixed).reshape(feats.shape)


def total_body(turns, *refs):
    stay, leave = refs[-2:]
    for side in range(2):
        total = jnp.zeros(stay.shape[1:], WIDE)
        for part, turn in zip(refs, turns):
            if turn % 2 == side:
                total = total + part[...].astype(WIDE)
        stay[side] = total[0]
        leave[side] = total[1].astype(NARROW)


def owner_body(stay, got, in_grad, out_grad):
    _, c, x = place()
    quarter = stay.shape[-1]
    for value, part in (
        (stay[0], 2 * x + c),
        (stay[1], 2 * (1 - x) + c),
        (got[0], 2 * x + 1 - c),
        (got[1], 2 * (1 - x) + 1 - c),
    ):
        lanes = pl.ds(pl.multiple_of(part * quarter, quarter), quarter)
        in_grad[:, lanes] = value[0].astype(WIDE)
        out_grad[:, lanes] = value[1].astype(WIDE)


def small_body(mine, other, kernel_grad, gain, bias, scale, in_bias, held):
    _, core_bit, _ = place()
    held[core_bit] = mine[...]
    held[1 - core_bit] = other[...]

    def take(row):
        return held[row // SMALL_ROWS, pl.ds(row % SMALL_ROWS, 1), :]

    for tap_row in range(TAPS):
        for tap_col in range(TAPS):
            kernel_grad[tap_row, pl.ds(tap_col, 1), :] = take(TAPS * tap_row + tap_col)
    row = TAPS * TAPS
    gain[...] = take(row)
    bias[...] = take(row + 1)
    scale[...] = take(row + 2)
    quarter = take(row).shape[1]
    for part in range(4):
        in_bias[:, pl.ds(part * quarter, quarter)] = take(row + 3 + part)


def flipped(blocks, axis, bit_set):
    return jnp.where(bit_set == 1, jnp.flip(blocks, axis), blocks)


def canonical(blocks, me, bit_count):
    tail = blocks.shape[1:]
    blocks = blocks.reshape((2,) * bit_count + tail)
    for spot in range(bit_count):
        blocks = flipped(blocks, bit_count - 1 - spot, (me >> spot) & 1)
    return blocks.reshape((2**bit_count,) + tail)


def per_device(
    features, cotangent, kernel, norm_gain, norm_bias, in_weight, in_bias, out_weight, layer_scale
):
    row_count, col_count, channels = features.shape
    own_rows, hidden_count = in_weight.shape
    pixels = row_count * col_count
    count = lax.axis_size("row")
    bit_count = count.bit_length() - 1
    me = lax.axis_index("row")
    group_index = lax.axis_index("grp")
    quarter = hidden_count // 4
    norm_scale = 1.0 / math.sqrt(pixels * count)
    patterns = count // 4
    copied = own_rows % 16 == 0
    gain_row = norm_gain.reshape(1, channels)
    bias_row = norm_bias.reshape(1, channels)
    scale_row = layer_scale.reshape(1, channels)
    rim = RIM * col_count
    padded = pltpu.VMEM((row_count + 2 * RIM, col_count + 2 * EDGE, channels), WIDE)

    piece = (2, own_rows, quarter)
    once = (features, cotangent, scale_row, kernel, gain_row, bias_row)
    own, core, outer, branch, in_bias_own, feats, cotan, scale, taps, gain, bias = run(
        split_body,
        (
            shaped((2,) + piece, NARROW),
            shaped((4 * own_rows + rim, channels), NARROW),
            shaped((rim, channels), NARROW),
            shaped((pixels, channels), NARROW),
            shaped((1, quarter)),
        )
        + tuple(shaped(x.shape) for x in once),
        in_weight,
        out_weight,
        in_bias.reshape(1, hidden_count),
        *once,
        scratch=(
            pltpu.VMEM(in_weight.shape, WIDE),
            pltpu.VMEM(out_weight.shape, WIDE),
            pltpu.VMEM((1, hidden_count), WIDE),
            pltpu.SemaphoreType.DMA((9,)),
        ),
        apart=True,
    )
    core_got = swap(core, 1)
    outer_got = swap_rim(outer)
    full_shape = shaped((2, 2, own_rows, quarter), NARROW)
    joined = run(
        join_body,
        (full_shape, shaped(piece, NARROW)) * 2,
        own,
        core_got,
    )
    pieces = []
    for side in range(2):
        full, sent = joined[2 * side : 2 * side + 2]
        here = [swap(sent, 4 * p + 2 * side) for p in range(2, patterns)]
        here = run(stack_body, (shaped((patterns - 2,) + piece, NARROW),), *here, order=8)[0]
        near = swap(full, 4 + 2 * side)
        pieces += [swap(full, 2) if side else full, near, here, swap_group(here)]

    normed, inv, acts = run(
        conv_body,
        (
            shaped((pixels, channels)),
            shaped((pixels, LANES)),
            shaped((2, pixels, channels), NARROW),
        ),
        feats,
        core_got,
        outer_got,
        taps,
        gain,
        bias,
        branch,
        scratch=(padded, pltpu.VMEM((pixels, channels), WIDE)),
    )
    acts = run(
        acts_body, (shaped((2, 2 * pixels, channels), NARROW),), acts, swap(acts, 2)
    )[0]
    acts_got = swap(acts, 1)

    if not copied:
        lines = []
        for pattern in range(patterns):
            for side in range(2):
                full, near, here, there = pieces[4 * side : 4 * side + 4]
                if pattern < 2:
                    lines.append(near if pattern else full)
                else:
                    pair = jnp.stack([here[pattern - 2], there[pattern - 2]])
                    lines.append(flipped(pair, 0, group_index))
        lines = jnp.moveaxis(jnp.stack(lines), 1, 2).reshape(count, 2, own_rows, quarter)
        lines = jnp.moveaxis(canonical(lines, me, bit_count), 1, 0)
        pieces = [lines.reshape(2, channels, quarter)]
    group = 4 * pixels
    both = (2, 2 * pixels, channels)
    keep, send, active, hidden, scale_part, in_bias_part = run(
        functools.partial(hidden_body, copied),
        (
            shaped(both),
            shaped(both, NARROW),
            shaped((group, quarter), NARROW),
            shaped((group, quarter), NARROW),
            shaped((1, channels)),
            shaped((1, quarter)),
        ),
        acts,
        acts_got,
        in_bias_own,
        scale,
        *pieces,
        scratch=(pltpu.VMEM((2, channels, quarter), NARROW),),
        mib=24,
    )
    half = (shaped((pixels, channels)), shaped((pixels, channels), NARROW))
    out_stay, out_leave, mixed_stay, mixed_leave = run(fold_body, half * 2, keep, swap(send, 1))
    out_got = swap(out_leave, 2)

    owned = (2, 2, own_rows, quarter)
    holder = run(
        functools.partial(weight_body, norm_scale),
        (shaped((2, channels, quarter)),),
        acts,
        acts_got,
        active,
        hidden,
        mib=24,
    )[0]
    conv_grad, rim_out, stay, leave = run(
        functools.partial(conv_grad_body, norm_scale),
        (
            shaped((pixels, channels)),
            shaped((rim, channels), NARROW),
            shaped((SMALL_ROWS, channels)),
            shaped((rim + SMALL_ROWS, channels)),
        ),
        out_stay,
        out_got,
        normed,
        inv,
        gain,
        feats,
        core_got,
        outer_got,
        scale_part,
        in_bias_part,
        scratch=(padded, pltpu.VMEM((2, SMALL_ROWS, channels), WIDE)),
    )
    rim_got = swap_rim(rim_out)
    leave_got = swap(leave, 1)
    sums = stay + leave_got[rim:]
    sums = sums + swap(sums, 2)
    early = sums
    for spot in range(2, bit_count):
        sums = sums + swap(sums, 1 << spot)

    turns = (*range(4, 2 * patterns), 2, 3, 1, 0)
    kinds = [NARROW if p else WIDE for p in turns]
    if copied:
        parts = []
        for some, after in ((slice(0, 2), out_leave), (slice(2, None), early)):
            parts += run(
                functools.partial(owners_body, turns[some]),
                tuple(shaped(owned, kind) for kind in kinds[some]),
                holder,
                after,
            )
    else:
        parts = holder.reshape(2, count, own_rows, quarter)
        parts = canonical(jnp.moveaxis(parts, 1, 0), me, bit_count)
        parts = parts.reshape(2 * patterns, 2, 2, own_rows, quarter)
        parts = [parts[p].astype(kind) for p, kind in zip(turns, kinds)]
    parts = [swap(part, 2 * p) if p else part for p, part in zip(turns, parts)]

    input_grad = run(
        input_grad_body,
        (shaped(features.shape),),
        conv_grad,
        leave_got,
        rim_got,
        taps,
        cotan,
        scratch=(padded,),
    )[0]
    output = run(
        output_body,
        (shaped(features.shape),),
        feats,
        scale,
        mixed_stay,
        swap(mixed_leave, 2),
    )[0]
    parts, input_grad, output = lax.optimization_barrier((parts, input_grad, output))

    stay, leave = run(
        functools.partial(total_body, turns),
        (shaped((2,) + piece), shaped((2,) + piece, NARROW)),
        *parts,
        order=20,
    )
    in_weight_grad, out_weight_grad = run(
        owner_body, (shaped((own_rows, hidden_count)),) * 2, stay, swap(leave, 1)
    )
    kernel_grad, gain_grad, bias_grad, scale_grad, in_bias_grad = run(
        small_body,
        (
            shaped(kernel.shape),
            shaped((1, channels)),
            shaped((1, channels)),
            shaped((1, channels)),
            shaped((1, hidden_count)),
        ),
        sums,
        swap(sums, 1),
        scratch=(pltpu.VMEM((2, SMALL_ROWS, channels), WIDE),),
    )
    return (
        output,
        input_grad,
        in_weight_grad,
        out_weight_grad,
        kernel_grad,
        gain_grad.reshape(channels),
        bias_grad.reshape(channels),
        in_bias_grad.reshape(hidden_count),
        scale_grad.reshape(channels),
    )


def solution(mesh):
    return jax.shard_map(
        per_device,
        mesh=mesh,
        in_specs=(
            P(("grp", "row"), None, None),
            P(("grp", "row"), None, None),
            P(),
            P(),
            P(),
            P("row", None),
            P(),
            P("row", None),
            P(),
        ),
        out_specs=(
            P(("grp", "row"), None, None),
            P(("grp", "row"), None, None),
            P(("grp", "row"), None),
            P(("grp", "row"), None),
            P("grp", None, None),
            P("grp"),
            P("grp"),
            P("grp"),
            P("grp"),
        ),
        check_vma=False,
    )
```

time: 92.6 us -> 93.8 us (1.013)
  waiting for transfers between devices: 21 us -> 29.2 us
  local copies, waits for them, and re-layouts: 4.15 us -> 0 us
  starting transfers between devices: 51.7 us -> 49.6 us
    ppermute x28 -> x26, waiting for transfers between devices: 15.8 us -> 26.6 us  [swap(): return lax.ppermute(value, 'row', [(i, i ^ bit) for i in range(count)])]
    unnamed x24 -> x0, local copies, waits for them, and re-layouts: 4.14 us -> none
    ppermute x4 -> x2, waiting for transfers between devices: 3.9 us -> 0.01 us  [swap_rim(): return lax.ppermute(value, 'row', pairs + [(j, i) for i, j in pairs])]
    ppermute x4 -> x2, starting transfers between devices: 11.4 us -> 7.67 us  [swap_rim(): return lax.ppermute(value, 'row', pairs + [(j, i) for i, j in pairs])]
    ppermute x28 -> x26, starting transfers between devices: 37.8 us -> 39.3 us  [swap(): return lax.ppermute(value, 'row', [(i, i ^ bit) for i in range(count)])]
    ppermute x2, waiting for transfers between devices: 1.23 us -> 2.57 us  [swap_group(): return lax.ppermute(value, 'grp', [(0, 1), (1, 0)])]
    pallas_call x18 -> x17, Pallas kernels: 14.4 us -> 13.7 us  [run(): pl.pallas_call(body, out_shape=outs, **extra, scratch_shapes=scratch, com...]
  transfers between devices with their start and end apart: 34 -> 30, of which waited for: 8 -> 9; matrix products, arithmetic and copies ran while one was open for 0% -> 0% of each run, Pallas kernels for 11% -> 8%
where the time goes in v4:
time: 93.8 us; the launch traced here: 93.4 us
  starting transfers between devices  49.6 us (53%)
  waiting for transfers between devices  29.2 us (31%)
  Pallas kernels  13.7 us (15%)
    ppermute x26, starting transfers between devices, swap(): return lax.ppermute(value, 'row', [(i, i ^ bit) for i in range(count)])  39.3 us
    ppermute x26, waiting for transfers between devices, swap(): return lax.ppermute(value, 'row', [(i, i ^ bit) for i in range(count)])  26.6 us
    pallas_call x17, Pallas kernels, run(): pl.pallas_call(body, out_shape=outs, **extra, scratch_shapes=scratch, com...  13.7 us
    ppermute x2, starting transfers between devices, swap_rim(): return lax.ppermute(value, 'row', pairs + [(j, i) for i, j in pairs])  7.67 us
    ppermute x2, waiting for transfers between devices, swap_group(): return lax.ppermute(value, 'grp', [(0, 1), (1, 0)])  2.57 us
    ppermute x2, starting transfers between devices, swap_group(): return lax.ppermute(value, 'grp', [(0, 1), (1, 0)])  2.54 us
  transfers between devices with their start and end apart: 30, of which 9 were waited for; matrix products, arithmetic and copies ran while one was open for 0% of the time, Pallas kernels for 8%

profile of v4, /device:TPU:1, one launch (start us, length us, event | category | flops | bytes accessed | tf_op | source)
XLA Modules:
  0.0 93.4 jit_solution(879038374324426208)
XLA Ops:
  0.6 1.3 %shard_map.160 = (bf16[2,2,32,512]{3,2,1,0:T(8,128)(2,1)S(1)}, bf16[224,512]{1,0:T(8,128)(2,1)S(1)}, bf16[96,512]{1,0:T(8,128)(2,1)S(1)}, bf16[128,512]{1,0:T(8,...) custom-call(f32[32,2048]{1,0:T(8,128)} %refs_0_.1, ...), custom_call_target="tpu_custom_call" | custom-call | tf_op jit(solution)/shard_map/pallas_call | solution.py:44
  2.1 4.5 %collective-permute-start.1 = (bf16[96,512]{1,0:T(8,128)(2,1)S(1)}, bf16[96,512]{1,0:T(8,128)(2,1)S(1)}, u32[]{:S(2)}, u32[]{:S(2)}) collective-permute-start(bf16[96,512]{1,0:T(8,128)(2,1)S(1)} %get-tuple-element.70), channel_id=1, source_target_pairs={{1,2},{3,4},{5,6},{7,8},{9,10},{11,12},{13,14},{2,1},{4,3},{6,5},{... | collective-permute-start | bytes 294920 | tf_op jit(solution)/shard_map/ppermute | solution.py:28
  6.6 3.4 %collective-permute-start.10 = (bf16[2,32,512]{2,1,0:T(8,128)(2,1)S(1)}, bf16[2,32,512]{2,1,0:T(8,128)(2,1)S(1)}, u32[]{:S(2)}, u32[]{:S(2)}) collective-permute-start(bf16[2,32,512]{2,1,0:T(8,128)(2,1)S(1)} %get-tuple-element.82), channel_id=1, source_target_pairs={{0,10},{1,11},{2,8},{3,9},{4,14},{5,15},{6,12},{7,13},{8,2},{9,3},... | collective-permute-start | bytes 196616 | tf_op jit(solution)/shard_map/ppermute | solution.py:22
  11.0 1.4 %collective-permute-start.5 = (bf16[2,32,512]{2,1,0:T(8,128)(2,1)S(1)}, bf16[2,32,512]{2,1,0:T(8,128)(2,1)S(1)}, u32[]{:S(2)}, u32[]{:S(2)}) collective-permute-start(bf16[2,32,512]{2,1,0:T(8,128)(2,1)S(1)} %get-tuple-element.80), channel_id=1, source_target_pairs={{0,8},{1,9},{2,10},{3,11},{4,12},{5,13},{6,14},{7,15},{8,0},{9,1},... | collective-permute-start | bytes 196616 | tf_op jit(solution)/shard_map/ppermute | solution.py:22
  14.4 2.4 %shard_map.161 = (f32[128,512]{1,0:T(8,128)S(1)}, f32[128,128]{1,0:T(8,128)S(1)}, bf16[2,128,512]{2,1,0:T(8,128)(2,1)S(1)}) custom-call(f32[4,32,512]{2,1,0:T(8,128)S(1)} %get-tuple-element.68.feats.refs_5_, bf16[224,512]{1,0:T(8,128)(2,1)S(1)} %collective-permute-done.core_got.other.refs_6_, bf16[96,512]{1,0:T(8,128)(2,1)S(1)} %collective-permute-done.1.outer.refs_7_, ...), custom_call_target="tpu_custom_call" | custom-call | tf_op jit(solution)/shard_map/pallas_call | solution.py:44
  16.9 1.5 %collective-permute-start.9 = (bf16[2,2,32,512]{3,2,1,0:T(8,128)(2,1)S(1)}, bf16[2,2,32,512]{3,2,1,0:T(8,128)(2,1)S(1)}, u32[]{:S(2)}, u32[]{:S(2)}) collective-permute-start(bf16[2,2,32,512]{3,2,1,0:T(8,128)(2,1)S(1)} %get-tuple-element.81), channel_id=1, source_target_pairs={{0,6},{1,7},{2,4},{3,5},{4,2},{5,3},{6,0},{7,1},{8,14},{9,15},{10,... | collective-permute-start | bytes 393224 | tf_op jit(solution)/shard_map/ppermute | solution.py:22
  18.6 10.6 %collective-permute-done.2.got = bf16[2,128,512]{2,1,0:T(8,128)(2,1)S(1)} collective-permute-done((bf16[2,128,512]{2,1,0:T(8,128)(2,1)S(1)}, bf16[2,128,512]{2,1,0:T(8,128)(2,1)S(1)}, u32[]{:S(2)}, u32[]{:S(2)}) %collective-permute-start.2) | collective-permute-done | bytes 262176 | tf_op jit(solution)/shard_map/ppermute | solution.py:22
  31.9 1.8 %collective-permute-done.4.refs_5_ = bf16[2,2,32,512]{3,2,1,0:T(8,128)(2,1)S(1)} collective-permute-done((bf16[2,2,32,512]{3,2,1,0:T(8,128)(2,1)S(1)}, bf16[2,2,32,512]{3,2,1,0:T(8,128)(2,1)S(1)}, u32[]{:S(2)}, u32[]{:S(2)}) %collective-permute-start.4) | collective-permute-done | bytes 131104 | tf_op jit(solution)/shard_map/ppermute | solution.py:22
  34.9 2.6 %collective-permute-done.7.refs_7_ = bf16[2,2,32,512]{3,2,1,0:T(8,128)(2,1)S(1)} collective-permute-done((bf16[2,2,32,512]{3,2,1,0:T(8,128)(2,1)S(1)}, bf16[2,2,32,512]{3,2,1,0:T(8,128)(2,1)S(1)}, u32[]{:S(2)}, u32[]{:S(2)}) %collective-permute-start.7) | collective-permute-done | bytes 131104 | tf_op jit(solution)/shard_map/ppermute | solution.py:36
  37.5 1.7 %shard_map.166 = (f32[2,256,512]{2,1,0:T(8,128)S(1)}, bf16[2,256,512]{2,1,0:T(8,128)(2,1)S(1)}, bf16[512,512]{1,0:T(8,128)(2,1)S(1)}, bf16[512,512]{1,0:T(8,128)...) custom-call(bf16[2,256,512]{2,1,0:T(8,128)(2,1)S(1)} %shard_map.162.refs_0_, ...), custom_call_target="tpu_custom_call" | custom-call | tf_op jit(solution)/shard_map/pallas_call | solution.py:44
  39.2 2.7 %collective-permute-start.13 = (bf16[2,256,512]{2,1,0:T(8,128)(2,1)S(1)}, bf16[2,256,512]{2,1,0:T(8,128)(2,1)S(1)}, u32[]{:S(2)}, u32[]{:S(2)}) collective-permute-start(bf16[2,256,512]{2,1,0:T(8,128)(2,1)S(1)} %get-tuple-element.86), channel_id=1, source_target_pairs={{0,1},{1,0},{2,3},{3,2},{4,5},{5,4},{6,7},{7,6},{8,9},{9,8},{10,11... | collective-permute-start | bytes 1572872 | tf_op jit(solution)/shard_map/ppermute | solution.py:22
  41.9 1.5 %collective-permute-done.13.got = bf16[2,256,512]{2,1,0:T(8,128)(2,1)S(1)} collective-permute-done((bf16[2,256,512]{2,1,0:T(8,128)(2,1)S(1)}, bf16[2,256,512]{2,1,0:T(8,128)(2,1)S(1)}, u32[]{:S(2)}, u32[]{:S(2)}) %collective-permute-start.13) | collective-permute-done | bytes 524320 | tf_op jit(solution)/shard_map/ppermute | solution.py:22
  43.6 4.7 %collective-permute-done.16.refs_1_ = bf16[128,512]{1,0:T(8,128)(2,1)S(1)} collective-permute-done((bf16[128,512]{1,0:T(8,128)(2,1)S(1)}, bf16[128,512]{1,0:T(8,128)(2,1)S(1)}, u32[]{:S(2)}, u32[]{:S(2)}) %collective-permute-start.16) | collective-permute-done | bytes 131104 | tf_op jit(solution)/shard_map/ppermute | solution.py:22
  48.3 1.9 %shard_map.170 = (f32[128,512]{1,0:T(8,128)S(1)}, bf16[96,512]{1,0:T(8,128)(2,1)S(1)}, f32[28,512]{1,0:T(8,128)S(1)}, f32[124,512]{1,0:T(8,128)S(1)}) custom-call(f32[128,512]{1,0:T(8,128)S(1)} %get-tuple-element.90.refs_0_, bf16[128,512]{1,0:T(8,128)(2,1)S(1)} %collective-permute-done.16.refs_1_, f32[128,512]{1,0:T(8,128)S(1)} %get-tuple-element.91.refs_2_, ...), custom_call_target="tpu_custom_call" | custom-call | tf_op jit(solution)/shard_map/pallas_call | solution.py:44
  52.4 3.2 %collective-permute-start.14 = (bf16[2,2,32,512]{3,2,1,0:T(8,128)(2,1)S(1)}, bf16[2,2,32,512]{3,2,1,0:T(8,128)(2,1)S(1)}, u32[]{:S(2)}, u32[]{:S(2)}) collective-permute-start(bf16[2,2,32,512]{3,2,1,0:T(8,128)(2,1)S(1)} %get-tuple-element.88), channel_id=1, source_target_pairs={{0,8},{1,9},{2,10},{3,11},{4,12},{5,13},{6,14},{7,15},{8,0},{9,1},... | collective-permute-start | bytes 393224 | tf_op jit(solution)/shard_map/ppermute | solution.py:22
  56.0 3.2 %collective-permute-start.24 = (bf16[96,512]{1,0:T(8,128)(2,1)S(1)}, bf16[96,512]{1,0:T(8,128)(2,1)S(1)}, u32[]{:S(2)}, u32[]{:S(2)}) collective-permute-start(bf16[96,512]{1,0:T(8,128)(2,1)S(1)} %get-tuple-element.104), channel_id=1, source_target_pairs={{1,2},{3,4},{5,6},{7,8},{9,10},{11,12},{13,14},{2,1},{4,3},{6,5},{... | collective-permute-start | bytes 294920 | tf_op jit(solution)/shard_map/ppermute | solution.py:28
  60.3 3.1 %collective-permute-done.18 = f32[28,512]{1,0:T(8,128)S(1)} collective-permute-done((f32[28,512]{1,0:T(8,128)S(1)}, f32[28,512]{1,0:T(8,128)S(1)}, u32[]{:S(2)}, u32[]{:S(2)}) %collective-permute-start.18) | collective-permute-done | bytes 57376 | tf_op jit(solution)/shard_map/ppermute | solution.py:22
  63.5 2.9 %collective-permute-start.19 = (bf16[2,2,32,512]{3,2,1,0:T(8,128)(2,1)S(1)}, bf16[2,2,32,512]{3,2,1,0:T(8,128)(2,1)S(1)}, u32[]{:S(2)}, u32[]{:S(2)}) collective-permute-start(bf16[2,2,32,512]{3,2,1,0:T(8,128)(2,1)S(1)} %get-tuple-element.97), channel_id=1, source_target_pairs={{0,12},{1,13},{2,14},{3,15},{4,8},{5,9},{6,10},{7,11},{8,4},{9,5},... | collective-permute-start | bytes 393224 | tf_op jit(solution)/shard_map/ppermute | solution.py:22
  66.4 2.1 %collective-permute-start.20 = (bf16[2,2,32,512]{3,2,1,0:T(8,128)(2,1)S(1)}, bf16[2,2,32,512]{3,2,1,0:T(8,128)(2,1)S(1)}, u32[]{:S(2)}, u32[]{:S(2)}) collective-permute-start(bf16[2,2,32,512]{3,2,1,0:T(8,128)(2,1)S(1)} %get-tuple-element.98), channel_id=1, source_target_pairs={{0,14},{1,15},{2,12},{3,13},{4,10},{5,11},{6,8},{7,9},{8,6},{9,7},... | collective-permute-start | bytes 393224 | tf_op jit(solution)/shard_map/ppermute | solution.py:22
  69.6 3.2 %collective-permute-start.22 = (bf16[2,2,32,512]{3,2,1,0:T(8,128)(2,1)S(1)}, bf16[2,2,32,512]{3,2,1,0:T(8,128)(2,1)S(1)}, u32[]{:S(2)}, u32[]{:S(2)}) collective-permute-start(bf16[2,2,32,512]{3,2,1,0:T(8,128)(2,1)S(1)} %get-tuple-element.100), channel_id=1, source_target_pairs={{0,6},{1,7},{2,4},{3,5},{4,2},{5,3},{6,0},{7,1},{8,14},{9,15},{10,... | collective-permute-start | bytes 393224 | tf_op jit(solution)/shard_map/ppermute | solution.py:22
  73.5 2.9 %shard_map.172 = f32[4,32,512]{2,1,0:T(8,128)} custom-call(f32[128,512]{1,0:T(8,128)S(1)} %get-tuple-element.103.grad, f32[124,512]{1,0:T(8,128)S(1)} %collective-permute-done.17.core_got, bf16[96,512]{1,0:T(8,128)(2,1)S(1)} %collective-permute-done.24.outer, f32[7,7,512]{2,1,0:T(8,128)S(1)} %get-tuple-element.71.kernel, ...), custom_call_target="tpu_custom_call" | custom-call | tf_op jit(solution)/shard_map/pallas_call | solution.py:44
  76.4 3.8 %collective-permute-start.27 = (f32[28,512]{1,0:T(8,128)S(1)}, f32[28,512]{1,0:T(8,128)S(1)}, u32[]{:S(2)}, u32[]{:S(2)}) collective-permute-start(f32[28,512]{1,0:T(8,128)S(1)} %add.13.after), channel_id=1, source_target_pairs={{0,4},{1,5},{2,6},{3,7},{4,0},{5,1},{6,2},{7,3},{8,12},{9,13},{10,... | collective-permute-start | bytes 172040 | tf_op jit(solution)/shard_map/ppermute | solution.py:22
  82.2 4.9 %collective-permute-start.28 = (f32[28,512]{1,0:T(8,128)S(1)}, f32[28,512]{1,0:T(8,128)S(1)}, u32[]{:S(2)}, u32[]{:S(2)}) collective-permute-start(f32[28,512]{1,0:T(8,128)S(1)} %add.14), channel_id=1, source_target_pairs={{0,8},{1,9},{2,10},{3,11},{4,12},{5,13},{6,14},{7,15},{8,0},{9,1},... | collective-permute-start | bytes 172040 | tf_op jit(solution)/shard_map/ppermute | solution.py:22
  87.1 3.2 %collective-permute-done.28 = f32[28,512]{1,0:T(8,128)S(1)} collective-permute-done((f32[28,512]{1,0:T(8,128)S(1)}, f32[28,512]{1,0:T(8,128)S(1)}, u32[]{:S(2)}, u32[]{:S(2)}) %collective-permute-start.28) | collective-permute-done | bytes 57376 | tf_op jit(solution)/shard_map/ppermute | solution.py:22
  (57 shorter events, 18.3 us)
Async XLA Ops:
  2.1 11.1 %collective-permute-start.1 = (bf16[96,512]{1,0:T(8,128)(2,1)S(1)}, bf16[96,512]{1,0:T(8,128)(2,1)S(1)}, u32[]{:S(2)}, u32[]{:S(2)}) collective-permute-start(bf16[96,512]{1,0:T(8,128)(2,1)S(1)} %get-tuple-element.70), channel_id=1, source_target_pairs={{1,2},{3,4},{5,6},{7,8},{9,10},{11,12},{13,14},{2,1},{4,3},{6,5},{... | collective-permute-start | bytes 294920 | tf_op jit(solution)/shard_map/ppermute | solution.py:28
  6.6 10.3 %collective-permute-start.10 = (bf16[2,32,512]{2,1,0:T(8,128)(2,1)S(1)}, bf16[2,32,512]{2,1,0:T(8,128)(2,1)S(1)}, u32[]{:S(2)}, u32[]{:S(2)}) collective-permute-start(bf16[2,32,512]{2,1,0:T(8,128)(2,1)S(1)} %get-tuple-element.82), channel_id=1, source_target_pairs={{0,10},{1,11},{2,8},{3,9},{4,14},{5,15},{6,12},{7,13},{8,2},{9,3},... | collective-permute-start | bytes 196616 | tf_op jit(solution)/shard_map/ppermute | solution.py:22
  10.0 8.4 %collective-permute-start.11 = (bf16[2,32,512]{2,1,0:T(8,128)(2,1)S(1)}, bf16[2,32,512]{2,1,0:T(8,128)(2,1)S(1)}, u32[]{:S(2)}, u32[]{:S(2)}) collective-permute-start(bf16[2,32,512]{2,1,0:T(8,128)(2,1)S(1)} %get-tuple-element.82), channel_id=1, source_target_pairs={{0,14},{1,15},{2,12},{3,13},{4,10},{5,11},{6,8},{7,9},{8,6},{9,7},... | collective-permute-start | bytes 196616 | tf_op jit(solution)/shard_map/ppermute | solution.py:22
  11.0 18.3 %collective-permute-start.5 = (bf16[2,32,512]{2,1,0:T(8,128)(2,1)S(1)}, bf16[2,32,512]{2,1,0:T(8,128)(2,1)S(1)}, u32[]{:S(2)}, u32[]{:S(2)}) collective-permute-start(bf16[2,32,512]{2,1,0:T(8,128)(2,1)S(1)} %get-tuple-element.80), channel_id=1, source_target_pairs={{0,8},{1,9},{2,10},{3,11},{4,12},{5,13},{6,14},{7,15},{8,0},{9,1},... | collective-permute-start | bytes 196616 | tf_op jit(solution)/shard_map/ppermute | solution.py:22
  12.4 18.2 %collective-permute-start.6 = (bf16[2,32,512]{2,1,0:T(8,128)(2,1)S(1)}, bf16[2,32,512]{2,1,0:T(8,128)(2,1)S(1)}, u32[]{:S(2)}, u32[]{:S(2)}) collective-permute-start(bf16[2,32,512]{2,1,0:T(8,128)(2,1)S(1)} %get-tuple-element.80), channel_id=1, source_target_pairs={{0,12},{1,13},{2,14},{3,15},{4,8},{5,9},{6,10},{7,11},{8,4},{9,5},... | collective-permute-start | bytes 196616 | tf_op jit(solution)/shard_map/ppermute | solution.py:22
  13.2 21.7 %collective-permute-start.8 = (bf16[2,2,32,512]{3,2,1,0:T(8,128)(2,1)S(1)}, bf16[2,2,32,512]{3,2,1,0:T(8,128)(2,1)S(1)}, u32[]{:S(2)}, u32[]{:S(2)}) collective-permute-start(bf16[2,2,32,512]{3,2,1,0:T(8,128)(2,1)S(1)} %get-tuple-element.81), channel_id=1, source_target_pairs={{0,2},{1,3},{2,0},{3,1},{4,6},{5,7},{6,4},{7,5},{8,10},{9,11},{10,... | collective-permute-start | bytes 393224 | tf_op jit(solution)/shard_map/ppermute | solution.py:22
  16.9 18.0 %collective-permute-start.9 = (bf16[2,2,32,512]{3,2,1,0:T(8,128)(2,1)S(1)}, bf16[2,2,32,512]{3,2,1,0:T(8,128)(2,1)S(1)}, u32[]{:S(2)}, u32[]{:S(2)}) collective-permute-start(bf16[2,2,32,512]{3,2,1,0:T(8,128)(2,1)S(1)} %get-tuple-element.81), channel_id=1, source_target_pairs={{0,6},{1,7},{2,4},{3,5},{4,2},{5,3},{6,0},{7,1},{8,14},{9,15},{10,... | collective-permute-start | bytes 393224 | tf_op jit(solution)/shard_map/ppermute | solution.py:22
  18.3 10.9 %collective-permute-start.2 = (bf16[2,128,512]{2,1,0:T(8,128)(2,1)S(1)}, bf16[2,128,512]{2,1,0:T(8,128)(2,1)S(1)}, u32[]{:S(2)}, u32[]{:S(2)}) collective-permute-start(bf16[2,128,512]{2,1,0:T(8,128)(2,1)S(1)} %get-tuple-element.75.mine), channel_id=1, source_target_pairs={{0,2},{1,3},{2,0},{3,1},{4,6},{5,7},{6,4},{7,5},{8,10},{9,11},{10,... | collective-permute-start | bytes 786440 | tf_op jit(solution)/shard_map/ppermute | solution.py:22
  29.3 5.6 %collective-permute-start.12 = (bf16[2,2,32,512]{3,2,1,0:T(8,128)(2,1)S(1)}, bf16[2,2,32,512]{3,2,1,0:T(8,128)(2,1)S(1)}, u32[]{:S(2)}, u32[]{:S(2)}) collective-permute-start(bf16[2,2,32,512]{3,2,1,0:T(8,128)(2,1)S(1)} %shard_map.165.refs_10_), channel_id=1, source_target_pairs={{0,16},{16,0},{1,17},{17,1},{2,18},{18,2},{3,19},{19,3},{4,20},{20... | collective-permute-start | bytes 393224 | tf_op jit(solution)/shard_map/ppermute | solution.py:36
  30.6 6.9 %collective-permute-start.3 = (bf16[2,256,512]{2,1,0:T(8,128)(2,1)S(1)}, bf16[2,256,512]{2,1,0:T(8,128)(2,1)S(1)}, u32[]{:S(2)}, u32[]{:S(2)}) collective-permute-start(bf16[2,256,512]{2,1,0:T(8,128)(2,1)S(1)} %shard_map.162.refs_0_), channel_id=1, source_target_pairs={{0,1},{1,0},{2,3},{3,2},{4,5},{5,4},{6,7},{7,6},{8,9},{9,8},{10,11... | collective-permute-start | bytes 1572872 | tf_op jit(solution)/shard_map/ppermute | solution.py:22
  43.5 4.8 %collective-permute-start.16 = (bf16[128,512]{1,0:T(8,128)(2,1)S(1)}, bf16[128,512]{1,0:T(8,128)(2,1)S(1)}, u32[]{:S(2)}, u32[]{:S(2)}) collective-permute-start(bf16[128,512]{1,0:T(8,128)(2,1)S(1)} %get-tuple-element.87.after), channel_id=1, source_target_pairs={{0,2},{1,3},{2,0},{3,1},{4,6},{5,7},{6,4},{7,5},{8,10},{9,11},{10,... | collective-permute-start | bytes 393224 | tf_op jit(solution)/shard_map/ppermute | solution.py:22
  50.3 8.9 %collective-permute-start.17 = (f32[124,512]{1,0:T(8,128)S(1)}, f32[124,512]{1,0:T(8,128)S(1)}, u32[]{:S(2)}, u32[]{:S(2)}) collective-permute-start(f32[124,512]{1,0:T(8,128)S(1)} %get-tuple-element.96), channel_id=1, source_target_pairs={{0,1},{1,0},{2,3},{3,2},{4,5},{5,4},{6,7},{7,6},{8,9},{9,8},{10,11... | collective-permute-start | bytes 761864 | tf_op jit(solution)/shard_map/ppermute | solution.py:22
  52.3 14.2 %collective-permute-start.25 = (bf16[128,512]{1,0:T(8,128)(2,1)S(1)}, bf16[128,512]{1,0:T(8,128)(2,1)S(1)}, u32[]{:S(2)}, u32[]{:S(2)}) collective-permute-start(bf16[128,512]{1,0:T(8,128)(2,1)S(1)} %get-tuple-element.107), channel_id=1, source_target_pairs={{0,2},{1,3},{2,0},{3,1},{4,6},{5,7},{6,4},{7,5},{8,10},{9,11},{10,... | collective-permute-start | bytes 393224 | tf_op jit(solution)/shard_map/ppermute | solution.py:22
  52.4 16.2 %collective-permute-start.14 = (bf16[2,2,32,512]{3,2,1,0:T(8,128)(2,1)S(1)}, bf16[2,2,32,512]{3,2,1,0:T(8,128)(2,1)S(1)}, u32[]{:S(2)}, u32[]{:S(2)}) collective-permute-start(bf16[2,2,32,512]{3,2,1,0:T(8,128)(2,1)S(1)} %get-tuple-element.88), channel_id=1, source_target_pairs={{0,8},{1,9},{2,10},{3,11},{4,12},{5,13},{6,14},{7,15},{8,0},{9,1},... | collective-permute-start | bytes 393224 | tf_op jit(solution)/shard_map/ppermute | solution.py:22
  55.6 14.0 %collective-permute-start.15 = (bf16[2,2,32,512]{3,2,1,0:T(8,128)(2,1)S(1)}, bf16[2,2,32,512]{3,2,1,0:T(8,128)(2,1)S(1)}, u32[]{:S(2)}, u32[]{:S(2)}) collective-permute-start(bf16[2,2,32,512]{3,2,1,0:T(8,128)(2,1)S(1)} %get-tuple-element.89), channel_id=1, source_target_pairs={{0,10},{1,11},{2,8},{3,9},{4,14},{5,15},{6,12},{7,13},{8,2},{9,3},... | collective-permute-start | bytes 393224 | tf_op jit(solution)/shard_map/ppermute | solution.py:22
  56.0 16.8 %collective-permute-start.24 = (bf16[96,512]{1,0:T(8,128)(2,1)S(1)}, bf16[96,512]{1,0:T(8,128)(2,1)S(1)}, u32[]{:S(2)}, u32[]{:S(2)}) collective-permute-start(bf16[96,512]{1,0:T(8,128)(2,1)S(1)} %get-tuple-element.104), channel_id=1, source_target_pairs={{1,2},{3,4},{5,6},{7,8},{9,10},{11,12},{13,14},{2,1},{4,3},{6,5},{... | collective-permute-start | bytes 294920 | tf_op jit(solution)/shard_map/ppermute | solution.py:28
  63.5 12.9 %collective-permute-start.19 = (bf16[2,2,32,512]{3,2,1,0:T(8,128)(2,1)S(1)}, bf16[2,2,32,512]{3,2,1,0:T(8,128)(2,1)S(1)}, u32[]{:S(2)}, u32[]{:S(2)}) collective-permute-start(bf16[2,2,32,512]{3,2,1,0:T(8,128)(2,1)S(1)} %get-tuple-element.97), channel_id=1, source_target_pairs={{0,12},{1,13},{2,14},{3,15},{4,8},{5,9},{6,10},{7,11},{8,4},{9,5},... | collective-permute-start | bytes 393224 | tf_op jit(solution)/shard_map/ppermute | solution.py:22
  66.4 13.7 %collective-permute-start.20 = (bf16[2,2,32,512]{3,2,1,0:T(8,128)(2,1)S(1)}, bf16[2,2,32,512]{3,2,1,0:T(8,128)(2,1)S(1)}, u32[]{:S(2)}, u32[]{:S(2)}) collective-permute-start(bf16[2,2,32,512]{3,2,1,0:T(8,128)(2,1)S(1)} %get-tuple-element.98), channel_id=1, source_target_pairs={{0,14},{1,15},{2,12},{3,13},{4,10},{5,11},{6,8},{7,9},{8,6},{9,7},... | collective-permute-start | bytes 393224 | tf_op jit(solution)/shard_map/ppermute | solution.py:22
  68.5 11.6 %collective-permute-start.21 = (bf16[2,2,32,512]{3,2,1,0:T(8,128)(2,1)S(1)}, bf16[2,2,32,512]{3,2,1,0:T(8,128)(2,1)S(1)}, u32[]{:S(2)}, u32[]{:S(2)}) collective-permute-start(bf16[2,2,32,512]{3,2,1,0:T(8,128)(2,1)S(1)} %get-tuple-element.99), channel_id=1, source_target_pairs={{0,4},{1,5},{2,6},{3,7},{4,0},{5,1},{6,2},{7,3},{8,12},{9,13},{10,... | collective-permute-start | bytes 393224 | tf_op jit(solution)/shard_map/ppermute | solution.py:22
  69.6 11.4 %collective-permute-start.22 = (bf16[2,2,32,512]{3,2,1,0:T(8,128)(2,1)S(1)}, bf16[2,2,32,512]{3,2,1,0:T(8,128)(2,1)S(1)}, u32[]{:S(2)}, u32[]{:S(2)}) collective-permute-start(bf16[2,2,32,512]{3,2,1,0:T(8,128)(2,1)S(1)} %get-tuple-element.100), channel_id=1, source_target_pairs={{0,6},{1,7},{2,4},{3,5},{4,2},{5,3},{6,0},{7,1},{8,14},{9,15},{10,... | collective-permute-start | bytes 393224 | tf_op jit(solution)/shard_map/ppermute | solution.py:22
  72.7 8.3 %collective-permute-start.23 = (bf16[2,2,32,512]{3,2,1,0:T(8,128)(2,1)S(1)}, bf16[2,2,32,512]{3,2,1,0:T(8,128)(2,1)S(1)}, u32[]{:S(2)}, u32[]{:S(2)}) collective-permute-start(bf16[2,2,32,512]{3,2,1,0:T(8,128)(2,1)S(1)} %get-tuple-element.101), channel_id=1, source_target_pairs={{0,2},{1,3},{2,0},{3,1},{4,6},{5,7},{6,4},{7,5},{8,10},{9,11},{10,... | collective-permute-start | bytes 393224 | tf_op jit(solution)/shard_map/ppermute | solution.py:22
  76.4 5.9 %collective-permute-start.27 = (f32[28,512]{1,0:T(8,128)S(1)}, f32[28,512]{1,0:T(8,128)S(1)}, u32[]{:S(2)}, u32[]{:S(2)}) collective-permute-start(f32[28,512]{1,0:T(8,128)S(1)} %add.13.after), channel_id=1, source_target_pairs={{0,4},{1,5},{2,6},{3,7},{4,0},{5,1},{6,2},{7,3},{8,12},{9,13},{10,... | collective-permute-start | bytes 172040 | tf_op jit(solution)/shard_map/ppermute | solution.py:22
  81.1 11.4 %collective-permute-start.26 = (bf16[2,2,32,512]{3,2,1,0:T(8,128)(2,1)S(1)}, bf16[2,2,32,512]{3,2,1,0:T(8,128)(2,1)S(1)}, u32[]{:S(2)}, u32[]{:S(2)}) collective-permute-start(bf16[2,2,32,512]{3,2,1,0:T(8,128)(2,1)S(1)} %get-tuple-element.119), channel_id=1, source_target_pairs={{0,1},{1,0},{2,3},{3,2},{4,5},{5,4},{6,7},{7,6},{8,9},{9,8},{10,11... | collective-permute-start | bytes 393224 | tf_op jit(solution)/shard_map/ppermute | solution.py:22
  82.2 8.0 %collective-permute-start.28 = (f32[28,512]{1,0:T(8,128)S(1)}, f32[28,512]{1,0:T(8,128)S(1)}, u32[]{:S(2)}, u32[]{:S(2)}) collective-permute-start(f32[28,512]{1,0:T(8,128)S(1)} %add.14), channel_id=1, source_target_pairs={{0,8},{1,9},{2,10},{3,11},{4,12},{5,13},{6,14},{7,15},{8,0},{9,1},... | collective-permute-start | bytes 172040 | tf_op jit(solution)/shard_map/ppermute | solution.py:22
  (6 other events, 22.8 us)

commit v5 on v4

--- a/solution.py
+++ b/solution.py
@@ -112,7 +112,8 @@
         sent[...] = full[group]
 
 
-def acts_body(mine, got, acts):
+def acts_body(mine, got, *refs):
+    acts = refs[-1]
     pixels = mine.shape[1]
     acts[:, :pixels] = mine[...]
     acts[:, pixels:] = got[...]
@@ -246,15 +247,19 @@
 
 
 def owners_body(turns, holder, after, *targets):
-    del after
     me, _, _ = place()
-    own = targets[0].shape[2]
+    own = holder.shape[1] // lax.axis_size("row")
     for pattern, target in zip(turns, targets):
         for c in range(2):
             device = jnp.bitwise_xor(me, 2 * pattern + c)
             rows = pl.ds(pl.multiple_of(device * own, own), own)
             for which in range(2):
-                target[c, which] = holder[which, rows, :].astype(target.dtype)
+                start = (2 * c + which) * own
+                target[start : start + own, :] = holder[which, rows, :].astype(target.dtype)
+        if target.shape[0] > 4 * own:
+            target[4 * own : 4 * own + SMALL_ROWS, :] = after[...].astype(target.dtype)
+            rest = target.shape[0] - 4 * own - SMALL_ROWS
+            target[4 * own + SMALL_ROWS :, :] = jnp.zeros((rest, target.shape[1]), target.dtype)
 
 
 def fold_body(kept, got, stay, leave, mixed_stay, mixed_leave):
@@ -266,7 +271,7 @@
 
 def conv_grad_body(norm_scale, *refs):
     kept, got, normed, inv, gain, feats, core_got, outer, scale, in_bias = refs[:10]
-    grad, rim_out, stay, leave, padded, small = refs[10:]
+    grad, inner_out, rim_out, stay, leave, padded, small = refs[10:]
     rows, cols, channels = feats.shape
     me, c, _ = place()
     out_grad = kept[...] + got[...].astype(WIDE)
@@ -279,7 +284,7 @@
     pixels = rows * cols
     rim = RIM * cols
     rim_out[...] = jnp.where(c == 0, result[:rim], result[pixels - rim :]).astype(NARROW)
-    leave[:rim, :] = jnp.where(c == 0, result[pixels - rim :], result[:rim])
+    inner_out[...] = jnp.where(c == 0, result[pixels - rim :], result[:rim]).astype(NARROW)
     fill(padded, feats[...], core_got[core_got.shape[0] - rim :, :], outer[...])
 
     def put(row, lanes, total):
@@ -312,12 +317,12 @@
         own_part = jnp.where(lax.rem(me, 4) == part, 1.0, 0.0)
         put(row + 3 + part, everything, own_part * in_bias[...])
     stay[...] = small[c]
-    leave[rim:, :] = small[1 - c]
-
-
-def input_grad_body(grad, core_got, outer, kernel, cotan, result, padded):
+    leave[...] = small[1 - c]
+
+
+def input_grad_body(grad, inner, outer, kernel, cotan, result, padded):
     rows, cols, channels = cotan.shape
-    fill(padded, grad[...].reshape(cotan.shape), core_got[: RIM * cols, :], outer[...])
+    fill(padded, grad[...].reshape(cotan.shape), inner[...], outer[...])
 
     @pl.loop(0, channels // LANES)
     def _(step):
@@ -334,34 +339,39 @@
 
 
 def total_body(turns, *refs):
-    stay, leave = refs[-2:]
+    parts, sums = refs[: len(turns)], refs[len(turns) : -3]
+    stay, leave, half = refs[-3:]
+    own = stay.shape[2]
     for side in range(2):
-        total = jnp.zeros(stay.shape[1:], WIDE)
-        for part, turn in zip(refs, turns):
+        total = jnp.zeros(parts[0].shape, WIDE)
+        for part, turn in zip(parts, turns):
             if turn % 2 == side:
                 total = total + part[...].astype(WIDE)
-        stay[side] = total[0]
-        leave[side] = total[1].astype(NARROW)
-
-
-def owner_body(stay, got, in_grad, out_grad):
+        for which in range(2):
+            stay[side, which] = total[which * own : (which + 1) * own]
+        leave[2 * side * own : 2 * (side + 1) * own, :] = total[2 * own :]
+    total = sums[0][...]
+    for one in sums[1:]:
+        total = total + one[...].astype(WIDE)
+    half[...] = total
+    leave[4 * own :, :] = total
+
+
+def final_body(stay, got, half, *refs):
+    in_grad, out_grad, kernel_grad, gain, bias, scale, in_bias, held = refs
     _, c, x = place()
     quarter = stay.shape[-1]
-    for value, part in (
-        (stay[0], 2 * x + c),
-        (stay[1], 2 * (1 - x) + c),
-        (got[0], 2 * x + 1 - c),
-        (got[1], 2 * (1 - x) + 1 - c),
-    ):
-        lanes = pl.ds(pl.multiple_of(part * quarter, quarter), quarter)
-        in_grad[:, lanes] = value[0].astype(WIDE)
-        out_grad[:, lanes] = value[1].astype(WIDE)
-
-
-def small_body(mine, other, kernel_grad, gain, bias, scale, in_bias, held):
-    _, core_bit, _ = place()
-    held[core_bit] = mine[...]
-    held[1 - core_bit] = other[...]
+    own = stay.shape[2]
+    for side in range(2):
+        part = 2 * jnp.bitwise_xor(x, side)
+        near = pl.ds(pl.multiple_of((part + c) * quarter, quarter), quarter)
+        far = pl.ds(pl.multiple_of((part + 1 - c) * quarter, quarter), quarter)
+        for which, target in enumerate((in_grad, out_grad)):
+            start = (2 * side + which) * own
+            target[:, near] = stay[side, which]
+            target[:, far] = got[start : start + own, :]
+    held[c] = half[...]
+    held[1 - c] = got[4 * own :, :]
 
     def take(row):
         return held[row // SMALL_ROWS, pl.ds(row % SMALL_ROWS, 1), :]
@@ -373,7 +383,6 @@
     gain[...] = take(row)
     bias[...] = take(row + 1)
     scale[...] = take(row + 2)
-    quarter = take(row).shape[1]
     for part in range(4):
         in_bias[:, pl.ds(part * quarter, quarter)] = take(row + 3 + part)
 
@@ -467,8 +476,13 @@
         branch,
         scratch=(padded, pltpu.VMEM((pixels, channels), WIDE)),
     )
+    first_blocks = [pieces[k] for k in (1, 4, 5, 7)]
     acts = run(
-        acts_body, (shaped((2, 2 * pixels, channels), NARROW),), acts, swap(acts, 2)
+        acts_body,
+        (shaped((2, 2 * pixels, channels), NARROW),),
+        acts,
+        swap(acts, 2),
+        *first_blocks,
     )[0]
     acts_got = swap(acts, 1)
 
@@ -509,7 +523,6 @@
     out_stay, out_leave, mixed_stay, mixed_leave = run(fold_body, half * 2, keep, swap(send, 1))
     out_got = swap(out_leave, 2)
 
-    owned = (2, 2, own_rows, quarter)
     holder = run(
         functools.partial(weight_body, norm_scale),
         (shaped((2, channels, quarter)),),
@@ -519,13 +532,14 @@
         hidden,
         mib=24,
     )[0]
-    conv_grad, rim_out, stay, leave = run(
+    conv_grad, inner_out, rim_out, stay, leave = run(
         functools.partial(conv_grad_body, norm_scale),
         (
             shaped((pixels, channels)),
             shaped((rim, channels), NARROW),
+            shaped((rim, channels), NARROW),
             shaped((SMALL_ROWS, channels)),
-            shaped((rim + SMALL_ROWS, channels)),
+            shaped((SMALL_ROWS, channels)),
         ),
         out_stay,
         out_got,
@@ -540,36 +554,47 @@
         scratch=(padded, pltpu.VMEM((2, SMALL_ROWS, channels), WIDE)),
     )
     rim_got = swap_rim(rim_out)
-    leave_got = swap(leave, 1)
-    sums = stay + leave_got[rim:]
+    inner_got = swap(inner_out, 1)
+    sums = stay + swap(leave, 1)
+
+    far_turns = (*range(2 * patterns - 1, 4, -2), 3, 1)
+    near_turns = (*range(4, 2 * patterns, 2), 2, 0)
+    owned = 4 * own_rows
+    if copied:
+        parts = run(
+            functools.partial(owners_body, far_turns),
+            (shaped((owned, quarter), NARROW),) * len(far_turns),
+            holder,
+            out_leave,
+        )
+    else:
+        flat = holder.reshape(2, count, own_rows, quarter)
+        flat = canonical(jnp.moveaxis(flat, 1, 0), me, bit_count)
+        flat = flat.reshape(2 * patterns, owned, quarter)
+        parts = [flat[p].astype(NARROW) for p in far_turns]
+    far_parts = [swap(part, 2 * p) for p, part in zip(far_turns, parts)]
+    sums, far_parts = lax.optimization_barrier((sums, far_parts))
     sums = sums + swap(sums, 2)
-    early = sums
-    for spot in range(2, bit_count):
-        sums = sums + swap(sums, 1 << spot)
-
-    turns = (*range(4, 2 * patterns), 2, 3, 1, 0)
-    kinds = [NARROW if p else WIDE for p in turns]
     if copied:
-        parts = []
-        for some, after in ((slice(0, 2), out_leave), (slice(2, None), early)):
-            parts += run(
-                functools.partial(owners_body, turns[some]),
-                tuple(shaped(owned, kind) for kind in kinds[some]),
-                holder,
-                after,
-            )
+        joint = shaped((owned + 32, quarter), NARROW)
+        *parts, near_own = run(
+            functools.partial(owners_body, near_turns),
+            (joint,) * (len(near_turns) - 1) + (shaped((owned, quarter)),),
+            holder,
+            sums,
+        )
+        parts = [swap(part, 2 * p) for p, part in zip(near_turns, parts)]
+        sums_parts = [part[owned : owned + SMALL_ROWS] for part in parts]
+        near_parts = [part[:owned] for part in parts] + [near_own]
     else:
-        parts = holder.reshape(2, count, own_rows, quarter)
-        parts = canonical(jnp.moveaxis(parts, 1, 0), me, bit_count)
-        parts = parts.reshape(2 * patterns, 2, 2, own_rows, quarter)
-        parts = [parts[p].astype(kind) for p, kind in zip(turns, kinds)]
-    parts = [swap(part, 2 * p) if p else part for p, part in zip(turns, parts)]
+        near_parts = [swap(flat[p].astype(NARROW), 2 * p) for p in near_turns[:-1]] + [flat[0]]
+        sums_parts = [swap(sums.astype(NARROW), 2 * p) for p in near_turns[:-1]]
 
     input_grad = run(
         input_grad_body,
         (shaped(features.shape),),
         conv_grad,
-        leave_got,
+        inner_got,
         rim_got,
         taps,
         cotan,
@@ -583,28 +608,42 @@
         mixed_stay,
         swap(mixed_leave, 2),
     )[0]
+    parts = list(far_parts) + near_parts
     parts, input_grad, output = lax.optimization_barrier((parts, input_grad, output))
 
-    stay, leave = run(
-        functools.partial(total_body, turns),
-        (shaped((2,) + piece), shaped((2,) + piece, NARROW)),
+    stay, leave, half_sums = run(
+        functools.partial(total_body, far_turns + near_turns),
+        (
+            shaped((2, 2, own_rows, quarter)),
+            shaped((owned + SMALL_ROWS, quarter)),
+            shaped((SMALL_ROWS, channels)),
+        ),
         *parts,
-        order=20,
-    )
-    in_weight_grad, out_weight_grad = run(
-        owner_body, (shaped((own_rows, hidden_count)),) * 2, stay, swap(leave, 1)
-    )
-    kernel_grad, gain_grad, bias_grad, scale_grad, in_bias_grad = run(
-        small_body,
+        sums,
+        *sums_parts,
+    )
+    (
+        in_weight_grad,
+        out_weight_grad,
+        kernel_grad,
+        gain_grad,
+        bias_grad,
+        scale_grad,
+        in_bias_grad,
+    ) = run(
+        final_body,
         (
+            shaped((own_rows, hidden_count)),
+            shaped((own_rows, hidden_count)),
             shaped(kernel.shape),
             shaped((1, channels)),
             shaped((1, channels)),
             shaped((1, channels)),
             shaped((1, hidden_count)),
         ),
-        sums,
-        swap(sums, 1),
+        stay,
+        swap(leave, 1),
+        half_sums,
         scratch=(pltpu.VMEM((2, SMALL_ROWS, channels), WIDE),),
     )
     return (

time: 93.8 us -> 82.7 us (0.88)
  the two profiles are of different devices: /device:TPU:1 before, /device:TPU:17 now
where the time goes in v5:
time: 82.7 us; the launch traced here: 82.5 us
  starting transfers between devices  46.6 us (56%)
  waiting for transfers between devices  21.9 us (26%)
  Pallas kernels  13.1 us (16%)
  between operations  0.83 us (1%)
    ppermute x24, starting transfers between devices, swap(): return lax.ppermute(value, 'row', [(i, i ^ bit) for i in range(count)])  38.1 us
    ppermute x24, waiting for transfers between devices, swap(): return lax.ppermute(value, 'row', [(i, i ^ bit) for i in range(count)])  15.7 us
    pallas_call x16, Pallas kernels, run(): pl.pallas_call(body, out_shape=outs, **extra, scratch_shapes=scratch, com...  13.1 us
    ppermute x2, starting transfers between devices, swap_rim(): return lax.ppermute(value, 'row', pairs + [(j, i) for i, j in pairs])  5.9 us
    ppermute x2, waiting for transfers between devices, swap_group(): return lax.ppermute(value, 'grp', [(0, 1), (1, 0)])  3.08 us
    ppermute x2, waiting for transfers between devices, swap_rim(): return lax.ppermute(value, 'row', pairs + [(j, i) for i, j in pairs])  3.08 us
    ppermute x2, starting transfers between devices, swap_group(): return lax.ppermute(value, 'grp', [(0, 1), (1, 0)])  2.61 us
  transfers between devices with their start and end apart: 28, of which 14 were waited for; matrix products, arithmetic and copies ran while one was open for 0% of the time, Pallas kernels for 11%

profile of v5, /device:TPU:17, one launch (start us, length us, event | category | flops | bytes accessed | tf_op | source)
XLA Modules:
  0.0 82.5 jit_solution(1147079645085714359)
XLA Ops:
  0.6 1.3 %shard_map.160 = (bf16[2,2,32,512]{3,2,1,0:T(8,128)(2,1)S(1)}, bf16[224,512]{1,0:T(8,128)(2,1)S(1)}, bf16[96,512]{1,0:T(8,128)(2,1)S(1)}, bf16[128,512]{1,0:T(8,...) custom-call(f32[32,2048]{1,0:T(8,128)} %refs_0_.1, ...), custom_call_target="tpu_custom_call" | custom-call | tf_op jit(solution)/shard_map/pallas_call | solution.py:44
  2.7 3.0 %collective-permute-start.1 = (bf16[96,512]{1,0:T(8,128)(2,1)S(1)}, bf16[96,512]{1,0:T(8,128)(2,1)S(1)}, u32[]{:S(2)}, u32[]{:S(2)}) collective-permute-start(bf16[96,512]{1,0:T(8,128)(2,1)S(1)} %get-tuple-element.77), channel_id=1, source_target_pairs={{1,2},{3,4},{5,6},{7,8},{9,10},{11,12},{13,14},{2,1},{4,3},{6,5},{... | collective-permute-start | bytes 294920 | tf_op jit(solution)/shard_map/ppermute | solution.py:28
  7.0 3.1 %collective-permute-start.6 = (bf16[2,32,512]{2,1,0:T(8,128)(2,1)S(1)}, bf16[2,32,512]{2,1,0:T(8,128)(2,1)S(1)}, u32[]{:S(2)}, u32[]{:S(2)}) collective-permute-start(bf16[2,32,512]{2,1,0:T(8,128)(2,1)S(1)} %get-tuple-element.86), channel_id=1, source_target_pairs={{0,10},{1,11},{2,8},{3,9},{4,14},{5,15},{6,12},{7,13},{8,2},{9,3},... | collective-permute-start | bytes 196616 | tf_op jit(solution)/shard_map/ppermute | solution.py:22
  11.1 1.7 %collective-permute-start.3 = (bf16[2,2,32,512]{3,2,1,0:T(8,128)(2,1)S(1)}, bf16[2,2,32,512]{3,2,1,0:T(8,128)(2,1)S(1)}, u32[]{:S(2)}, u32[]{:S(2)}) collective-permute-start(bf16[2,2,32,512]{3,2,1,0:T(8,128)(2,1)S(1)} %get-tuple-element.84.refs_4_), channel_id=1, source_target_pairs={{0,4},{1,5},{2,6},{3,7},{4,0},{5,1},{6,2},{7,3},{8,12},{9,13},{10,... | collective-permute-start | bytes 393224 | tf_op jit(solution)/shard_map/ppermute | solution.py:22
  12.8 2.4 %shard_map.161 = (f32[128,512]{1,0:T(8,128)S(1)}, f32[128,128]{1,0:T(8,128)S(1)}, bf16[2,128,512]{2,1,0:T(8,128)(2,1)S(1)}) custom-call(f32[4,32,512]{2,1,0:T(8,128)S(1)} %get-tuple-element.75.feats.refs_5_, bf16[224,512]{1,0:T(8,128)(2,1)S(1)} %collective-permute-done.core_got.other.refs_6_, bf16[96,512]{1,0:T(8,128)(2,1)S(1)} %collective-permute-done.1.outer.refs_7_, ...), custom_call_target="tpu_custom_call" | custom-call | tf_op jit(solution)/shard_map/pallas_call | solution.py:44
  17.5 2.2 %collective-permute-start.11 = (bf16[2,32,512]{2,1,0:T(8,128)(2,1)S(1)}, bf16[2,32,512]{2,1,0:T(8,128)(2,1)S(1)}, u32[]{:S(2)}, u32[]{:S(2)}) collective-permute-start(bf16[2,32,512]{2,1,0:T(8,128)(2,1)S(1)} %get-tuple-element.89), channel_id=1, source_target_pairs={{0,12},{1,13},{2,14},{3,15},{4,8},{5,9},{6,10},{7,11},{8,4},{9,5},... | collective-permute-start | bytes 196616 | tf_op jit(solution)/shard_map/ppermute | solution.py:22
  19.7 2.1 %collective-permute-start.10 = (bf16[2,32,512]{2,1,0:T(8,128)(2,1)S(1)}, bf16[2,32,512]{2,1,0:T(8,128)(2,1)S(1)}, u32[]{:S(2)}, u32[]{:S(2)}) collective-permute-start(bf16[2,32,512]{2,1,0:T(8,128)(2,1)S(1)} %get-tuple-element.89), channel_id=1, source_target_pairs={{0,8},{1,9},{2,10},{3,11},{4,12},{5,13},{6,14},{7,15},{8,0},{9,1},... | collective-permute-start | bytes 196616 | tf_op jit(solution)/shard_map/ppermute | solution.py:22
  21.8 2.8 %collective-permute-done.2.got = bf16[2,128,512]{2,1,0:T(8,128)(2,1)S(1)} collective-permute-done((bf16[2,128,512]{2,1,0:T(8,128)(2,1)S(1)}, bf16[2,128,512]{2,1,0:T(8,128)(2,1)S(1)}, u32[]{:S(2)}, u32[]{:S(2)}) %collective-permute-start.2) | collective-permute-done | bytes 262176 | tf_op jit(solution)/shard_map/ppermute | solution.py:22
  27.1 3.1 %collective-permute-done.12.refs_7_ = bf16[2,2,32,512]{3,2,1,0:T(8,128)(2,1)S(1)} collective-permute-done((bf16[2,2,32,512]{3,2,1,0:T(8,128)(2,1)S(1)}, bf16[2,2,32,512]{3,2,1,0:T(8,128)(2,1)S(1)}, u32[]{:S(2)}, u32[]{:S(2)}) %collective-permute-start.12) | collective-permute-done | bytes 131104 | tf_op jit(solution)/shard_map/ppermute | solution.py:36
  30.2 1.7 %shard_map.166 = (f32[2,256,512]{2,1,0:T(8,128)S(1)}, bf16[2,256,512]{2,1,0:T(8,128)(2,1)S(1)}, bf16[512,512]{1,0:T(8,128)(2,1)S(1)}, bf16[512,512]{1,0:T(8,128)...) custom-call(bf16[2,256,512]{2,1,0:T(8,128)(2,1)S(1)} %shard_map.164.refs_0_, ...), custom_call_target="tpu_custom_call" | custom-call | tf_op jit(solution)/shard_map/pallas_call | solution.py:44
  31.9 1.7 %collective-permute-start.13 = (bf16[2,256,512]{2,1,0:T(8,128)(2,1)S(1)}, bf16[2,256,512]{2,1,0:T(8,128)(2,1)S(1)}, u32[]{:S(2)}, u32[]{:S(2)}) collective-permute-start(bf16[2,256,512]{2,1,0:T(8,128)(2,1)S(1)} %get-tuple-element.91), channel_id=1, source_target_pairs={{0,1},{1,0},{2,3},{3,2},{4,5},{5,4},{6,7},{7,6},{8,9},{9,8},{10,11... | collective-permute-start | bytes 1572872 | tf_op jit(solution)/shard_map/ppermute | solution.py:22
  33.6 1.5 %collective-permute-done.13.got = bf16[2,256,512]{2,1,0:T(8,128)(2,1)S(1)} collective-permute-done((bf16[2,256,512]{2,1,0:T(8,128)(2,1)S(1)}, bf16[2,256,512]{2,1,0:T(8,128)(2,1)S(1)}, u32[]{:S(2)}, u32[]{:S(2)}) %collective-permute-start.13) | collective-permute-done | bytes 524320 | tf_op jit(solution)/shard_map/ppermute | solution.py:22
  38.2 3.8 %collective-permute-start.17 = (bf16[128,512]{1,0:T(8,128)(2,1)S(1)}, bf16[128,512]{1,0:T(8,128)(2,1)S(1)}, u32[]{:S(2)}, u32[]{:S(2)}) collective-permute-start(bf16[128,512]{1,0:T(8,128)(2,1)S(1)} %get-tuple-element.103), channel_id=1, source_target_pairs={{0,10},{1,11},{2,8},{3,9},{4,14},{5,15},{6,12},{7,13},{8,2},{9,3},... | collective-permute-start | bytes 393224 | tf_op jit(solution)/shard_map/ppermute | solution.py:22
  43.4 1.9 %shard_map.168 = (f32[128,512]{1,0:T(8,128)S(1)}, bf16[96,512]{1,0:T(8,128)(2,1)S(1)}, bf16[96,512]{1,0:T(8,128)(2,1)S(1)}, f32[28,512]{1,0:T(8,128)S(1)}, f32[28,512]{1,0:T(8,128)S(1)}) custom-call(f32[128,512]{1,0:T(8,128)S(1)} %get-tuple-element.92.refs_0_, bf16[128,512]{1,0:T(8,128)(2,1)S(1)} %collective-permute-done.14.refs_1_, ...), custom_call_target="tpu_custom_call" | custom-call | tf_op jit(solution)/shard_map/pallas_call | solution.py:44
  45.3 1.6 %collective-permute-start.15 = (f32[28,512]{1,0:T(8,128)S(1)}, f32[28,512]{1,0:T(8,128)S(1)}, u32[]{:S(2)}, u32[]{:S(2)}) collective-permute-start(f32[28,512]{1,0:T(8,128)S(1)} %get-tuple-element.99), channel_id=1, source_target_pairs={{0,1},{1,0},{2,3},{3,2},{4,5},{5,4},{6,7},{7,6},{8,9},{9,8},{10,11... | collective-permute-start | bytes 172040 | tf_op jit(solution)/shard_map/ppermute | solution.py:22
  48.0 2.3 %collective-permute-done.17.refs_1_ = bf16[128,512]{1,0:T(8,128)(2,1)S(1)} collective-permute-done((bf16[128,512]{1,0:T(8,128)(2,1)S(1)}, bf16[128,512]{1,0:T(8,128)(2,1)S(1)}, u32[]{:S(2)}, u32[]{:S(2)}) %collective-permute-start.17) | collective-permute-done | bytes 131104 | tf_op jit(solution)/shard_map/ppermute | solution.py:22
  53.4 3.1 %collective-permute-done.20 = f32[28,512]{1,0:T(8,128)S(1)} collective-permute-done((f32[28,512]{1,0:T(8,128)S(1)}, f32[28,512]{1,0:T(8,128)S(1)}, u32[]{:S(2)}, u32[]{:S(2)}) %collective-permute-start.20) | collective-permute-done | bytes 57376 | tf_op jit(solution)/shard_map/ppermute | solution.py:22
  56.6 2.7 %collective-permute-start.21 = (bf16[160,512]{1,0:T(8,128)(2,1)S(1)}, bf16[160,512]{1,0:T(8,128)(2,1)S(1)}, u32[]{:S(2)}, u32[]{:S(2)}) collective-permute-start(bf16[160,512]{1,0:T(8,128)(2,1)S(1)} %get-tuple-element.111), channel_id=1, source_target_pairs={{0,8},{1,9},{2,10},{3,11},{4,12},{5,13},{6,14},{7,15},{8,0},{9,1},... | collective-permute-start | bytes 491528 | tf_op jit(solution)/shard_map/ppermute | solution.py:22
  60.6 3.1 %collective-permute-start.24 = (bf16[96,512]{1,0:T(8,128)(2,1)S(1)}, bf16[96,512]{1,0:T(8,128)(2,1)S(1)}, u32[]{:S(2)}, u32[]{:S(2)}) collective-permute-start(bf16[96,512]{1,0:T(8,128)(2,1)S(1)} %get-tuple-element.116), channel_id=1, source_target_pairs={{0,1},{1,0},{2,3},{3,2},{4,5},{5,4},{6,7},{7,6},{8,9},{9,8},{10,11... | collective-permute-start | bytes 294920 | tf_op jit(solution)/shard_map/ppermute | solution.py:22
  63.7 2.9 %collective-permute-start.25 = (bf16[96,512]{1,0:T(8,128)(2,1)S(1)}, bf16[96,512]{1,0:T(8,128)(2,1)S(1)}, u32[]{:S(2)}, u32[]{:S(2)}) collective-permute-start(bf16[96,512]{1,0:T(8,128)(2,1)S(1)} %get-tuple-element.117), channel_id=1, source_target_pairs={{1,2},{3,4},{5,6},{7,8},{9,10},{11,12},{13,14},{2,1},{4,3},{6,5},{... | collective-permute-start | bytes 294920 | tf_op jit(solution)/shard_map/ppermute | solution.py:28
  67.3 2.6 %collective-permute-done.25.outer = bf16[96,512]{1,0:T(8,128)(2,1)S(1)} collective-permute-done((bf16[96,512]{1,0:T(8,128)(2,1)S(1)}, bf16[96,512]{1,0:T(8,128)(2,1)S(1)}, u32[]{:S(2)}, u32[]{:S(2)}) %collective-permute-start.25) | collective-permute-done | bytes 98336 | tf_op jit(solution)/shard_map/ppermute | solution.py:28
  69.9 2.9 %shard_map.172 = f32[4,32,512]{2,1,0:T(8,128)} custom-call(f32[128,512]{1,0:T(8,128)S(1)} %get-tuple-element.115.grad, bf16[96,512]{1,0:T(8,128)(2,1)S(1)} %collective-permute-done.24.inner, bf16[96,512]{1,0:T(8,128)(2,1)S(1)} %collective-permute-done.25.outer, f32[7,7,512]{2,1,0:T(8,128)S(1)} %get-tuple-element.78.kernel, ...), custom_call_target="tpu_custom_call" | custom-call | tf_op jit(solution)/shard_map/pallas_call | solution.py:44
  72.8 1.6 %collective-permute-done.22 = bf16[160,512]{1,0:T(8,128)(2,1)S(1)} collective-permute-done((bf16[160,512]{1,0:T(8,128)(2,1)S(1)}, bf16[160,512]{1,0:T(8,128)(2,1)S(1)}, u32[]{:S(2)}, u32[]{:S(2)}) %collective-permute-start.22) | collective-permute-done | bytes 163872 | tf_op jit(solution)/shard_map/ppermute | solution.py:22
  74.6 5.8 %collective-permute-start.27 = (f32[156,512]{1,0:T(8,128)S(1)}, f32[156,512]{1,0:T(8,128)S(1)}, u32[]{:S(2)}, u32[]{:S(2)}) collective-permute-start(f32[156,512]{1,0:T(8,128)S(1)} %get-tuple-element.132), channel_id=1, source_target_pairs={{0,1},{1,0},{2,3},{3,2},{4,5},{5,4},{6,7},{7,6},{8,9},{9,8},{10,11... | collective-permute-start | bytes 958472 | tf_op jit(solution)/shard_map/ppermute | solution.py:22
  (56 shorter events, 20.9 us)
Async XLA Ops:
  2.7 8.4 %collective-permute-start.1 = (bf16[96,512]{1,0:T(8,128)(2,1)S(1)}, bf16[96,512]{1,0:T(8,128)(2,1)S(1)}, u32[]{:S(2)}, u32[]{:S(2)}) collective-permute-start(bf16[96,512]{1,0:T(8,128)(2,1)S(1)} %get-tuple-element.77), channel_id=1, source_target_pairs={{1,2},{3,4},{5,6},{7,8},{9,10},{11,12},{13,14},{2,1},{4,3},{6,5},{... | collective-permute-start | bytes 294920 | tf_op jit(solution)/shard_map/ppermute | solution.py:28
  5.8 9.4 %collective-permute-start.7 = (bf16[2,32,512]{2,1,0:T(8,128)(2,1)S(1)}, bf16[2,32,512]{2,1,0:T(8,128)(2,1)S(1)}, u32[]{:S(2)}, u32[]{:S(2)}) collective-permute-start(bf16[2,32,512]{2,1,0:T(8,128)(2,1)S(1)} %get-tuple-element.86), channel_id=1, source_target_pairs={{0,14},{1,15},{2,12},{3,13},{4,10},{5,11},{6,8},{7,9},{8,6},{9,7},... | collective-permute-start | bytes 196616 | tf_op jit(solution)/shard_map/ppermute | solution.py:22
  7.0 9.0 %collective-permute-start.6 = (bf16[2,32,512]{2,1,0:T(8,128)(2,1)S(1)}, bf16[2,32,512]{2,1,0:T(8,128)(2,1)S(1)}, u32[]{:S(2)}, u32[]{:S(2)}) collective-permute-start(bf16[2,32,512]{2,1,0:T(8,128)(2,1)S(1)} %get-tuple-element.86), channel_id=1, source_target_pairs={{0,10},{1,11},{2,8},{3,9},{4,14},{5,15},{6,12},{7,13},{8,2},{9,3},... | collective-permute-start | bytes 196616 | tf_op jit(solution)/shard_map/ppermute | solution.py:22
  10.1 9.5 %collective-permute-start.5 = (bf16[2,2,32,512]{3,2,1,0:T(8,128)(2,1)S(1)}, bf16[2,2,32,512]{3,2,1,0:T(8,128)(2,1)S(1)}, u32[]{:S(2)}, u32[]{:S(2)}) collective-permute-start(bf16[2,2,32,512]{3,2,1,0:T(8,128)(2,1)S(1)} %get-tuple-element.85), channel_id=1, source_target_pairs={{0,6},{1,7},{2,4},{3,5},{4,2},{5,3},{6,0},{7,1},{8,14},{9,15},{10,... | collective-permute-start | bytes 393224 | tf_op jit(solution)/shard_map/ppermute | solution.py:22
  10.4 11.4 %collective-permute-start.4 = (bf16[2,2,32,512]{3,2,1,0:T(8,128)(2,1)S(1)}, bf16[2,2,32,512]{3,2,1,0:T(8,128)(2,1)S(1)}, u32[]{:S(2)}, u32[]{:S(2)}) collective-permute-start(bf16[2,2,32,512]{3,2,1,0:T(8,128)(2,1)S(1)} %get-tuple-element.85), channel_id=1, source_target_pairs={{0,2},{1,3},{2,0},{3,1},{4,6},{5,7},{6,4},{7,5},{8,10},{9,11},{10,... | collective-permute-start | bytes 393224 | tf_op jit(solution)/shard_map/ppermute | solution.py:22
  11.1 6.4 %collective-permute-start.3 = (bf16[2,2,32,512]{3,2,1,0:T(8,128)(2,1)S(1)}, bf16[2,2,32,512]{3,2,1,0:T(8,128)(2,1)S(1)}, u32[]{:S(2)}, u32[]{:S(2)}) collective-permute-start(bf16[2,2,32,512]{3,2,1,0:T(8,128)(2,1)S(1)} %get-tuple-element.84.refs_4_), channel_id=1, source_target_pairs={{0,4},{1,5},{2,6},{3,7},{4,0},{5,1},{6,2},{7,3},{8,12},{9,13},{10,... | collective-permute-start | bytes 393224 | tf_op jit(solution)/shard_map/ppermute | solution.py:22
  15.2 9.3 %collective-permute-start.2 = (bf16[2,128,512]{2,1,0:T(8,128)(2,1)S(1)}, bf16[2,128,512]{2,1,0:T(8,128)(2,1)S(1)}, u32[]{:S(2)}, u32[]{:S(2)}) collective-permute-start(bf16[2,128,512]{2,1,0:T(8,128)(2,1)S(1)} %get-tuple-element.82.mine), channel_id=1, source_target_pairs={{0,2},{1,3},{2,0},{3,1},{4,6},{5,7},{6,4},{7,5},{8,10},{9,11},{10,... | collective-permute-start | bytes 786440 | tf_op jit(solution)/shard_map/ppermute | solution.py:22
  16.0 5.8 %collective-permute-start.8 = (bf16[2,2,32,512]{3,2,1,0:T(8,128)(2,1)S(1)}, bf16[2,2,32,512]{3,2,1,0:T(8,128)(2,1)S(1)}, u32[]{:S(2)}, u32[]{:S(2)}) collective-permute-start(bf16[2,2,32,512]{3,2,1,0:T(8,128)(2,1)S(1)} %shard_map.163.refs_10_), channel_id=1, source_target_pairs={{0,16},{16,0},{1,17},{17,1},{2,18},{18,2},{3,19},{19,3},{4,20},{20... | collective-permute-start | bytes 393224 | tf_op jit(solution)/shard_map/ppermute | solution.py:36
  17.5 8.2 %collective-permute-start.11 = (bf16[2,32,512]{2,1,0:T(8,128)(2,1)S(1)}, bf16[2,32,512]{2,1,0:T(8,128)(2,1)S(1)}, u32[]{:S(2)}, u32[]{:S(2)}) collective-permute-start(bf16[2,32,512]{2,1,0:T(8,128)(2,1)S(1)} %get-tuple-element.89), channel_id=1, source_target_pairs={{0,12},{1,13},{2,14},{3,15},{4,8},{5,9},{6,10},{7,11},{8,4},{9,5},... | collective-permute-start | bytes 196616 | tf_op jit(solution)/shard_map/ppermute | solution.py:22
  19.7 6.1 %collective-permute-start.10 = (bf16[2,32,512]{2,1,0:T(8,128)(2,1)S(1)}, bf16[2,32,512]{2,1,0:T(8,128)(2,1)S(1)}, u32[]{:S(2)}, u32[]{:S(2)}) collective-permute-start(bf16[2,32,512]{2,1,0:T(8,128)(2,1)S(1)} %get-tuple-element.89), channel_id=1, source_target_pairs={{0,8},{1,9},{2,10},{3,11},{4,12},{5,13},{6,14},{7,15},{8,0},{9,1},... | collective-permute-start | bytes 196616 | tf_op jit(solution)/shard_map/ppermute | solution.py:22
  24.6 5.6 %collective-permute-start.9 = (bf16[2,256,512]{2,1,0:T(8,128)(2,1)S(1)}, bf16[2,256,512]{2,1,0:T(8,128)(2,1)S(1)}, u32[]{:S(2)}, u32[]{:S(2)}) collective-permute-start(bf16[2,256,512]{2,1,0:T(8,128)(2,1)S(1)} %shard_map.164.refs_0_), channel_id=1, source_target_pairs={{0,1},{1,0},{2,3},{3,2},{4,5},{5,4},{6,7},{7,6},{8,9},{9,8},{10,11... | collective-permute-start | bytes 1572872 | tf_op jit(solution)/shard_map/ppermute | solution.py:22
  25.8 4.4 %collective-permute-start.12 = (bf16[2,2,32,512]{3,2,1,0:T(8,128)(2,1)S(1)}, bf16[2,2,32,512]{3,2,1,0:T(8,128)(2,1)S(1)}, u32[]{:S(2)}, u32[]{:S(2)}) collective-permute-start(bf16[2,2,32,512]{3,2,1,0:T(8,128)(2,1)S(1)} %shard_map.165.refs_6_), channel_id=1, source_target_pairs={{0,16},{16,0},{1,17},{17,1},{2,18},{18,2},{3,19},{19,3},{4,20},{20... | collective-permute-start | bytes 393224 | tf_op jit(solution)/shard_map/ppermute | solution.py:36
  35.2 8.1 %collective-permute-start.14 = (bf16[128,512]{1,0:T(8,128)(2,1)S(1)}, bf16[128,512]{1,0:T(8,128)(2,1)S(1)}, u32[]{:S(2)}, u32[]{:S(2)}) collective-permute-start(bf16[128,512]{1,0:T(8,128)(2,1)S(1)} %get-tuple-element.93.after), channel_id=1, source_target_pairs={{0,2},{1,3},{2,0},{3,1},{4,6},{5,7},{6,4},{7,5},{8,10},{9,11},{10,... | collective-permute-start | bytes 393224 | tf_op jit(solution)/shard_map/ppermute | solution.py:22
  37.1 10.8 %collective-permute-start.16 = (bf16[128,512]{1,0:T(8,128)(2,1)S(1)}, bf16[128,512]{1,0:T(8,128)(2,1)S(1)}, u32[]{:S(2)}, u32[]{:S(2)}) collective-permute-start(bf16[128,512]{1,0:T(8,128)(2,1)S(1)} %get-tuple-element.102), channel_id=1, source_target_pairs={{0,14},{1,15},{2,12},{3,13},{4,10},{5,11},{6,8},{7,9},{8,6},{9,7},... | collective-permute-start | bytes 393224 | tf_op jit(solution)/shard_map/ppermute | solution.py:22
  38.2 12.0 %collective-permute-start.17 = (bf16[128,512]{1,0:T(8,128)(2,1)S(1)}, bf16[128,512]{1,0:T(8,128)(2,1)S(1)}, u32[]{:S(2)}, u32[]{:S(2)}) collective-permute-start(bf16[128,512]{1,0:T(8,128)(2,1)S(1)} %get-tuple-element.103), channel_id=1, source_target_pairs={{0,10},{1,11},{2,8},{3,9},{4,14},{5,15},{6,12},{7,13},{8,2},{9,3},... | collective-permute-start | bytes 393224 | tf_op jit(solution)/shard_map/ppermute | solution.py:22
  42.0 9.0 %collective-permute-start.18 = (bf16[128,512]{1,0:T(8,128)(2,1)S(1)}, bf16[128,512]{1,0:T(8,128)(2,1)S(1)}, u32[]{:S(2)}, u32[]{:S(2)}) collective-permute-start(bf16[128,512]{1,0:T(8,128)(2,1)S(1)} %get-tuple-element.104), channel_id=1, source_target_pairs={{0,6},{1,7},{2,4},{3,5},{4,2},{5,3},{6,0},{7,1},{8,14},{9,15},{10,... | collective-permute-start | bytes 393224 | tf_op jit(solution)/shard_map/ppermute | solution.py:22
  42.0 10.3 %collective-permute-start.19 = (bf16[128,512]{1,0:T(8,128)(2,1)S(1)}, bf16[128,512]{1,0:T(8,128)(2,1)S(1)}, u32[]{:S(2)}, u32[]{:S(2)}) collective-permute-start(bf16[128,512]{1,0:T(8,128)(2,1)S(1)} %get-tuple-element.105), channel_id=1, source_target_pairs={{0,2},{1,3},{2,0},{3,1},{4,6},{5,7},{6,4},{7,5},{8,10},{9,11},{10,... | collective-permute-start | bytes 393224 | tf_op jit(solution)/shard_map/ppermute | solution.py:22
  47.8 15.9 %collective-permute-start.26 = (bf16[128,512]{1,0:T(8,128)(2,1)S(1)}, bf16[128,512]{1,0:T(8,128)(2,1)S(1)}, u32[]{:S(2)}, u32[]{:S(2)}) collective-permute-start(bf16[128,512]{1,0:T(8,128)(2,1)S(1)} %get-tuple-element.120), channel_id=1, source_target_pairs={{0,2},{1,3},{2,0},{3,1},{4,6},{5,7},{6,4},{7,5},{8,10},{9,11},{10,... | collective-permute-start | bytes 393224 | tf_op jit(solution)/shard_map/ppermute | solution.py:22
  56.6 16.2 %collective-permute-start.21 = (bf16[160,512]{1,0:T(8,128)(2,1)S(1)}, bf16[160,512]{1,0:T(8,128)(2,1)S(1)}, u32[]{:S(2)}, u32[]{:S(2)}) collective-permute-start(bf16[160,512]{1,0:T(8,128)(2,1)S(1)} %get-tuple-element.111), channel_id=1, source_target_pairs={{0,8},{1,9},{2,10},{3,11},{4,12},{5,13},{6,14},{7,15},{8,0},{9,1},... | collective-permute-start | bytes 491528 | tf_op jit(solution)/shard_map/ppermute | solution.py:22
  59.3 15.1 %collective-permute-start.22 = (bf16[160,512]{1,0:T(8,128)(2,1)S(1)}, bf16[160,512]{1,0:T(8,128)(2,1)S(1)}, u32[]{:S(2)}, u32[]{:S(2)}) collective-permute-start(bf16[160,512]{1,0:T(8,128)(2,1)S(1)} %get-tuple-element.112), channel_id=1, source_target_pairs={{0,12},{1,13},{2,14},{3,15},{4,8},{5,9},{6,10},{7,11},{8,4},{9,5},... | collective-permute-start | bytes 491528 | tf_op jit(solution)/shard_map/ppermute | solution.py:22
  60.3 14.1 %collective-permute-start.23 = (bf16[160,512]{1,0:T(8,128)(2,1)S(1)}, bf16[160,512]{1,0:T(8,128)(2,1)S(1)}, u32[]{:S(2)}, u32[]{:S(2)}) collective-permute-start(bf16[160,512]{1,0:T(8,128)(2,1)S(1)} %get-tuple-element.113), channel_id=1, source_target_pairs={{0,4},{1,5},{2,6},{3,7},{4,0},{5,1},{6,2},{7,3},{8,12},{9,13},{10,... | collective-permute-start | bytes 491528 | tf_op jit(solution)/shard_map/ppermute | solution.py:22
  60.6 6.8 %collective-permute-start.24 = (bf16[96,512]{1,0:T(8,128)(2,1)S(1)}, bf16[96,512]{1,0:T(8,128)(2,1)S(1)}, u32[]{:S(2)}, u32[]{:S(2)}) collective-permute-start(bf16[96,512]{1,0:T(8,128)(2,1)S(1)} %get-tuple-element.116), channel_id=1, source_target_pairs={{0,1},{1,0},{2,3},{3,2},{4,5},{5,4},{6,7},{7,6},{8,9},{9,8},{10,11... | collective-permute-start | bytes 294920 | tf_op jit(solution)/shard_map/ppermute | solution.py:22
  63.7 6.2 %collective-permute-start.25 = (bf16[96,512]{1,0:T(8,128)(2,1)S(1)}, bf16[96,512]{1,0:T(8,128)(2,1)S(1)}, u32[]{:S(2)}, u32[]{:S(2)}) collective-permute-start(bf16[96,512]{1,0:T(8,128)(2,1)S(1)} %get-tuple-element.117), channel_id=1, source_target_pairs={{1,2},{3,4},{5,6},{7,8},{9,10},{11,12},{13,14},{2,1},{4,3},{6,5},{... | collective-permute-start | bytes 294920 | tf_op jit(solution)/shard_map/ppermute | solution.py:28
  74.6 7.1 %collective-permute-start.27 = (f32[156,512]{1,0:T(8,128)S(1)}, f32[156,512]{1,0:T(8,128)S(1)}, u32[]{:S(2)}, u32[]{:S(2)}) collective-permute-start(f32[156,512]{1,0:T(8,128)S(1)} %get-tuple-element.132), channel_id=1, source_target_pairs={{0,1},{1,0},{2,3},{3,2},{4,5},{5,4},{6,7},{7,6},{8,9},{9,8},{10,11... | collective-permute-start | bytes 958472 | tf_op jit(solution)/shard_map/ppermute | solution.py:22
  (4 other events, 13.6 us)

commit v6 on v5

--- a/solution.py
+++ b/solution.py
@@ -113,10 +113,16 @@
 
 
 def acts_body(mine, got, *refs):
-    acts = refs[-1]
-    pixels = mine.shape[1]
-    acts[:, :pixels] = mine[...]
-    acts[:, pixels:] = got[...]
+    acts, full = refs[-2:]
+    pixels = acts.shape[1] // 2
+    for which in range(2):
+        rows = slice(which * pixels, (which + 1) * pixels)
+        acts[which, :pixels] = mine[rows, :]
+        acts[which, pixels:] = got[rows, :]
+        own = full.shape[2]
+        for core in range(2):
+            start = 2 * pixels + (2 * which + core) * own
+            full[which, core] = got[start : start + own, :]
 
 
 def stack_body(*refs):
@@ -154,7 +160,7 @@
 
 
 def conv_body(
-    feats, core_got, outer, kernel, gain, bias, branch, normed, inv, acts, padded, result
+    feats, core_got, outer, kernel, gain, bias, branch, full, normed, inv, acts, padded, result
 ):
     rows, cols, channels = feats.shape
     start = core_got.shape[0] - RIM * cols
@@ -174,8 +180,14 @@
     value = centred * spread
     normed[...] = value
     inv[...] = jnp.broadcast_to(spread, inv.shape)
-    acts[0] = (value * gain[...] + bias[...]).astype(NARROW)
-    acts[1] = branch[...]
+    pixels = rows * cols
+    acts[:pixels, :] = (value * gain[...] + bias[...]).astype(NARROW)
+    acts[pixels : 2 * pixels, :] = branch[...]
+    own = full.shape[2]
+    for which in range(2):
+        for core in range(2):
+            start = 2 * pixels + (2 * which + core) * own
+            acts[start : start + own, :] = full[which, core]
 
 
 def hidden_body(copied, *refs):
@@ -458,14 +470,14 @@
         here = [swap(sent, 4 * p + 2 * side) for p in range(2, patterns)]
         here = run(stack_body, (shaped((patterns - 2,) + piece, NARROW),), *here, order=8)[0]
         near = swap(full, 4 + 2 * side)
-        pieces += [swap(full, 2) if side else full, near, here, swap_group(here)]
-
-    normed, inv, acts = run(
+        pieces += [full, near, here, swap_group(here)]
+
+    normed, inv, sent = run(
         conv_body,
         (
             shaped((pixels, channels)),
             shaped((pixels, LANES)),
-            shaped((2, pixels, channels), NARROW),
+            shaped((2 * pixels + 4 * own_rows, channels), NARROW),
         ),
         feats,
         core_got,
@@ -474,16 +486,17 @@
         gain,
         bias,
         branch,
+        joined[2],
         scratch=(padded, pltpu.VMEM((pixels, channels), WIDE)),
     )
-    first_blocks = [pieces[k] for k in (1, 4, 5, 7)]
-    acts = run(
+    first_blocks = [pieces[k] for k in (1, 3, 5, 7)]
+    acts, pieces[4] = run(
         acts_body,
-        (shaped((2, 2 * pixels, channels), NARROW),),
-        acts,
-        swap(acts, 2),
+        (shaped((2, 2 * pixels, channels), NARROW), full_shape),
+        sent,
+        swap(sent, 2),
         *first_blocks,
-    )[0]
+    )
     acts_got = swap(acts, 1)
 
     if not copied:
@@ -557,8 +570,8 @@
     inner_got = swap(inner_out, 1)
     sums = stay + swap(leave, 1)
 
-    far_turns = (*range(2 * patterns - 1, 4, -2), 3, 1)
-    near_turns = (*range(4, 2 * patterns, 2), 2, 0)
+    far_turns = (*range(2 * patterns - 1, 4, -2), 3)
+    near_turns = (*range(4, 2 * patterns, 2), 2, 1, 0)
     owned = 4 * own_rows
     if copied:
         parts = run(
@@ -575,20 +588,22 @@
     far_parts = [swap(part, 2 * p) for p, part in zip(far_turns, parts)]
     sums, far_parts = lax.optimization_barrier((sums, far_parts))
     sums = sums + swap(sums, 2)
+    sums, mixed_leave = lax.optimization_barrier((sums, mixed_leave))
     if copied:
         joint = shaped((owned + 32, quarter), NARROW)
-        *parts, near_own = run(
+        *parts, side_part, near_own = run(
             functools.partial(owners_body, near_turns),
-            (joint,) * (len(near_turns) - 1) + (shaped((owned, quarter)),),
+            (joint,) * (len(near_turns) - 2)
+            + (shaped((owned, quarter), NARROW), shaped((owned, quarter))),
             holder,
             sums,
         )
         parts = [swap(part, 2 * p) for p, part in zip(near_turns, parts)]
         sums_parts = [part[owned : owned + SMALL_ROWS] for part in parts]
-        near_parts = [part[:owned] for part in parts] + [near_own]
+        near_parts = [part[:owned] for part in parts] + [swap(side_part, 2), near_own]
     else:
         near_parts = [swap(flat[p].astype(NARROW), 2 * p) for p in near_turns[:-1]] + [flat[0]]
-        sums_parts = [swap(sums.astype(NARROW), 2 * p) for p in near_turns[:-1]]
+        sums_parts = [swap(sums.astype(NARROW), 2 * p) for p in near_turns[:-2]]
 
     input_grad = run(
         input_grad_body,

time: 82.7 us -> 74.8 us (0.904)
  the two profiles are of different devices: /device:TPU:17 before, /device:TPU:1 now
where the time goes in v6:
time: 74.8 us; the launch traced here: 74.3 us
  starting transfers between devices  39 us (52%)
  waiting for transfers between devices  21.3 us (28%)
  Pallas kernels  13.1 us (18%)
  between operations  0.85 us (1%)
    ppermute x23, starting transfers between devices, swap(): return lax.ppermute(value, 'row', [(i, i ^ bit) for i in range(count)])  28.6 us
    ppermute x23, waiting for transfers between devices, swap(): return lax.ppermute(value, 'row', [(i, i ^ bit) for i in range(count)])  17.8 us
    pallas_call x16, Pallas kernels, run(): pl.pallas_call(body, out_shape=outs, **extra, scratch_shapes=scratch, com...  13.1 us
    ppermute x2, starting transfers between devices, swap_rim(): return lax.ppermute(value, 'row', pairs + [(j, i) for i, j in pairs])  7.81 us
    ppermute x2, waiting for transfers between devices, swap_group(): return lax.ppermute(value, 'grp', [(0, 1), (1, 0)])  3.56 us
    ppermute x2, starting transfers between devices, swap_group(): return lax.ppermute(value, 'grp', [(0, 1), (1, 0)])  2.61 us
  transfers between devices with their start and end apart: 27, of which 14 were waited for; matrix products, arithmetic and copies ran while one was open for 0% of the time, Pallas kernels for 12%

profile of v6, /device:TPU:1, one launch (start us, length us, event | category | flops | bytes accessed | tf_op | source)
XLA Modules:
  0.0 74.3 jit_solution(6562855454618000747)
XLA Ops:
  0.6 1.3 %shard_map.160 = (bf16[2,2,32,512]{3,2,1,0:T(8,128)(2,1)S(1)}, bf16[224,512]{1,0:T(8,128)(2,1)S(1)}, bf16[96,512]{1,0:T(8,128)(2,1)S(1)}, bf16[128,512]{1,0:T(8,...) custom-call(f32[32,2048]{1,0:T(8,128)} %refs_0_.1, ...), custom_call_target="tpu_custom_call" | custom-call | tf_op jit(solution)/shard_map/pallas_call | solution.py:44
  2.1 4.5 %collective-permute-start.1 = (bf16[96,512]{1,0:T(8,128)(2,1)S(1)}, bf16[96,512]{1,0:T(8,128)(2,1)S(1)}, u32[]{:S(2)}, u32[]{:S(2)}) collective-permute-start(bf16[96,512]{1,0:T(8,128)(2,1)S(1)} %get-tuple-element.80), channel_id=1, source_target_pairs={{1,2},{3,4},{5,6},{7,8},{9,10},{11,12},{13,14},{2,1},{4,3},{6,5},{... | collective-permute-start | bytes 294920 | tf_op jit(solution)/shard_map/ppermute | solution.py:28
  6.6 2.4 %collective-permute-start.9 = (bf16[2,32,512]{2,1,0:T(8,128)(2,1)S(1)}, bf16[2,32,512]{2,1,0:T(8,128)(2,1)S(1)}, u32[]{:S(2)}, u32[]{:S(2)}) collective-permute-start(bf16[2,32,512]{2,1,0:T(8,128)(2,1)S(1)} %get-tuple-element.90), channel_id=1, source_target_pairs={{0,14},{1,15},{2,12},{3,13},{4,10},{5,11},{6,8},{7,9},{8,6},{9,7},... | collective-permute-start | bytes 196616 | tf_op jit(solution)/shard_map/ppermute | solution.py:22
  10.1 2.2 %collective-permute-start.5 = (bf16[2,32,512]{2,1,0:T(8,128)(2,1)S(1)}, bf16[2,32,512]{2,1,0:T(8,128)(2,1)S(1)}, u32[]{:S(2)}, u32[]{:S(2)}) collective-permute-start(bf16[2,32,512]{2,1,0:T(8,128)(2,1)S(1)} %get-tuple-element.89), channel_id=1, source_target_pairs={{0,12},{1,13},{2,14},{3,15},{4,8},{5,9},{6,10},{7,11},{8,4},{9,5},... | collective-permute-start | bytes 196616 | tf_op jit(solution)/shard_map/ppermute | solution.py:22
  13.3 1.3 %collective-permute-start.7 = (bf16[2,2,32,512]{3,2,1,0:T(8,128)(2,1)S(1)}, bf16[2,2,32,512]{3,2,1,0:T(8,128)(2,1)S(1)}, u32[]{:S(2)}, u32[]{:S(2)}) collective-permute-start(bf16[2,2,32,512]{3,2,1,0:T(8,128)(2,1)S(1)} %get-tuple-element.86.full), channel_id=1, source_target_pairs={{0,6},{1,7},{2,4},{3,5},{4,2},{5,3},{6,0},{7,1},{8,14},{9,15},{10,... | collective-permute-start | bytes 393224 | tf_op jit(solution)/shard_map/ppermute | solution.py:22
  14.6 2.4 %shard_map.162 = (f32[128,512]{1,0:T(8,128)S(1)}, f32[128,128]{1,0:T(8,128)S(1)}, bf16[384,512]{1,0:T(8,128)(2,1)S(1)}) custom-call(f32[4,32,512]{2,1,0:T(8,128)S(1)} %get-tuple-element.78.feats.refs_5_, bf16[224,512]{1,0:T(8,128)(2,1)S(1)} %collective-permute-done.other.core_got.refs_6_, bf16[96,512]{1,0:T(8,128)(2,1)S(1)} %collective-permute-done.1.outer.refs_7_, ...), custom_call_target="tpu_custom_call" | custom-call | tf_op jit(solution)/shard_map/pallas_call | solution.py:44
  18.4 2.4 %collective-permute-start.2 = (bf16[384,512]{1,0:T(8,128)(2,1)S(1)}, bf16[384,512]{1,0:T(8,128)(2,1)S(1)}, u32[]{:S(2)}, u32[]{:S(2)}) collective-permute-start(bf16[384,512]{1,0:T(8,128)(2,1)S(1)} %get-tuple-element.87.mine), channel_id=1, source_target_pairs={{0,2},{1,3},{2,0},{3,1},{4,6},{5,7},{6,4},{7,5},{8,10},{9,11},{10,... | collective-permute-start | bytes 1179656 | tf_op jit(solution)/shard_map/ppermute | solution.py:22
  25.1 2.9 %collective-permute-done.6.refs_1_.refs_7_ = bf16[2,2,32,512]{3,2,1,0:T(8,128)(2,1)S(1)} collective-permute-done((bf16[2,2,32,512]{3,2,1,0:T(8,128)(2,1)S(1)}, bf16[2,2,32,512]{3,2,1,0:T(8,128)(2,1)S(1)}, u32[]{:S(2)}, u32[]{:S(2)}) %collective-permute-start.6) | collective-permute-done | bytes 131104 | tf_op jit(solution)/shard_map/ppermute | solution.py:36
  28.0 1.6 %collective-permute-done.2.got = bf16[384,512]{1,0:T(8,128)(2,1)S(1)} collective-permute-done((bf16[384,512]{1,0:T(8,128)(2,1)S(1)}, bf16[384,512]{1,0:T(8,128)(2,1)S(1)}, u32[]{:S(2)}, u32[]{:S(2)}) %collective-permute-start.2) | collective-permute-done | bytes 393248 | tf_op jit(solution)/shard_map/ppermute | solution.py:22
  29.6 1.9 %collective-permute-start.11 = (bf16[2,256,512]{2,1,0:T(8,128)(2,1)S(1)}, bf16[2,256,512]{2,1,0:T(8,128)(2,1)S(1)}, u32[]{:S(2)}, u32[]{:S(2)}) collective-permute-start(bf16[2,256,512]{2,1,0:T(8,128)(2,1)S(1)} %get-tuple-element.91.refs_0_), channel_id=1, source_target_pairs={{0,1},{1,0},{2,3},{3,2},{4,5},{5,4},{6,7},{7,6},{8,9},{9,8},{10,11... | collective-permute-start | bytes 1572872 | tf_op jit(solution)/shard_map/ppermute | solution.py:22
  31.5 1.5 %collective-permute-done.11.refs_1_ = bf16[2,256,512]{2,1,0:T(8,128)(2,1)S(1)} collective-permute-done((bf16[2,256,512]{2,1,0:T(8,128)(2,1)S(1)}, bf16[2,256,512]{2,1,0:T(8,128)(2,1)S(1)}, u32[]{:S(2)}, u32[]{:S(2)}) %collective-permute-start.11) | collective-permute-done | bytes 524320 | tf_op jit(solution)/shard_map/ppermute | solution.py:22
  33.0 1.7 %shard_map.166 = (f32[2,256,512]{2,1,0:T(8,128)S(1)}, bf16[2,256,512]{2,1,0:T(8,128)(2,1)S(1)}, bf16[512,512]{1,0:T(8,128)(2,1)S(1)}, bf16[512,512]{1,0:T(8,128)...) custom-call(bf16[2,256,512]{2,1,0:T(8,128)(2,1)S(1)} %get-tuple-element.91.refs_0_, ...), custom_call_target="tpu_custom_call" | custom-call | tf_op jit(solution)/shard_map/pallas_call | solution.py:44
  35.2 1.5 %collective-permute-done.12.got = bf16[2,256,512]{2,1,0:T(8,128)(2,1)S(1)} collective-permute-done((bf16[2,256,512]{2,1,0:T(8,128)(2,1)S(1)}, bf16[2,256,512]{2,1,0:T(8,128)(2,1)S(1)}, u32[]{:S(2)}, u32[]{:S(2)}) %collective-permute-start.12) | collective-permute-done | bytes 524320 | tf_op jit(solution)/shard_map/ppermute | solution.py:22
  38.9 3.1 %collective-permute-start.15 = (bf16[128,512]{1,0:T(8,128)(2,1)S(1)}, bf16[128,512]{1,0:T(8,128)(2,1)S(1)}, u32[]{:S(2)}, u32[]{:S(2)}) collective-permute-start(bf16[128,512]{1,0:T(8,128)(2,1)S(1)} %get-tuple-element.107), channel_id=1, source_target_pairs={{0,14},{1,15},{2,12},{3,13},{4,10},{5,11},{6,8},{7,9},{8,6},{9,7},... | collective-permute-start | bytes 393224 | tf_op jit(solution)/shard_map/ppermute | solution.py:22
  42.0 1.4 %collective-permute-start.17 = (bf16[128,512]{1,0:T(8,128)(2,1)S(1)}, bf16[128,512]{1,0:T(8,128)(2,1)S(1)}, u32[]{:S(2)}, u32[]{:S(2)}) collective-permute-start(bf16[128,512]{1,0:T(8,128)(2,1)S(1)} %get-tuple-element.109), channel_id=1, source_target_pairs={{0,6},{1,7},{2,4},{3,5},{4,2},{5,3},{6,0},{7,1},{8,14},{9,15},{10,... | collective-permute-start | bytes 393224 | tf_op jit(solution)/shard_map/ppermute | solution.py:22
  43.4 1.9 %shard_map.168 = (f32[128,512]{1,0:T(8,128)S(1)}, bf16[96,512]{1,0:T(8,128)(2,1)S(1)}, bf16[96,512]{1,0:T(8,128)(2,1)S(1)}, f32[28,512]{1,0:T(8,128)S(1)}, f32[28,512]{1,0:T(8,128)S(1)}) custom-call(f32[128,512]{1,0:T(8,128)S(1)} %get-tuple-element.97.refs_0_, bf16[128,512]{1,0:T(8,128)(2,1)S(1)} %collective-permute-done.13.refs_1_, ...), custom_call_target="tpu_custom_call" | custom-call | tf_op jit(solution)/shard_map/pallas_call | solution.py:44
  45.3 1.6 %collective-permute-start.14 = (f32[28,512]{1,0:T(8,128)S(1)}, f32[28,512]{1,0:T(8,128)S(1)}, u32[]{:S(2)}, u32[]{:S(2)}) collective-permute-start(f32[28,512]{1,0:T(8,128)S(1)} %get-tuple-element.104), channel_id=1, source_target_pairs={{0,1},{1,0},{2,3},{3,2},{4,5},{5,4},{6,7},{7,6},{8,9},{9,8},{10,11... | collective-permute-start | bytes 172040 | tf_op jit(solution)/shard_map/ppermute | solution.py:22
  47.8 3.3 %collective-permute-start.24 = (bf16[96,512]{1,0:T(8,128)(2,1)S(1)}, bf16[96,512]{1,0:T(8,128)(2,1)S(1)}, u32[]{:S(2)}, u32[]{:S(2)}) collective-permute-start(bf16[96,512]{1,0:T(8,128)(2,1)S(1)} %get-tuple-element.123), channel_id=1, source_target_pairs={{1,2},{3,4},{5,6},{7,8},{9,10},{11,12},{13,14},{2,1},{4,3},{6,5},{... | collective-permute-start | bytes 294920 | tf_op jit(solution)/shard_map/ppermute | solution.py:28
  51.2 1.5 %collective-permute-done.16.refs_1_ = bf16[128,512]{1,0:T(8,128)(2,1)S(1)} collective-permute-done((bf16[128,512]{1,0:T(8,128)(2,1)S(1)}, bf16[128,512]{1,0:T(8,128)(2,1)S(1)}, u32[]{:S(2)}, u32[]{:S(2)}) %collective-permute-start.16) | collective-permute-done | bytes 131104 | tf_op jit(solution)/shard_map/ppermute | solution.py:22
  53.2 2.6 %collective-permute-done.18 = f32[28,512]{1,0:T(8,128)S(1)} collective-permute-done((f32[28,512]{1,0:T(8,128)S(1)}, f32[28,512]{1,0:T(8,128)S(1)}, u32[]{:S(2)}, u32[]{:S(2)}) %collective-permute-start.18) | collective-permute-done | bytes 57376 | tf_op jit(solution)/shard_map/ppermute | solution.py:22
  56.8 2.3 %collective-permute-start.20 = (bf16[160,512]{1,0:T(8,128)(2,1)S(1)}, bf16[160,512]{1,0:T(8,128)(2,1)S(1)}, u32[]{:S(2)}, u32[]{:S(2)}) collective-permute-start(bf16[160,512]{1,0:T(8,128)(2,1)S(1)} %get-tuple-element.117), channel_id=1, source_target_pairs={{0,12},{1,13},{2,14},{3,15},{4,8},{5,9},{6,10},{7,11},{8,4},{9,5},... | collective-permute-start | bytes 491528 | tf_op jit(solution)/shard_map/ppermute | solution.py:22
  60.8 2.9 %shard_map.172 = f32[4,32,512]{2,1,0:T(8,128)} custom-call(f32[128,512]{1,0:T(8,128)S(1)} %get-tuple-element.121.grad, bf16[96,512]{1,0:T(8,128)(2,1)S(1)} %collective-permute-done.23.inner, bf16[96,512]{1,0:T(8,128)(2,1)S(1)} %collective-permute-done.24.outer, f32[7,7,512]{2,1,0:T(8,128)S(1)} %get-tuple-element.81.kernel, ...), custom_call_target="tpu_custom_call" | custom-call | tf_op jit(solution)/shard_map/pallas_call | solution.py:44
  64.4 4.9 %collective-permute-done.19 = bf16[160,512]{1,0:T(8,128)(2,1)S(1)} collective-permute-done((bf16[160,512]{1,0:T(8,128)(2,1)S(1)}, bf16[160,512]{1,0:T(8,128)(2,1)S(1)}, u32[]{:S(2)}, u32[]{:S(2)}) %collective-permute-start.19) | collective-permute-done | bytes 163872 | tf_op jit(solution)/shard_map/ppermute | solution.py:22
  69.7 2.5 %collective-permute-start.26 = (f32[156,512]{1,0:T(8,128)S(1)}, f32[156,512]{1,0:T(8,128)S(1)}, u32[]{:S(2)}, u32[]{:S(2)}) collective-permute-start(f32[156,512]{1,0:T(8,128)S(1)} %get-tuple-element.138), channel_id=1, source_target_pairs={{0,1},{1,0},{2,3},{3,2},{4,5},{5,4},{6,7},{7,6},{8,9},{9,8},{10,11... | collective-permute-start | bytes 958472 | tf_op jit(solution)/shard_map/ppermute | solution.py:22
  (54 shorter events, 17.8 us)
Async XLA Ops:
  2.0 4.6 %collective-permute-start = (bf16[224,512]{1,0:T(8,128)(2,1)S(1)}, bf16[224,512]{1,0:T(8,128)(2,1)S(1)}, u32[]{:S(2)}, u32[]{:S(2)}) collective-permute-start(bf16[224,512]{1,0:T(8,128)(2,1)S(1)} %get-tuple-element.79), channel_id=1, source_target_pairs={{0,1},{1,0},{2,3},{3,2},{4,5},{5,4},{6,7},{7,6},{8,9},{9,8},{10,11... | collective-permute-start | bytes 688136 | tf_op jit(solution)/shard_map/ppermute | solution.py:22
  2.1 11.2 %collective-permute-start.1 = (bf16[96,512]{1,0:T(8,128)(2,1)S(1)}, bf16[96,512]{1,0:T(8,128)(2,1)S(1)}, u32[]{:S(2)}, u32[]{:S(2)}) collective-permute-start(bf16[96,512]{1,0:T(8,128)(2,1)S(1)} %get-tuple-element.80), channel_id=1, source_target_pairs={{1,2},{3,4},{5,6},{7,8},{9,10},{11,12},{13,14},{2,1},{4,3},{6,5},{... | collective-permute-start | bytes 294920 | tf_op jit(solution)/shard_map/ppermute | solution.py:28
  6.6 10.4 %collective-permute-start.9 = (bf16[2,32,512]{2,1,0:T(8,128)(2,1)S(1)}, bf16[2,32,512]{2,1,0:T(8,128)(2,1)S(1)}, u32[]{:S(2)}, u32[]{:S(2)}) collective-permute-start(bf16[2,32,512]{2,1,0:T(8,128)(2,1)S(1)} %get-tuple-element.90), channel_id=1, source_target_pairs={{0,14},{1,15},{2,12},{3,13},{4,10},{5,11},{6,8},{7,9},{8,6},{9,7},... | collective-permute-start | bytes 196616 | tf_op jit(solution)/shard_map/ppermute | solution.py:22
  9.0 9.4 %collective-permute-start.8 = (bf16[2,32,512]{2,1,0:T(8,128)(2,1)S(1)}, bf16[2,32,512]{2,1,0:T(8,128)(2,1)S(1)}, u32[]{:S(2)}, u32[]{:S(2)}) collective-permute-start(bf16[2,32,512]{2,1,0:T(8,128)(2,1)S(1)} %get-tuple-element.90), channel_id=1, source_target_pairs={{0,10},{1,11},{2,8},{3,9},{4,14},{5,15},{6,12},{7,13},{8,2},{9,3},... | collective-permute-start | bytes 196616 | tf_op jit(solution)/shard_map/ppermute | solution.py:22
  10.1 10.8 %collective-permute-start.5 = (bf16[2,32,512]{2,1,0:T(8,128)(2,1)S(1)}, bf16[2,32,512]{2,1,0:T(8,128)(2,1)S(1)}, u32[]{:S(2)}, u32[]{:S(2)}) collective-permute-start(bf16[2,32,512]{2,1,0:T(8,128)(2,1)S(1)} %get-tuple-element.89), channel_id=1, source_target_pairs={{0,12},{1,13},{2,14},{3,15},{4,8},{5,9},{6,10},{7,11},{8,4},{9,5},... | collective-permute-start | bytes 196616 | tf_op jit(solution)/shard_map/ppermute | solution.py:22
  12.3 10.3 %collective-permute-start.4 = (bf16[2,32,512]{2,1,0:T(8,128)(2,1)S(1)}, bf16[2,32,512]{2,1,0:T(8,128)(2,1)S(1)}, u32[]{:S(2)}, u32[]{:S(2)}) collective-permute-start(bf16[2,32,512]{2,1,0:T(8,128)(2,1)S(1)} %get-tuple-element.89), channel_id=1, source_target_pairs={{0,8},{1,9},{2,10},{3,11},{4,12},{5,13},{6,14},{7,15},{8,0},{9,1},... | collective-permute-start | bytes 196616 | tf_op jit(solution)/shard_map/ppermute | solution.py:22
  13.3 10.6 %collective-permute-start.7 = (bf16[2,2,32,512]{3,2,1,0:T(8,128)(2,1)S(1)}, bf16[2,2,32,512]{3,2,1,0:T(8,128)(2,1)S(1)}, u32[]{:S(2)}, u32[]{:S(2)}) collective-permute-start(bf16[2,2,32,512]{3,2,1,0:T(8,128)(2,1)S(1)} %get-tuple-element.86.full), channel_id=1, source_target_pairs={{0,6},{1,7},{2,4},{3,5},{4,2},{5,3},{6,0},{7,1},{8,14},{9,15},{10,... | collective-permute-start | bytes 393224 | tf_op jit(solution)/shard_map/ppermute | solution.py:22
  17.1 7.3 %collective-permute-start.3 = (bf16[2,2,32,512]{3,2,1,0:T(8,128)(2,1)S(1)}, bf16[2,2,32,512]{3,2,1,0:T(8,128)(2,1)S(1)}, u32[]{:S(2)}, u32[]{:S(2)}) collective-permute-start(bf16[2,2,32,512]{3,2,1,0:T(8,128)(2,1)S(1)} %get-tuple-element.88.refs_4_), channel_id=1, source_target_pairs={{0,4},{1,5},{2,6},{3,7},{4,0},{5,1},{6,2},{7,3},{8,12},{9,13},{10,... | collective-permute-start | bytes 393224 | tf_op jit(solution)/shard_map/ppermute | solution.py:22
  18.4 11.1 %collective-permute-start.2 = (bf16[384,512]{1,0:T(8,128)(2,1)S(1)}, bf16[384,512]{1,0:T(8,128)(2,1)S(1)}, u32[]{:S(2)}, u32[]{:S(2)}) collective-permute-start(bf16[384,512]{1,0:T(8,128)(2,1)S(1)} %get-tuple-element.87.mine), channel_id=1, source_target_pairs={{0,2},{1,3},{2,0},{3,1},{4,6},{5,7},{6,4},{7,5},{8,10},{9,11},{10,... | collective-permute-start | bytes 1179656 | tf_op jit(solution)/shard_map/ppermute | solution.py:22
  20.9 4.2 %collective-permute-start.10 = (bf16[2,2,32,512]{3,2,1,0:T(8,128)(2,1)S(1)}, bf16[2,2,32,512]{3,2,1,0:T(8,128)(2,1)S(1)}, u32[]{:S(2)}, u32[]{:S(2)}) collective-permute-start(bf16[2,2,32,512]{3,2,1,0:T(8,128)(2,1)S(1)} %shard_map.164.refs_10_), channel_id=1, source_target_pairs={{0,16},{16,0},{1,17},{17,1},{2,18},{18,2},{3,19},{19,3},{4,20},{20... | collective-permute-start | bytes 393224 | tf_op jit(solution)/shard_map/ppermute | solution.py:36
  22.6 5.4 %collective-permute-start.6 = (bf16[2,2,32,512]{3,2,1,0:T(8,128)(2,1)S(1)}, bf16[2,2,32,512]{3,2,1,0:T(8,128)(2,1)S(1)}, u32[]{:S(2)}, u32[]{:S(2)}) collective-permute-start(bf16[2,2,32,512]{3,2,1,0:T(8,128)(2,1)S(1)} %shard_map.163.refs_6_), channel_id=1, source_target_pairs={{0,16},{16,0},{1,17},{17,1},{2,18},{18,2},{3,19},{19,3},{4,20},{20... | collective-permute-start | bytes 393224 | tf_op jit(solution)/shard_map/ppermute | solution.py:36
  29.6 3.4 %collective-permute-start.11 = (bf16[2,256,512]{2,1,0:T(8,128)(2,1)S(1)}, bf16[2,256,512]{2,1,0:T(8,128)(2,1)S(1)}, u32[]{:S(2)}, u32[]{:S(2)}) collective-permute-start(bf16[2,256,512]{2,1,0:T(8,128)(2,1)S(1)} %get-tuple-element.91.refs_0_), channel_id=1, source_target_pairs={{0,1},{1,0},{2,3},{3,2},{4,5},{5,4},{6,7},{7,6},{8,9},{9,8},{10,11... | collective-permute-start | bytes 1572872 | tf_op jit(solution)/shard_map/ppermute | solution.py:22
  36.8 6.6 %collective-permute-start.13 = (bf16[128,512]{1,0:T(8,128)(2,1)S(1)}, bf16[128,512]{1,0:T(8,128)(2,1)S(1)}, u32[]{:S(2)}, u32[]{:S(2)}) collective-permute-start(bf16[128,512]{1,0:T(8,128)(2,1)S(1)} %get-tuple-element.98.after), channel_id=1, source_target_pairs={{0,2},{1,3},{2,0},{3,1},{4,6},{5,7},{6,4},{7,5},{8,10},{9,11},{10,... | collective-permute-start | bytes 393224 | tf_op jit(solution)/shard_map/ppermute | solution.py:22
  38.9 12.3 %collective-permute-start.15 = (bf16[128,512]{1,0:T(8,128)(2,1)S(1)}, bf16[128,512]{1,0:T(8,128)(2,1)S(1)}, u32[]{:S(2)}, u32[]{:S(2)}) collective-permute-start(bf16[128,512]{1,0:T(8,128)(2,1)S(1)} %get-tuple-element.107), channel_id=1, source_target_pairs={{0,14},{1,15},{2,12},{3,13},{4,10},{5,11},{6,8},{7,9},{8,6},{9,7},... | collective-permute-start | bytes 393224 | tf_op jit(solution)/shard_map/ppermute | solution.py:22
  42.0 10.7 %collective-permute-start.16 = (bf16[128,512]{1,0:T(8,128)(2,1)S(1)}, bf16[128,512]{1,0:T(8,128)(2,1)S(1)}, u32[]{:S(2)}, u32[]{:S(2)}) collective-permute-start(bf16[128,512]{1,0:T(8,128)(2,1)S(1)} %get-tuple-element.108), channel_id=1, source_target_pairs={{0,10},{1,11},{2,8},{3,9},{4,14},{5,15},{6,12},{7,13},{8,2},{9,3},... | collective-permute-start | bytes 393224 | tf_op jit(solution)/shard_map/ppermute | solution.py:22
  42.0 10.7 %collective-permute-start.17 = (bf16[128,512]{1,0:T(8,128)(2,1)S(1)}, bf16[128,512]{1,0:T(8,128)(2,1)S(1)}, u32[]{:S(2)}, u32[]{:S(2)}) collective-permute-start(bf16[128,512]{1,0:T(8,128)(2,1)S(1)} %get-tuple-element.109), channel_id=1, source_target_pairs={{0,6},{1,7},{2,4},{3,5},{4,2},{5,3},{6,0},{7,1},{8,14},{9,15},{10,... | collective-permute-start | bytes 393224 | tf_op jit(solution)/shard_map/ppermute | solution.py:22
  46.9 12.4 %collective-permute-start.23 = (bf16[96,512]{1,0:T(8,128)(2,1)S(1)}, bf16[96,512]{1,0:T(8,128)(2,1)S(1)}, u32[]{:S(2)}, u32[]{:S(2)}) collective-permute-start(bf16[96,512]{1,0:T(8,128)(2,1)S(1)} %get-tuple-element.122), channel_id=1, source_target_pairs={{0,1},{1,0},{2,3},{3,2},{4,5},{5,4},{6,7},{7,6},{8,9},{9,8},{10,11... | collective-permute-start | bytes 294920 | tf_op jit(solution)/shard_map/ppermute | solution.py:22
  47.8 11.8 %collective-permute-start.24 = (bf16[96,512]{1,0:T(8,128)(2,1)S(1)}, bf16[96,512]{1,0:T(8,128)(2,1)S(1)}, u32[]{:S(2)}, u32[]{:S(2)}) collective-permute-start(bf16[96,512]{1,0:T(8,128)(2,1)S(1)} %get-tuple-element.123), channel_id=1, source_target_pairs={{1,2},{3,4},{5,6},{7,8},{9,10},{11,12},{13,14},{2,1},{4,3},{6,5},{... | collective-permute-start | bytes 294920 | tf_op jit(solution)/shard_map/ppermute | solution.py:28
  55.9 13.4 %collective-permute-start.19 = (bf16[160,512]{1,0:T(8,128)(2,1)S(1)}, bf16[160,512]{1,0:T(8,128)(2,1)S(1)}, u32[]{:S(2)}, u32[]{:S(2)}) collective-permute-start(bf16[160,512]{1,0:T(8,128)(2,1)S(1)} %get-tuple-element.116), channel_id=1, source_target_pairs={{0,8},{1,9},{2,10},{3,11},{4,12},{5,13},{6,14},{7,15},{8,0},{9,1},... | collective-permute-start | bytes 491528 | tf_op jit(solution)/shard_map/ppermute | solution.py:22
  56.8 12.5 %collective-permute-start.20 = (bf16[160,512]{1,0:T(8,128)(2,1)S(1)}, bf16[160,512]{1,0:T(8,128)(2,1)S(1)}, u32[]{:S(2)}, u32[]{:S(2)}) collective-permute-start(bf16[160,512]{1,0:T(8,128)(2,1)S(1)} %get-tuple-element.117), channel_id=1, source_target_pairs={{0,12},{1,13},{2,14},{3,15},{4,8},{5,9},{6,10},{7,11},{8,4},{9,5},... | collective-permute-start | bytes 491528 | tf_op jit(solution)/shard_map/ppermute | solution.py:22
  59.1 10.4 %collective-permute-start.21 = (bf16[160,512]{1,0:T(8,128)(2,1)S(1)}, bf16[160,512]{1,0:T(8,128)(2,1)S(1)}, u32[]{:S(2)}, u32[]{:S(2)}) collective-permute-start(bf16[160,512]{1,0:T(8,128)(2,1)S(1)} %get-tuple-element.118), channel_id=1, source_target_pairs={{0,4},{1,5},{2,6},{3,7},{4,0},{5,1},{6,2},{7,3},{8,12},{9,13},{10,... | collective-permute-start | bytes 491528 | tf_op jit(solution)/shard_map/ppermute | solution.py:22
  59.3 4.3 %collective-permute-start.25 = (bf16[128,512]{1,0:T(8,128)(2,1)S(1)}, bf16[128,512]{1,0:T(8,128)(2,1)S(1)}, u32[]{:S(2)}, u32[]{:S(2)}) collective-permute-start(bf16[128,512]{1,0:T(8,128)(2,1)S(1)} %get-tuple-element.126), channel_id=1, source_target_pairs={{0,2},{1,3},{2,0},{3,1},{4,6},{5,7},{6,4},{7,5},{8,10},{9,11},{10,... | collective-permute-start | bytes 393224 | tf_op jit(solution)/shard_map/ppermute | solution.py:22
  59.6 9.9 %collective-permute-start.22 = (bf16[128,512]{1,0:T(8,128)(2,1)S(1)}, bf16[128,512]{1,0:T(8,128)(2,1)S(1)}, u32[]{:S(2)}, u32[]{:S(2)}) collective-permute-start(bf16[128,512]{1,0:T(8,128)(2,1)S(1)} %get-tuple-element.119), channel_id=1, source_target_pairs={{0,2},{1,3},{2,0},{3,1},{4,6},{5,7},{6,4},{7,5},{8,10},{9,11},{10,... | collective-permute-start | bytes 393224 | tf_op jit(solution)/shard_map/ppermute | solution.py:22
  69.7 3.8 %collective-permute-start.26 = (f32[156,512]{1,0:T(8,128)S(1)}, f32[156,512]{1,0:T(8,128)S(1)}, u32[]{:S(2)}, u32[]{:S(2)}) collective-permute-start(f32[156,512]{1,0:T(8,128)S(1)} %get-tuple-element.138), channel_id=1, source_target_pairs={{0,1},{1,0},{2,3},{3,2},{4,5},{5,4},{6,7},{7,6},{8,9},{9,8},{10,11... | collective-permute-start | bytes 958472 | tf_op jit(solution)/shard_map/ppermute | solution.py:22
  (3 other events, 7.6 us)

commit v7 on v6

--- a/solution.py
+++ b/solution.py
@@ -30,6 +30,15 @@
 
 def shaped(shape, dtype=WIDE):
     return jax.ShapeDtypeStruct(shape, dtype)
+
+
+def swap_far(value, pair, side):
+    count = lax.axis_size("row")
+    pairs = []
+    for group in range(2):
+        bits = 4 * (2 * pair + group) + 2 * side
+        pairs += [(group * count + i, group * count + (i ^ bits)) for i in range(count)]
+    return lax.ppermute(value, ("grp", "row"), pairs)
 
 
 def swap_group(value):
@@ -101,33 +110,34 @@
         copy.wait()
 
 
-def join_body(mine, other, *targets):
-    group = lax.axis_index("grp")
-    for side in range(2):
-        full, sent = targets[2 * side : 2 * side + 2]
-        own_rows = mine.shape[2]
+def join_body(mine, other, branch, *targets):
+    own = mine.shape[2]
+    sent = targets[2]
+    pixels = branch.shape[0]
+    sent[:pixels, :] = branch[...]
+    for side, full in enumerate(targets[:2]):
         for which in range(2):
+            rows = pl.ds((2 * side + which) * own, own)
             full[which, 0] = mine[side, which]
-            full[which, 1] = other[pl.ds((2 * side + which) * own_rows, own_rows), :]
-        sent[...] = full[group]
-
-
-def acts_body(mine, got, *refs):
+            full[which, 1] = other[rows, :]
+            if side:
+                start = pixels + 2 * which * own
+                sent[start : start + own, :] = mine[side, which]
+                sent[start + own : start + 2 * own, :] = other[rows, :]
+
+
+def acts_body(normed, branch, normed_got, sent_got, *refs):
     acts, full = refs[-2:]
-    pixels = acts.shape[1] // 2
+    pixels = branch.shape[0]
+    acts[0, :pixels] = normed[...]
+    acts[0, pixels:] = normed_got[...]
+    acts[1, :pixels] = branch[...]
+    acts[1, pixels:] = sent_got[:pixels, :]
+    own = full.shape[2]
     for which in range(2):
-        rows = slice(which * pixels, (which + 1) * pixels)
-        acts[which, :pixels] = mine[rows, :]
-        acts[which, pixels:] = got[rows, :]
-        own = full.shape[2]
         for core in range(2):
-            start = 2 * pixels + (2 * which + core) * own
-            full[which, core] = got[start : start + own, :]
-
-
-def stack_body(*refs):
-    for place_in, ref in enumerate(refs[:-1]):
-        refs[-1][place_in] = ref[...]
+            start = pixels + (2 * which + core) * own
+            full[which, core] = sent_got[start : start + own, :]
 
 
 def fill(padded, block, inner, outer):
@@ -160,7 +170,7 @@
 
 
 def conv_body(
-    feats, core_got, outer, kernel, gain, bias, branch, full, normed, inv, acts, padded, result
+    feats, core_got, outer, kernel, gain, bias, normed, inv, narrow, padded, result
 ):
     rows, cols, channels = feats.shape
     start = core_got.shape[0] - RIM * cols
@@ -180,14 +190,7 @@
     value = centred * spread
     normed[...] = value
     inv[...] = jnp.broadcast_to(spread, inv.shape)
-    pixels = rows * cols
-    acts[:pixels, :] = (value * gain[...] + bias[...]).astype(NARROW)
-    acts[pixels : 2 * pixels, :] = branch[...]
-    own = full.shape[2]
-    for which in range(2):
-        for core in range(2):
-            start = 2 * pixels + (2 * which + core) * own
-            acts[start : start + own, :] = full[which, core]
+    narrow[...] = (value * gain[...] + bias[...]).astype(NARROW)
 
 
 def hidden_body(copied, *refs):
@@ -201,19 +204,17 @@
     if copied:
         own = pieces[0].shape[2]
         group = lax.axis_index("grp")
+        each = len(pieces) // 2
         for side in range(2):
-            full, near, here, there = pieces[4 * side : 4 * side + 4]
-            for pattern in range(patterns):
+            blocks = pieces[side * each : (side + 1) * each]
+            for spot, block in enumerate(blocks):
+                other = jnp.bitwise_xor(group, spot % 2)
+                pattern = spot if spot < 2 else 2 * (spot // 2) + other
                 for c in range(2):
                     device = jnp.bitwise_xor(me, 4 * pattern + 2 * side + c)
                     rows = pl.ds(pl.multiple_of(device * own, own), own)
-                    if pattern < 2:
-                        source = near if pattern else full
-                        weights[0, rows, :] = source[0, c]
-                        weights[1, rows, :] = source[1, c]
-                    else:
-                        weights[group, rows, :] = here[pattern - 2, c]
-                        weights[1 - group, rows, :] = there[pattern - 2, c]
+                    for which in range(2):
+                        weights[which, rows, :] = block[which, c]
     else:
         weights[...] = pieces[0][...]
     in_narrow = weights.at[0]
@@ -460,24 +461,26 @@
     full_shape = shaped((2, 2, own_rows, quarter), NARROW)
     joined = run(
         join_body,
-        (full_shape, shaped(piece, NARROW)) * 2,
+        (full_shape, full_shape, shaped((pixels + 4 * own_rows, channels), NARROW)),
         own,
         core_got,
-    )
+        branch,
+    )
+    sent_got = swap(joined[2], 2)
     pieces = []
-    for side in range(2):
-        full, sent = joined[2 * side : 2 * side + 2]
-        here = [swap(sent, 4 * p + 2 * side) for p in range(2, patterns)]
-        here = run(stack_body, (shaped((patterns - 2,) + piece, NARROW),), *here, order=8)[0]
-        near = swap(full, 4 + 2 * side)
-        pieces += [full, near, here, swap_group(here)]
-
-    normed, inv, sent = run(
+    for side, full in enumerate(joined[:2]):
+        pieces += [full, swap(full, 4 + 2 * side)]
+        for pair in range(1, patterns // 2):
+            here = swap_far(full, pair, side)
+            pieces += [here, swap_group(here)]
+    each = len(pieces) // 2
+
+    normed, inv, normed_out = run(
         conv_body,
         (
             shaped((pixels, channels)),
             shaped((pixels, LANES)),
-            shaped((2 * pixels + 4 * own_rows, channels), NARROW),
+            shaped((pixels, channels), NARROW),
         ),
         feats,
         core_got,
@@ -485,16 +488,16 @@
         taps,
         gain,
         bias,
-        branch,
-        joined[2],
         scratch=(padded, pltpu.VMEM((pixels, channels), WIDE)),
     )
-    first_blocks = [pieces[k] for k in (1, 3, 5, 7)]
-    acts, pieces[4] = run(
+    first_blocks = [block for k, block in enumerate(pieces) if k % each and k != each - 1]
+    acts, pieces[each] = run(
         acts_body,
         (shaped((2, 2 * pixels, channels), NARROW), full_shape),
-        sent,
-        swap(sent, 2),
+        normed_out,
+        branch,
+        swap(normed_out, 2),
+        sent_got,
         *first_blocks,
     )
     acts_got = swap(acts, 1)
@@ -503,12 +506,12 @@
         lines = []
         for pattern in range(patterns):
             for side in range(2):
-                full, near, here, there = pieces[4 * side : 4 * side + 4]
+                blocks = pieces[side * each : (side + 1) * each]
                 if pattern < 2:
-                    lines.append(near if pattern else full)
+                    lines.append(blocks[pattern])
                 else:
-                    pair = jnp.stack([here[pattern - 2], there[pattern - 2]])
-                    lines.append(flipped(pair, 0, group_index))
+                    pair = jnp.stack(blocks[pattern - pattern % 2 : pattern - pattern % 2 + 2])
+                    lines.append(flipped(pair, 0, group_index)[pattern % 2])
         lines = jnp.moveaxis(jnp.stack(lines), 1, 2).reshape(count, 2, own_rows, quarter)
         lines = jnp.moveaxis(canonical(lines, me, bit_count), 1, 0)
         pieces = [lines.reshape(2, channels, quarter)]

time: 74.8 us -> 81.5 us (1.090)
  waiting for transfers between devices: 21.3 us -> 30.4 us
  starting transfers between devices: 39 us -> 36.5 us
    ppermute x2, waiting for transfers between devices: 0.01 us -> 8.9 us  [swap_rim(): return lax.ppermute(value, 'row', pairs + [(j, i) for i, j in pairs])]
    ppermute x23 -> x20, starting transfers between devices: 28.6 us -> 21.9 us  [swap(): return lax.ppermute(value, 'row', [(i, i ^ bit) for i in range(count)])]
    ppermute x0 -> x2, starting transfers between devices: none -> 4.55 us  [swap_far(): return lax.ppermute(value, ('grp', 'row'), pairs)]
    ppermute x2, starting transfers between devices: 7.81 us -> 5.65 us  [swap_rim(): return lax.ppermute(value, 'row', pairs + [(j, i) for i, j in pairs])]
    ppermute x2, starting transfers between devices: 2.61 us -> 4.4 us  [swap_group(): return lax.ppermute(value, 'grp', [(0, 1), (1, 0)])]
    ppermute x23 -> x20, waiting for transfers between devices: 17.8 us -> 17.4 us  [swap(): return lax.ppermute(value, 'row', [(i, i ^ bit) for i in range(count)])]
    pallas_call x16 -> x14, Pallas kernels: 13.1 us -> 13.1 us  [run(): pl.pallas_call(body, out_shape=outs, **extra, scratch_shapes=scratch, com...]
  transfers between devices with their start and end apart: 27 -> 26, of which waited for: 14 -> 11; matrix products, arithmetic and copies ran while one was open for 0% -> 0% of each run, Pallas kernels for 12% -> 11%
where the time goes in v7:
time: 81.5 us; the launch traced here: 80.9 us
  starting transfers between devices  36.5 us (45%)
  waiting for transfers between devices  30.4 us (37%)
  Pallas kernels  13.1 us (16%)
  between operations  0.85 us (1%)
    ppermute x20, starting transfers between devices, swap(): return lax.ppermute(value, 'row', [(i, i ^ bit) for i in range(count)])  21.9 us
    ppermute x20, waiting for transfers between devices, swap(): return lax.ppermute(value, 'row', [(i, i ^ bit) for i in range(count)])  17.4 us
    pallas_call x14, Pallas kernels, run(): pl.pallas_call(body, out_shape=outs, **extra, scratch_shapes=scratch, com...  13.1 us
    ppermute x2, waiting for transfers between devices, swap_rim(): return lax.ppermute(value, 'row', pairs + [(j, i) for i, j in pairs])  8.9 us
    ppermute x2, starting transfers between devices, swap_rim(): return lax.ppermute(value, 'row', pairs + [(j, i) for i, j in pairs])  5.65 us
    ppermute x2, starting transfers between devices, swap_far(): return lax.ppermute(value, ('grp', 'row'), pairs)  4.55 us
    ppermute x2, starting transfers between devices, swap_group(): return lax.ppermute(value, 'grp', [(0, 1), (1, 0)])  4.4 us
    ppermute x2, waiting for transfers between devices, swap_group(): return lax.ppermute(value, 'grp', [(0, 1), (1, 0)])  4.13 us
  transfers between devices with their start and end apart: 26, of which 11 were waited for; matrix products, arithmetic and copies ran while one was open for 0% of the time, Pallas kernels for 11%

profile of v7, /device:TPU:1, one launch (start us, length us, event | category | flops | bytes accessed | tf_op | source)
XLA Modules:
  0.0 80.9 jit_solution(2360203491353843949)
XLA Ops:
  0.6 1.3 %shard_map.160 = (bf16[2,2,32,512]{3,2,1,0:T(8,128)(2,1)S(1)}, bf16[224,512]{1,0:T(8,128)(2,1)S(1)}, bf16[96,512]{1,0:T(8,128)(2,1)S(1)}, bf16[128,512]{1,0:T(8,...) custom-call(f32[32,2048]{1,0:T(8,128)} %refs_0_.1, ...), custom_call_target="tpu_custom_call" | custom-call | tf_op jit(solution)/shard_map/pallas_call | solution.py:53
  2.1 1.4 %collective-permute-done.core_got.other.refs_6_ = bf16[224,512]{1,0:T(8,128)(2,1)S(1)} collective-permute-done((bf16[224,512]{1,0:T(8,128)(2,1)S(1)}, bf16[224,512]{1,0:T(8,128)(2,1)S(1)}, u32[]{:S(2)}, u32[]{:S(2)}) %collective-permute-start) | collective-permute-done | bytes 229408 | tf_op jit(solution)/shard_map/ppermute | solution.py:22
  3.6 4.4 %collective-permute-start.7 = (bf16[2,2,32,512]{3,2,1,0:T(8,128)(2,1)S(1)}, bf16[2,2,32,512]{3,2,1,0:T(8,128)(2,1)S(1)}, u32[]{:S(2)}, u32[]{:S(2)}) collective-permute-start(bf16[2,2,32,512]{3,2,1,0:T(8,128)(2,1)S(1)} %get-tuple-element.88), channel_id=1, source_target_pairs={{0,10},{1,11},{2,8},{3,9},{4,14},{5,15},{6,12},{7,13},{8,2},{9,3},... | collective-permute-start | bytes 393224 | tf_op jit(solution)/shard_map/ppermute | solution.py:41
  10.5 3.2 %collective-permute-start.1 = (bf16[96,512]{1,0:T(8,128)(2,1)S(1)}, bf16[96,512]{1,0:T(8,128)(2,1)S(1)}, u32[]{:S(2)}, u32[]{:S(2)}) collective-permute-start(bf16[96,512]{1,0:T(8,128)(2,1)S(1)} %get-tuple-element.79), channel_id=1, source_target_pairs={{1,2},{3,4},{5,6},{7,8},{9,10},{11,12},{13,14},{2,1},{4,3},{6,5},{... | collective-permute-start | bytes 294920 | tf_op jit(solution)/shard_map/ppermute | solution.py:28
  13.9 8.9 %collective-permute-done.1.outer.refs_7_ = bf16[96,512]{1,0:T(8,128)(2,1)S(1)} collective-permute-done((bf16[96,512]{1,0:T(8,128)(2,1)S(1)}, bf16[96,512]{1,0:T(8,128)(2,1)S(1)}, u32[]{:S(2)}, u32[]{:S(2)}) %collective-permute-start.1) | collective-permute-done | bytes 98336 | tf_op jit(solution)/shard_map/ppermute | solution.py:28
  24.0 2.4 %shard_map.161 = (f32[128,512]{1,0:T(8,128)S(1)}, f32[128,128]{1,0:T(8,128)S(1)}, bf16[128,512]{1,0:T(8,128)(2,1)S(1)}) custom-call(f32[4,32,512]{2,1,0:T(8,128)S(1)} %get-tuple-element.77.feats.refs_5_, bf16[224,512]{1,0:T(8,128)(2,1)S(1)} %collective-permute-done.core_got.other.refs_6_, bf16[96,512]{1,0:T(8,128)(2,1)S(1)} %collective-permute-done.1.outer.refs_7_, ...), custom_call_target="tpu_custom_call" | custom-call | tf_op jit(solution)/shard_map/pallas_call | solution.py:53
  26.6 2.6 %collective-permute-start.8 = (bf16[2,2,32,512]{3,2,1,0:T(8,128)(2,1)S(1)}, bf16[2,2,32,512]{3,2,1,0:T(8,128)(2,1)S(1)}, u32[]{:S(2)}, u32[]{:S(2)}) collective-permute-start(bf16[2,2,32,512]{3,2,1,0:T(8,128)(2,1)S(1)} %collective-permute-done.7.refs_3_.refs_10_), channel_id=1, source_target_pairs={{0,16},{16,0},{1,17},{17,1},{2,18},{18,2},{3,19},{19,3},{4,20},{20... | collective-permute-start | bytes 393224 | tf_op jit(solution)/shard_map/ppermute | solution.py:45
  29.2 2.3 %collective-permute-done.2.normed_got = bf16[128,512]{1,0:T(8,128)(2,1)S(1)} collective-permute-done((bf16[128,512]{1,0:T(8,128)(2,1)S(1)}, bf16[128,512]{1,0:T(8,128)(2,1)S(1)}, u32[]{:S(2)}, u32[]{:S(2)}) %collective-permute-start.2) | collective-permute-done | bytes 131104 | tf_op jit(solution)/shard_map/ppermute | solution.py:22
  31.9 2.7 %collective-permute-start.9 = (bf16[2,256,512]{2,1,0:T(8,128)(2,1)S(1)}, bf16[2,256,512]{2,1,0:T(8,128)(2,1)S(1)}, u32[]{:S(2)}, u32[]{:S(2)}) collective-permute-start(bf16[2,256,512]{2,1,0:T(8,128)(2,1)S(1)} %get-tuple-element.89.refs_0_), channel_id=1, source_target_pairs={{0,1},{1,0},{2,3},{3,2},{4,5},{5,4},{6,7},{7,6},{8,9},{9,8},{10,11... | collective-permute-start | bytes 1572872 | tf_op jit(solution)/shard_map/ppermute | solution.py:22
  34.6 1.8 %collective-permute-start.10 = (bf16[2,2,32,512]{3,2,1,0:T(8,128)(2,1)S(1)}, bf16[2,2,32,512]{3,2,1,0:T(8,128)(2,1)S(1)}, u32[]{:S(2)}, u32[]{:S(2)}) collective-permute-start(bf16[2,2,32,512]{3,2,1,0:T(8,128)(2,1)S(1)} %collective-permute-done.5.refs_1_.refs_6_), channel_id=1, source_target_pairs={{0,16},{16,0},{1,17},{17,1},{2,18},{18,2},{3,19},{19,3},{4,20},{20... | collective-permute-start | bytes 393224 | tf_op jit(solution)/shard_map/ppermute | solution.py:45
  36.4 3.8 %collective-permute-done.10.refs_7_ = bf16[2,2,32,512]{3,2,1,0:T(8,128)(2,1)S(1)} collective-permute-done((bf16[2,2,32,512]{3,2,1,0:T(8,128)(2,1)S(1)}, bf16[2,2,32,512]{3,2,1,0:T(8,128)(2,1)S(1)}, u32[]{:S(2)}, u32[]{:S(2)}) %collective-permute-start.10) | collective-permute-done | bytes 131104 | tf_op jit(solution)/shard_map/ppermute | solution.py:45
  40.2 1.7 %shard_map.164 = (f32[2,256,512]{2,1,0:T(8,128)S(1)}, bf16[2,256,512]{2,1,0:T(8,128)(2,1)S(1)}, bf16[512,512]{1,0:T(8,128)(2,1)S(1)}, bf16[512,512]{1,0:T(8,128)...) custom-call(bf16[2,256,512]{2,1,0:T(8,128)(2,1)S(1)} %get-tuple-element.89.refs_0_, ...), custom_call_target="tpu_custom_call" | custom-call | tf_op jit(solution)/shard_map/pallas_call | solution.py:53
  42.6 1.5 %collective-permute-done.11.got = bf16[2,256,512]{2,1,0:T(8,128)(2,1)S(1)} collective-permute-done((bf16[2,256,512]{2,1,0:T(8,128)(2,1)S(1)}, bf16[2,256,512]{2,1,0:T(8,128)(2,1)S(1)}, u32[]{:S(2)}, u32[]{:S(2)}) %collective-permute-start.11) | collective-permute-done | bytes 524320 | tf_op jit(solution)/shard_map/ppermute | solution.py:22
  45.4 2.0 %collective-permute-start.14 = (bf16[128,512]{1,0:T(8,128)(2,1)S(1)}, bf16[128,512]{1,0:T(8,128)(2,1)S(1)}, u32[]{:S(2)}, u32[]{:S(2)}) collective-permute-start(bf16[128,512]{1,0:T(8,128)(2,1)S(1)} %get-tuple-element.105), channel_id=1, source_target_pairs={{0,14},{1,15},{2,12},{3,13},{4,10},{5,11},{6,8},{7,9},{8,6},{9,7},... | collective-permute-start | bytes 393224 | tf_op jit(solution)/shard_map/ppermute | solution.py:22
  47.5 3.3 %collective-permute-start.16 = (bf16[128,512]{1,0:T(8,128)(2,1)S(1)}, bf16[128,512]{1,0:T(8,128)(2,1)S(1)}, u32[]{:S(2)}, u32[]{:S(2)}) collective-permute-start(bf16[128,512]{1,0:T(8,128)(2,1)S(1)} %get-tuple-element.107), channel_id=1, source_target_pairs={{0,6},{1,7},{2,4},{3,5},{4,2},{5,3},{6,0},{7,1},{8,14},{9,15},{10,... | collective-permute-start | bytes 393224 | tf_op jit(solution)/shard_map/ppermute | solution.py:22
  50.8 1.9 %shard_map.166 = (f32[128,512]{1,0:T(8,128)S(1)}, bf16[96,512]{1,0:T(8,128)(2,1)S(1)}, bf16[96,512]{1,0:T(8,128)(2,1)S(1)}, f32[28,512]{1,0:T(8,128)S(1)}, f32[28,512]{1,0:T(8,128)S(1)}) custom-call(f32[128,512]{1,0:T(8,128)S(1)} %get-tuple-element.95.refs_0_, bf16[128,512]{1,0:T(8,128)(2,1)S(1)} %collective-permute-done.12.refs_1_, ...), custom_call_target="tpu_custom_call" | custom-call | tf_op jit(solution)/shard_map/pallas_call | solution.py:53
  52.8 1.6 %collective-permute-start.13 = (f32[28,512]{1,0:T(8,128)S(1)}, f32[28,512]{1,0:T(8,128)S(1)}, u32[]{:S(2)}, u32[]{:S(2)}) collective-permute-start(f32[28,512]{1,0:T(8,128)S(1)} %get-tuple-element.102), channel_id=1, source_target_pairs={{0,1},{1,0},{2,3},{3,2},{4,5},{5,4},{6,7},{7,6},{8,9},{9,8},{10,11... | collective-permute-start | bytes 172040 | tf_op jit(solution)/shard_map/ppermute | solution.py:22
  55.2 2.4 %collective-permute-start.23 = (bf16[96,512]{1,0:T(8,128)(2,1)S(1)}, bf16[96,512]{1,0:T(8,128)(2,1)S(1)}, u32[]{:S(2)}, u32[]{:S(2)}) collective-permute-start(bf16[96,512]{1,0:T(8,128)(2,1)S(1)} %get-tuple-element.121), channel_id=1, source_target_pairs={{1,2},{3,4},{5,6},{7,8},{9,10},{11,12},{13,14},{2,1},{4,3},{6,5},{... | collective-permute-start | bytes 294920 | tf_op jit(solution)/shard_map/ppermute | solution.py:28
  57.7 2.0 %collective-permute-done.15.refs_1_ = bf16[128,512]{1,0:T(8,128)(2,1)S(1)} collective-permute-done((bf16[128,512]{1,0:T(8,128)(2,1)S(1)}, bf16[128,512]{1,0:T(8,128)(2,1)S(1)}, u32[]{:S(2)}, u32[]{:S(2)}) %collective-permute-start.15) | collective-permute-done | bytes 131104 | tf_op jit(solution)/shard_map/ppermute | solution.py:22
  60.8 2.0 %collective-permute-done.17 = f32[28,512]{1,0:T(8,128)S(1)} collective-permute-done((f32[28,512]{1,0:T(8,128)S(1)}, f32[28,512]{1,0:T(8,128)S(1)}, u32[]{:S(2)}, u32[]{:S(2)}) %collective-permute-start.17) | collective-permute-done | bytes 57376 | tf_op jit(solution)/shard_map/ppermute | solution.py:22
  63.1 1.9 %collective-permute-start.19 = (bf16[160,512]{1,0:T(8,128)(2,1)S(1)}, bf16[160,512]{1,0:T(8,128)(2,1)S(1)}, u32[]{:S(2)}, u32[]{:S(2)}) collective-permute-start(bf16[160,512]{1,0:T(8,128)(2,1)S(1)} %get-tuple-element.115), channel_id=1, source_target_pairs={{0,12},{1,13},{2,14},{3,15},{4,8},{5,9},{6,10},{7,11},{8,4},{9,5},... | collective-permute-start | bytes 491528 | tf_op jit(solution)/shard_map/ppermute | solution.py:22
  67.1 2.9 %shard_map.170 = f32[4,32,512]{2,1,0:T(8,128)} custom-call(f32[128,512]{1,0:T(8,128)S(1)} %get-tuple-element.119.grad, bf16[96,512]{1,0:T(8,128)(2,1)S(1)} %collective-permute-done.22.inner, bf16[96,512]{1,0:T(8,128)(2,1)S(1)} %collective-permute-done.23.outer, f32[7,7,512]{2,1,0:T(8,128)S(1)} %get-tuple-element.80.kernel, ...), custom_call_target="tpu_custom_call" | custom-call | tf_op jit(solution)/shard_map/pallas_call | solution.py:53
  70.7 5.9 %collective-permute-done.18 = bf16[160,512]{1,0:T(8,128)(2,1)S(1)} collective-permute-done((bf16[160,512]{1,0:T(8,128)(2,1)S(1)}, bf16[160,512]{1,0:T(8,128)(2,1)S(1)}, u32[]{:S(2)}, u32[]{:S(2)}) %collective-permute-start.18) | collective-permute-done | bytes 163872 | tf_op jit(solution)/shard_map/ppermute | solution.py:22
  76.9 1.9 %collective-permute-start.25 = (f32[156,512]{1,0:T(8,128)S(1)}, f32[156,512]{1,0:T(8,128)S(1)}, u32[]{:S(2)}, u32[]{:S(2)}) collective-permute-start(f32[156,512]{1,0:T(8,128)S(1)} %get-tuple-element.136), channel_id=1, source_target_pairs={{0,1},{1,0},{2,3},{3,2},{4,5},{5,4},{6,7},{7,6},{8,9},{9,8},{10,11... | collective-permute-start | bytes 958472 | tf_op jit(solution)/shard_map/ppermute | solution.py:22
  (50 shorter events, 14.0 us)
Async XLA Ops:
  3.6 22.9 %collective-permute-start.7 = (bf16[2,2,32,512]{3,2,1,0:T(8,128)(2,1)S(1)}, bf16[2,2,32,512]{3,2,1,0:T(8,128)(2,1)S(1)}, u32[]{:S(2)}, u32[]{:S(2)}) collective-permute-start(bf16[2,2,32,512]{3,2,1,0:T(8,128)(2,1)S(1)} %get-tuple-element.88), channel_id=1, source_target_pairs={{0,10},{1,11},{2,8},{3,9},{4,14},{5,15},{6,12},{7,13},{8,2},{9,3},... | collective-permute-start | bytes 393224 | tf_op jit(solution)/shard_map/ppermute | solution.py:41
  8.0 18.5 %collective-permute-start.6 = (bf16[2,2,32,512]{3,2,1,0:T(8,128)(2,1)S(1)}, bf16[2,2,32,512]{3,2,1,0:T(8,128)(2,1)S(1)}, u32[]{:S(2)}, u32[]{:S(2)}) collective-permute-start(bf16[2,2,32,512]{3,2,1,0:T(8,128)(2,1)S(1)} %get-tuple-element.88), channel_id=1, source_target_pairs={{0,6},{1,7},{2,4},{3,5},{4,2},{5,3},{6,0},{7,1},{8,14},{9,15},{10,... | collective-permute-start | bytes 393224 | tf_op jit(solution)/shard_map/ppermute | solution.py:22
  9.3 22.6 %collective-permute-start.3 = (bf16[256,512]{1,0:T(8,128)(2,1)S(1)}, bf16[256,512]{1,0:T(8,128)(2,1)S(1)}, u32[]{:S(2)}, u32[]{:S(2)}) collective-permute-start(bf16[256,512]{1,0:T(8,128)(2,1)S(1)} %get-tuple-element.86), channel_id=1, source_target_pairs={{0,2},{1,3},{2,0},{3,1},{4,6},{5,7},{6,4},{7,5},{8,10},{9,11},{10,... | collective-permute-start | bytes 786440 | tf_op jit(solution)/shard_map/ppermute | solution.py:22
  10.5 12.3 %collective-permute-start.1 = (bf16[96,512]{1,0:T(8,128)(2,1)S(1)}, bf16[96,512]{1,0:T(8,128)(2,1)S(1)}, u32[]{:S(2)}, u32[]{:S(2)}) collective-permute-start(bf16[96,512]{1,0:T(8,128)(2,1)S(1)} %get-tuple-element.79), channel_id=1, source_target_pairs={{1,2},{3,4},{5,6},{7,8},{9,10},{11,12},{13,14},{2,1},{4,3},{6,5},{... | collective-permute-start | bytes 294920 | tf_op jit(solution)/shard_map/ppermute | solution.py:28
  13.8 15.5 %collective-permute-start.5 = (bf16[2,2,32,512]{3,2,1,0:T(8,128)(2,1)S(1)}, bf16[2,2,32,512]{3,2,1,0:T(8,128)(2,1)S(1)}, u32[]{:S(2)}, u32[]{:S(2)}) collective-permute-start(bf16[2,2,32,512]{3,2,1,0:T(8,128)(2,1)S(1)} %get-tuple-element.87.refs_4_), channel_id=1, source_target_pairs={{0,8},{1,9},{2,10},{3,11},{4,12},{5,13},{6,14},{7,15},{8,0},{9,1},... | collective-permute-start | bytes 393224 | tf_op jit(solution)/shard_map/ppermute | solution.py:41
  22.8 6.4 %collective-permute-start.4 = (bf16[2,2,32,512]{3,2,1,0:T(8,128)(2,1)S(1)}, bf16[2,2,32,512]{3,2,1,0:T(8,128)(2,1)S(1)}, u32[]{:S(2)}, u32[]{:S(2)}) collective-permute-start(bf16[2,2,32,512]{3,2,1,0:T(8,128)(2,1)S(1)} %get-tuple-element.87.refs_4_), channel_id=1, source_target_pairs={{0,4},{1,5},{2,6},{3,7},{4,0},{5,1},{6,2},{7,3},{8,12},{9,13},{10,... | collective-permute-start | bytes 393224 | tf_op jit(solution)/shard_map/ppermute | solution.py:22
  26.5 5.0 %collective-permute-start.2 = (bf16[128,512]{1,0:T(8,128)(2,1)S(1)}, bf16[128,512]{1,0:T(8,128)(2,1)S(1)}, u32[]{:S(2)}, u32[]{:S(2)}) collective-permute-start(bf16[128,512]{1,0:T(8,128)(2,1)S(1)} %get-tuple-element.83.normed), channel_id=1, source_target_pairs={{0,2},{1,3},{2,0},{3,1},{4,6},{5,7},{6,4},{7,5},{8,10},{9,11},{10,... | collective-permute-start | bytes 393224 | tf_op jit(solution)/shard_map/ppermute | solution.py:22
  26.6 5.3 %collective-permute-start.8 = (bf16[2,2,32,512]{3,2,1,0:T(8,128)(2,1)S(1)}, bf16[2,2,32,512]{3,2,1,0:T(8,128)(2,1)S(1)}, u32[]{:S(2)}, u32[]{:S(2)}) collective-permute-start(bf16[2,2,32,512]{3,2,1,0:T(8,128)(2,1)S(1)} %collective-permute-done.7.refs_3_.refs_10_), channel_id=1, source_target_pairs={{0,16},{16,0},{1,17},{17,1},{2,18},{18,2},{3,19},{19,3},{4,20},{20... | collective-permute-start | bytes 393224 | tf_op jit(solution)/shard_map/ppermute | solution.py:45
  31.9 8.2 %collective-permute-start.9 = (bf16[2,256,512]{2,1,0:T(8,128)(2,1)S(1)}, bf16[2,256,512]{2,1,0:T(8,128)(2,1)S(1)}, u32[]{:S(2)}, u32[]{:S(2)}) collective-permute-start(bf16[2,256,512]{2,1,0:T(8,128)(2,1)S(1)} %get-tuple-element.89.refs_0_), channel_id=1, source_target_pairs={{0,1},{1,0},{2,3},{3,2},{4,5},{5,4},{6,7},{7,6},{8,9},{9,8},{10,11... | collective-permute-start | bytes 1572872 | tf_op jit(solution)/shard_map/ppermute | solution.py:22
  34.6 5.5 %collective-permute-start.10 = (bf16[2,2,32,512]{3,2,1,0:T(8,128)(2,1)S(1)}, bf16[2,2,32,512]{3,2,1,0:T(8,128)(2,1)S(1)}, u32[]{:S(2)}, u32[]{:S(2)}) collective-permute-start(bf16[2,2,32,512]{3,2,1,0:T(8,128)(2,1)S(1)} %collective-permute-done.5.refs_1_.refs_6_), channel_id=1, source_target_pairs={{0,16},{16,0},{1,17},{17,1},{2,18},{18,2},{3,19},{19,3},{4,20},{20... | collective-permute-start | bytes 393224 | tf_op jit(solution)/shard_map/ppermute | solution.py:45
  44.3 6.6 %collective-permute-start.12 = (bf16[128,512]{1,0:T(8,128)(2,1)S(1)}, bf16[128,512]{1,0:T(8,128)(2,1)S(1)}, u32[]{:S(2)}, u32[]{:S(2)}) collective-permute-start(bf16[128,512]{1,0:T(8,128)(2,1)S(1)} %get-tuple-element.96.after), channel_id=1, source_target_pairs={{0,2},{1,3},{2,0},{3,1},{4,6},{5,7},{6,4},{7,5},{8,10},{9,11},{10,... | collective-permute-start | bytes 393224 | tf_op jit(solution)/shard_map/ppermute | solution.py:22
  45.4 12.3 %collective-permute-start.14 = (bf16[128,512]{1,0:T(8,128)(2,1)S(1)}, bf16[128,512]{1,0:T(8,128)(2,1)S(1)}, u32[]{:S(2)}, u32[]{:S(2)}) collective-permute-start(bf16[128,512]{1,0:T(8,128)(2,1)S(1)} %get-tuple-element.105), channel_id=1, source_target_pairs={{0,14},{1,15},{2,12},{3,13},{4,10},{5,11},{6,8},{7,9},{8,6},{9,7},... | collective-permute-start | bytes 393224 | tf_op jit(solution)/shard_map/ppermute | solution.py:22
  47.4 12.3 %collective-permute-start.15 = (bf16[128,512]{1,0:T(8,128)(2,1)S(1)}, bf16[128,512]{1,0:T(8,128)(2,1)S(1)}, u32[]{:S(2)}, u32[]{:S(2)}) collective-permute-start(bf16[128,512]{1,0:T(8,128)(2,1)S(1)} %get-tuple-element.106), channel_id=1, source_target_pairs={{0,10},{1,11},{2,8},{3,9},{4,14},{5,15},{6,12},{7,13},{8,2},{9,3},... | collective-permute-start | bytes 393224 | tf_op jit(solution)/shard_map/ppermute | solution.py:22
  47.5 12.2 %collective-permute-start.16 = (bf16[128,512]{1,0:T(8,128)(2,1)S(1)}, bf16[128,512]{1,0:T(8,128)(2,1)S(1)}, u32[]{:S(2)}, u32[]{:S(2)}) collective-permute-start(bf16[128,512]{1,0:T(8,128)(2,1)S(1)} %get-tuple-element.107), channel_id=1, source_target_pairs={{0,6},{1,7},{2,4},{3,5},{4,2},{5,3},{6,0},{7,1},{8,14},{9,15},{10,... | collective-permute-start | bytes 393224 | tf_op jit(solution)/shard_map/ppermute | solution.py:22
  52.8 2.5 %collective-permute-start.13 = (f32[28,512]{1,0:T(8,128)S(1)}, f32[28,512]{1,0:T(8,128)S(1)}, u32[]{:S(2)}, u32[]{:S(2)}) collective-permute-start(f32[28,512]{1,0:T(8,128)S(1)} %get-tuple-element.102), channel_id=1, source_target_pairs={{0,1},{1,0},{2,3},{3,2},{4,5},{5,4},{6,7},{7,6},{8,9},{9,8},{10,11... | collective-permute-start | bytes 172040 | tf_op jit(solution)/shard_map/ppermute | solution.py:22
  54.3 11.3 %collective-permute-start.22 = (bf16[96,512]{1,0:T(8,128)(2,1)S(1)}, bf16[96,512]{1,0:T(8,128)(2,1)S(1)}, u32[]{:S(2)}, u32[]{:S(2)}) collective-permute-start(bf16[96,512]{1,0:T(8,128)(2,1)S(1)} %get-tuple-element.120), channel_id=1, source_target_pairs={{0,1},{1,0},{2,3},{3,2},{4,5},{5,4},{6,7},{7,6},{8,9},{9,8},{10,11... | collective-permute-start | bytes 294920 | tf_op jit(solution)/shard_map/ppermute | solution.py:22
  55.2 11.5 %collective-permute-start.23 = (bf16[96,512]{1,0:T(8,128)(2,1)S(1)}, bf16[96,512]{1,0:T(8,128)(2,1)S(1)}, u32[]{:S(2)}, u32[]{:S(2)}) collective-permute-start(bf16[96,512]{1,0:T(8,128)(2,1)S(1)} %get-tuple-element.121), channel_id=1, source_target_pairs={{1,2},{3,4},{5,6},{7,8},{9,10},{11,12},{13,14},{2,1},{4,3},{6,5},{... | collective-permute-start | bytes 294920 | tf_op jit(solution)/shard_map/ppermute | solution.py:28
  59.7 3.1 %collective-permute-start.17 = (f32[28,512]{1,0:T(8,128)S(1)}, f32[28,512]{1,0:T(8,128)S(1)}, u32[]{:S(2)}, u32[]{:S(2)}) collective-permute-start(f32[28,512]{1,0:T(8,128)S(1)} %add.6), channel_id=1, source_target_pairs={{0,2},{1,3},{2,0},{3,1},{4,6},{5,7},{6,4},{7,5},{8,10},{9,11},{10,... | collective-permute-start | bytes 172040 | tf_op jit(solution)/shard_map/ppermute | solution.py:22
  62.9 13.7 %collective-permute-start.18 = (bf16[160,512]{1,0:T(8,128)(2,1)S(1)}, bf16[160,512]{1,0:T(8,128)(2,1)S(1)}, u32[]{:S(2)}, u32[]{:S(2)}) collective-permute-start(bf16[160,512]{1,0:T(8,128)(2,1)S(1)} %get-tuple-element.114), channel_id=1, source_target_pairs={{0,8},{1,9},{2,10},{3,11},{4,12},{5,13},{6,14},{7,15},{8,0},{9,1},... | collective-permute-start | bytes 491528 | tf_op jit(solution)/shard_map/ppermute | solution.py:22
  63.1 13.6 %collective-permute-start.19 = (bf16[160,512]{1,0:T(8,128)(2,1)S(1)}, bf16[160,512]{1,0:T(8,128)(2,1)S(1)}, u32[]{:S(2)}, u32[]{:S(2)}) collective-permute-start(bf16[160,512]{1,0:T(8,128)(2,1)S(1)} %get-tuple-element.115), channel_id=1, source_target_pairs={{0,12},{1,13},{2,14},{3,15},{4,8},{5,9},{6,10},{7,11},{8,4},{9,5},... | collective-permute-start | bytes 491528 | tf_op jit(solution)/shard_map/ppermute | solution.py:22
  65.0 11.7 %collective-permute-start.20 = (bf16[160,512]{1,0:T(8,128)(2,1)S(1)}, bf16[160,512]{1,0:T(8,128)(2,1)S(1)}, u32[]{:S(2)}, u32[]{:S(2)}) collective-permute-start(bf16[160,512]{1,0:T(8,128)(2,1)S(1)} %get-tuple-element.116), channel_id=1, source_target_pairs={{0,4},{1,5},{2,6},{3,7},{4,0},{5,1},{6,2},{7,3},{8,12},{9,13},{10,... | collective-permute-start | bytes 491528 | tf_op jit(solution)/shard_map/ppermute | solution.py:22
  65.6 4.3 %collective-permute-start.24 = (bf16[128,512]{1,0:T(8,128)(2,1)S(1)}, bf16[128,512]{1,0:T(8,128)(2,1)S(1)}, u32[]{:S(2)}, u32[]{:S(2)}) collective-permute-start(bf16[128,512]{1,0:T(8,128)(2,1)S(1)} %get-tuple-element.124), channel_id=1, source_target_pairs={{0,2},{1,3},{2,0},{3,1},{4,6},{5,7},{6,4},{7,5},{8,10},{9,11},{10,... | collective-permute-start | bytes 393224 | tf_op jit(solution)/shard_map/ppermute | solution.py:22
  66.7 10.0 %collective-permute-start.21 = (bf16[128,512]{1,0:T(8,128)(2,1)S(1)}, bf16[128,512]{1,0:T(8,128)(2,1)S(1)}, u32[]{:S(2)}, u32[]{:S(2)}) collective-permute-start(bf16[128,512]{1,0:T(8,128)(2,1)S(1)} %get-tuple-element.117), channel_id=1, source_target_pairs={{0,2},{1,3},{2,0},{3,1},{4,6},{5,7},{6,4},{7,5},{8,10},{9,11},{10,... | collective-permute-start | bytes 393224 | tf_op jit(solution)/shard_map/ppermute | solution.py:22
  76.9 3.1 %collective-permute-start.25 = (f32[156,512]{1,0:T(8,128)S(1)}, f32[156,512]{1,0:T(8,128)S(1)}, u32[]{:S(2)}, u32[]{:S(2)}) collective-permute-start(f32[156,512]{1,0:T(8,128)S(1)} %get-tuple-element.136), channel_id=1, source_target_pairs={{0,1},{1,0},{2,3},{3,2},{4,5},{5,4},{6,7},{7,6},{8,9},{9,8},{10,11... | collective-permute-start | bytes 958472 | tf_op jit(solution)/shard_map/ppermute | solution.py:22
  (2 other events, 3.8 us)

commit v8 on v7

--- a/solution.py
+++ b/solution.py
@@ -110,7 +110,8 @@
         copy.wait()
 
 
-def join_body(mine, other, branch, *targets):
+def join_body(mine, other, branch, after, *targets):
+    del after
     own = mine.shape[2]
     sent = targets[2]
     pixels = branch.shape[0]
@@ -197,9 +198,8 @@
     patterns = lax.axis_size("row") // 4
     me, _, _ = place()
     acts, in_bias = refs[:2], refs[2]
-    scale = refs[3]
-    pieces = refs[4:-7]
-    keep, send, active, hidden, scale_part, bias_part, weights = refs[-7:]
+    pieces = refs[3:-7]
+    keep, send, active, hidden, out_copy, bias_part, weights = refs[-7:]
     half = acts[0].shape[1]
     if copied:
         own = pieces[0].shape[2]
@@ -219,9 +219,9 @@
         weights[...] = pieces[0][...]
     in_narrow = weights.at[0]
     out_narrow = weights.at[1]
+    out_copy[...] = weights[1]
     bias_row = in_bias[...]
     total = jnp.zeros_like(bias_row)
-    scale_total = jnp.zeros_like(scale_part)
     for side in (1, 0):
         preact = dot(acts[side][0], in_narrow[...], ((1,), (0,))) + bias_row
         act_grad = dot(acts[side][1], out_narrow[...], ((1,), (0,)))
@@ -235,28 +235,31 @@
         narrow = grad.astype(NARROW)
         hidden[rows, :] = narrow
         out_grad = dot(narrow, in_narrow[...], ((1,), (1,)))
-        mixed = dot(activated, out_narrow[...], ((1,), (1,)))
-        scale_total = scale_total + jnp.sum(
-            mixed * acts[side][1].astype(WIDE), axis=0, keepdims=True
-        )
         if side:
-            send[0] = out_grad.astype(NARROW)
-            send[1] = mixed.astype(NARROW)
+            send[...] = out_grad.astype(NARROW)
         else:
-            keep[0] = out_grad
-            keep[1] = mixed
+            keep[...] = out_grad
     bias_part[...] = total
-    scale_part[...] = scale_total / scale[...]
 
 
 def weight_body(norm_scale, *refs):
-    acts, (active, hidden, holder) = refs[:2], refs[2:]
+    acts, (active, hidden, out_narrow, scale) = refs[:2], refs[2:6]
+    holder, keep, send, scale_part = refs[6:]
     half = acts[0].shape[1]
     first, second = pl.ds(0, half), pl.ds(half, half)
     for which, right in enumerate((hidden, active)):
         grad = dot(acts[0][which], right[first, :], ((0,), (0,)))
         grad = grad + dot(acts[1][which], right[second, :], ((0,), (0,)))
         holder[which] = norm_scale * grad
+    total = jnp.zeros_like(scale_part)
+    for side, rows in enumerate((first, second)):
+        mixed = dot(active[rows, :], out_narrow[...], ((1,), (1,)))
+        total = total + jnp.sum(mixed * acts[side][1].astype(WIDE), axis=0, keepdims=True)
+        if side:
+            send[...] = mixed.astype(NARROW)
+        else:
+            keep[...] = mixed
+    scale_part[...] = total / scale[...]
 
 
 def owners_body(turns, holder, after, *targets):
@@ -275,11 +278,10 @@
             target[4 * own + SMALL_ROWS :, :] = jnp.zeros((rest, target.shape[1]), target.dtype)
 
 
-def fold_body(kept, got, stay, leave, mixed_stay, mixed_leave):
+def fold_body(kept, got, stay, leave):
     size = stay.shape[0]
-    for which, (near, away) in enumerate(((stay, leave), (mixed_stay, mixed_leave))):
-        near[...] = kept[which, :size] + got[which, :size].astype(WIDE)
-        away[...] = (kept[which, size:] + got[which, size:].astype(WIDE)).astype(NARROW)
+    stay[...] = kept[:size] + got[:size].astype(WIDE)
+    leave[...] = (kept[size:] + got[size:].astype(WIDE)).astype(NARROW)
 
 
 def conv_grad_body(norm_scale, *refs):
@@ -465,6 +467,7 @@
         own,
         core_got,
         branch,
+        outer_got,
     )
     sent_got = swap(joined[2], 2)
     pieces = []
@@ -516,38 +519,43 @@
         lines = jnp.moveaxis(canonical(lines, me, bit_count), 1, 0)
         pieces = [lines.reshape(2, channels, quarter)]
     group = 4 * pixels
-    both = (2, 2 * pixels, channels)
-    keep, send, active, hidden, scale_part, in_bias_part = run(
+    keep, send, active, hidden, out_narrow, in_bias_part = run(
         functools.partial(hidden_body, copied),
         (
-            shaped(both),
-            shaped(both, NARROW),
+            shaped((2 * pixels, channels)),
+            shaped((2 * pixels, channels), NARROW),
             shaped((group, quarter), NARROW),
             shaped((group, quarter), NARROW),
-            shaped((1, channels)),
+            shaped((channels, quarter), NARROW),
             shaped((1, quarter)),
         ),
         acts,
         acts_got,
         in_bias_own,
-        scale,
         *pieces,
         scratch=(pltpu.VMEM((2, channels, quarter), NARROW),),
         mib=24,
     )
     half = (shaped((pixels, channels)), shaped((pixels, channels), NARROW))
-    out_stay, out_leave, mixed_stay, mixed_leave = run(fold_body, half * 2, keep, swap(send, 1))
+    out_stay, out_leave = run(fold_body, half, keep, swap(send, 1))
     out_got = swap(out_leave, 2)
 
-    holder = run(
+    holder, mixed_keep, mixed_send, scale_part = run(
         functools.partial(weight_body, norm_scale),
-        (shaped((2, channels, quarter)),),
+        (
+            shaped((2, channels, quarter)),
+            shaped((2 * pixels, channels)),
+            shaped((2 * pixels, channels), NARROW),
+            shaped((1, channels)),
+        ),
         acts,
         acts_got,
         active,
         hidden,
+        out_narrow,
+        scale,
         mib=24,
-    )[0]
+    )
     conv_grad, inner_out, rim_out, stay, leave = run(
         functools.partial(conv_grad_body, norm_scale),
         (
@@ -569,8 +577,6 @@
         in_bias_part,
         scratch=(padded, pltpu.VMEM((2, SMALL_ROWS, channels), WIDE)),
     )
-    rim_got = swap_rim(rim_out)
-    inner_got = swap(inner_out, 1)
     sums = stay + swap(leave, 1)
 
     far_turns = (*range(2 * patterns - 1, 4, -2), 3)
@@ -589,9 +595,13 @@
         flat = flat.reshape(2 * patterns, owned, quarter)
         parts = [flat[p].astype(NARROW) for p in far_turns]
     far_parts = [swap(part, 2 * p) for p, part in zip(far_turns, parts)]
-    sums, far_parts = lax.optimization_barrier((sums, far_parts))
+    sums, far_parts[0] = lax.optimization_barrier((sums, far_parts[0]))
     sums = sums + swap(sums, 2)
-    sums, mixed_leave = lax.optimization_barrier((sums, mixed_leave))
+    rim_got = swap_rim(rim_out)
+    inner_got = swap(inner_out, 1)
+    sums, far_parts, rim_got, inner_got = lax.optimization_barrier(
+        (sums, far_parts, rim_got, inner_got)
+    )
     if copied:
         joint = shaped((owned + 32, quarter), NARROW)
         *parts, side_part, near_own = run(
@@ -601,6 +611,7 @@
             holder,
             sums,
         )
+        parts, mixed_send = lax.optimization_barrier((parts, mixed_send))
         parts = [swap(part, 2 * p) for p, part in zip(near_turns, parts)]
         sums_parts = [part[owned : owned + SMALL_ROWS] for part in parts]
         near_parts = [part[:owned] for part in parts] + [swap(side_part, 2), near_own]
@@ -608,6 +619,7 @@
         near_parts = [swap(flat[p].astype(NARROW), 2 * p) for p in near_turns[:-1]] + [flat[0]]
         sums_parts = [swap(sums.astype(NARROW), 2 * p) for p in near_turns[:-2]]
 
+    mixed_stay, mixed_leave = run(fold_body, half, mixed_keep, swap(mixed_send, 1))
     input_grad = run(
         input_grad_body,
         (shaped(features.shape),),

time: 81.5 us -> 82 us (level)
  starting transfers between devices: 36.5 us -> 39.3 us
  waiting for transfers between devices: 30.4 us -> 27.6 us
    ppermute x2, waiting for transfers between devices: 8.9 us -> 2.29 us  [swap_rim(): return lax.ppermute(value, 'row', pairs + [(j, i) for i, j in pairs])]
    ppermute x2, starting transfers between devices: 4.4 us -> 0.98 us  [swap_group(): return lax.ppermute(value, 'grp', [(0, 1), (1, 0)])]
    ppermute x2, waiting for transfers between devices: 0.01 us -> 2.88 us  [swap_far(): return lax.ppermute(value, ('grp', 'row'), pairs)]
    ppermute x20 -> x21, starting transfers between devices: 21.9 us -> 24.6 us  [swap(): return lax.ppermute(value, 'row', [(i, i ^ bit) for i in range(count)])]
    ppermute x2, starting transfers between devices: 5.65 us -> 7.79 us  [swap_rim(): return lax.ppermute(value, 'row', pairs + [(j, i) for i, j in pairs])]
    ppermute x2, starting transfers between devices: 4.55 us -> 5.92 us  [swap_far(): return lax.ppermute(value, ('grp', 'row'), pairs)]
    ppermute x20 -> x21, waiting for transfers between devices: 17.4 us -> 18.3 us  [swap(): return lax.ppermute(value, 'row', [(i, i ^ bit) for i in range(count)])]
    pallas_call x14 -> x15, Pallas kernels: 13.1 us -> 13.1 us  [run(): pl.pallas_call(body, out_shape=outs, **extra, scratch_shapes=scratch, com...]
  transfers between devices with their start and end apart: 26 -> 27, of which waited for: 11 -> 12; matrix products, arithmetic and copies ran while one was open for 0% -> 0% of each run, Pallas kernels for 11% -> 11%
where the time goes in v8:
time: 82 us; the launch traced here: 80.9 us
  starting transfers between devices  39.3 us (48%)
  waiting for transfers between devices  27.6 us (34%)
  Pallas kernels  13.1 us (16%)
  between operations  0.86 us (1%)
    ppermute x21, starting transfers between devices, swap(): return lax.ppermute(value, 'row', [(i, i ^ bit) for i in range(count)])  24.6 us
    ppermute x21, waiting for transfers between devices, swap(): return lax.ppermute(value, 'row', [(i, i ^ bit) for i in range(count)])  18.3 us
    pallas_call x15, Pallas kernels, run(): pl.pallas_call(body, out_shape=outs, **extra, scratch_shapes=scratch, com...  13.1 us
    ppermute x2, starting transfers between devices, swap_rim(): return lax.ppermute(value, 'row', pairs + [(j, i) for i, j in pairs])  7.79 us
    ppermute x2, starting transfers between devices, swap_far(): return lax.ppermute(value, ('grp', 'row'), pairs)  5.92 us
    ppermute x2, waiting for transfers between devices, swap_group(): return lax.ppermute(value, 'grp', [(0, 1), (1, 0)])  4.1 us
    ppermute x2, waiting for transfers between devices, swap_far(): return lax.ppermute(value, ('grp', 'row'), pairs)  2.88 us
    ppermute x2, waiting for transfers between devices, swap_rim(): return lax.ppermute(value, 'row', pairs + [(j, i) for i, j in pairs])  2.29 us
  transfers between devices with their start and end apart: 27, of which 12 were waited for; matrix products, arithmetic and copies ran while one was open for 0% of the time, Pallas kernels for 11%

profile of v8, /device:TPU:1, one launch (start us, length us, event | category | flops | bytes accessed | tf_op | source)
XLA Modules:
  0.0 80.9 jit_solution(14043233588429242647)
XLA Ops:
  2.1 4.5 %collective-permute-start.1 = (bf16[96,512]{1,0:T(8,128)(2,1)S(1)}, bf16[96,512]{1,0:T(8,128)(2,1)S(1)}, u32[]{:S(2)}, u32[]{:S(2)}) collective-permute-start(bf16[96,512]{1,0:T(8,128)(2,1)S(1)} %get-tuple-element.89), channel_id=1, source_target_pairs={{1,2},{3,4},{5,6},{7,8},{9,10},{11,12},{13,14},{2,1},{4,3},{6,5},{... | collective-permute-start | bytes 294920 | tf_op jit(solution)/shard_map/ppermute | solution.py:28
  6.6 2.3 %collective-permute-done.1.outer.after.refs_7_ = bf16[96,512]{1,0:T(8,128)(2,1)S(1)} collective-permute-done((bf16[96,512]{1,0:T(8,128)(2,1)S(1)}, bf16[96,512]{1,0:T(8,128)(2,1)S(1)}, u32[]{:S(2)}, u32[]{:S(2)}) %collective-permute-start.1) | collective-permute-done | bytes 98336 | tf_op jit(solution)/shard_map/ppermute | solution.py:28
  8.9 4.8 %collective-permute-start.7 = (bf16[2,2,32,512]{3,2,1,0:T(8,128)(2,1)S(1)}, bf16[2,2,32,512]{3,2,1,0:T(8,128)(2,1)S(1)}, u32[]{:S(2)}, u32[]{:S(2)}) collective-permute-start(bf16[2,2,32,512]{3,2,1,0:T(8,128)(2,1)S(1)} %get-tuple-element.98), channel_id=1, source_target_pairs={{0,10},{1,11},{2,8},{3,9},{4,14},{5,15},{6,12},{7,13},{8,2},{9,3},... | collective-permute-start | bytes 393224 | tf_op jit(solution)/shard_map/ppermute | solution.py:41
  13.7 1.4 %collective-permute-start.6 = (bf16[2,2,32,512]{3,2,1,0:T(8,128)(2,1)S(1)}, bf16[2,2,32,512]{3,2,1,0:T(8,128)(2,1)S(1)}, u32[]{:S(2)}, u32[]{:S(2)}) collective-permute-start(bf16[2,2,32,512]{3,2,1,0:T(8,128)(2,1)S(1)} %get-tuple-element.98), channel_id=1, source_target_pairs={{0,6},{1,7},{2,4},{3,5},{4,2},{5,3},{6,0},{7,1},{8,14},{9,15},{10,... | collective-permute-start | bytes 393224 | tf_op jit(solution)/shard_map/ppermute | solution.py:22
  16.4 2.4 %shard_map.161 = (f32[128,512]{1,0:T(8,128)S(1)}, f32[128,128]{1,0:T(8,128)S(1)}, bf16[128,512]{1,0:T(8,128)(2,1)S(1)}) custom-call(f32[4,32,512]{2,1,0:T(8,128)S(1)} %get-tuple-element.87.feats.refs_5_, bf16[224,512]{1,0:T(8,128)(2,1)S(1)} %collective-permute-done.core_got.other.refs_6_, bf16[96,512]{1,0:T(8,128)(2,1)S(1)} %collective-permute-done.1.outer.after.refs_7_, ...), custom_call_target="tpu_custom_call" | custom-call | tf_op jit(solution)/shard_map/pallas_call | solution.py:53
  19.8 1.4 %collective-permute-start.2 = (bf16[128,512]{1,0:T(8,128)(2,1)S(1)}, bf16[128,512]{1,0:T(8,128)(2,1)S(1)}, u32[]{:S(2)}, u32[]{:S(2)}) collective-permute-start(bf16[128,512]{1,0:T(8,128)(2,1)S(1)} %get-tuple-element.93.normed), channel_id=1, source_target_pairs={{0,2},{1,3},{2,0},{3,1},{4,6},{5,7},{6,4},{7,5},{8,10},{9,11},{10,... | collective-permute-start | bytes 393224 | tf_op jit(solution)/shard_map/ppermute | solution.py:22
  21.2 2.6 %collective-permute-done.6.refs_2_.refs_8_ = bf16[2,2,32,512]{3,2,1,0:T(8,128)(2,1)S(1)} collective-permute-done((bf16[2,2,32,512]{3,2,1,0:T(8,128)(2,1)S(1)}, bf16[2,2,32,512]{3,2,1,0:T(8,128)(2,1)S(1)}, u32[]{:S(2)}, u32[]{:S(2)}) %collective-permute-start.6) | collective-permute-done | bytes 131104 | tf_op jit(solution)/shard_map/ppermute | solution.py:22
  23.8 1.9 %collective-permute-done.5.refs_1_.refs_5_ = bf16[2,2,32,512]{3,2,1,0:T(8,128)(2,1)S(1)} collective-permute-done((bf16[2,2,32,512]{3,2,1,0:T(8,128)(2,1)S(1)}, bf16[2,2,32,512]{3,2,1,0:T(8,128)(2,1)S(1)}, u32[]{:S(2)}, u32[]{:S(2)}) %collective-permute-start.5) | collective-permute-done | bytes 131104 | tf_op jit(solution)/shard_map/ppermute | solution.py:41
  26.1 3.1 %collective-permute-done.2.normed_got = bf16[128,512]{1,0:T(8,128)(2,1)S(1)} collective-permute-done((bf16[128,512]{1,0:T(8,128)(2,1)S(1)}, bf16[128,512]{1,0:T(8,128)(2,1)S(1)}, u32[]{:S(2)}, u32[]{:S(2)}) %collective-permute-start.2) | collective-permute-done | bytes 131104 | tf_op jit(solution)/shard_map/ppermute | solution.py:22
  30.8 4.1 %collective-permute-done.10.refs_6_ = bf16[2,2,32,512]{3,2,1,0:T(8,128)(2,1)S(1)} collective-permute-done((bf16[2,2,32,512]{3,2,1,0:T(8,128)(2,1)S(1)}, bf16[2,2,32,512]{3,2,1,0:T(8,128)(2,1)S(1)}, u32[]{:S(2)}, u32[]{:S(2)}) %collective-permute-start.10) | collective-permute-done | bytes 131104 | tf_op jit(solution)/shard_map/ppermute | solution.py:45
  34.9 1.4 %shard_map.164 = (f32[256,512]{1,0:T(8,128)S(1)}, bf16[256,512]{1,0:T(8,128)(2,1)S(1)}, bf16[512,512]{1,0:T(8,128)(2,1)S(1)}, bf16[512,512]{1,0:T(8,128)(2,1)S(1...) custom-call(bf16[2,256,512]{2,1,0:T(8,128)(2,1)S(1)} %get-tuple-element.99.refs_0_, ...), custom_call_target="tpu_custom_call" | custom-call | tf_op jit(solution)/shard_map/pallas_call | solution.py:53
  38.5 1.4 %collective-permute-start.12 = (bf16[128,512]{1,0:T(8,128)(2,1)S(1)}, bf16[128,512]{1,0:T(8,128)(2,1)S(1)}, u32[]{:S(2)}, u32[]{:S(2)}) collective-permute-start(bf16[128,512]{1,0:T(8,128)(2,1)S(1)} %get-tuple-element.105.after), channel_id=1, source_target_pairs={{0,2},{1,3},{2,0},{3,1},{4,6},{5,7},{6,4},{7,5},{8,10},{9,11},{10,... | collective-permute-start | bytes 393224 | tf_op jit(solution)/shard_map/ppermute | solution.py:22
  41.0 2.3 %collective-permute-start.14 = (bf16[128,512]{1,0:T(8,128)(2,1)S(1)}, bf16[128,512]{1,0:T(8,128)(2,1)S(1)}, u32[]{:S(2)}, u32[]{:S(2)}) collective-permute-start(bf16[128,512]{1,0:T(8,128)(2,1)S(1)} %get-tuple-element.117), channel_id=1, source_target_pairs={{0,14},{1,15},{2,12},{3,13},{4,10},{5,11},{6,8},{7,9},{8,6},{9,7},... | collective-permute-start | bytes 393224 | tf_op jit(solution)/shard_map/ppermute | solution.py:22
  43.3 1.9 %shard_map.167 = (f32[128,512]{1,0:T(8,128)S(1)}, bf16[96,512]{1,0:T(8,128)(2,1)S(1)}, bf16[96,512]{1,0:T(8,128)(2,1)S(1)}, f32[28,512]{1,0:T(8,128)S(1)}, f32[28,512]{1,0:T(8,128)S(1)}) custom-call(f32[128,512]{1,0:T(8,128)S(1)} %get-tuple-element.104.refs_0_, bf16[128,512]{1,0:T(8,128)(2,1)S(1)} %collective-permute-done.12.refs_1_, ...), custom_call_target="tpu_custom_call" | custom-call | tf_op jit(solution)/shard_map/pallas_call | solution.py:53
  46.5 2.6 %collective-permute-start.16 = (bf16[128,512]{1,0:T(8,128)(2,1)S(1)}, bf16[128,512]{1,0:T(8,128)(2,1)S(1)}, u32[]{:S(2)}, u32[]{:S(2)}) collective-permute-start(bf16[128,512]{1,0:T(8,128)(2,1)S(1)} %get-tuple-element.120), channel_id=1, source_target_pairs={{0,10},{1,11},{2,8},{3,9},{4,14},{5,15},{6,12},{7,13},{8,2},{9,3},... | collective-permute-start | bytes 393224 | tf_op jit(solution)/shard_map/ppermute | solution.py:22
  50.1 3.3 %collective-permute-start.18 = (bf16[96,512]{1,0:T(8,128)(2,1)S(1)}, bf16[96,512]{1,0:T(8,128)(2,1)S(1)}, u32[]{:S(2)}, u32[]{:S(2)}) collective-permute-start(bf16[96,512]{1,0:T(8,128)(2,1)S(1)} %get-tuple-element.122), channel_id=1, source_target_pairs={{1,2},{3,4},{5,6},{7,8},{9,10},{11,12},{13,14},{2,1},{4,3},{6,5},{... | collective-permute-start | bytes 294920 | tf_op jit(solution)/shard_map/ppermute | solution.py:28
  53.5 1.3 %collective-permute-start.15 = (f32[28,512]{1,0:T(8,128)S(1)}, f32[28,512]{1,0:T(8,128)S(1)}, u32[]{:S(2)}, u32[]{:S(2)}) collective-permute-start(f32[28,512]{1,0:T(8,128)S(1)} %add.6), channel_id=1, source_target_pairs={{0,2},{1,3},{2,0},{3,1},{4,6},{5,7},{6,4},{7,5},{8,10},{9,11},{10,... | collective-permute-start | bytes 172040 | tf_op jit(solution)/shard_map/ppermute | solution.py:22
  54.9 4.4 %collective-permute-done.15 = f32[28,512]{1,0:T(8,128)S(1)} collective-permute-done((f32[28,512]{1,0:T(8,128)S(1)}, f32[28,512]{1,0:T(8,128)S(1)}, u32[]{:S(2)}, u32[]{:S(2)}) %collective-permute-start.15) | collective-permute-done | bytes 57376 | tf_op jit(solution)/shard_map/ppermute | solution.py:22
  60.0 4.3 %collective-permute-start.20 = (bf16[160,512]{1,0:T(8,128)(2,1)S(1)}, bf16[160,512]{1,0:T(8,128)(2,1)S(1)}, u32[]{:S(2)}, u32[]{:S(2)}) collective-permute-start(bf16[160,512]{1,0:T(8,128)(2,1)S(1)} %get-tuple-element.132), channel_id=1, source_target_pairs={{0,8},{1,9},{2,10},{3,11},{4,12},{5,13},{6,14},{7,15},{8,0},{9,1},... | collective-permute-start | bytes 491528 | tf_op jit(solution)/shard_map/ppermute | solution.py:22
  64.3 2.1 %collective-permute-start.21 = (bf16[160,512]{1,0:T(8,128)(2,1)S(1)}, bf16[160,512]{1,0:T(8,128)(2,1)S(1)}, u32[]{:S(2)}, u32[]{:S(2)}) collective-permute-start(bf16[160,512]{1,0:T(8,128)(2,1)S(1)} %get-tuple-element.133), channel_id=1, source_target_pairs={{0,12},{1,13},{2,14},{3,15},{4,8},{5,9},{6,10},{7,11},{8,4},{9,5},... | collective-permute-start | bytes 491528 | tf_op jit(solution)/shard_map/ppermute | solution.py:22
  66.5 1.5 %collective-permute-start.23 = (bf16[128,512]{1,0:T(8,128)(2,1)S(1)}, bf16[128,512]{1,0:T(8,128)(2,1)S(1)}, u32[]{:S(2)}, u32[]{:S(2)}) collective-permute-start(bf16[128,512]{1,0:T(8,128)(2,1)S(1)} %get-tuple-element.135), channel_id=1, source_target_pairs={{0,2},{1,3},{2,0},{3,1},{4,6},{5,7},{6,4},{7,5},{8,10},{9,11},{10,... | collective-permute-start | bytes 393224 | tf_op jit(solution)/shard_map/ppermute | solution.py:22
  68.0 2.9 %shard_map.170 = f32[4,32,512]{2,1,0:T(8,128)} custom-call(f32[128,512]{1,0:T(8,128)S(1)} %get-tuple-element.137.grad, bf16[96,512]{1,0:T(8,128)(2,1)S(1)} %collective-permute-done.19.inner, bf16[96,512]{1,0:T(8,128)(2,1)S(1)} %collective-permute-done.18.outer, f32[7,7,512]{2,1,0:T(8,128)S(1)} %get-tuple-element.90.kernel, ...), custom_call_target="tpu_custom_call" | custom-call | tf_op jit(solution)/shard_map/pallas_call | solution.py:53
  70.8 5.0 %collective-permute-done.20 = bf16[160,512]{1,0:T(8,128)(2,1)S(1)} collective-permute-done((bf16[160,512]{1,0:T(8,128)(2,1)S(1)}, bf16[160,512]{1,0:T(8,128)(2,1)S(1)}, u32[]{:S(2)}, u32[]{:S(2)}) %collective-permute-start.20) | collective-permute-done | bytes 163872 | tf_op jit(solution)/shard_map/ppermute | solution.py:22
  77.2 1.6 %collective-permute-start.26 = (f32[156,512]{1,0:T(8,128)S(1)}, f32[156,512]{1,0:T(8,128)S(1)}, u32[]{:S(2)}, u32[]{:S(2)}) collective-permute-start(f32[156,512]{1,0:T(8,128)S(1)} %get-tuple-element.156), channel_id=1, source_target_pairs={{0,1},{1,0},{2,3},{3,2},{4,5},{5,4},{6,7},{7,6},{8,9},{9,8},{10,11... | collective-permute-start | bytes 958472 | tf_op jit(solution)/shard_map/ppermute | solution.py:22
  (53 shorter events, 15.4 us)
Async XLA Ops:
  2.0 6.9 %collective-permute-start = (bf16[224,512]{1,0:T(8,128)(2,1)S(1)}, bf16[224,512]{1,0:T(8,128)(2,1)S(1)}, u32[]{:S(2)}, u32[]{:S(2)}) collective-permute-start(bf16[224,512]{1,0:T(8,128)(2,1)S(1)} %get-tuple-element.88), channel_id=1, source_target_pairs={{0,1},{1,0},{2,3},{3,2},{4,5},{5,4},{6,7},{7,6},{8,9},{9,8},{10,11... | collective-permute-start | bytes 688136 | tf_op jit(solution)/shard_map/ppermute | solution.py:22
  2.1 6.8 %collective-permute-start.1 = (bf16[96,512]{1,0:T(8,128)(2,1)S(1)}, bf16[96,512]{1,0:T(8,128)(2,1)S(1)}, u32[]{:S(2)}, u32[]{:S(2)}) collective-permute-start(bf16[96,512]{1,0:T(8,128)(2,1)S(1)} %get-tuple-element.89), channel_id=1, source_target_pairs={{1,2},{3,4},{5,6},{7,8},{9,10},{11,12},{13,14},{2,1},{4,3},{6,5},{... | collective-permute-start | bytes 294920 | tf_op jit(solution)/shard_map/ppermute | solution.py:28
  8.9 10.9 %collective-permute-start.7 = (bf16[2,2,32,512]{3,2,1,0:T(8,128)(2,1)S(1)}, bf16[2,2,32,512]{3,2,1,0:T(8,128)(2,1)S(1)}, u32[]{:S(2)}, u32[]{:S(2)}) collective-permute-start(bf16[2,2,32,512]{3,2,1,0:T(8,128)(2,1)S(1)} %get-tuple-element.98), channel_id=1, source_target_pairs={{0,10},{1,11},{2,8},{3,9},{4,14},{5,15},{6,12},{7,13},{8,2},{9,3},... | collective-permute-start | bytes 393224 | tf_op jit(solution)/shard_map/ppermute | solution.py:41
  13.7 10.1 %collective-permute-start.6 = (bf16[2,2,32,512]{3,2,1,0:T(8,128)(2,1)S(1)}, bf16[2,2,32,512]{3,2,1,0:T(8,128)(2,1)S(1)}, u32[]{:S(2)}, u32[]{:S(2)}) collective-permute-start(bf16[2,2,32,512]{3,2,1,0:T(8,128)(2,1)S(1)} %get-tuple-element.98), channel_id=1, source_target_pairs={{0,6},{1,7},{2,4},{3,5},{4,2},{5,3},{6,0},{7,1},{8,14},{9,15},{10,... | collective-permute-start | bytes 393224 | tf_op jit(solution)/shard_map/ppermute | solution.py:22
  15.2 14.0 %collective-permute-start.3 = (bf16[256,512]{1,0:T(8,128)(2,1)S(1)}, bf16[256,512]{1,0:T(8,128)(2,1)S(1)}, u32[]{:S(2)}, u32[]{:S(2)}) collective-permute-start(bf16[256,512]{1,0:T(8,128)(2,1)S(1)} %get-tuple-element.96), channel_id=1, source_target_pairs={{0,2},{1,3},{2,0},{3,1},{4,6},{5,7},{6,4},{7,5},{8,10},{9,11},{10,... | collective-permute-start | bytes 786440 | tf_op jit(solution)/shard_map/ppermute | solution.py:22
  15.2 10.6 %collective-permute-start.5 = (bf16[2,2,32,512]{3,2,1,0:T(8,128)(2,1)S(1)}, bf16[2,2,32,512]{3,2,1,0:T(8,128)(2,1)S(1)}, u32[]{:S(2)}, u32[]{:S(2)}) collective-permute-start(bf16[2,2,32,512]{3,2,1,0:T(8,128)(2,1)S(1)} %get-tuple-element.97.refs_3_), channel_id=1, source_target_pairs={{0,8},{1,9},{2,10},{3,11},{4,12},{5,13},{6,14},{7,15},{8,0},{9,1},... | collective-permute-start | bytes 393224 | tf_op jit(solution)/shard_map/ppermute | solution.py:41
  16.3 9.8 %collective-permute-start.4 = (bf16[2,2,32,512]{3,2,1,0:T(8,128)(2,1)S(1)}, bf16[2,2,32,512]{3,2,1,0:T(8,128)(2,1)S(1)}, u32[]{:S(2)}, u32[]{:S(2)}) collective-permute-start(bf16[2,2,32,512]{3,2,1,0:T(8,128)(2,1)S(1)} %get-tuple-element.97.refs_3_), channel_id=1, source_target_pairs={{0,4},{1,5},{2,6},{3,7},{4,0},{5,1},{6,2},{7,3},{8,12},{9,13},{10,... | collective-permute-start | bytes 393224 | tf_op jit(solution)/shard_map/ppermute | solution.py:22
  19.8 9.4 %collective-permute-start.2 = (bf16[128,512]{1,0:T(8,128)(2,1)S(1)}, bf16[128,512]{1,0:T(8,128)(2,1)S(1)}, u32[]{:S(2)}, u32[]{:S(2)}) collective-permute-start(bf16[128,512]{1,0:T(8,128)(2,1)S(1)} %get-tuple-element.93.normed), channel_id=1, source_target_pairs={{0,2},{1,3},{2,0},{3,1},{4,6},{5,7},{6,4},{7,5},{8,10},{9,11},{10,... | collective-permute-start | bytes 393224 | tf_op jit(solution)/shard_map/ppermute | solution.py:22
  23.8 5.3 %collective-permute-start.8 = (bf16[2,2,32,512]{3,2,1,0:T(8,128)(2,1)S(1)}, bf16[2,2,32,512]{3,2,1,0:T(8,128)(2,1)S(1)}, u32[]{:S(2)}, u32[]{:S(2)}) collective-permute-start(bf16[2,2,32,512]{3,2,1,0:T(8,128)(2,1)S(1)} %collective-permute-done.7.refs_3_.refs_9_), channel_id=1, source_target_pairs={{0,16},{16,0},{1,17},{17,1},{2,18},{18,2},{3,19},{19,3},{4,20},{20... | collective-permute-start | bytes 393224 | tf_op jit(solution)/shard_map/ppermute | solution.py:45
  29.2 5.7 %collective-permute-start.9 = (bf16[2,256,512]{2,1,0:T(8,128)(2,1)S(1)}, bf16[2,256,512]{2,1,0:T(8,128)(2,1)S(1)}, u32[]{:S(2)}, u32[]{:S(2)}) collective-permute-start(bf16[2,256,512]{2,1,0:T(8,128)(2,1)S(1)} %get-tuple-element.99.refs_0_), channel_id=1, source_target_pairs={{0,1},{1,0},{2,3},{3,2},{4,5},{5,4},{6,7},{7,6},{8,9},{9,8},{10,11... | collective-permute-start | bytes 1572872 | tf_op jit(solution)/shard_map/ppermute | solution.py:22
  29.8 5.1 %collective-permute-start.10 = (bf16[2,2,32,512]{3,2,1,0:T(8,128)(2,1)S(1)}, bf16[2,2,32,512]{3,2,1,0:T(8,128)(2,1)S(1)}, u32[]{:S(2)}, u32[]{:S(2)}) collective-permute-start(bf16[2,2,32,512]{3,2,1,0:T(8,128)(2,1)S(1)} %collective-permute-done.5.refs_1_.refs_5_), channel_id=1, source_target_pairs={{0,16},{16,0},{1,17},{17,1},{2,18},{18,2},{3,19},{19,3},{4,20},{20... | collective-permute-start | bytes 393224 | tf_op jit(solution)/shard_map/ppermute | solution.py:45
  41.0 12.5 %collective-permute-start.14 = (bf16[128,512]{1,0:T(8,128)(2,1)S(1)}, bf16[128,512]{1,0:T(8,128)(2,1)S(1)}, u32[]{:S(2)}, u32[]{:S(2)}) collective-permute-start(bf16[128,512]{1,0:T(8,128)(2,1)S(1)} %get-tuple-element.117), channel_id=1, source_target_pairs={{0,14},{1,15},{2,12},{3,13},{4,10},{5,11},{6,8},{7,9},{8,6},{9,7},... | collective-permute-start | bytes 393224 | tf_op jit(solution)/shard_map/ppermute | solution.py:22
  45.3 8.1 %collective-permute-start.13 = (f32[28,512]{1,0:T(8,128)S(1)}, f32[28,512]{1,0:T(8,128)S(1)}, u32[]{:S(2)}, u32[]{:S(2)}) collective-permute-start(f32[28,512]{1,0:T(8,128)S(1)} %get-tuple-element.115), channel_id=1, source_target_pairs={{0,1},{1,0},{2,3},{3,2},{4,5},{5,4},{6,7},{7,6},{8,9},{9,8},{10,11... | collective-permute-start | bytes 172040 | tf_op jit(solution)/shard_map/ppermute | solution.py:22
  46.5 12.8 %collective-permute-start.16 = (bf16[128,512]{1,0:T(8,128)(2,1)S(1)}, bf16[128,512]{1,0:T(8,128)(2,1)S(1)}, u32[]{:S(2)}, u32[]{:S(2)}) collective-permute-start(bf16[128,512]{1,0:T(8,128)(2,1)S(1)} %get-tuple-element.120), channel_id=1, source_target_pairs={{0,10},{1,11},{2,8},{3,9},{4,14},{5,15},{6,12},{7,13},{8,2},{9,3},... | collective-permute-start | bytes 393224 | tf_op jit(solution)/shard_map/ppermute | solution.py:22
  49.1 10.2 %collective-permute-start.17 = (bf16[128,512]{1,0:T(8,128)(2,1)S(1)}, bf16[128,512]{1,0:T(8,128)(2,1)S(1)}, u32[]{:S(2)}, u32[]{:S(2)}) collective-permute-start(bf16[128,512]{1,0:T(8,128)(2,1)S(1)} %get-tuple-element.121), channel_id=1, source_target_pairs={{0,6},{1,7},{2,4},{3,5},{4,2},{5,3},{6,0},{7,1},{8,14},{9,15},{10,... | collective-permute-start | bytes 393224 | tf_op jit(solution)/shard_map/ppermute | solution.py:22
  50.1 9.2 %collective-permute-start.18 = (bf16[96,512]{1,0:T(8,128)(2,1)S(1)}, bf16[96,512]{1,0:T(8,128)(2,1)S(1)}, u32[]{:S(2)}, u32[]{:S(2)}) collective-permute-start(bf16[96,512]{1,0:T(8,128)(2,1)S(1)} %get-tuple-element.122), channel_id=1, source_target_pairs={{1,2},{3,4},{5,6},{7,8},{9,10},{11,12},{13,14},{2,1},{4,3},{6,5},{... | collective-permute-start | bytes 294920 | tf_op jit(solution)/shard_map/ppermute | solution.py:28
  53.4 5.9 %collective-permute-start.19 = (bf16[96,512]{1,0:T(8,128)(2,1)S(1)}, bf16[96,512]{1,0:T(8,128)(2,1)S(1)}, u32[]{:S(2)}, u32[]{:S(2)}) collective-permute-start(bf16[96,512]{1,0:T(8,128)(2,1)S(1)} %get-tuple-element.123), channel_id=1, source_target_pairs={{0,1},{1,0},{2,3},{3,2},{4,5},{5,4},{6,7},{7,6},{8,9},{9,8},{10,11... | collective-permute-start | bytes 294920 | tf_op jit(solution)/shard_map/ppermute | solution.py:22
  53.5 5.8 %collective-permute-start.15 = (f32[28,512]{1,0:T(8,128)S(1)}, f32[28,512]{1,0:T(8,128)S(1)}, u32[]{:S(2)}, u32[]{:S(2)}) collective-permute-start(f32[28,512]{1,0:T(8,128)S(1)} %add.6), channel_id=1, source_target_pairs={{0,2},{1,3},{2,0},{3,1},{4,6},{5,7},{6,4},{7,5},{8,10},{9,11},{10,... | collective-permute-start | bytes 172040 | tf_op jit(solution)/shard_map/ppermute | solution.py:22
  59.4 6.9 %collective-permute-start.24 = (bf16[256,512]{1,0:T(8,128)(2,1)S(1)}, bf16[256,512]{1,0:T(8,128)(2,1)S(1)}, u32[]{:S(2)}, u32[]{:S(2)}) collective-permute-start(bf16[256,512]{1,0:T(8,128)(2,1)S(1)} %get-tuple-element.142), channel_id=1, source_target_pairs={{0,1},{1,0},{2,3},{3,2},{4,5},{5,4},{6,7},{7,6},{8,9},{9,8},{10,11... | collective-permute-start | bytes 786440 | tf_op jit(solution)/shard_map/ppermute | solution.py:22
  60.0 15.9 %collective-permute-start.20 = (bf16[160,512]{1,0:T(8,128)(2,1)S(1)}, bf16[160,512]{1,0:T(8,128)(2,1)S(1)}, u32[]{:S(2)}, u32[]{:S(2)}) collective-permute-start(bf16[160,512]{1,0:T(8,128)(2,1)S(1)} %get-tuple-element.132), channel_id=1, source_target_pairs={{0,8},{1,9},{2,10},{3,11},{4,12},{5,13},{6,14},{7,15},{8,0},{9,1},... | collective-permute-start | bytes 491528 | tf_op jit(solution)/shard_map/ppermute | solution.py:22
  64.3 11.6 %collective-permute-start.21 = (bf16[160,512]{1,0:T(8,128)(2,1)S(1)}, bf16[160,512]{1,0:T(8,128)(2,1)S(1)}, u32[]{:S(2)}, u32[]{:S(2)}) collective-permute-start(bf16[160,512]{1,0:T(8,128)(2,1)S(1)} %get-tuple-element.133), channel_id=1, source_target_pairs={{0,12},{1,13},{2,14},{3,15},{4,8},{5,9},{6,10},{7,11},{8,4},{9,5},... | collective-permute-start | bytes 491528 | tf_op jit(solution)/shard_map/ppermute | solution.py:22
  66.3 9.9 %collective-permute-start.22 = (bf16[160,512]{1,0:T(8,128)(2,1)S(1)}, bf16[160,512]{1,0:T(8,128)(2,1)S(1)}, u32[]{:S(2)}, u32[]{:S(2)}) collective-permute-start(bf16[160,512]{1,0:T(8,128)(2,1)S(1)} %get-tuple-element.134), channel_id=1, source_target_pairs={{0,4},{1,5},{2,6},{3,7},{4,0},{5,1},{6,2},{7,3},{8,12},{9,13},{10,... | collective-permute-start | bytes 491528 | tf_op jit(solution)/shard_map/ppermute | solution.py:22
  66.4 9.9 %collective-permute-start.25 = (bf16[128,512]{1,0:T(8,128)(2,1)S(1)}, bf16[128,512]{1,0:T(8,128)(2,1)S(1)}, u32[]{:S(2)}, u32[]{:S(2)}) collective-permute-start(bf16[128,512]{1,0:T(8,128)(2,1)S(1)} %get-tuple-element.144), channel_id=1, source_target_pairs={{0,2},{1,3},{2,0},{3,1},{4,6},{5,7},{6,4},{7,5},{8,10},{9,11},{10,... | collective-permute-start | bytes 393224 | tf_op jit(solution)/shard_map/ppermute | solution.py:22
  66.5 10.6 %collective-permute-start.23 = (bf16[128,512]{1,0:T(8,128)(2,1)S(1)}, bf16[128,512]{1,0:T(8,128)(2,1)S(1)}, u32[]{:S(2)}, u32[]{:S(2)}) collective-permute-start(bf16[128,512]{1,0:T(8,128)(2,1)S(1)} %get-tuple-element.135), channel_id=1, source_target_pairs={{0,2},{1,3},{2,0},{3,1},{4,6},{5,7},{6,4},{7,5},{8,10},{9,11},{10,... | collective-permute-start | bytes 393224 | tf_op jit(solution)/shard_map/ppermute | solution.py:22
  (3 other events, 9.8 us)

commit v9 on v8

--- a/solution.py
+++ b/solution.py
@@ -96,9 +96,9 @@
                 else:
                     core[pl.ds((2 * side + which) * own_rows, own_rows), :] = value
     copies[0].wait()
-    first = feats[:RIM].astype(NARROW).reshape(RIM * cols, channels)
-    last = feats[rows - RIM :].astype(NARROW).reshape(RIM * cols, channels)
-    core[4 * own_rows :, :] = jnp.where(even, last, first)
+    first = feats[:RIM].reshape(RIM * cols, channels)
+    last = feats[rows - RIM :].reshape(RIM * cols, channels)
+    core[4 * own_rows :, :] = jnp.where(even, last, first).astype(NARROW)
     outer[...] = jnp.where(even, first, last)
     copies[1].wait()
     copies[2].wait()
@@ -110,8 +110,7 @@
         copy.wait()
 
 
-def join_body(mine, other, branch, after, *targets):
-    del after
+def join_body(mine, other, branch, *targets):
     own = mine.shape[2]
     sent = targets[2]
     pixels = branch.shape[0]
@@ -441,7 +440,7 @@
         (
             shaped((2,) + piece, NARROW),
             shaped((4 * own_rows + rim, channels), NARROW),
-            shaped((rim, channels), NARROW),
+            shaped((rim, channels)),
             shaped((pixels, channels), NARROW),
             shaped((1, quarter)),
         )
@@ -467,7 +466,6 @@
         own,
         core_got,
         branch,
-        outer_got,
     )
     sent_got = swap(joined[2], 2)
     pieces = []
@@ -493,7 +491,7 @@
         bias,
         scratch=(padded, pltpu.VMEM((pixels, channels), WIDE)),
     )
-    first_blocks = [block for k, block in enumerate(pieces) if k % each and k != each - 1]
+    first_blocks = [block for k, block in enumerate(pieces) if k % each]
     acts, pieces[each] = run(
         acts_body,
         (shaped((2, 2 * pixels, channels), NARROW), full_shape),
@@ -579,8 +577,8 @@
     )
     sums = stay + swap(leave, 1)
 
-    far_turns = (*range(2 * patterns - 1, 4, -2), 3)
-    near_turns = (*range(4, 2 * patterns, 2), 2, 1, 0)
+    far_turns = tuple(range(2 * patterns - 1, 4, -2))
+    near_turns = (*range(4, 2 * patterns, 2), 2, 3, 1, 0)
     owned = 4 * own_rows
     if copied:
         parts = run(
@@ -597,29 +595,37 @@
     far_parts = [swap(part, 2 * p) for p, part in zip(far_turns, parts)]
     sums, far_parts[0] = lax.optimization_barrier((sums, far_parts[0]))
     sums = sums + swap(sums, 2)
-    rim_got = swap_rim(rim_out)
-    inner_got = swap(inner_out, 1)
-    sums, far_parts, rim_got, inner_got = lax.optimization_barrier(
-        (sums, far_parts, rim_got, inner_got)
-    )
+    sums, far_parts = lax.optimization_barrier((sums, far_parts))
+    joint = shaped((owned + 32, quarter), NARROW)
+    plain = shaped((owned, quarter), NARROW)
     if copied:
-        joint = shaped((owned + 32, quarter), NARROW)
-        *parts, side_part, near_own = run(
-            functools.partial(owners_body, near_turns),
-            (joint,) * (len(near_turns) - 2)
-            + (shaped((owned, quarter), NARROW), shaped((owned, quarter))),
+        first_joint = run(
+            functools.partial(owners_body, near_turns[:-4]),
+            (joint,) * (len(near_turns) - 4),
             holder,
             sums,
         )
-        parts, mixed_send = lax.optimization_barrier((parts, mixed_send))
-        parts = [swap(part, 2 * p) for p, part in zip(near_turns, parts)]
+    rim_got = swap_rim(rim_out)
+    inner_got = swap(inner_out, 1)
+    mixed_stay, mixed_leave = run(fold_body, half, mixed_keep, swap(mixed_send, 1))
+    mixed_got = swap(mixed_leave, 2)
+    sums, rim_got, inner_got, mixed_got = lax.optimization_barrier(
+        (sums, rim_got, inner_got, mixed_got)
+    )
+    if copied:
+        next_joint, *plains, near_own = run(
+            functools.partial(owners_body, near_turns[-4:]),
+            (joint, plain, plain, shaped((owned, quarter))),
+            holder,
+            sums,
+        )
+        parts = [swap(part, 2 * p) for p, part in zip(near_turns, (*first_joint, next_joint))]
         sums_parts = [part[owned : owned + SMALL_ROWS] for part in parts]
-        near_parts = [part[:owned] for part in parts] + [swap(side_part, 2), near_own]
+        near_parts = [part[:owned] for part in parts]
+        near_parts += [swap(plains[0], 6), swap(plains[1], 2), near_own]
     else:
         near_parts = [swap(flat[p].astype(NARROW), 2 * p) for p in near_turns[:-1]] + [flat[0]]
-        sums_parts = [swap(sums.astype(NARROW), 2 * p) for p in near_turns[:-2]]
-
-    mixed_stay, mixed_leave = run(fold_body, half, mixed_keep, swap(mixed_send, 1))
+        sums_parts = [swap(sums.astype(NARROW), 2 * p) for p in near_turns[:-3]]
     input_grad = run(
         input_grad_body,
         (shaped(features.shape),),
@@ -636,7 +642,7 @@
         feats,
         scale,
         mixed_stay,
-        swap(mixed_leave, 2),
+        mixed_got,
     )[0]
     parts = list(far_parts) + near_parts
     parts, input_grad, output = lax.optimization_barrier((parts, input_grad, output))

time: 82 us -> 81.8 us (level)
  starting transfers between devices: 39.3 us -> 40.8 us
  waiting for transfers between devices: 27.6 us -> 26.4 us
    ppermute x21, starting transfers between devices: 24.6 us -> 28.6 us  [swap(): return lax.ppermute(value, 'row', [(i, i ^ bit) for i in range(count)])]
    ppermute x2, waiting for transfers between devices: 2.88 us -> 0.01 us  [swap_far(): return lax.ppermute(value, ('grp', 'row'), pairs)]
    ppermute x21, waiting for transfers between devices: 18.3 us -> 21.1 us  [swap(): return lax.ppermute(value, 'row', [(i, i ^ bit) for i in range(count)])]
    ppermute x2, starting transfers between devices: 5.92 us -> 3.41 us  [swap_far(): return lax.ppermute(value, ('grp', 'row'), pairs)]
    ppermute x2, waiting for transfers between devices: 4.1 us -> 2.69 us  [swap_group(): return lax.ppermute(value, 'grp', [(0, 1), (1, 0)])]
    pallas_call x15 -> x16, Pallas kernels: 13.1 us -> 13.1 us  [run(): pl.pallas_call(body, out_shape=outs, **extra, scratch_shapes=scratch, com...]
  transfers between devices with their start and end apart: 27 -> 27, of which waited for: 12 -> 9; matrix products, arithmetic and copies ran while one was open for 0% -> 0% of each run, Pallas kernels for 11% -> 11%
where the time goes in v9:
time: 81.8 us; the launch traced here: 81.3 us
  starting transfers between devices  40.8 us (50%)
  waiting for transfers between devices  26.4 us (32%)
  Pallas kernels  13.1 us (16%)
  between operations  0.91 us (1%)
    ppermute x21, starting transfers between devices, swap(): return lax.ppermute(value, 'row', [(i, i ^ bit) for i in range(count)])  28.6 us
    ppermute x21, waiting for transfers between devices, swap(): return lax.ppermute(value, 'row', [(i, i ^ bit) for i in range(count)])  21.1 us
    pallas_call x16, Pallas kernels, run(): pl.pallas_call(body, out_shape=outs, **extra, scratch_shapes=scratch, com...  13.1 us
    ppermute x2, starting transfers between devices, swap_rim(): return lax.ppermute(value, 'row', pairs + [(j, i) for i, j in pairs])  7.23 us
    ppermute x2, starting transfers between devices, swap_far(): return lax.ppermute(value, ('grp', 'row'), pairs)  3.41 us
    ppermute x2, waiting for transfers between devices, swap_group(): return lax.ppermute(value, 'grp', [(0, 1), (1, 0)])  2.69 us
    ppermute x2, waiting for transfers between devices, swap_rim(): return lax.ppermute(value, 'row', pairs + [(j, i) for i, j in pairs])  2.65 us
  transfers between devices with their start and end apart: 27, of which 9 were waited for; matrix products, arithmetic and copies ran while one was open for 0% of the time, Pallas kernels for 11%

profile of v9, /device:TPU:1, one launch (start us, length us, event | category | flops | bytes accessed | tf_op | source)
XLA Modules:
  0.0 81.3 jit_solution(3046389091081404955)
XLA Ops:
  0.6 1.3 %shard_map.160 = (bf16[2,2,32,512]{3,2,1,0:T(8,128)(2,1)S(1)}, bf16[224,512]{1,0:T(8,128)(2,1)S(1)}, f32[96,512]{1,0:T(8,128)S(1)}, bf16[128,512]{1,0:T(8,128)(2...) custom-call(f32[32,2048]{1,0:T(8,128)} %refs_0_.1, ...), custom_call_target="tpu_custom_call" | custom-call | tf_op jit(solution)/shard_map/pallas_call | solution.py:53
  2.1 4.5 %collective-permute-start.1 = (f32[96,512]{1,0:T(8,128)S(1)}, f32[96,512]{1,0:T(8,128)S(1)}, u32[]{:S(2)}, u32[]{:S(2)}) collective-permute-start(f32[96,512]{1,0:T(8,128)S(1)} %get-tuple-element.86), channel_id=1, source_target_pairs={{1,2},{3,4},{5,6},{7,8},{9,10},{11,12},{13,14},{2,1},{4,3},{6,5},{... | collective-permute-start | bytes 589832 | tf_op jit(solution)/shard_map/ppermute | solution.py:28
  6.6 3.4 %collective-permute-start.8 = (bf16[2,2,32,512]{3,2,1,0:T(8,128)(2,1)S(1)}, bf16[2,2,32,512]{3,2,1,0:T(8,128)(2,1)S(1)}, u32[]{:S(2)}, u32[]{:S(2)}) collective-permute-start(bf16[2,2,32,512]{3,2,1,0:T(8,128)(2,1)S(1)} %get-tuple-element.95), channel_id=1, source_target_pairs={{0,10},{1,11},{2,8},{3,9},{4,14},{5,15},{6,12},{7,13},{8,2},{9,3},... | collective-permute-start | bytes 393224 | tf_op jit(solution)/shard_map/ppermute | solution.py:41
  12.5 2.6 %collective-permute-done.1.outer.refs_7_ = f32[96,512]{1,0:T(8,128)S(1)} collective-permute-done((f32[96,512]{1,0:T(8,128)S(1)}, f32[96,512]{1,0:T(8,128)S(1)}, u32[]{:S(2)}, u32[]{:S(2)}) %collective-permute-start.1) | collective-permute-done | bytes 196640 | tf_op jit(solution)/shard_map/ppermute | solution.py:28
  15.2 6.2 %collective-permute-start.4 = (bf16[2,2,32,512]{3,2,1,0:T(8,128)(2,1)S(1)}, bf16[2,2,32,512]{3,2,1,0:T(8,128)(2,1)S(1)}, u32[]{:S(2)}, u32[]{:S(2)}) collective-permute-start(bf16[2,2,32,512]{3,2,1,0:T(8,128)(2,1)S(1)} %get-tuple-element.94.refs_3_), channel_id=1, source_target_pairs={{0,4},{1,5},{2,6},{3,7},{4,0},{5,1},{6,2},{7,3},{8,12},{9,13},{10,... | collective-permute-start | bytes 393224 | tf_op jit(solution)/shard_map/ppermute | solution.py:22
  21.4 2.4 %shard_map.161 = (f32[128,512]{1,0:T(8,128)S(1)}, f32[128,128]{1,0:T(8,128)S(1)}, bf16[128,512]{1,0:T(8,128)(2,1)S(1)}) custom-call(f32[4,32,512]{2,1,0:T(8,128)S(1)} %get-tuple-element.84.feats.refs_5_, bf16[224,512]{1,0:T(8,128)(2,1)S(1)} %collective-permute-done.core_got.other.refs_6_, f32[96,512]{1,0:T(8,128)S(1)} %collective-permute-done.1.outer.refs_7_, ...), custom_call_target="tpu_custom_call" | custom-call | tf_op jit(solution)/shard_map/pallas_call | solution.py:53
  24.0 1.4 %collective-permute-start.6 = (bf16[2,2,32,512]{3,2,1,0:T(8,128)(2,1)S(1)}, bf16[2,2,32,512]{3,2,1,0:T(8,128)(2,1)S(1)}, u32[]{:S(2)}, u32[]{:S(2)}) collective-permute-start(bf16[2,2,32,512]{3,2,1,0:T(8,128)(2,1)S(1)} %collective-permute-done.5.refs_1_.refs_5_), channel_id=1, source_target_pairs={{0,16},{16,0},{1,17},{17,1},{2,18},{18,2},{3,19},{19,3},{4,20},{20... | collective-permute-start | bytes 393224 | tf_op jit(solution)/shard_map/ppermute | solution.py:45
  25.4 3.1 %collective-permute-done.2.normed_got = bf16[128,512]{1,0:T(8,128)(2,1)S(1)} collective-permute-done((bf16[128,512]{1,0:T(8,128)(2,1)S(1)}, bf16[128,512]{1,0:T(8,128)(2,1)S(1)}, u32[]{:S(2)}, u32[]{:S(2)}) %collective-permute-start.2) | collective-permute-done | bytes 131104 | tf_op jit(solution)/shard_map/ppermute | solution.py:22
  28.5 2.7 %collective-permute-done.6.refs_2_.refs_6_ = bf16[2,2,32,512]{3,2,1,0:T(8,128)(2,1)S(1)} collective-permute-done((bf16[2,2,32,512]{3,2,1,0:T(8,128)(2,1)S(1)}, bf16[2,2,32,512]{3,2,1,0:T(8,128)(2,1)S(1)}, u32[]{:S(2)}, u32[]{:S(2)}) %collective-permute-start.6) | collective-permute-done | bytes 131104 | tf_op jit(solution)/shard_map/ppermute | solution.py:45
  31.3 1.5 %collective-permute-start.10 = (bf16[2,256,512]{2,1,0:T(8,128)(2,1)S(1)}, bf16[2,256,512]{2,1,0:T(8,128)(2,1)S(1)}, u32[]{:S(2)}, u32[]{:S(2)}) collective-permute-start(bf16[2,256,512]{2,1,0:T(8,128)(2,1)S(1)} %get-tuple-element.96.refs_0_), channel_id=1, source_target_pairs={{0,1},{1,0},{2,3},{3,2},{4,5},{5,4},{6,7},{7,6},{8,9},{9,8},{10,11... | collective-permute-start | bytes 1572872 | tf_op jit(solution)/shard_map/ppermute | solution.py:22
  32.8 1.5 %collective-permute-done.10.refs_1_ = bf16[2,256,512]{2,1,0:T(8,128)(2,1)S(1)} collective-permute-done((bf16[2,256,512]{2,1,0:T(8,128)(2,1)S(1)}, bf16[2,256,512]{2,1,0:T(8,128)(2,1)S(1)}, u32[]{:S(2)}, u32[]{:S(2)}) %collective-permute-start.10) | collective-permute-done | bytes 524320 | tf_op jit(solution)/shard_map/ppermute | solution.py:22
  34.3 1.4 %shard_map.164 = (f32[256,512]{1,0:T(8,128)S(1)}, bf16[256,512]{1,0:T(8,128)(2,1)S(1)}, bf16[512,512]{1,0:T(8,128)(2,1)S(1)}, bf16[512,512]{1,0:T(8,128)(2,1)S(1...) custom-call(bf16[2,256,512]{2,1,0:T(8,128)(2,1)S(1)} %get-tuple-element.96.refs_0_, ...), custom_call_target="tpu_custom_call" | custom-call | tf_op jit(solution)/shard_map/pallas_call | solution.py:53
  38.1 3.0 %collective-permute-start.14 = (bf16[128,512]{1,0:T(8,128)(2,1)S(1)}, bf16[128,512]{1,0:T(8,128)(2,1)S(1)}, u32[]{:S(2)}, u32[]{:S(2)}) collective-permute-start(bf16[128,512]{1,0:T(8,128)(2,1)S(1)} %get-tuple-element.114), channel_id=1, source_target_pairs={{0,14},{1,15},{2,12},{3,13},{4,10},{5,11},{6,8},{7,9},{8,6},{9,7},... | collective-permute-start | bytes 393224 | tf_op jit(solution)/shard_map/ppermute | solution.py:22
  42.3 1.9 %shard_map.167 = (f32[128,512]{1,0:T(8,128)S(1)}, bf16[96,512]{1,0:T(8,128)(2,1)S(1)}, bf16[96,512]{1,0:T(8,128)(2,1)S(1)}, f32[28,512]{1,0:T(8,128)S(1)}, f32[28,512]{1,0:T(8,128)S(1)}) custom-call(f32[128,512]{1,0:T(8,128)S(1)} %get-tuple-element.101.refs_0_, bf16[128,512]{1,0:T(8,128)(2,1)S(1)} %collective-permute-done.12.refs_1_, ...), custom_call_target="tpu_custom_call" | custom-call | tf_op jit(solution)/shard_map/pallas_call | solution.py:53
  44.2 1.3 %collective-permute-start.13 = (f32[28,512]{1,0:T(8,128)S(1)}, f32[28,512]{1,0:T(8,128)S(1)}, u32[]{:S(2)}, u32[]{:S(2)}) collective-permute-start(f32[28,512]{1,0:T(8,128)S(1)} %get-tuple-element.112), channel_id=1, source_target_pairs={{0,1},{1,0},{2,3},{3,2},{4,5},{5,4},{6,7},{7,6},{8,9},{9,8},{10,11... | collective-permute-start | bytes 172040 | tf_op jit(solution)/shard_map/ppermute | solution.py:22
  45.5 3.2 %collective-permute-start.16 = (bf16[128,512]{1,0:T(8,128)(2,1)S(1)}, bf16[128,512]{1,0:T(8,128)(2,1)S(1)}, u32[]{:S(2)}, u32[]{:S(2)}) collective-permute-start(bf16[128,512]{1,0:T(8,128)(2,1)S(1)} %get-tuple-element.117), channel_id=1, source_target_pairs={{0,10},{1,11},{2,8},{3,9},{4,14},{5,15},{6,12},{7,13},{8,2},{9,3},... | collective-permute-start | bytes 393224 | tf_op jit(solution)/shard_map/ppermute | solution.py:22
  49.9 2.8 %collective-permute-start.19 = (bf16[96,512]{1,0:T(8,128)(2,1)S(1)}, bf16[96,512]{1,0:T(8,128)(2,1)S(1)}, u32[]{:S(2)}, u32[]{:S(2)}) collective-permute-start(bf16[96,512]{1,0:T(8,128)(2,1)S(1)} %get-tuple-element.123), channel_id=1, source_target_pairs={{1,2},{3,4},{5,6},{7,8},{9,10},{11,12},{13,14},{2,1},{4,3},{6,5},{... | collective-permute-start | bytes 294920 | tf_op jit(solution)/shard_map/ppermute | solution.py:28
  53.8 4.6 %collective-permute-done.15 = f32[28,512]{1,0:T(8,128)S(1)} collective-permute-done((f32[28,512]{1,0:T(8,128)S(1)}, f32[28,512]{1,0:T(8,128)S(1)}, u32[]{:S(2)}, u32[]{:S(2)}) %collective-permute-start.15) | collective-permute-done | bytes 57376 | tf_op jit(solution)/shard_map/ppermute | solution.py:22
  59.7 1.6 %collective-permute-start.18 = (bf16[160,512]{1,0:T(8,128)(2,1)S(1)}, bf16[160,512]{1,0:T(8,128)(2,1)S(1)}, u32[]{:S(2)}, u32[]{:S(2)}) collective-permute-start(bf16[160,512]{1,0:T(8,128)(2,1)S(1)} %get-tuple-element.122), channel_id=1, source_target_pairs={{0,12},{1,13},{2,14},{3,15},{4,8},{5,9},{6,10},{7,11},{8,4},{9,5},... | collective-permute-start | bytes 491528 | tf_op jit(solution)/shard_map/ppermute | solution.py:22
  61.3 3.1 %collective-permute-start.24 = (bf16[128,512]{1,0:T(8,128)(2,1)S(1)}, bf16[128,512]{1,0:T(8,128)(2,1)S(1)}, u32[]{:S(2)}, u32[]{:S(2)}) collective-permute-start(bf16[128,512]{1,0:T(8,128)(2,1)S(1)} %get-tuple-element.130), channel_id=1, source_target_pairs={{0,6},{1,7},{2,4},{3,5},{4,2},{5,3},{6,0},{7,1},{8,14},{9,15},{10,... | collective-permute-start | bytes 393224 | tf_op jit(solution)/shard_map/ppermute | solution.py:22
  65.2 2.9 %shard_map.172 = f32[4,32,512]{2,1,0:T(8,128)} custom-call(f32[128,512]{1,0:T(8,128)S(1)} %get-tuple-element.133.grad, bf16[96,512]{1,0:T(8,128)(2,1)S(1)} %collective-permute-done.20.inner, bf16[96,512]{1,0:T(8,128)(2,1)S(1)} %collective-permute-done.19.outer, f32[7,7,512]{2,1,0:T(8,128)S(1)} %get-tuple-element.87.kernel, ...), custom_call_target="tpu_custom_call" | custom-call | tf_op jit(solution)/shard_map/pallas_call | solution.py:53
  68.0 4.4 %collective-permute-done.17 = bf16[160,512]{1,0:T(8,128)(2,1)S(1)} collective-permute-done((bf16[160,512]{1,0:T(8,128)(2,1)S(1)}, bf16[160,512]{1,0:T(8,128)(2,1)S(1)}, u32[]{:S(2)}, u32[]{:S(2)}) %collective-permute-start.17) | collective-permute-done | bytes 163872 | tf_op jit(solution)/shard_map/ppermute | solution.py:22
  72.5 5.0 %collective-permute-done.24.refs_5_ = bf16[128,512]{1,0:T(8,128)(2,1)S(1)} collective-permute-done((bf16[128,512]{1,0:T(8,128)(2,1)S(1)}, bf16[128,512]{1,0:T(8,128)(2,1)S(1)}, u32[]{:S(2)}, u32[]{:S(2)}) %collective-permute-start.24) | collective-permute-done | bytes 131104 | tf_op jit(solution)/shard_map/ppermute | solution.py:22
  77.7 1.5 %collective-permute-start.26 = (f32[156,512]{1,0:T(8,128)S(1)}, f32[156,512]{1,0:T(8,128)S(1)}, u32[]{:S(2)}, u32[]{:S(2)}) collective-permute-start(f32[156,512]{1,0:T(8,128)S(1)} %get-tuple-element.150), channel_id=1, source_target_pairs={{0,1},{1,0},{2,3},{3,2},{4,5},{5,4},{6,7},{7,6},{8,9},{9,8},{10,11... | collective-permute-start | bytes 958472 | tf_op jit(solution)/shard_map/ppermute | solution.py:22
  (54 shorter events, 13.1 us)
Async XLA Ops:
  2.0 4.6 %collective-permute-start = (bf16[224,512]{1,0:T(8,128)(2,1)S(1)}, bf16[224,512]{1,0:T(8,128)(2,1)S(1)}, u32[]{:S(2)}, u32[]{:S(2)}) collective-permute-start(bf16[224,512]{1,0:T(8,128)(2,1)S(1)} %get-tuple-element.85), channel_id=1, source_target_pairs={{0,1},{1,0},{2,3},{3,2},{4,5},{5,4},{6,7},{7,6},{8,9},{9,8},{10,11... | collective-permute-start | bytes 688136 | tf_op jit(solution)/shard_map/ppermute | solution.py:22
  2.1 13.1 %collective-permute-start.1 = (f32[96,512]{1,0:T(8,128)S(1)}, f32[96,512]{1,0:T(8,128)S(1)}, u32[]{:S(2)}, u32[]{:S(2)}) collective-permute-start(f32[96,512]{1,0:T(8,128)S(1)} %get-tuple-element.86), channel_id=1, source_target_pairs={{1,2},{3,4},{5,6},{7,8},{9,10},{11,12},{13,14},{2,1},{4,3},{6,5},{... | collective-permute-start | bytes 589832 | tf_op jit(solution)/shard_map/ppermute | solution.py:28
  6.6 17.2 %collective-permute-start.8 = (bf16[2,2,32,512]{3,2,1,0:T(8,128)(2,1)S(1)}, bf16[2,2,32,512]{3,2,1,0:T(8,128)(2,1)S(1)}, u32[]{:S(2)}, u32[]{:S(2)}) collective-permute-start(bf16[2,2,32,512]{3,2,1,0:T(8,128)(2,1)S(1)} %get-tuple-element.95), channel_id=1, source_target_pairs={{0,10},{1,11},{2,8},{3,9},{4,14},{5,15},{6,12},{7,13},{8,2},{9,3},... | collective-permute-start | bytes 393224 | tf_op jit(solution)/shard_map/ppermute | solution.py:41
  10.0 13.9 %collective-permute-start.7 = (bf16[2,2,32,512]{3,2,1,0:T(8,128)(2,1)S(1)}, bf16[2,2,32,512]{3,2,1,0:T(8,128)(2,1)S(1)}, u32[]{:S(2)}, u32[]{:S(2)}) collective-permute-start(bf16[2,2,32,512]{3,2,1,0:T(8,128)(2,1)S(1)} %get-tuple-element.95), channel_id=1, source_target_pairs={{0,6},{1,7},{2,4},{3,5},{4,2},{5,3},{6,0},{7,1},{8,14},{9,15},{10,... | collective-permute-start | bytes 393224 | tf_op jit(solution)/shard_map/ppermute | solution.py:22
  11.2 12.8 %collective-permute-start.5 = (bf16[2,2,32,512]{3,2,1,0:T(8,128)(2,1)S(1)}, bf16[2,2,32,512]{3,2,1,0:T(8,128)(2,1)S(1)}, u32[]{:S(2)}, u32[]{:S(2)}) collective-permute-start(bf16[2,2,32,512]{3,2,1,0:T(8,128)(2,1)S(1)} %get-tuple-element.94.refs_3_), channel_id=1, source_target_pairs={{0,8},{1,9},{2,10},{3,11},{4,12},{5,13},{6,14},{7,15},{8,0},{9,1},... | collective-permute-start | bytes 393224 | tf_op jit(solution)/shard_map/ppermute | solution.py:41
  11.3 20.0 %collective-permute-start.3 = (bf16[256,512]{1,0:T(8,128)(2,1)S(1)}, bf16[256,512]{1,0:T(8,128)(2,1)S(1)}, u32[]{:S(2)}, u32[]{:S(2)}) collective-permute-start(bf16[256,512]{1,0:T(8,128)(2,1)S(1)} %get-tuple-element.93), channel_id=1, source_target_pairs={{0,2},{1,3},{2,0},{3,1},{4,6},{5,7},{6,4},{7,5},{8,10},{9,11},{10,... | collective-permute-start | bytes 786440 | tf_op jit(solution)/shard_map/ppermute | solution.py:22
  15.2 10.3 %collective-permute-start.4 = (bf16[2,2,32,512]{3,2,1,0:T(8,128)(2,1)S(1)}, bf16[2,2,32,512]{3,2,1,0:T(8,128)(2,1)S(1)}, u32[]{:S(2)}, u32[]{:S(2)}) collective-permute-start(bf16[2,2,32,512]{3,2,1,0:T(8,128)(2,1)S(1)} %get-tuple-element.94.refs_3_), channel_id=1, source_target_pairs={{0,4},{1,5},{2,6},{3,7},{4,0},{5,1},{6,2},{7,3},{8,12},{9,13},{10,... | collective-permute-start | bytes 393224 | tf_op jit(solution)/shard_map/ppermute | solution.py:22
  23.8 4.7 %collective-permute-start.2 = (bf16[128,512]{1,0:T(8,128)(2,1)S(1)}, bf16[128,512]{1,0:T(8,128)(2,1)S(1)}, u32[]{:S(2)}, u32[]{:S(2)}) collective-permute-start(bf16[128,512]{1,0:T(8,128)(2,1)S(1)} %get-tuple-element.90.normed), channel_id=1, source_target_pairs={{0,2},{1,3},{2,0},{3,1},{4,6},{5,7},{6,4},{7,5},{8,10},{9,11},{10,... | collective-permute-start | bytes 393224 | tf_op jit(solution)/shard_map/ppermute | solution.py:22
  23.9 4.6 %collective-permute-start.9 = (bf16[2,2,32,512]{3,2,1,0:T(8,128)(2,1)S(1)}, bf16[2,2,32,512]{3,2,1,0:T(8,128)(2,1)S(1)}, u32[]{:S(2)}, u32[]{:S(2)}) collective-permute-start(bf16[2,2,32,512]{3,2,1,0:T(8,128)(2,1)S(1)} %collective-permute-done.8.refs_4_.refs_9_), channel_id=1, source_target_pairs={{0,16},{16,0},{1,17},{17,1},{2,18},{18,2},{3,19},{19,3},{4,20},{20... | collective-permute-start | bytes 393224 | tf_op jit(solution)/shard_map/ppermute | solution.py:45
  24.0 7.2 %collective-permute-start.6 = (bf16[2,2,32,512]{3,2,1,0:T(8,128)(2,1)S(1)}, bf16[2,2,32,512]{3,2,1,0:T(8,128)(2,1)S(1)}, u32[]{:S(2)}, u32[]{:S(2)}) collective-permute-start(bf16[2,2,32,512]{3,2,1,0:T(8,128)(2,1)S(1)} %collective-permute-done.5.refs_1_.refs_5_), channel_id=1, source_target_pairs={{0,16},{16,0},{1,17},{17,1},{2,18},{18,2},{3,19},{19,3},{4,20},{20... | collective-permute-start | bytes 393224 | tf_op jit(solution)/shard_map/ppermute | solution.py:45
  37.3 11.4 %collective-permute-start.21 = (bf16[256,512]{1,0:T(8,128)(2,1)S(1)}, bf16[256,512]{1,0:T(8,128)(2,1)S(1)}, u32[]{:S(2)}, u32[]{:S(2)}) collective-permute-start(bf16[256,512]{1,0:T(8,128)(2,1)S(1)} %get-tuple-element.126), channel_id=1, source_target_pairs={{0,1},{1,0},{2,3},{3,2},{4,5},{5,4},{6,7},{7,6},{8,9},{9,8},{10,11... | collective-permute-start | bytes 786440 | tf_op jit(solution)/shard_map/ppermute | solution.py:22
  37.5 4.8 %collective-permute-start.12 = (bf16[128,512]{1,0:T(8,128)(2,1)S(1)}, bf16[128,512]{1,0:T(8,128)(2,1)S(1)}, u32[]{:S(2)}, u32[]{:S(2)}) collective-permute-start(bf16[128,512]{1,0:T(8,128)(2,1)S(1)} %get-tuple-element.102.after), channel_id=1, source_target_pairs={{0,2},{1,3},{2,0},{3,1},{4,6},{5,7},{6,4},{7,5},{8,10},{9,11},{10,... | collective-permute-start | bytes 393224 | tf_op jit(solution)/shard_map/ppermute | solution.py:22
  38.1 14.7 %collective-permute-start.14 = (bf16[128,512]{1,0:T(8,128)(2,1)S(1)}, bf16[128,512]{1,0:T(8,128)(2,1)S(1)}, u32[]{:S(2)}, u32[]{:S(2)}) collective-permute-start(bf16[128,512]{1,0:T(8,128)(2,1)S(1)} %get-tuple-element.114), channel_id=1, source_target_pairs={{0,14},{1,15},{2,12},{3,13},{4,10},{5,11},{6,8},{7,9},{8,6},{9,7},... | collective-permute-start | bytes 393224 | tf_op jit(solution)/shard_map/ppermute | solution.py:22
  44.2 8.4 %collective-permute-start.13 = (f32[28,512]{1,0:T(8,128)S(1)}, f32[28,512]{1,0:T(8,128)S(1)}, u32[]{:S(2)}, u32[]{:S(2)}) collective-permute-start(f32[28,512]{1,0:T(8,128)S(1)} %get-tuple-element.112), channel_id=1, source_target_pairs={{0,1},{1,0},{2,3},{3,2},{4,5},{5,4},{6,7},{7,6},{8,9},{9,8},{10,11... | collective-permute-start | bytes 172040 | tf_op jit(solution)/shard_map/ppermute | solution.py:22
  45.5 12.9 %collective-permute-start.16 = (bf16[128,512]{1,0:T(8,128)(2,1)S(1)}, bf16[128,512]{1,0:T(8,128)(2,1)S(1)}, u32[]{:S(2)}, u32[]{:S(2)}) collective-permute-start(bf16[128,512]{1,0:T(8,128)(2,1)S(1)} %get-tuple-element.117), channel_id=1, source_target_pairs={{0,10},{1,11},{2,8},{3,9},{4,14},{5,15},{6,12},{7,13},{8,2},{9,3},... | collective-permute-start | bytes 393224 | tf_op jit(solution)/shard_map/ppermute | solution.py:22
  48.7 9.7 %collective-permute-start.22 = (bf16[128,512]{1,0:T(8,128)(2,1)S(1)}, bf16[128,512]{1,0:T(8,128)(2,1)S(1)}, u32[]{:S(2)}, u32[]{:S(2)}) collective-permute-start(bf16[128,512]{1,0:T(8,128)(2,1)S(1)} %get-tuple-element.127), channel_id=1, source_target_pairs={{0,2},{1,3},{2,0},{3,1},{4,6},{5,7},{6,4},{7,5},{8,10},{9,11},{10,... | collective-permute-start | bytes 393224 | tf_op jit(solution)/shard_map/ppermute | solution.py:22
  49.9 8.6 %collective-permute-start.19 = (bf16[96,512]{1,0:T(8,128)(2,1)S(1)}, bf16[96,512]{1,0:T(8,128)(2,1)S(1)}, u32[]{:S(2)}, u32[]{:S(2)}) collective-permute-start(bf16[96,512]{1,0:T(8,128)(2,1)S(1)} %get-tuple-element.123), channel_id=1, source_target_pairs={{1,2},{3,4},{5,6},{7,8},{9,10},{11,12},{13,14},{2,1},{4,3},{6,5},{... | collective-permute-start | bytes 294920 | tf_op jit(solution)/shard_map/ppermute | solution.py:28
  52.7 5.8 %collective-permute-start.20 = (bf16[96,512]{1,0:T(8,128)(2,1)S(1)}, bf16[96,512]{1,0:T(8,128)(2,1)S(1)}, u32[]{:S(2)}, u32[]{:S(2)}) collective-permute-start(bf16[96,512]{1,0:T(8,128)(2,1)S(1)} %get-tuple-element.124), channel_id=1, source_target_pairs={{0,1},{1,0},{2,3},{3,2},{4,5},{5,4},{6,7},{7,6},{8,9},{9,8},{10,11... | collective-permute-start | bytes 294920 | tf_op jit(solution)/shard_map/ppermute | solution.py:22
  52.8 5.6 %collective-permute-start.15 = (f32[28,512]{1,0:T(8,128)S(1)}, f32[28,512]{1,0:T(8,128)S(1)}, u32[]{:S(2)}, u32[]{:S(2)}) collective-permute-start(f32[28,512]{1,0:T(8,128)S(1)} %add.6), channel_id=1, source_target_pairs={{0,2},{1,3},{2,0},{3,1},{4,6},{5,7},{6,4},{7,5},{8,10},{9,11},{10,... | collective-permute-start | bytes 172040 | tf_op jit(solution)/shard_map/ppermute | solution.py:22
  58.6 13.9 %collective-permute-start.17 = (bf16[160,512]{1,0:T(8,128)(2,1)S(1)}, bf16[160,512]{1,0:T(8,128)(2,1)S(1)}, u32[]{:S(2)}, u32[]{:S(2)}) collective-permute-start(bf16[160,512]{1,0:T(8,128)(2,1)S(1)} %get-tuple-element.121), channel_id=1, source_target_pairs={{0,8},{1,9},{2,10},{3,11},{4,12},{5,13},{6,14},{7,15},{8,0},{9,1},... | collective-permute-start | bytes 491528 | tf_op jit(solution)/shard_map/ppermute | solution.py:22
  59.7 12.7 %collective-permute-start.18 = (bf16[160,512]{1,0:T(8,128)(2,1)S(1)}, bf16[160,512]{1,0:T(8,128)(2,1)S(1)}, u32[]{:S(2)}, u32[]{:S(2)}) collective-permute-start(bf16[160,512]{1,0:T(8,128)(2,1)S(1)} %get-tuple-element.122), channel_id=1, source_target_pairs={{0,12},{1,13},{2,14},{3,15},{4,8},{5,9},{6,10},{7,11},{8,4},{9,5},... | collective-permute-start | bytes 491528 | tf_op jit(solution)/shard_map/ppermute | solution.py:22
  61.3 11.2 %collective-permute-start.23 = (bf16[160,512]{1,0:T(8,128)(2,1)S(1)}, bf16[160,512]{1,0:T(8,128)(2,1)S(1)}, u32[]{:S(2)}, u32[]{:S(2)}) collective-permute-start(bf16[160,512]{1,0:T(8,128)(2,1)S(1)} %get-tuple-element.129), channel_id=1, source_target_pairs={{0,4},{1,5},{2,6},{3,7},{4,0},{5,1},{6,2},{7,3},{8,12},{9,13},{10,... | collective-permute-start | bytes 491528 | tf_op jit(solution)/shard_map/ppermute | solution.py:22
  61.3 16.2 %collective-permute-start.24 = (bf16[128,512]{1,0:T(8,128)(2,1)S(1)}, bf16[128,512]{1,0:T(8,128)(2,1)S(1)}, u32[]{:S(2)}, u32[]{:S(2)}) collective-permute-start(bf16[128,512]{1,0:T(8,128)(2,1)S(1)} %get-tuple-element.130), channel_id=1, source_target_pairs={{0,6},{1,7},{2,4},{3,5},{4,2},{5,3},{6,0},{7,1},{8,14},{9,15},{10,... | collective-permute-start | bytes 393224 | tf_op jit(solution)/shard_map/ppermute | solution.py:22
  64.4 13.1 %collective-permute-start.25 = (bf16[128,512]{1,0:T(8,128)(2,1)S(1)}, bf16[128,512]{1,0:T(8,128)(2,1)S(1)}, u32[]{:S(2)}, u32[]{:S(2)}) collective-permute-start(bf16[128,512]{1,0:T(8,128)(2,1)S(1)} %get-tuple-element.131), channel_id=1, source_target_pairs={{0,2},{1,3},{2,0},{3,1},{4,6},{5,7},{6,4},{7,5},{8,10},{9,11},{10,... | collective-permute-start | bytes 393224 | tf_op jit(solution)/shard_map/ppermute | solution.py:22
  (3 other events, 7.5 us)

commit v10 on v6

--- a/solution.py
+++ b/solution.py
@@ -194,9 +194,8 @@
     patterns = lax.axis_size("row") // 4
     me, _, _ = place()
     acts, in_bias = refs[:2], refs[2]
-    scale = refs[3]
-    pieces = refs[4:-7]
-    keep, send, active, hidden, scale_part, bias_part, weights = refs[-7:]
+    pieces = refs[3:-7]
+    keep, send, active, hidden, out_copy, bias_part, weights = refs[-7:]
     half = acts[0].shape[1]
     if copied:
         own = pieces[0].shape[2]
@@ -218,9 +217,9 @@
         weights[...] = pieces[0][...]
     in_narrow = weights.at[0]
     out_narrow = weights.at[1]
+    out_copy[...] = weights[1]
     bias_row = in_bias[...]
     total = jnp.zeros_like(bias_row)
-    scale_total = jnp.zeros_like(scale_part)
     for side in (1, 0):
         preact = dot(acts[side][0], in_narrow[...], ((1,), (0,))) + bias_row
         act_grad = dot(acts[side][1], out_narrow[...], ((1,), (0,)))
@@ -234,28 +233,31 @@
         narrow = grad.astype(NARROW)
         hidden[rows, :] = narrow
         out_grad = dot(narrow, in_narrow[...], ((1,), (1,)))
-        mixed = dot(activated, out_narrow[...], ((1,), (1,)))
-        scale_total = scale_total + jnp.sum(
-            mixed * acts[side][1].astype(WIDE), axis=0, keepdims=True
-        )
         if side:
-            send[0] = out_grad.astype(NARROW)
-            send[1] = mixed.astype(NARROW)
+            send[...] = out_grad.astype(NARROW)
         else:
-            keep[0] = out_grad
-            keep[1] = mixed
+            keep[...] = out_grad
     bias_part[...] = total
-    scale_part[...] = scale_total / scale[...]
 
 
 def weight_body(norm_scale, *refs):
-    acts, (active, hidden, holder) = refs[:2], refs[2:]
+    acts, (active, hidden, out_narrow, scale) = refs[:2], refs[2:6]
+    holder, keep, send, scale_part = refs[6:]
     half = acts[0].shape[1]
     first, second = pl.ds(0, half), pl.ds(half, half)
     for which, right in enumerate((hidden, active)):
         grad = dot(acts[0][which], right[first, :], ((0,), (0,)))
         grad = grad + dot(acts[1][which], right[second, :], ((0,), (0,)))
         holder[which] = norm_scale * grad
+    total = jnp.zeros_like(scale_part)
+    for side, rows in enumerate((first, second)):
+        mixed = dot(active[rows, :], out_narrow[...], ((1,), (1,)))
+        total = total + jnp.sum(mixed * acts[side][1].astype(WIDE), axis=0, keepdims=True)
+        if side:
+            send[...] = mixed.astype(NARROW)
+        else:
+            keep[...] = mixed
+    scale_part[...] = total / scale[...]
 
 
 def owners_body(turns, holder, after, *targets):
@@ -274,11 +276,10 @@
             target[4 * own + SMALL_ROWS :, :] = jnp.zeros((rest, target.shape[1]), target.dtype)
 
 
-def fold_body(kept, got, stay, leave, mixed_stay, mixed_leave):
+def fold_body(kept, got, stay, leave):
     size = stay.shape[0]
-    for which, (near, away) in enumerate(((stay, leave), (mixed_stay, mixed_leave))):
-        near[...] = kept[which, :size] + got[which, :size].astype(WIDE)
-        away[...] = (kept[which, size:] + got[which, size:].astype(WIDE)).astype(NARROW)
+    stay[...] = kept[:size] + got[:size].astype(WIDE)
+    leave[...] = (kept[size:] + got[size:].astype(WIDE)).astype(NARROW)
 
 
 def conv_grad_body(norm_scale, *refs):
@@ -513,38 +514,43 @@
         lines = jnp.moveaxis(canonical(lines, me, bit_count), 1, 0)
         pieces = [lines.reshape(2, channels, quarter)]
     group = 4 * pixels
-    both = (2, 2 * pixels, channels)
-    keep, send, active, hidden, scale_part, in_bias_part = run(
+    keep, send, active, hidden, out_narrow, in_bias_part = run(
         functools.partial(hidden_body, copied),
         (
-            shaped(both),
-            shaped(both, NARROW),
+            shaped((2 * pixels, channels)),
+            shaped((2 * pixels, channels), NARROW),
             shaped((group, quarter), NARROW),
             shaped((group, quarter), NARROW),
-            shaped((1, channels)),
+            shaped((channels, quarter), NARROW),
             shaped((1, quarter)),
         ),
         acts,
         acts_got,
         in_bias_own,
-        scale,
         *pieces,
         scratch=(pltpu.VMEM((2, channels, quarter), NARROW),),
         mib=24,
     )
     half = (shaped((pixels, channels)), shaped((pixels, channels), NARROW))
-    out_stay, out_leave, mixed_stay, mixed_leave = run(fold_body, half * 2, keep, swap(send, 1))
+    out_stay, out_leave = run(fold_body, half, keep, swap(send, 1))
     out_got = swap(out_leave, 2)
 
-    holder = run(
+    holder, mixed_keep, mixed_send, scale_part = run(
         functools.partial(weight_body, norm_scale),
-        (shaped((2, channels, quarter)),),
+        (
+            shaped((2, channels, quarter)),
+            shaped((2 * pixels, channels)),
+            shaped((2 * pixels, channels), NARROW),
+            shaped((1, channels)),
+        ),
         acts,
         acts_got,
         active,
         hidden,
+        out_narrow,
+        scale,
         mib=24,
-    )[0]
+    )
     conv_grad, inner_out, rim_out, stay, leave = run(
         functools.partial(conv_grad_body, norm_scale),
         (
@@ -570,13 +576,13 @@
     inner_got = swap(inner_out, 1)
     sums = stay + swap(leave, 1)
 
-    far_turns = (*range(2 * patterns - 1, 4, -2), 3)
-    near_turns = (*range(4, 2 * patterns, 2), 2, 1, 0)
+    first_turns = (*range(2 * patterns - 2, 3, -2), 2)
+    next_turns = (*range(2 * patterns - 1, 4, -2), 3, 1, 0)
     owned = 4 * own_rows
     if copied:
         parts = run(
-            functools.partial(owners_body, far_turns),
-            (shaped((owned, quarter), NARROW),) * len(far_turns),
+            functools.partial(owners_body, first_turns),
+            (shaped((owned, quarter), NARROW),) * len(first_turns),
             holder,
             out_leave,
         )
@@ -584,26 +590,29 @@
         flat = holder.reshape(2, count, own_rows, quarter)
         flat = canonical(jnp.moveaxis(flat, 1, 0), me, bit_count)
         flat = flat.reshape(2 * patterns, owned, quarter)
-        parts = [flat[p].astype(NARROW) for p in far_turns]
-    far_parts = [swap(part, 2 * p) for p, part in zip(far_turns, parts)]
-    sums, far_parts = lax.optimization_barrier((sums, far_parts))
+        parts = [flat[p].astype(NARROW) for p in first_turns]
+    first_parts = [swap(part, 2 * p) for p, part in zip(first_turns, parts)]
+    sums, first_parts = lax.optimization_barrier((sums, first_parts))
     sums = sums + swap(sums, 2)
-    sums, mixed_leave = lax.optimization_barrier((sums, mixed_leave))
+    sums, mixed_send, rim_got, inner_got = lax.optimization_barrier(
+        (sums, mixed_send, rim_got, inner_got)
+    )
+    mixed_stay, mixed_leave = run(fold_body, half, mixed_keep, swap(mixed_send, 1))
     if copied:
         joint = shaped((owned + 32, quarter), NARROW)
         *parts, side_part, near_own = run(
-            functools.partial(owners_body, near_turns),
-            (joint,) * (len(near_turns) - 2)
+            functools.partial(owners_body, next_turns),
+            (joint,) * (len(next_turns) - 2)
             + (shaped((owned, quarter), NARROW), shaped((owned, quarter))),
             holder,
             sums,
         )
-        parts = [swap(part, 2 * p) for p, part in zip(near_turns, parts)]
+        parts = [swap(part, 2 * p) for p, part in zip(next_turns, parts)]
         sums_parts = [part[owned : owned + SMALL_ROWS] for part in parts]
-        near_parts = [part[:owned] for part in parts] + [swap(side_part, 2), near_own]
+        next_parts = [part[:owned] for part in parts] + [swap(side_part, 2), near_own]
     else:
-        near_parts = [swap(flat[p].astype(NARROW), 2 * p) for p in near_turns[:-1]] + [flat[0]]
-        sums_parts = [swap(sums.astype(NARROW), 2 * p) for p in near_turns[:-2]]
+        next_parts = [swap(flat[p].astype(NARROW), 2 * p) for p in next_turns[:-1]] + [flat[0]]
+        sums_parts = [swap(sums.astype(NARROW), 2 * p) for p in next_turns[:-2]]
 
     input_grad = run(
         input_grad_body,
@@ -623,11 +632,11 @@
         mixed_stay,
         swap(mixed_leave, 2),
     )[0]
-    parts = list(far_parts) + near_parts
+    parts = list(first_parts) + next_parts
     parts, input_grad, output = lax.optimization_barrier((parts, input_grad, output))
 
     stay, leave, half_sums = run(
-        functools.partial(total_body, far_turns + near_turns),
+        functools.partial(total_body, first_turns + next_turns),
         (
             shaped((2, 2, own_rows, quarter)),
             shaped((owned + SMALL_ROWS, quarter)),

time: 74.8 us -> 81.3 us (1.087)
  waiting for transfers between devices: 21.3 us -> 28.6 us
  starting transfers between devices: 39 us -> 38.1 us
    ppermute x23 -> x24, waiting for transfers between devices: 17.8 us -> 25.1 us  [swap(): return lax.ppermute(value, 'row', [(i, i ^ bit) for i in range(count)])]
    ppermute x2, starting transfers between devices: 7.81 us -> 6.53 us  [swap_rim(): return lax.ppermute(value, 'row', pairs + [(j, i) for i, j in pairs])]
    ppermute x23 -> x24, starting transfers between devices: 28.6 us -> 29 us  [swap(): return lax.ppermute(value, 'row', [(i, i ^ bit) for i in range(count)])]
    pallas_call x16 -> x17, Pallas kernels: 13.1 us -> 13.1 us  [run(): pl.pallas_call(body, out_shape=outs, **extra, scratch_shapes=scratch, com...]
  transfers between devices with their start and end apart: 27 -> 28, of which waited for: 14 -> 13; matrix products, arithmetic and copies ran while one was open for 0% -> 0% of each run, Pallas kernels for 12% -> 11%
where the time goes in v10:
time: 81.3 us; the launch traced here: 80.8 us
  starting transfers between devices  38.1 us (47%)
  waiting for transfers between devices  28.6 us (35%)
  Pallas kernels  13.1 us (16%)
  between operations  0.87 us (1%)
    ppermute x24, starting transfers between devices, swap(): return lax.ppermute(value, 'row', [(i, i ^ bit) for i in range(count)])  29 us
    ppermute x24, waiting for transfers between devices, swap(): return lax.ppermute(value, 'row', [(i, i ^ bit) for i in range(count)])  25.1 us
    pallas_call x17, Pallas kernels, run(): pl.pallas_call(body, out_shape=outs, **extra, scratch_shapes=scratch, com...  13.1 us
    ppermute x2, starting transfers between devices, swap_rim(): return lax.ppermute(value, 'row', pairs + [(j, i) for i, j in pairs])  6.53 us
    ppermute x2, waiting for transfers between devices, swap_group(): return lax.ppermute(value, 'grp', [(0, 1), (1, 0)])  3.56 us
    ppermute x2, starting transfers between devices, swap_group(): return lax.ppermute(value, 'grp', [(0, 1), (1, 0)])  2.61 us
  transfers between devices with their start and end apart: 28, of which 13 were waited for; matrix products, arithmetic and copies ran while one was open for 0% of the time, Pallas kernels for 11%

profile of v10, /device:TPU:1, one launch (start us, length us, event | category | flops | bytes accessed | tf_op | source)
XLA Modules:
  0.0 80.8 jit_solution(10208556172954367103)
XLA Ops:
  0.6 1.3 %shard_map.160 = (bf16[2,2,32,512]{3,2,1,0:T(8,128)(2,1)S(1)}, bf16[224,512]{1,0:T(8,128)(2,1)S(1)}, bf16[96,512]{1,0:T(8,128)(2,1)S(1)}, bf16[128,512]{1,0:T(8,...) custom-call(f32[32,2048]{1,0:T(8,128)} %refs_0_.1, ...), custom_call_target="tpu_custom_call" | custom-call | tf_op jit(solution)/shard_map/pallas_call | solution.py:44
  2.1 4.5 %collective-permute-start.1 = (bf16[96,512]{1,0:T(8,128)(2,1)S(1)}, bf16[96,512]{1,0:T(8,128)(2,1)S(1)}, u32[]{:S(2)}, u32[]{:S(2)}) collective-permute-start(bf16[96,512]{1,0:T(8,128)(2,1)S(1)} %get-tuple-element.86), channel_id=1, source_target_pairs={{1,2},{3,4},{5,6},{7,8},{9,10},{11,12},{13,14},{2,1},{4,3},{6,5},{... | collective-permute-start | bytes 294920 | tf_op jit(solution)/shard_map/ppermute | solution.py:28
  6.6 2.4 %collective-permute-start.9 = (bf16[2,32,512]{2,1,0:T(8,128)(2,1)S(1)}, bf16[2,32,512]{2,1,0:T(8,128)(2,1)S(1)}, u32[]{:S(2)}, u32[]{:S(2)}) collective-permute-start(bf16[2,32,512]{2,1,0:T(8,128)(2,1)S(1)} %get-tuple-element.96), channel_id=1, source_target_pairs={{0,14},{1,15},{2,12},{3,13},{4,10},{5,11},{6,8},{7,9},{8,6},{9,7},... | collective-permute-start | bytes 196616 | tf_op jit(solution)/shard_map/ppermute | solution.py:22
  10.1 2.2 %collective-permute-start.5 = (bf16[2,32,512]{2,1,0:T(8,128)(2,1)S(1)}, bf16[2,32,512]{2,1,0:T(8,128)(2,1)S(1)}, u32[]{:S(2)}, u32[]{:S(2)}) collective-permute-start(bf16[2,32,512]{2,1,0:T(8,128)(2,1)S(1)} %get-tuple-element.95), channel_id=1, source_target_pairs={{0,12},{1,13},{2,14},{3,15},{4,8},{5,9},{6,10},{7,11},{8,4},{9,5},... | collective-permute-start | bytes 196616 | tf_op jit(solution)/shard_map/ppermute | solution.py:22
  13.3 1.3 %collective-permute-start.7 = (bf16[2,2,32,512]{3,2,1,0:T(8,128)(2,1)S(1)}, bf16[2,2,32,512]{3,2,1,0:T(8,128)(2,1)S(1)}, u32[]{:S(2)}, u32[]{:S(2)}) collective-permute-start(bf16[2,2,32,512]{3,2,1,0:T(8,128)(2,1)S(1)} %get-tuple-element.92.full), channel_id=1, source_target_pairs={{0,6},{1,7},{2,4},{3,5},{4,2},{5,3},{6,0},{7,1},{8,14},{9,15},{10,... | collective-permute-start | bytes 393224 | tf_op jit(solution)/shard_map/ppermute | solution.py:22
  14.6 2.4 %shard_map.162 = (f32[128,512]{1,0:T(8,128)S(1)}, f32[128,128]{1,0:T(8,128)S(1)}, bf16[384,512]{1,0:T(8,128)(2,1)S(1)}) custom-call(f32[4,32,512]{2,1,0:T(8,128)S(1)} %get-tuple-element.84.feats.refs_5_, bf16[224,512]{1,0:T(8,128)(2,1)S(1)} %collective-permute-done.other.core_got.refs_6_, bf16[96,512]{1,0:T(8,128)(2,1)S(1)} %collective-permute-done.1.outer.refs_7_, ...), custom_call_target="tpu_custom_call" | custom-call | tf_op jit(solution)/shard_map/pallas_call | solution.py:44
  18.4 2.4 %collective-permute-start.2 = (bf16[384,512]{1,0:T(8,128)(2,1)S(1)}, bf16[384,512]{1,0:T(8,128)(2,1)S(1)}, u32[]{:S(2)}, u32[]{:S(2)}) collective-permute-start(bf16[384,512]{1,0:T(8,128)(2,1)S(1)} %get-tuple-element.93.mine), channel_id=1, source_target_pairs={{0,2},{1,3},{2,0},{3,1},{4,6},{5,7},{6,4},{7,5},{8,10},{9,11},{10,... | collective-permute-start | bytes 1179656 | tf_op jit(solution)/shard_map/ppermute | solution.py:22
  25.1 2.9 %collective-permute-done.6.refs_1_.refs_6_ = bf16[2,2,32,512]{3,2,1,0:T(8,128)(2,1)S(1)} collective-permute-done((bf16[2,2,32,512]{3,2,1,0:T(8,128)(2,1)S(1)}, bf16[2,2,32,512]{3,2,1,0:T(8,128)(2,1)S(1)}, u32[]{:S(2)}, u32[]{:S(2)}) %collective-permute-start.6) | collective-permute-done | bytes 131104 | tf_op jit(solution)/shard_map/ppermute | solution.py:36
  28.0 1.6 %collective-permute-done.2.got = bf16[384,512]{1,0:T(8,128)(2,1)S(1)} collective-permute-done((bf16[384,512]{1,0:T(8,128)(2,1)S(1)}, bf16[384,512]{1,0:T(8,128)(2,1)S(1)}, u32[]{:S(2)}, u32[]{:S(2)}) %collective-permute-start.2) | collective-permute-done | bytes 393248 | tf_op jit(solution)/shard_map/ppermute | solution.py:22
  29.6 1.9 %collective-permute-start.11 = (bf16[2,256,512]{2,1,0:T(8,128)(2,1)S(1)}, bf16[2,256,512]{2,1,0:T(8,128)(2,1)S(1)}, u32[]{:S(2)}, u32[]{:S(2)}) collective-permute-start(bf16[2,256,512]{2,1,0:T(8,128)(2,1)S(1)} %get-tuple-element.97.refs_0_), channel_id=1, source_target_pairs={{0,1},{1,0},{2,3},{3,2},{4,5},{5,4},{6,7},{7,6},{8,9},{9,8},{10,11... | collective-permute-start | bytes 1572872 | tf_op jit(solution)/shard_map/ppermute | solution.py:22
  31.5 1.5 %collective-permute-done.11.refs_1_ = bf16[2,256,512]{2,1,0:T(8,128)(2,1)S(1)} collective-permute-done((bf16[2,256,512]{2,1,0:T(8,128)(2,1)S(1)}, bf16[2,256,512]{2,1,0:T(8,128)(2,1)S(1)}, u32[]{:S(2)}, u32[]{:S(2)}) %collective-permute-start.11) | collective-permute-done | bytes 524320 | tf_op jit(solution)/shard_map/ppermute | solution.py:22
  33.0 1.4 %shard_map.166 = (f32[256,512]{1,0:T(8,128)S(1)}, bf16[256,512]{1,0:T(8,128)(2,1)S(1)}, bf16[512,512]{1,0:T(8,128)(2,1)S(1)}, bf16[512,512]{1,0:T(8,128)(2,1)S(1...) custom-call(bf16[2,256,512]{2,1,0:T(8,128)(2,1)S(1)} %get-tuple-element.97.refs_0_, ...), custom_call_target="tpu_custom_call" | custom-call | tf_op jit(solution)/shard_map/pallas_call | solution.py:44
  38.5 2.6 %collective-permute-start.15 = (bf16[128,512]{1,0:T(8,128)(2,1)S(1)}, bf16[128,512]{1,0:T(8,128)(2,1)S(1)}, u32[]{:S(2)}, u32[]{:S(2)}) collective-permute-start(bf16[128,512]{1,0:T(8,128)(2,1)S(1)} %get-tuple-element.115), channel_id=1, source_target_pairs={{0,12},{1,13},{2,14},{3,15},{4,8},{5,9},{6,10},{7,11},{8,4},{9,5},... | collective-permute-start | bytes 393224 | tf_op jit(solution)/shard_map/ppermute | solution.py:22
  42.1 1.9 %shard_map.169 = (f32[128,512]{1,0:T(8,128)S(1)}, bf16[96,512]{1,0:T(8,128)(2,1)S(1)}, bf16[96,512]{1,0:T(8,128)(2,1)S(1)}, f32[28,512]{1,0:T(8,128)S(1)}, f32[28,512]{1,0:T(8,128)S(1)}) custom-call(f32[128,512]{1,0:T(8,128)S(1)} %get-tuple-element.102.refs_0_, bf16[128,512]{1,0:T(8,128)(2,1)S(1)} %collective-permute-done.13.refs_1_, ...), custom_call_target="tpu_custom_call" | custom-call | tf_op jit(solution)/shard_map/pallas_call | solution.py:44
  44.1 1.6 %collective-permute-start.14 = (f32[28,512]{1,0:T(8,128)S(1)}, f32[28,512]{1,0:T(8,128)S(1)}, u32[]{:S(2)}, u32[]{:S(2)}) collective-permute-start(f32[28,512]{1,0:T(8,128)S(1)} %get-tuple-element.113), channel_id=1, source_target_pairs={{0,1},{1,0},{2,3},{3,2},{4,5},{5,4},{6,7},{7,6},{8,9},{9,8},{10,11... | collective-permute-start | bytes 172040 | tf_op jit(solution)/shard_map/ppermute | solution.py:22
  45.6 2.1 %collective-permute-start.19 = (bf16[96,512]{1,0:T(8,128)(2,1)S(1)}, bf16[96,512]{1,0:T(8,128)(2,1)S(1)}, u32[]{:S(2)}, u32[]{:S(2)}) collective-permute-start(bf16[96,512]{1,0:T(8,128)(2,1)S(1)} %get-tuple-element.123), channel_id=1, source_target_pairs={{1,2},{3,4},{5,6},{7,8},{9,10},{11,12},{13,14},{2,1},{4,3},{6,5},{... | collective-permute-start | bytes 294920 | tf_op jit(solution)/shard_map/ppermute | solution.py:28
  47.8 3.6 %collective-permute-done.16.refs_1_ = bf16[128,512]{1,0:T(8,128)(2,1)S(1)} collective-permute-done((bf16[128,512]{1,0:T(8,128)(2,1)S(1)}, bf16[128,512]{1,0:T(8,128)(2,1)S(1)}, u32[]{:S(2)}, u32[]{:S(2)}) %collective-permute-start.16) | collective-permute-done | bytes 131104 | tf_op jit(solution)/shard_map/ppermute | solution.py:22
  51.9 2.6 %collective-permute-done.18 = f32[28,512]{1,0:T(8,128)S(1)} collective-permute-done((f32[28,512]{1,0:T(8,128)S(1)}, f32[28,512]{1,0:T(8,128)S(1)}, u32[]{:S(2)}, u32[]{:S(2)}) %collective-permute-start.18) | collective-permute-done | bytes 57376 | tf_op jit(solution)/shard_map/ppermute | solution.py:22
  54.5 1.8 %collective-permute-start.25 = (bf16[256,512]{1,0:T(8,128)(2,1)S(1)}, bf16[256,512]{1,0:T(8,128)(2,1)S(1)}, u32[]{:S(2)}, u32[]{:S(2)}) collective-permute-start(bf16[256,512]{1,0:T(8,128)(2,1)S(1)} %get-tuple-element.136), channel_id=1, source_target_pairs={{0,1},{1,0},{2,3},{3,2},{4,5},{5,4},{6,7},{7,6},{8,9},{9,8},{10,11... | collective-permute-start | bytes 786440 | tf_op jit(solution)/shard_map/ppermute | solution.py:22
  56.4 3.1 %collective-permute-start.21 = (bf16[160,512]{1,0:T(8,128)(2,1)S(1)}, bf16[160,512]{1,0:T(8,128)(2,1)S(1)}, u32[]{:S(2)}, u32[]{:S(2)}) collective-permute-start(bf16[160,512]{1,0:T(8,128)(2,1)S(1)} %get-tuple-element.126), channel_id=1, source_target_pairs={{0,14},{1,15},{2,12},{3,13},{4,10},{5,11},{6,8},{7,9},{8,6},{9,7},... | collective-permute-start | bytes 491528 | tf_op jit(solution)/shard_map/ppermute | solution.py:22
  59.5 1.8 %collective-permute-start.23 = (bf16[160,512]{1,0:T(8,128)(2,1)S(1)}, bf16[160,512]{1,0:T(8,128)(2,1)S(1)}, u32[]{:S(2)}, u32[]{:S(2)}) collective-permute-start(bf16[160,512]{1,0:T(8,128)(2,1)S(1)} %get-tuple-element.128), channel_id=1, source_target_pairs={{0,6},{1,7},{2,4},{3,5},{4,2},{5,3},{6,0},{7,1},{8,14},{9,15},{10,... | collective-permute-start | bytes 491528 | tf_op jit(solution)/shard_map/ppermute | solution.py:22
  62.8 2.9 %shard_map.172 = f32[4,32,512]{2,1,0:T(8,128)} custom-call(f32[128,512]{1,0:T(8,128)S(1)} %get-tuple-element.131.grad, bf16[96,512]{1,0:T(8,128)(2,1)S(1)} %collective-permute-done.20.inner, bf16[96,512]{1,0:T(8,128)(2,1)S(1)} %collective-permute-done.19.outer, f32[7,7,512]{2,1,0:T(8,128)S(1)} %get-tuple-element.87.kernel, ...), custom_call_target="tpu_custom_call" | custom-call | tf_op jit(solution)/shard_map/pallas_call | solution.py:44
  65.7 9.2 %collective-permute-done.22 = bf16[160,512]{1,0:T(8,128)(2,1)S(1)} collective-permute-done((bf16[160,512]{1,0:T(8,128)(2,1)S(1)}, bf16[160,512]{1,0:T(8,128)(2,1)S(1)}, u32[]{:S(2)}, u32[]{:S(2)}) %collective-permute-start.22) | collective-permute-done | bytes 163872 | tf_op jit(solution)/shard_map/ppermute | solution.py:22
  75.8 2.3 %collective-permute-done.24.refs_6_ = bf16[128,512]{1,0:T(8,128)(2,1)S(1)} collective-permute-done((bf16[128,512]{1,0:T(8,128)(2,1)S(1)}, bf16[128,512]{1,0:T(8,128)(2,1)S(1)}, u32[]{:S(2)}, u32[]{:S(2)}) %collective-permute-start.24) | collective-permute-done | bytes 131104 | tf_op jit(solution)/shard_map/ppermute | solution.py:22
  (57 shorter events, 18.7 us)
Async XLA Ops:
  2.0 4.6 %collective-permute-start = (bf16[224,512]{1,0:T(8,128)(2,1)S(1)}, bf16[224,512]{1,0:T(8,128)(2,1)S(1)}, u32[]{:S(2)}, u32[]{:S(2)}) collective-permute-start(bf16[224,512]{1,0:T(8,128)(2,1)S(1)} %get-tuple-element.85), channel_id=1, source_target_pairs={{0,1},{1,0},{2,3},{3,2},{4,5},{5,4},{6,7},{7,6},{8,9},{9,8},{10,11... | collective-permute-start | bytes 688136 | tf_op jit(solution)/shard_map/ppermute | solution.py:22
  2.1 11.2 %collective-permute-start.1 = (bf16[96,512]{1,0:T(8,128)(2,1)S(1)}, bf16[96,512]{1,0:T(8,128)(2,1)S(1)}, u32[]{:S(2)}, u32[]{:S(2)}) collective-permute-start(bf16[96,512]{1,0:T(8,128)(2,1)S(1)} %get-tuple-element.86), channel_id=1, source_target_pairs={{1,2},{3,4},{5,6},{7,8},{9,10},{11,12},{13,14},{2,1},{4,3},{6,5},{... | collective-permute-start | bytes 294920 | tf_op jit(solution)/shard_map/ppermute | solution.py:28
  6.6 10.4 %collective-permute-start.9 = (bf16[2,32,512]{2,1,0:T(8,128)(2,1)S(1)}, bf16[2,32,512]{2,1,0:T(8,128)(2,1)S(1)}, u32[]{:S(2)}, u32[]{:S(2)}) collective-permute-start(bf16[2,32,512]{2,1,0:T(8,128)(2,1)S(1)} %get-tuple-element.96), channel_id=1, source_target_pairs={{0,14},{1,15},{2,12},{3,13},{4,10},{5,11},{6,8},{7,9},{8,6},{9,7},... | collective-permute-start | bytes 196616 | tf_op jit(solution)/shard_map/ppermute | solution.py:22
  9.0 9.4 %collective-permute-start.8 = (bf16[2,32,512]{2,1,0:T(8,128)(2,1)S(1)}, bf16[2,32,512]{2,1,0:T(8,128)(2,1)S(1)}, u32[]{:S(2)}, u32[]{:S(2)}) collective-permute-start(bf16[2,32,512]{2,1,0:T(8,128)(2,1)S(1)} %get-tuple-element.96), channel_id=1, source_target_pairs={{0,10},{1,11},{2,8},{3,9},{4,14},{5,15},{6,12},{7,13},{8,2},{9,3},... | collective-permute-start | bytes 196616 | tf_op jit(solution)/shard_map/ppermute | solution.py:22
  10.1 10.8 %collective-permute-start.5 = (bf16[2,32,512]{2,1,0:T(8,128)(2,1)S(1)}, bf16[2,32,512]{2,1,0:T(8,128)(2,1)S(1)}, u32[]{:S(2)}, u32[]{:S(2)}) collective-permute-start(bf16[2,32,512]{2,1,0:T(8,128)(2,1)S(1)} %get-tuple-element.95), channel_id=1, source_target_pairs={{0,12},{1,13},{2,14},{3,15},{4,8},{5,9},{6,10},{7,11},{8,4},{9,5},... | collective-permute-start | bytes 196616 | tf_op jit(solution)/shard_map/ppermute | solution.py:22
  12.3 10.3 %collective-permute-start.4 = (bf16[2,32,512]{2,1,0:T(8,128)(2,1)S(1)}, bf16[2,32,512]{2,1,0:T(8,128)(2,1)S(1)}, u32[]{:S(2)}, u32[]{:S(2)}) collective-permute-start(bf16[2,32,512]{2,1,0:T(8,128)(2,1)S(1)} %get-tuple-element.95), channel_id=1, source_target_pairs={{0,8},{1,9},{2,10},{3,11},{4,12},{5,13},{6,14},{7,15},{8,0},{9,1},... | collective-permute-start | bytes 196616 | tf_op jit(solution)/shard_map/ppermute | solution.py:22
  13.3 10.6 %collective-permute-start.7 = (bf16[2,2,32,512]{3,2,1,0:T(8,128)(2,1)S(1)}, bf16[2,2,32,512]{3,2,1,0:T(8,128)(2,1)S(1)}, u32[]{:S(2)}, u32[]{:S(2)}) collective-permute-start(bf16[2,2,32,512]{3,2,1,0:T(8,128)(2,1)S(1)} %get-tuple-element.92.full), channel_id=1, source_target_pairs={{0,6},{1,7},{2,4},{3,5},{4,2},{5,3},{6,0},{7,1},{8,14},{9,15},{10,... | collective-permute-start | bytes 393224 | tf_op jit(solution)/shard_map/ppermute | solution.py:22
  17.1 7.3 %collective-permute-start.3 = (bf16[2,2,32,512]{3,2,1,0:T(8,128)(2,1)S(1)}, bf16[2,2,32,512]{3,2,1,0:T(8,128)(2,1)S(1)}, u32[]{:S(2)}, u32[]{:S(2)}) collective-permute-start(bf16[2,2,32,512]{3,2,1,0:T(8,128)(2,1)S(1)} %get-tuple-element.94.refs_3_), channel_id=1, source_target_pairs={{0,4},{1,5},{2,6},{3,7},{4,0},{5,1},{6,2},{7,3},{8,12},{9,13},{10,... | collective-permute-start | bytes 393224 | tf_op jit(solution)/shard_map/ppermute | solution.py:22
  18.4 11.1 %collective-permute-start.2 = (bf16[384,512]{1,0:T(8,128)(2,1)S(1)}, bf16[384,512]{1,0:T(8,128)(2,1)S(1)}, u32[]{:S(2)}, u32[]{:S(2)}) collective-permute-start(bf16[384,512]{1,0:T(8,128)(2,1)S(1)} %get-tuple-element.93.mine), channel_id=1, source_target_pairs={{0,2},{1,3},{2,0},{3,1},{4,6},{5,7},{6,4},{7,5},{8,10},{9,11},{10,... | collective-permute-start | bytes 1179656 | tf_op jit(solution)/shard_map/ppermute | solution.py:22
  20.9 4.2 %collective-permute-start.10 = (bf16[2,2,32,512]{3,2,1,0:T(8,128)(2,1)S(1)}, bf16[2,2,32,512]{3,2,1,0:T(8,128)(2,1)S(1)}, u32[]{:S(2)}, u32[]{:S(2)}) collective-permute-start(bf16[2,2,32,512]{3,2,1,0:T(8,128)(2,1)S(1)} %shard_map.164.refs_9_), channel_id=1, source_target_pairs={{0,16},{16,0},{1,17},{17,1},{2,18},{18,2},{3,19},{19,3},{4,20},{20... | collective-permute-start | bytes 393224 | tf_op jit(solution)/shard_map/ppermute | solution.py:36
  22.6 5.4 %collective-permute-start.6 = (bf16[2,2,32,512]{3,2,1,0:T(8,128)(2,1)S(1)}, bf16[2,2,32,512]{3,2,1,0:T(8,128)(2,1)S(1)}, u32[]{:S(2)}, u32[]{:S(2)}) collective-permute-start(bf16[2,2,32,512]{3,2,1,0:T(8,128)(2,1)S(1)} %shard_map.163.refs_5_), channel_id=1, source_target_pairs={{0,16},{16,0},{1,17},{17,1},{2,18},{18,2},{3,19},{19,3},{4,20},{20... | collective-permute-start | bytes 393224 | tf_op jit(solution)/shard_map/ppermute | solution.py:36
  36.1 6.0 %collective-permute-start.13 = (bf16[128,512]{1,0:T(8,128)(2,1)S(1)}, bf16[128,512]{1,0:T(8,128)(2,1)S(1)}, u32[]{:S(2)}, u32[]{:S(2)}) collective-permute-start(bf16[128,512]{1,0:T(8,128)(2,1)S(1)} %get-tuple-element.103.after), channel_id=1, source_target_pairs={{0,2},{1,3},{2,0},{3,1},{4,6},{5,7},{6,4},{7,5},{8,10},{9,11},{10,... | collective-permute-start | bytes 393224 | tf_op jit(solution)/shard_map/ppermute | solution.py:22
  38.5 9.3 %collective-permute-start.15 = (bf16[128,512]{1,0:T(8,128)(2,1)S(1)}, bf16[128,512]{1,0:T(8,128)(2,1)S(1)}, u32[]{:S(2)}, u32[]{:S(2)}) collective-permute-start(bf16[128,512]{1,0:T(8,128)(2,1)S(1)} %get-tuple-element.115), channel_id=1, source_target_pairs={{0,12},{1,13},{2,14},{3,15},{4,8},{5,9},{6,10},{7,11},{8,4},{9,5},... | collective-permute-start | bytes 393224 | tf_op jit(solution)/shard_map/ppermute | solution.py:22
  41.1 10.3 %collective-permute-start.16 = (bf16[128,512]{1,0:T(8,128)(2,1)S(1)}, bf16[128,512]{1,0:T(8,128)(2,1)S(1)}, u32[]{:S(2)}, u32[]{:S(2)}) collective-permute-start(bf16[128,512]{1,0:T(8,128)(2,1)S(1)} %get-tuple-element.116), channel_id=1, source_target_pairs={{0,8},{1,9},{2,10},{3,11},{4,12},{5,13},{6,14},{7,15},{8,0},{9,1},... | collective-permute-start | bytes 393224 | tf_op jit(solution)/shard_map/ppermute | solution.py:22
  41.1 10.3 %collective-permute-start.17 = (bf16[128,512]{1,0:T(8,128)(2,1)S(1)}, bf16[128,512]{1,0:T(8,128)(2,1)S(1)}, u32[]{:S(2)}, u32[]{:S(2)}) collective-permute-start(bf16[128,512]{1,0:T(8,128)(2,1)S(1)} %get-tuple-element.117), channel_id=1, source_target_pairs={{0,4},{1,5},{2,6},{3,7},{4,0},{5,1},{6,2},{7,3},{8,12},{9,13},{10,... | collective-permute-start | bytes 393224 | tf_op jit(solution)/shard_map/ppermute | solution.py:22
  44.1 3.6 %collective-permute-start.14 = (f32[28,512]{1,0:T(8,128)S(1)}, f32[28,512]{1,0:T(8,128)S(1)}, u32[]{:S(2)}, u32[]{:S(2)}) collective-permute-start(f32[28,512]{1,0:T(8,128)S(1)} %get-tuple-element.113), channel_id=1, source_target_pairs={{0,1},{1,0},{2,3},{3,2},{4,5},{5,4},{6,7},{7,6},{8,9},{9,8},{10,11... | collective-permute-start | bytes 172040 | tf_op jit(solution)/shard_map/ppermute | solution.py:22
  45.6 8.9 %collective-permute-start.19 = (bf16[96,512]{1,0:T(8,128)(2,1)S(1)}, bf16[96,512]{1,0:T(8,128)(2,1)S(1)}, u32[]{:S(2)}, u32[]{:S(2)}) collective-permute-start(bf16[96,512]{1,0:T(8,128)(2,1)S(1)} %get-tuple-element.123), channel_id=1, source_target_pairs={{1,2},{3,4},{5,6},{7,8},{9,10},{11,12},{13,14},{2,1},{4,3},{6,5},{... | collective-permute-start | bytes 294920 | tf_op jit(solution)/shard_map/ppermute | solution.py:28
  47.7 6.8 %collective-permute-start.20 = (bf16[96,512]{1,0:T(8,128)(2,1)S(1)}, bf16[96,512]{1,0:T(8,128)(2,1)S(1)}, u32[]{:S(2)}, u32[]{:S(2)}) collective-permute-start(bf16[96,512]{1,0:T(8,128)(2,1)S(1)} %get-tuple-element.124), channel_id=1, source_target_pairs={{0,1},{1,0},{2,3},{3,2},{4,5},{5,4},{6,7},{7,6},{8,9},{9,8},{10,11... | collective-permute-start | bytes 294920 | tf_op jit(solution)/shard_map/ppermute | solution.py:22
  54.5 6.7 %collective-permute-start.25 = (bf16[256,512]{1,0:T(8,128)(2,1)S(1)}, bf16[256,512]{1,0:T(8,128)(2,1)S(1)}, u32[]{:S(2)}, u32[]{:S(2)}) collective-permute-start(bf16[256,512]{1,0:T(8,128)(2,1)S(1)} %get-tuple-element.136), channel_id=1, source_target_pairs={{0,1},{1,0},{2,3},{3,2},{4,5},{5,4},{6,7},{7,6},{8,9},{9,8},{10,11... | collective-permute-start | bytes 786440 | tf_op jit(solution)/shard_map/ppermute | solution.py:22
  56.4 9.3 %collective-permute-start.21 = (bf16[160,512]{1,0:T(8,128)(2,1)S(1)}, bf16[160,512]{1,0:T(8,128)(2,1)S(1)}, u32[]{:S(2)}, u32[]{:S(2)}) collective-permute-start(bf16[160,512]{1,0:T(8,128)(2,1)S(1)} %get-tuple-element.126), channel_id=1, source_target_pairs={{0,14},{1,15},{2,12},{3,13},{4,10},{5,11},{6,8},{7,9},{8,6},{9,7},... | collective-permute-start | bytes 491528 | tf_op jit(solution)/shard_map/ppermute | solution.py:22
  59.5 15.5 %collective-permute-start.22 = (bf16[160,512]{1,0:T(8,128)(2,1)S(1)}, bf16[160,512]{1,0:T(8,128)(2,1)S(1)}, u32[]{:S(2)}, u32[]{:S(2)}) collective-permute-start(bf16[160,512]{1,0:T(8,128)(2,1)S(1)} %get-tuple-element.127), channel_id=1, source_target_pairs={{0,10},{1,11},{2,8},{3,9},{4,14},{5,15},{6,12},{7,13},{8,2},{9,3},... | collective-permute-start | bytes 491528 | tf_op jit(solution)/shard_map/ppermute | solution.py:22
  59.5 15.5 %collective-permute-start.23 = (bf16[160,512]{1,0:T(8,128)(2,1)S(1)}, bf16[160,512]{1,0:T(8,128)(2,1)S(1)}, u32[]{:S(2)}, u32[]{:S(2)}) collective-permute-start(bf16[160,512]{1,0:T(8,128)(2,1)S(1)} %get-tuple-element.128), channel_id=1, source_target_pairs={{0,6},{1,7},{2,4},{3,5},{4,2},{5,3},{6,0},{7,1},{8,14},{9,15},{10,... | collective-permute-start | bytes 491528 | tf_op jit(solution)/shard_map/ppermute | solution.py:22
  61.3 13.7 %collective-permute-start.26 = (bf16[128,512]{1,0:T(8,128)(2,1)S(1)}, bf16[128,512]{1,0:T(8,128)(2,1)S(1)}, u32[]{:S(2)}, u32[]{:S(2)}) collective-permute-start(bf16[128,512]{1,0:T(8,128)(2,1)S(1)} %get-tuple-element.138), channel_id=1, source_target_pairs={{0,2},{1,3},{2,0},{3,1},{4,6},{5,7},{6,4},{7,5},{8,10},{9,11},{10,... | collective-permute-start | bytes 393224 | tf_op jit(solution)/shard_map/ppermute | solution.py:22
  62.2 15.8 %collective-permute-start.24 = (bf16[128,512]{1,0:T(8,128)(2,1)S(1)}, bf16[128,512]{1,0:T(8,128)(2,1)S(1)}, u32[]{:S(2)}, u32[]{:S(2)}) collective-permute-start(bf16[128,512]{1,0:T(8,128)(2,1)S(1)} %get-tuple-element.129), channel_id=1, source_target_pairs={{0,2},{1,3},{2,0},{3,1},{4,6},{5,7},{6,4},{7,5},{8,10},{9,11},{10,... | collective-permute-start | bytes 393224 | tf_op jit(solution)/shard_map/ppermute | solution.py:22
  (4 other events, 10.0 us)

commit v11 on v10

--- a/solution.py
+++ b/solution.py
@@ -551,6 +551,7 @@
         scale,
         mib=24,
     )
+    mixed_stay, mixed_leave = run(fold_body, half, mixed_keep, swap(mixed_send, 1))
     conv_grad, inner_out, rim_out, stay, leave = run(
         functools.partial(conv_grad_body, norm_scale),
         (
@@ -576,8 +577,8 @@
     inner_got = swap(inner_out, 1)
     sums = stay + swap(leave, 1)
 
-    first_turns = (*range(2 * patterns - 2, 3, -2), 2)
-    next_turns = (*range(2 * patterns - 1, 4, -2), 3, 1, 0)
+    first_turns = (*range(2 * patterns - 1, 4, -2), 3)
+    next_turns = (*range(4, 2 * patterns, 2), 2, 1, 0)
     owned = 4 * own_rows
     if copied:
         parts = run(
@@ -594,10 +595,7 @@
     first_parts = [swap(part, 2 * p) for p, part in zip(first_turns, parts)]
     sums, first_parts = lax.optimization_barrier((sums, first_parts))
     sums = sums + swap(sums, 2)
-    sums, mixed_send, rim_got, inner_got = lax.optimization_barrier(
-        (sums, mixed_send, rim_got, inner_got)
-    )
-    mixed_stay, mixed_leave = run(fold_body, half, mixed_keep, swap(mixed_send, 1))
+    sums, mixed_leave = lax.optimization_barrier((sums, mixed_leave))
     if copied:
         joint = shaped((owned + 32, quarter), NARROW)
         *parts, side_part, near_own = run(

time: 81.3 us -> 73.4 us (0.903)
  waiting for transfers between devices: 28.6 us -> 17.3 us
  starting transfers between devices: 38.1 us -> 41.6 us
    ppermute x24, waiting for transfers between devices: 25.1 us -> 13.7 us  [swap(): return lax.ppermute(value, 'row', [(i, i ^ bit) for i in range(count)])]
    ppermute x24, starting transfers between devices: 29 us -> 32.1 us  [swap(): return lax.ppermute(value, 'row', [(i, i ^ bit) for i in range(count)])]
  transfers between devices with their start and end apart: 28 -> 28, of which waited for: 13 -> 11; matrix products, arithmetic and copies ran while one was open for 0% -> 0% of each run, Pallas kernels for 11% -> 13%
where the time goes in v11:
time: 73.4 us; the launch traced here: 72.9 us
  starting transfers between devices  41.6 us (57%)
  waiting for transfers between devices  17.3 us (24%)
  Pallas kernels  13.1 us (18%)
  between operations  0.86 us (1%)
    ppermute x24, starting transfers between devices, swap(): return lax.ppermute(value, 'row', [(i, i ^ bit) for i in range(count)])  32.1 us
    ppermute x24, waiting for transfers between devices, swap(): return lax.ppermute(value, 'row', [(i, i ^ bit) for i in range(count)])  13.7 us
    pallas_call x17, Pallas kernels, run(): pl.pallas_call(body, out_shape=outs, **extra, scratch_shapes=scratch, com...  13.1 us
    ppermute x2, starting transfers between devices, swap_rim(): return lax.ppermute(value, 'row', pairs + [(j, i) for i, j in pairs])  6.8 us
    ppermute x2, waiting for transfers between devices, swap_group(): return lax.ppermute(value, 'grp', [(0, 1), (1, 0)])  3.56 us
    ppermute x2, starting transfers between devices, swap_group(): return lax.ppermute(value, 'grp', [(0, 1), (1, 0)])  2.61 us
  transfers between devices with their start and end apart: 28, of which 11 were waited for; matrix products, arithmetic and copies ran while one was open for 0% of the time, Pallas kernels for 13%

profile of v11, /device:TPU:1, one launch (start us, length us, event | category | flops | bytes accessed | tf_op | source)
XLA Modules:
  0.0 72.9 jit_solution(15595352647106605285)
XLA Ops:
  0.6 1.3 %shard_map.160 = (bf16[2,2,32,512]{3,2,1,0:T(8,128)(2,1)S(1)}, bf16[224,512]{1,0:T(8,128)(2,1)S(1)}, bf16[96,512]{1,0:T(8,128)(2,1)S(1)}, bf16[128,512]{1,0:T(8,...) custom-call(f32[32,2048]{1,0:T(8,128)} %refs_0_.1, ...), custom_call_target="tpu_custom_call" | custom-call | tf_op jit(solution)/shard_map/pallas_call | solution.py:44
  2.1 4.5 %collective-permute-start.1 = (bf16[96,512]{1,0:T(8,128)(2,1)S(1)}, bf16[96,512]{1,0:T(8,128)(2,1)S(1)}, u32[]{:S(2)}, u32[]{:S(2)}) collective-permute-start(bf16[96,512]{1,0:T(8,128)(2,1)S(1)} %get-tuple-element.84), channel_id=1, source_target_pairs={{1,2},{3,4},{5,6},{7,8},{9,10},{11,12},{13,14},{2,1},{4,3},{6,5},{... | collective-permute-start | bytes 294920 | tf_op jit(solution)/shard_map/ppermute | solution.py:28
  6.6 2.4 %collective-permute-start.9 = (bf16[2,32,512]{2,1,0:T(8,128)(2,1)S(1)}, bf16[2,32,512]{2,1,0:T(8,128)(2,1)S(1)}, u32[]{:S(2)}, u32[]{:S(2)}) collective-permute-start(bf16[2,32,512]{2,1,0:T(8,128)(2,1)S(1)} %get-tuple-element.94), channel_id=1, source_target_pairs={{0,14},{1,15},{2,12},{3,13},{4,10},{5,11},{6,8},{7,9},{8,6},{9,7},... | collective-permute-start | bytes 196616 | tf_op jit(solution)/shard_map/ppermute | solution.py:22
  10.1 2.2 %collective-permute-start.5 = (bf16[2,32,512]{2,1,0:T(8,128)(2,1)S(1)}, bf16[2,32,512]{2,1,0:T(8,128)(2,1)S(1)}, u32[]{:S(2)}, u32[]{:S(2)}) collective-permute-start(bf16[2,32,512]{2,1,0:T(8,128)(2,1)S(1)} %get-tuple-element.93), channel_id=1, source_target_pairs={{0,12},{1,13},{2,14},{3,15},{4,8},{5,9},{6,10},{7,11},{8,4},{9,5},... | collective-permute-start | bytes 196616 | tf_op jit(solution)/shard_map/ppermute | solution.py:22
  14.6 2.4 %shard_map.162 = (f32[128,512]{1,0:T(8,128)S(1)}, f32[128,128]{1,0:T(8,128)S(1)}, bf16[384,512]{1,0:T(8,128)(2,1)S(1)}) custom-call(f32[4,32,512]{2,1,0:T(8,128)S(1)} %get-tuple-element.82.feats.refs_5_, bf16[224,512]{1,0:T(8,128)(2,1)S(1)} %collective-permute-done.other.core_got.refs_6_, bf16[96,512]{1,0:T(8,128)(2,1)S(1)} %collective-permute-done.1.outer.refs_7_, ...), custom_call_target="tpu_custom_call" | custom-call | tf_op jit(solution)/shard_map/pallas_call | solution.py:44
  18.4 2.4 %collective-permute-start.2 = (bf16[384,512]{1,0:T(8,128)(2,1)S(1)}, bf16[384,512]{1,0:T(8,128)(2,1)S(1)}, u32[]{:S(2)}, u32[]{:S(2)}) collective-permute-start(bf16[384,512]{1,0:T(8,128)(2,1)S(1)} %get-tuple-element.91.mine), channel_id=1, source_target_pairs={{0,2},{1,3},{2,0},{3,1},{4,6},{5,7},{6,4},{7,5},{8,10},{9,11},{10,... | collective-permute-start | bytes 1179656 | tf_op jit(solution)/shard_map/ppermute | solution.py:22
  25.1 2.9 %collective-permute-done.6.refs_1_.refs_6_ = bf16[2,2,32,512]{3,2,1,0:T(8,128)(2,1)S(1)} collective-permute-done((bf16[2,2,32,512]{3,2,1,0:T(8,128)(2,1)S(1)}, bf16[2,2,32,512]{3,2,1,0:T(8,128)(2,1)S(1)}, u32[]{:S(2)}, u32[]{:S(2)}) %collective-permute-start.6) | collective-permute-done | bytes 131104 | tf_op jit(solution)/shard_map/ppermute | solution.py:36
  28.0 1.6 %collective-permute-done.2.got = bf16[384,512]{1,0:T(8,128)(2,1)S(1)} collective-permute-done((bf16[384,512]{1,0:T(8,128)(2,1)S(1)}, bf16[384,512]{1,0:T(8,128)(2,1)S(1)}, u32[]{:S(2)}, u32[]{:S(2)}) %collective-permute-start.2) | collective-permute-done | bytes 393248 | tf_op jit(solution)/shard_map/ppermute | solution.py:22
  29.6 1.9 %collective-permute-start.11 = (bf16[2,256,512]{2,1,0:T(8,128)(2,1)S(1)}, bf16[2,256,512]{2,1,0:T(8,128)(2,1)S(1)}, u32[]{:S(2)}, u32[]{:S(2)}) collective-permute-start(bf16[2,256,512]{2,1,0:T(8,128)(2,1)S(1)} %get-tuple-element.95.refs_0_), channel_id=1, source_target_pairs={{0,1},{1,0},{2,3},{3,2},{4,5},{5,4},{6,7},{7,6},{8,9},{9,8},{10,11... | collective-permute-start | bytes 1572872 | tf_op jit(solution)/shard_map/ppermute | solution.py:22
  31.5 1.5 %collective-permute-done.11.refs_1_ = bf16[2,256,512]{2,1,0:T(8,128)(2,1)S(1)} collective-permute-done((bf16[2,256,512]{2,1,0:T(8,128)(2,1)S(1)}, bf16[2,256,512]{2,1,0:T(8,128)(2,1)S(1)}, u32[]{:S(2)}, u32[]{:S(2)}) %collective-permute-start.11) | collective-permute-done | bytes 524320 | tf_op jit(solution)/shard_map/ppermute | solution.py:22
  33.0 1.4 %shard_map.166 = (f32[256,512]{1,0:T(8,128)S(1)}, bf16[256,512]{1,0:T(8,128)(2,1)S(1)}, bf16[512,512]{1,0:T(8,128)(2,1)S(1)}, bf16[512,512]{1,0:T(8,128)(2,1)S(1...) custom-call(bf16[2,256,512]{2,1,0:T(8,128)(2,1)S(1)} %get-tuple-element.95.refs_0_, ...), custom_call_target="tpu_custom_call" | custom-call | tf_op jit(solution)/shard_map/pallas_call | solution.py:44
  37.5 3.1 %collective-permute-start.15 = (bf16[128,512]{1,0:T(8,128)(2,1)S(1)}, bf16[128,512]{1,0:T(8,128)(2,1)S(1)}, u32[]{:S(2)}, u32[]{:S(2)}) collective-permute-start(bf16[128,512]{1,0:T(8,128)(2,1)S(1)} %get-tuple-element.113), channel_id=1, source_target_pairs={{0,14},{1,15},{2,12},{3,13},{4,10},{5,11},{6,8},{7,9},{8,6},{9,7},... | collective-permute-start | bytes 393224 | tf_op jit(solution)/shard_map/ppermute | solution.py:22
  40.6 1.4 %collective-permute-start.17 = (bf16[128,512]{1,0:T(8,128)(2,1)S(1)}, bf16[128,512]{1,0:T(8,128)(2,1)S(1)}, u32[]{:S(2)}, u32[]{:S(2)}) collective-permute-start(bf16[128,512]{1,0:T(8,128)(2,1)S(1)} %get-tuple-element.115), channel_id=1, source_target_pairs={{0,6},{1,7},{2,4},{3,5},{4,2},{5,3},{6,0},{7,1},{8,14},{9,15},{10,... | collective-permute-start | bytes 393224 | tf_op jit(solution)/shard_map/ppermute | solution.py:22
  42.0 1.9 %shard_map.169 = (f32[128,512]{1,0:T(8,128)S(1)}, bf16[96,512]{1,0:T(8,128)(2,1)S(1)}, bf16[96,512]{1,0:T(8,128)(2,1)S(1)}, f32[28,512]{1,0:T(8,128)S(1)}, f32[28,512]{1,0:T(8,128)S(1)}) custom-call(f32[128,512]{1,0:T(8,128)S(1)} %get-tuple-element.100.refs_0_, bf16[128,512]{1,0:T(8,128)(2,1)S(1)} %collective-permute-done.13.refs_1_, ...), custom_call_target="tpu_custom_call" | custom-call | tf_op jit(solution)/shard_map/pallas_call | solution.py:44
  44.0 1.6 %collective-permute-start.14 = (f32[28,512]{1,0:T(8,128)S(1)}, f32[28,512]{1,0:T(8,128)S(1)}, u32[]{:S(2)}, u32[]{:S(2)}) collective-permute-start(f32[28,512]{1,0:T(8,128)S(1)} %get-tuple-element.111), channel_id=1, source_target_pairs={{0,1},{1,0},{2,3},{3,2},{4,5},{5,4},{6,7},{7,6},{8,9},{9,8},{10,11... | collective-permute-start | bytes 172040 | tf_op jit(solution)/shard_map/ppermute | solution.py:22
  45.5 1.9 %collective-permute-start.24 = (bf16[96,512]{1,0:T(8,128)(2,1)S(1)}, bf16[96,512]{1,0:T(8,128)(2,1)S(1)}, u32[]{:S(2)}, u32[]{:S(2)}) collective-permute-start(bf16[96,512]{1,0:T(8,128)(2,1)S(1)} %get-tuple-element.130), channel_id=1, source_target_pairs={{0,1},{1,0},{2,3},{3,2},{4,5},{5,4},{6,7},{7,6},{8,9},{9,8},{10,11... | collective-permute-start | bytes 294920 | tf_op jit(solution)/shard_map/ppermute | solution.py:22
  47.4 2.3 %collective-permute-start.25 = (bf16[96,512]{1,0:T(8,128)(2,1)S(1)}, bf16[96,512]{1,0:T(8,128)(2,1)S(1)}, u32[]{:S(2)}, u32[]{:S(2)}) collective-permute-start(bf16[96,512]{1,0:T(8,128)(2,1)S(1)} %get-tuple-element.131), channel_id=1, source_target_pairs={{1,2},{3,4},{5,6},{7,8},{9,10},{11,12},{13,14},{2,1},{4,3},{6,5},{... | collective-permute-start | bytes 294920 | tf_op jit(solution)/shard_map/ppermute | solution.py:28
  49.8 1.5 %collective-permute-done.16.refs_1_ = bf16[128,512]{1,0:T(8,128)(2,1)S(1)} collective-permute-done((bf16[128,512]{1,0:T(8,128)(2,1)S(1)}, bf16[128,512]{1,0:T(8,128)(2,1)S(1)}, u32[]{:S(2)}, u32[]{:S(2)}) %collective-permute-start.16) | collective-permute-done | bytes 131104 | tf_op jit(solution)/shard_map/ppermute | solution.py:22
  51.9 2.5 %collective-permute-done.18 = f32[28,512]{1,0:T(8,128)S(1)} collective-permute-done((f32[28,512]{1,0:T(8,128)S(1)}, f32[28,512]{1,0:T(8,128)S(1)}, u32[]{:S(2)}, u32[]{:S(2)}) %collective-permute-start.18) | collective-permute-done | bytes 57376 | tf_op jit(solution)/shard_map/ppermute | solution.py:22
  55.7 2.3 %collective-permute-start.21 = (bf16[160,512]{1,0:T(8,128)(2,1)S(1)}, bf16[160,512]{1,0:T(8,128)(2,1)S(1)}, u32[]{:S(2)}, u32[]{:S(2)}) collective-permute-start(bf16[160,512]{1,0:T(8,128)(2,1)S(1)} %get-tuple-element.125), channel_id=1, source_target_pairs={{0,12},{1,13},{2,14},{3,15},{4,8},{5,9},{6,10},{7,11},{8,4},{9,5},... | collective-permute-start | bytes 491528 | tf_op jit(solution)/shard_map/ppermute | solution.py:22
  58.1 1.6 %collective-permute-start.26 = (bf16[128,512]{1,0:T(8,128)(2,1)S(1)}, bf16[128,512]{1,0:T(8,128)(2,1)S(1)}, u32[]{:S(2)}, u32[]{:S(2)}) collective-permute-start(bf16[128,512]{1,0:T(8,128)(2,1)S(1)} %get-tuple-element.134), channel_id=1, source_target_pairs={{0,2},{1,3},{2,0},{3,1},{4,6},{5,7},{6,4},{7,5},{8,10},{9,11},{10,... | collective-permute-start | bytes 393224 | tf_op jit(solution)/shard_map/ppermute | solution.py:22
  59.7 2.9 %shard_map.173 = f32[4,32,512]{2,1,0:T(8,128)} custom-call(f32[128,512]{1,0:T(8,128)S(1)} %get-tuple-element.129.grad, bf16[96,512]{1,0:T(8,128)(2,1)S(1)} %collective-permute-done.24.inner, bf16[96,512]{1,0:T(8,128)(2,1)S(1)} %collective-permute-done.25.outer, f32[7,7,512]{2,1,0:T(8,128)S(1)} %get-tuple-element.85.kernel, ...), custom_call_target="tpu_custom_call" | custom-call | tf_op jit(solution)/shard_map/pallas_call | solution.py:44
  63.3 3.4 %collective-permute-done.20 = bf16[160,512]{1,0:T(8,128)(2,1)S(1)} collective-permute-done((bf16[160,512]{1,0:T(8,128)(2,1)S(1)}, bf16[160,512]{1,0:T(8,128)(2,1)S(1)}, u32[]{:S(2)}, u32[]{:S(2)}) %collective-permute-start.20) | collective-permute-done | bytes 163872 | tf_op jit(solution)/shard_map/ppermute | solution.py:22
  67.0 3.8 %collective-permute-start.27 = (f32[156,512]{1,0:T(8,128)S(1)}, f32[156,512]{1,0:T(8,128)S(1)}, u32[]{:S(2)}, u32[]{:S(2)}) collective-permute-start(f32[156,512]{1,0:T(8,128)S(1)} %get-tuple-element.146), channel_id=1, source_target_pairs={{0,1},{1,0},{2,3},{3,2},{4,5},{5,4},{6,7},{7,6},{8,9},{9,8},{10,11... | collective-permute-start | bytes 958472 | tf_op jit(solution)/shard_map/ppermute | solution.py:22
  (57 shorter events, 17.3 us)
Async XLA Ops:
  2.0 4.6 %collective-permute-start = (bf16[224,512]{1,0:T(8,128)(2,1)S(1)}, bf16[224,512]{1,0:T(8,128)(2,1)S(1)}, u32[]{:S(2)}, u32[]{:S(2)}) collective-permute-start(bf16[224,512]{1,0:T(8,128)(2,1)S(1)} %get-tuple-element.83), channel_id=1, source_target_pairs={{0,1},{1,0},{2,3},{3,2},{4,5},{5,4},{6,7},{7,6},{8,9},{9,8},{10,11... | collective-permute-start | bytes 688136 | tf_op jit(solution)/shard_map/ppermute | solution.py:22
  2.1 11.2 %collective-permute-start.1 = (bf16[96,512]{1,0:T(8,128)(2,1)S(1)}, bf16[96,512]{1,0:T(8,128)(2,1)S(1)}, u32[]{:S(2)}, u32[]{:S(2)}) collective-permute-start(bf16[96,512]{1,0:T(8,128)(2,1)S(1)} %get-tuple-element.84), channel_id=1, source_target_pairs={{1,2},{3,4},{5,6},{7,8},{9,10},{11,12},{13,14},{2,1},{4,3},{6,5},{... | collective-permute-start | bytes 294920 | tf_op jit(solution)/shard_map/ppermute | solution.py:28
  6.6 10.4 %collective-permute-start.9 = (bf16[2,32,512]{2,1,0:T(8,128)(2,1)S(1)}, bf16[2,32,512]{2,1,0:T(8,128)(2,1)S(1)}, u32[]{:S(2)}, u32[]{:S(2)}) collective-permute-start(bf16[2,32,512]{2,1,0:T(8,128)(2,1)S(1)} %get-tuple-element.94), channel_id=1, source_target_pairs={{0,14},{1,15},{2,12},{3,13},{4,10},{5,11},{6,8},{7,9},{8,6},{9,7},... | collective-permute-start | bytes 196616 | tf_op jit(solution)/shard_map/ppermute | solution.py:22
  9.0 9.4 %collective-permute-start.8 = (bf16[2,32,512]{2,1,0:T(8,128)(2,1)S(1)}, bf16[2,32,512]{2,1,0:T(8,128)(2,1)S(1)}, u32[]{:S(2)}, u32[]{:S(2)}) collective-permute-start(bf16[2,32,512]{2,1,0:T(8,128)(2,1)S(1)} %get-tuple-element.94), channel_id=1, source_target_pairs={{0,10},{1,11},{2,8},{3,9},{4,14},{5,15},{6,12},{7,13},{8,2},{9,3},... | collective-permute-start | bytes 196616 | tf_op jit(solution)/shard_map/ppermute | solution.py:22
  10.1 10.8 %collective-permute-start.5 = (bf16[2,32,512]{2,1,0:T(8,128)(2,1)S(1)}, bf16[2,32,512]{2,1,0:T(8,128)(2,1)S(1)}, u32[]{:S(2)}, u32[]{:S(2)}) collective-permute-start(bf16[2,32,512]{2,1,0:T(8,128)(2,1)S(1)} %get-tuple-element.93), channel_id=1, source_target_pairs={{0,12},{1,13},{2,14},{3,15},{4,8},{5,9},{6,10},{7,11},{8,4},{9,5},... | collective-permute-start | bytes 196616 | tf_op jit(solution)/shard_map/ppermute | solution.py:22
  12.3 10.3 %collective-permute-start.4 = (bf16[2,32,512]{2,1,0:T(8,128)(2,1)S(1)}, bf16[2,32,512]{2,1,0:T(8,128)(2,1)S(1)}, u32[]{:S(2)}, u32[]{:S(2)}) collective-permute-start(bf16[2,32,512]{2,1,0:T(8,128)(2,1)S(1)} %get-tuple-element.93), channel_id=1, source_target_pairs={{0,8},{1,9},{2,10},{3,11},{4,12},{5,13},{6,14},{7,15},{8,0},{9,1},... | collective-permute-start | bytes 196616 | tf_op jit(solution)/shard_map/ppermute | solution.py:22
  13.3 10.6 %collective-permute-start.7 = (bf16[2,2,32,512]{3,2,1,0:T(8,128)(2,1)S(1)}, bf16[2,2,32,512]{3,2,1,0:T(8,128)(2,1)S(1)}, u32[]{:S(2)}, u32[]{:S(2)}) collective-permute-start(bf16[2,2,32,512]{3,2,1,0:T(8,128)(2,1)S(1)} %get-tuple-element.90.full), channel_id=1, source_target_pairs={{0,6},{1,7},{2,4},{3,5},{4,2},{5,3},{6,0},{7,1},{8,14},{9,15},{10,... | collective-permute-start | bytes 393224 | tf_op jit(solution)/shard_map/ppermute | solution.py:22
  17.1 7.3 %collective-permute-start.3 = (bf16[2,2,32,512]{3,2,1,0:T(8,128)(2,1)S(1)}, bf16[2,2,32,512]{3,2,1,0:T(8,128)(2,1)S(1)}, u32[]{:S(2)}, u32[]{:S(2)}) collective-permute-start(bf16[2,2,32,512]{3,2,1,0:T(8,128)(2,1)S(1)} %get-tuple-element.92.refs_3_), channel_id=1, source_target_pairs={{0,4},{1,5},{2,6},{3,7},{4,0},{5,1},{6,2},{7,3},{8,12},{9,13},{10,... | collective-permute-start | bytes 393224 | tf_op jit(solution)/shard_map/ppermute | solution.py:22
  18.4 11.1 %collective-permute-start.2 = (bf16[384,512]{1,0:T(8,128)(2,1)S(1)}, bf16[384,512]{1,0:T(8,128)(2,1)S(1)}, u32[]{:S(2)}, u32[]{:S(2)}) collective-permute-start(bf16[384,512]{1,0:T(8,128)(2,1)S(1)} %get-tuple-element.91.mine), channel_id=1, source_target_pairs={{0,2},{1,3},{2,0},{3,1},{4,6},{5,7},{6,4},{7,5},{8,10},{9,11},{10,... | collective-permute-start | bytes 1179656 | tf_op jit(solution)/shard_map/ppermute | solution.py:22
  20.9 4.2 %collective-permute-start.10 = (bf16[2,2,32,512]{3,2,1,0:T(8,128)(2,1)S(1)}, bf16[2,2,32,512]{3,2,1,0:T(8,128)(2,1)S(1)}, u32[]{:S(2)}, u32[]{:S(2)}) collective-permute-start(bf16[2,2,32,512]{3,2,1,0:T(8,128)(2,1)S(1)} %shard_map.164.refs_9_), channel_id=1, source_target_pairs={{0,16},{16,0},{1,17},{17,1},{2,18},{18,2},{3,19},{19,3},{4,20},{20... | collective-permute-start | bytes 393224 | tf_op jit(solution)/shard_map/ppermute | solution.py:36
  22.6 5.4 %collective-permute-start.6 = (bf16[2,2,32,512]{3,2,1,0:T(8,128)(2,1)S(1)}, bf16[2,2,32,512]{3,2,1,0:T(8,128)(2,1)S(1)}, u32[]{:S(2)}, u32[]{:S(2)}) collective-permute-start(bf16[2,2,32,512]{3,2,1,0:T(8,128)(2,1)S(1)} %shard_map.163.refs_5_), channel_id=1, source_target_pairs={{0,16},{16,0},{1,17},{17,1},{2,18},{18,2},{3,19},{19,3},{4,20},{20... | collective-permute-start | bytes 393224 | tf_op jit(solution)/shard_map/ppermute | solution.py:36
  35.9 15.9 %collective-permute-start.19 = (bf16[256,512]{1,0:T(8,128)(2,1)S(1)}, bf16[256,512]{1,0:T(8,128)(2,1)S(1)}, u32[]{:S(2)}, u32[]{:S(2)}) collective-permute-start(bf16[256,512]{1,0:T(8,128)(2,1)S(1)} %get-tuple-element.121), channel_id=1, source_target_pairs={{0,1},{1,0},{2,3},{3,2},{4,5},{5,4},{6,7},{7,6},{8,9},{9,8},{10,11... | collective-permute-start | bytes 786440 | tf_op jit(solution)/shard_map/ppermute | solution.py:22
  36.2 5.8 %collective-permute-start.13 = (bf16[128,512]{1,0:T(8,128)(2,1)S(1)}, bf16[128,512]{1,0:T(8,128)(2,1)S(1)}, u32[]{:S(2)}, u32[]{:S(2)}) collective-permute-start(bf16[128,512]{1,0:T(8,128)(2,1)S(1)} %get-tuple-element.101.after), channel_id=1, source_target_pairs={{0,2},{1,3},{2,0},{3,1},{4,6},{5,7},{6,4},{7,5},{8,10},{9,11},{10,... | collective-permute-start | bytes 393224 | tf_op jit(solution)/shard_map/ppermute | solution.py:22
  37.5 8.0 %collective-permute-start.15 = (bf16[128,512]{1,0:T(8,128)(2,1)S(1)}, bf16[128,512]{1,0:T(8,128)(2,1)S(1)}, u32[]{:S(2)}, u32[]{:S(2)}) collective-permute-start(bf16[128,512]{1,0:T(8,128)(2,1)S(1)} %get-tuple-element.113), channel_id=1, source_target_pairs={{0,14},{1,15},{2,12},{3,13},{4,10},{5,11},{6,8},{7,9},{8,6},{9,7},... | collective-permute-start | bytes 393224 | tf_op jit(solution)/shard_map/ppermute | solution.py:22
  40.6 10.7 %collective-permute-start.16 = (bf16[128,512]{1,0:T(8,128)(2,1)S(1)}, bf16[128,512]{1,0:T(8,128)(2,1)S(1)}, u32[]{:S(2)}, u32[]{:S(2)}) collective-permute-start(bf16[128,512]{1,0:T(8,128)(2,1)S(1)} %get-tuple-element.114), channel_id=1, source_target_pairs={{0,10},{1,11},{2,8},{3,9},{4,14},{5,15},{6,12},{7,13},{8,2},{9,3},... | collective-permute-start | bytes 393224 | tf_op jit(solution)/shard_map/ppermute | solution.py:22
  40.6 10.7 %collective-permute-start.17 = (bf16[128,512]{1,0:T(8,128)(2,1)S(1)}, bf16[128,512]{1,0:T(8,128)(2,1)S(1)}, u32[]{:S(2)}, u32[]{:S(2)}) collective-permute-start(bf16[128,512]{1,0:T(8,128)(2,1)S(1)} %get-tuple-element.115), channel_id=1, source_target_pairs={{0,6},{1,7},{2,4},{3,5},{4,2},{5,3},{6,0},{7,1},{8,14},{9,15},{10,... | collective-permute-start | bytes 393224 | tf_op jit(solution)/shard_map/ppermute | solution.py:22
  45.5 12.5 %collective-permute-start.24 = (bf16[96,512]{1,0:T(8,128)(2,1)S(1)}, bf16[96,512]{1,0:T(8,128)(2,1)S(1)}, u32[]{:S(2)}, u32[]{:S(2)}) collective-permute-start(bf16[96,512]{1,0:T(8,128)(2,1)S(1)} %get-tuple-element.130), channel_id=1, source_target_pairs={{0,1},{1,0},{2,3},{3,2},{4,5},{5,4},{6,7},{7,6},{8,9},{9,8},{10,11... | collective-permute-start | bytes 294920 | tf_op jit(solution)/shard_map/ppermute | solution.py:22
  47.4 12.2 %collective-permute-start.25 = (bf16[96,512]{1,0:T(8,128)(2,1)S(1)}, bf16[96,512]{1,0:T(8,128)(2,1)S(1)}, u32[]{:S(2)}, u32[]{:S(2)}) collective-permute-start(bf16[96,512]{1,0:T(8,128)(2,1)S(1)} %get-tuple-element.131), channel_id=1, source_target_pairs={{1,2},{3,4},{5,6},{7,8},{9,10},{11,12},{13,14},{2,1},{4,3},{6,5},{... | collective-permute-start | bytes 294920 | tf_op jit(solution)/shard_map/ppermute | solution.py:28
  54.5 12.2 %collective-permute-start.20 = (bf16[160,512]{1,0:T(8,128)(2,1)S(1)}, bf16[160,512]{1,0:T(8,128)(2,1)S(1)}, u32[]{:S(2)}, u32[]{:S(2)}) collective-permute-start(bf16[160,512]{1,0:T(8,128)(2,1)S(1)} %get-tuple-element.124), channel_id=1, source_target_pairs={{0,8},{1,9},{2,10},{3,11},{4,12},{5,13},{6,14},{7,15},{8,0},{9,1},... | collective-permute-start | bytes 491528 | tf_op jit(solution)/shard_map/ppermute | solution.py:22
  55.7 11.0 %collective-permute-start.21 = (bf16[160,512]{1,0:T(8,128)(2,1)S(1)}, bf16[160,512]{1,0:T(8,128)(2,1)S(1)}, u32[]{:S(2)}, u32[]{:S(2)}) collective-permute-start(bf16[160,512]{1,0:T(8,128)(2,1)S(1)} %get-tuple-element.125), channel_id=1, source_target_pairs={{0,12},{1,13},{2,14},{3,15},{4,8},{5,9},{6,10},{7,11},{8,4},{9,5},... | collective-permute-start | bytes 491528 | tf_op jit(solution)/shard_map/ppermute | solution.py:22
  58.0 8.8 %collective-permute-start.22 = (bf16[160,512]{1,0:T(8,128)(2,1)S(1)}, bf16[160,512]{1,0:T(8,128)(2,1)S(1)}, u32[]{:S(2)}, u32[]{:S(2)}) collective-permute-start(bf16[160,512]{1,0:T(8,128)(2,1)S(1)} %get-tuple-element.126), channel_id=1, source_target_pairs={{0,4},{1,5},{2,6},{3,7},{4,0},{5,1},{6,2},{7,3},{8,12},{9,13},{10,... | collective-permute-start | bytes 491528 | tf_op jit(solution)/shard_map/ppermute | solution.py:22
  58.1 4.5 %collective-permute-start.26 = (bf16[128,512]{1,0:T(8,128)(2,1)S(1)}, bf16[128,512]{1,0:T(8,128)(2,1)S(1)}, u32[]{:S(2)}, u32[]{:S(2)}) collective-permute-start(bf16[128,512]{1,0:T(8,128)(2,1)S(1)} %get-tuple-element.134), channel_id=1, source_target_pairs={{0,2},{1,3},{2,0},{3,1},{4,6},{5,7},{6,4},{7,5},{8,10},{9,11},{10,... | collective-permute-start | bytes 393224 | tf_op jit(solution)/shard_map/ppermute | solution.py:22
  59.6 7.2 %collective-permute-start.23 = (bf16[128,512]{1,0:T(8,128)(2,1)S(1)}, bf16[128,512]{1,0:T(8,128)(2,1)S(1)}, u32[]{:S(2)}, u32[]{:S(2)}) collective-permute-start(bf16[128,512]{1,0:T(8,128)(2,1)S(1)} %get-tuple-element.127), channel_id=1, source_target_pairs={{0,2},{1,3},{2,0},{3,1},{4,6},{5,7},{6,4},{7,5},{8,10},{9,11},{10,... | collective-permute-start | bytes 393224 | tf_op jit(solution)/shard_map/ppermute | solution.py:22
  67.0 5.0 %collective-permute-start.27 = (f32[156,512]{1,0:T(8,128)S(1)}, f32[156,512]{1,0:T(8,128)S(1)}, u32[]{:S(2)}, u32[]{:S(2)}) collective-permute-start(f32[156,512]{1,0:T(8,128)S(1)} %get-tuple-element.146), channel_id=1, source_target_pairs={{0,1},{1,0},{2,3},{3,2},{4,5},{5,4},{6,7},{7,6},{8,9},{9,8},{10,11... | collective-permute-start | bytes 958472 | tf_op jit(solution)/shard_map/ppermute | solution.py:22
  (4 other events, 11.7 us)

commit v12 on v11

--- a/solution.py
+++ b/solution.py
@@ -552,6 +552,7 @@
         mib=24,
     )
     mixed_stay, mixed_leave = run(fold_body, half, mixed_keep, swap(mixed_send, 1))
+    out_got, mixed_leave = lax.optimization_barrier((out_got, mixed_leave))
     conv_grad, inner_out, rim_out, stay, leave = run(
         functools.partial(conv_grad_body, norm_scale),
         (
@@ -578,12 +579,13 @@
     sums = stay + swap(leave, 1)
 
     first_turns = (*range(2 * patterns - 1, 4, -2), 3)
-    next_turns = (*range(4, 2 * patterns, 2), 2, 1, 0)
+    solo = 2 * patterns - 2
+    next_turns = (*range(4, solo, 2), 2, 1, 0)
     owned = 4 * own_rows
     if copied:
         parts = run(
-            functools.partial(owners_body, first_turns),
-            (shaped((owned, quarter), NARROW),) * len(first_turns),
+            functools.partial(owners_body, (*first_turns, solo)),
+            (shaped((owned, quarter), NARROW),) * (len(first_turns) + 1),
             holder,
             out_leave,
         )
@@ -591,11 +593,15 @@
         flat = holder.reshape(2, count, own_rows, quarter)
         flat = canonical(jnp.moveaxis(flat, 1, 0), me, bit_count)
         flat = flat.reshape(2 * patterns, owned, quarter)
-        parts = [flat[p].astype(NARROW) for p in first_turns]
+        parts = [flat[p].astype(NARROW) for p in (*first_turns, solo)]
     first_parts = [swap(part, 2 * p) for p, part in zip(first_turns, parts)]
-    sums, first_parts = lax.optimization_barrier((sums, first_parts))
+    solo_part = swap(parts[-1], 2 * solo)
+    first_parts[:2], sums = lax.optimization_barrier((first_parts[:2], sums))
     sums = sums + swap(sums, 2)
-    sums, mixed_leave = lax.optimization_barrier((sums, mixed_leave))
+    sums, mixed_leave, solo_part, first_parts, rim_got = lax.optimization_barrier(
+        (sums, mixed_leave, solo_part, first_parts, rim_got)
+    )
+    solo_sums = swap(sums.astype(NARROW), 2 * solo)
     if copied:
         joint = shaped((owned + 32, quarter), NARROW)
         *parts, side_part, near_own = run(
@@ -630,11 +636,12 @@
         mixed_stay,
         swap(mixed_leave, 2),
     )[0]
-    parts = list(first_parts) + next_parts
+    parts = [*first_parts, solo_part, *next_parts]
+    sums_parts.append(solo_sums)
     parts, input_grad, output = lax.optimization_barrier((parts, input_grad, output))
 
     stay, leave, half_sums = run(
-        functools.partial(total_body, first_turns + next_turns),
+        functools.partial(total_body, (*first_turns, solo, *next_turns)),
         (
             shaped((2, 2, own_rows, quarter)),
             shaped((owned + SMALL_ROWS, quarter)),

time: 73.4 us -> 75 us (1.022)
  waiting for transfers between devices: 17.3 us -> 18.8 us
    ppermute x24 -> x25, waiting for transfers between devices: 13.7 us -> 15.2 us  [swap(): return lax.ppermute(value, 'row', [(i, i ^ bit) for i in range(count)])]
    ppermute x24 -> x25, starting transfers between devices: 32.1 us -> 32 us  [swap(): return lax.ppermute(value, 'row', [(i, i ^ bit) for i in range(count)])]
  transfers between devices with their start and end apart: 28 -> 29, of which waited for: 11 -> 12; matrix products, arithmetic and copies ran while one was open for 0% -> 0% of each run, Pallas kernels for 13% -> 12%
where the time goes in v12:
time: 75 us; the launch traced here: 74.5 us
  starting transfers between devices  41.6 us (55%)
  waiting for transfers between devices  18.8 us (25%)
  Pallas kernels  13.1 us (17%)
  between operations  0.88 us (1%)
    ppermute x25, starting transfers between devices, swap(): return lax.ppermute(value, 'row', [(i, i ^ bit) for i in range(count)])  32 us
    ppermute x25, waiting for transfers between devices, swap(): return lax.ppermute(value, 'row', [(i, i ^ bit) for i in range(count)])  15.2 us
    pallas_call x17, Pallas kernels, run(): pl.pallas_call(body, out_shape=outs, **extra, scratch_shapes=scratch, com...  13.1 us
    ppermute x2, starting transfers between devices, swap_rim(): return lax.ppermute(value, 'row', pairs + [(j, i) for i, j in pairs])  7.06 us
    ppermute x2, waiting for transfers between devices, swap_group(): return lax.ppermute(value, 'grp', [(0, 1), (1, 0)])  3.56 us
    ppermute x2, starting transfers between devices, swap_group(): return lax.ppermute(value, 'grp', [(0, 1), (1, 0)])  2.61 us
  transfers between devices with their start and end apart: 29, of which 12 were waited for; matrix products, arithmetic and copies ran while one was open for 0% of the time, Pallas kernels for 12%

profile of v12, /device:TPU:1, one launch (start us, length us, event | category | flops | bytes accessed | tf_op | source)
XLA Modules:
  0.0 74.5 jit_solution(9638688565433468957)
XLA Ops:
  0.6 1.3 %shard_map.160 = (bf16[2,2,32,512]{3,2,1,0:T(8,128)(2,1)S(1)}, bf16[224,512]{1,0:T(8,128)(2,1)S(1)}, bf16[96,512]{1,0:T(8,128)(2,1)S(1)}, bf16[128,512]{1,0:T(8,...) custom-call(f32[32,2048]{1,0:T(8,128)} %refs_0_.1, ...), custom_call_target="tpu_custom_call" | custom-call | tf_op jit(solution)/shard_map/pallas_call | solution.py:44
  2.1 4.5 %collective-permute-start.1 = (bf16[96,512]{1,0:T(8,128)(2,1)S(1)}, bf16[96,512]{1,0:T(8,128)(2,1)S(1)}, u32[]{:S(2)}, u32[]{:S(2)}) collective-permute-start(bf16[96,512]{1,0:T(8,128)(2,1)S(1)} %get-tuple-element.90), channel_id=1, source_target_pairs={{1,2},{3,4},{5,6},{7,8},{9,10},{11,12},{13,14},{2,1},{4,3},{6,5},{... | collective-permute-start | bytes 294920 | tf_op jit(solution)/shard_map/ppermute | solution.py:28
  6.6 2.4 %collective-permute-start.9 = (bf16[2,32,512]{2,1,0:T(8,128)(2,1)S(1)}, bf16[2,32,512]{2,1,0:T(8,128)(2,1)S(1)}, u32[]{:S(2)}, u32[]{:S(2)}) collective-permute-start(bf16[2,32,512]{2,1,0:T(8,128)(2,1)S(1)} %get-tuple-element.100), channel_id=1, source_target_pairs={{0,14},{1,15},{2,12},{3,13},{4,10},{5,11},{6,8},{7,9},{8,6},{9,7},... | collective-permute-start | bytes 196616 | tf_op jit(solution)/shard_map/ppermute | solution.py:22
  10.1 2.2 %collective-permute-start.5 = (bf16[2,32,512]{2,1,0:T(8,128)(2,1)S(1)}, bf16[2,32,512]{2,1,0:T(8,128)(2,1)S(1)}, u32[]{:S(2)}, u32[]{:S(2)}) collective-permute-start(bf16[2,32,512]{2,1,0:T(8,128)(2,1)S(1)} %get-tuple-element.99), channel_id=1, source_target_pairs={{0,12},{1,13},{2,14},{3,15},{4,8},{5,9},{6,10},{7,11},{8,4},{9,5},... | collective-permute-start | bytes 196616 | tf_op jit(solution)/shard_map/ppermute | solution.py:22
  13.3 1.3 %collective-permute-start.7 = (bf16[2,2,32,512]{3,2,1,0:T(8,128)(2,1)S(1)}, bf16[2,2,32,512]{3,2,1,0:T(8,128)(2,1)S(1)}, u32[]{:S(2)}, u32[]{:S(2)}) collective-permute-start(bf16[2,2,32,512]{3,2,1,0:T(8,128)(2,1)S(1)} %get-tuple-element.96.full), channel_id=1, source_target_pairs={{0,6},{1,7},{2,4},{3,5},{4,2},{5,3},{6,0},{7,1},{8,14},{9,15},{10,... | collective-permute-start | bytes 393224 | tf_op jit(solution)/shard_map/ppermute | solution.py:22
  14.6 2.4 %shard_map.162 = (f32[128,512]{1,0:T(8,128)S(1)}, f32[128,128]{1,0:T(8,128)S(1)}, bf16[384,512]{1,0:T(8,128)(2,1)S(1)}) custom-call(f32[4,32,512]{2,1,0:T(8,128)S(1)} %get-tuple-element.88.feats.refs_5_, bf16[224,512]{1,0:T(8,128)(2,1)S(1)} %collective-permute-done.other.core_got.refs_6_, bf16[96,512]{1,0:T(8,128)(2,1)S(1)} %collective-permute-done.1.outer.refs_7_, ...), custom_call_target="tpu_custom_call" | custom-call | tf_op jit(solution)/shard_map/pallas_call | solution.py:44
  18.4 2.4 %collective-permute-start.2 = (bf16[384,512]{1,0:T(8,128)(2,1)S(1)}, bf16[384,512]{1,0:T(8,128)(2,1)S(1)}, u32[]{:S(2)}, u32[]{:S(2)}) collective-permute-start(bf16[384,512]{1,0:T(8,128)(2,1)S(1)} %get-tuple-element.97.mine), channel_id=1, source_target_pairs={{0,2},{1,3},{2,0},{3,1},{4,6},{5,7},{6,4},{7,5},{8,10},{9,11},{10,... | collective-permute-start | bytes 1179656 | tf_op jit(solution)/shard_map/ppermute | solution.py:22
  20.9 1.3 %collective-permute-start.10 = (bf16[2,2,32,512]{3,2,1,0:T(8,128)(2,1)S(1)}, bf16[2,2,32,512]{3,2,1,0:T(8,128)(2,1)S(1)}, u32[]{:S(2)}, u32[]{:S(2)}) collective-permute-start(bf16[2,2,32,512]{3,2,1,0:T(8,128)(2,1)S(1)} %shard_map.164.refs_9_), channel_id=1, source_target_pairs={{0,16},{16,0},{1,17},{17,1},{2,18},{18,2},{3,19},{19,3},{4,20},{20... | collective-permute-start | bytes 393224 | tf_op jit(solution)/shard_map/ppermute | solution.py:36
  22.6 1.3 %collective-permute-start.6 = (bf16[2,2,32,512]{3,2,1,0:T(8,128)(2,1)S(1)}, bf16[2,2,32,512]{3,2,1,0:T(8,128)(2,1)S(1)}, u32[]{:S(2)}, u32[]{:S(2)}) collective-permute-start(bf16[2,2,32,512]{3,2,1,0:T(8,128)(2,1)S(1)} %shard_map.163.refs_5_), channel_id=1, source_target_pairs={{0,16},{16,0},{1,17},{17,1},{2,18},{18,2},{3,19},{19,3},{4,20},{20... | collective-permute-start | bytes 393224 | tf_op jit(solution)/shard_map/ppermute | solution.py:36
  25.1 2.9 %collective-permute-done.6.refs_1_.refs_6_ = bf16[2,2,32,512]{3,2,1,0:T(8,128)(2,1)S(1)} collective-permute-done((bf16[2,2,32,512]{3,2,1,0:T(8,128)(2,1)S(1)}, bf16[2,2,32,512]{3,2,1,0:T(8,128)(2,1)S(1)}, u32[]{:S(2)}, u32[]{:S(2)}) %collective-permute-start.6) | collective-permute-done | bytes 131104 | tf_op jit(solution)/shard_map/ppermute | solution.py:36
  28.0 1.6 %collective-permute-done.2.got = bf16[384,512]{1,0:T(8,128)(2,1)S(1)} collective-permute-done((bf16[384,512]{1,0:T(8,128)(2,1)S(1)}, bf16[384,512]{1,0:T(8,128)(2,1)S(1)}, u32[]{:S(2)}, u32[]{:S(2)}) %collective-permute-start.2) | collective-permute-done | bytes 393248 | tf_op jit(solution)/shard_map/ppermute | solution.py:22
  29.6 1.9 %collective-permute-start.11 = (bf16[2,256,512]{2,1,0:T(8,128)(2,1)S(1)}, bf16[2,256,512]{2,1,0:T(8,128)(2,1)S(1)}, u32[]{:S(2)}, u32[]{:S(2)}) collective-permute-start(bf16[2,256,512]{2,1,0:T(8,128)(2,1)S(1)} %get-tuple-element.101.refs_0_), channel_id=1, source_target_pairs={{0,1},{1,0},{2,3},{3,2},{4,5},{5,4},{6,7},{7,6},{8,9},{9,8},{10,11... | collective-permute-start | bytes 1572872 | tf_op jit(solution)/shard_map/ppermute | solution.py:22
  31.5 1.5 %collective-permute-done.11.refs_1_ = bf16[2,256,512]{2,1,0:T(8,128)(2,1)S(1)} collective-permute-done((bf16[2,256,512]{2,1,0:T(8,128)(2,1)S(1)}, bf16[2,256,512]{2,1,0:T(8,128)(2,1)S(1)}, u32[]{:S(2)}, u32[]{:S(2)}) %collective-permute-start.11) | collective-permute-done | bytes 524320 | tf_op jit(solution)/shard_map/ppermute | solution.py:22
  33.0 1.4 %shard_map.166 = (f32[256,512]{1,0:T(8,128)S(1)}, bf16[256,512]{1,0:T(8,128)(2,1)S(1)}, bf16[512,512]{1,0:T(8,128)(2,1)S(1)}, bf16[512,512]{1,0:T(8,128)(2,1)S(1...) custom-call(bf16[2,256,512]{2,1,0:T(8,128)(2,1)S(1)} %get-tuple-element.101.refs_0_, ...), custom_call_target="tpu_custom_call" | custom-call | tf_op jit(solution)/shard_map/pallas_call | solution.py:44
  37.5 3.1 %collective-permute-start.13 = (bf16[128,512]{1,0:T(8,128)(2,1)S(1)}, bf16[128,512]{1,0:T(8,128)(2,1)S(1)}, u32[]{:S(2)}, u32[]{:S(2)}) collective-permute-start(bf16[128,512]{1,0:T(8,128)(2,1)S(1)} %get-tuple-element.112), channel_id=1, source_target_pairs={{0,14},{1,15},{2,12},{3,13},{4,10},{5,11},{6,8},{7,9},{8,6},{9,7},... | collective-permute-start | bytes 393224 | tf_op jit(solution)/shard_map/ppermute | solution.py:22
  41.0 1.9 %shard_map.171 = (f32[128,512]{1,0:T(8,128)S(1)}, bf16[96,512]{1,0:T(8,128)(2,1)S(1)}, bf16[96,512]{1,0:T(8,128)(2,1)S(1)}, f32[28,512]{1,0:T(8,128)S(1)}, f32[28,512]{1,0:T(8,128)S(1)}) custom-call(f32[128,512]{1,0:T(8,128)S(1)} %get-tuple-element.114.refs_0_, bf16[128,512]{1,0:T(8,128)(2,1)S(1)} %collective-permute-done.15.refs_1_, ...), custom_call_target="tpu_custom_call" | custom-call | tf_op jit(solution)/shard_map/pallas_call | solution.py:44
  44.2 3.0 %collective-permute-start.19 = (bf16[128,512]{1,0:T(8,128)(2,1)S(1)}, bf16[128,512]{1,0:T(8,128)(2,1)S(1)}, u32[]{:S(2)}, u32[]{:S(2)}) collective-permute-start(bf16[128,512]{1,0:T(8,128)(2,1)S(1)} %get-tuple-element.127), channel_id=1, source_target_pairs={{0,12},{1,13},{2,14},{3,15},{4,8},{5,9},{6,10},{7,11},{8,4},{9,5},... | collective-permute-start | bytes 393224 | tf_op jit(solution)/shard_map/ppermute | solution.py:22
  48.2 2.6 %collective-permute-start.21 = (bf16[96,512]{1,0:T(8,128)(2,1)S(1)}, bf16[96,512]{1,0:T(8,128)(2,1)S(1)}, u32[]{:S(2)}, u32[]{:S(2)}) collective-permute-start(bf16[96,512]{1,0:T(8,128)(2,1)S(1)} %get-tuple-element.131), channel_id=1, source_target_pairs={{1,2},{3,4},{5,6},{7,8},{9,10},{11,12},{13,14},{2,1},{4,3},{6,5},{... | collective-permute-start | bytes 294920 | tf_op jit(solution)/shard_map/ppermute | solution.py:28
  50.8 3.4 %collective-permute-done.14.refs_1_ = bf16[128,512]{1,0:T(8,128)(2,1)S(1)} collective-permute-done((bf16[128,512]{1,0:T(8,128)(2,1)S(1)}, bf16[128,512]{1,0:T(8,128)(2,1)S(1)}, u32[]{:S(2)}, u32[]{:S(2)}) %collective-permute-start.14) | collective-permute-done | bytes 131104 | tf_op jit(solution)/shard_map/ppermute | solution.py:22
  54.7 4.4 %collective-permute-done.18 = f32[28,512]{1,0:T(8,128)S(1)} collective-permute-done((f32[28,512]{1,0:T(8,128)S(1)}, f32[28,512]{1,0:T(8,128)S(1)}, u32[]{:S(2)}, u32[]{:S(2)}) %collective-permute-start.18) | collective-permute-done | bytes 57376 | tf_op jit(solution)/shard_map/ppermute | solution.py:22
  59.3 2.6 %collective-permute-start.23 = (bf16[160,512]{1,0:T(8,128)(2,1)S(1)}, bf16[160,512]{1,0:T(8,128)(2,1)S(1)}, u32[]{:S(2)}, u32[]{:S(2)}) collective-permute-start(bf16[160,512]{1,0:T(8,128)(2,1)S(1)} %get-tuple-element.138), channel_id=1, source_target_pairs={{0,4},{1,5},{2,6},{3,7},{4,0},{5,1},{6,2},{7,3},{8,12},{9,13},{10,... | collective-permute-start | bytes 491528 | tf_op jit(solution)/shard_map/ppermute | solution.py:22
  63.3 1.8 %collective-permute-start.25 = (bf16[96,512]{1,0:T(8,128)(2,1)S(1)}, bf16[96,512]{1,0:T(8,128)(2,1)S(1)}, u32[]{:S(2)}, u32[]{:S(2)}) collective-permute-start(bf16[96,512]{1,0:T(8,128)(2,1)S(1)} %get-tuple-element.142), channel_id=1, source_target_pairs={{0,1},{1,0},{2,3},{3,2},{4,5},{5,4},{6,7},{7,6},{8,9},{9,8},{10,11... | collective-permute-start | bytes 294920 | tf_op jit(solution)/shard_map/ppermute | solution.py:22
  67.2 2.9 %shard_map.173 = f32[4,32,512]{2,1,0:T(8,128)} custom-call(f32[128,512]{1,0:T(8,128)S(1)} %get-tuple-element.141.grad, bf16[96,512]{1,0:T(8,128)(2,1)S(1)} %collective-permute-done.25.inner, bf16[96,512]{1,0:T(8,128)(2,1)S(1)} %collective-permute-done.21.outer, f32[7,7,512]{2,1,0:T(8,128)S(1)} %get-tuple-element.91.kernel, ...), custom_call_target="tpu_custom_call" | custom-call | tf_op jit(solution)/shard_map/pallas_call | solution.py:44
  71.0 1.3 %collective-permute-start.28 = (f32[156,512]{1,0:T(8,128)S(1)}, f32[156,512]{1,0:T(8,128)S(1)}, u32[]{:S(2)}, u32[]{:S(2)}) collective-permute-start(f32[156,512]{1,0:T(8,128)S(1)} %get-tuple-element.158), channel_id=1, source_target_pairs={{0,1},{1,0},{2,3},{3,2},{4,5},{5,4},{6,7},{7,6},{8,9},{9,8},{10,11... | collective-permute-start | bytes 958472 | tf_op jit(solution)/shard_map/ppermute | solution.py:22
  (58 shorter events, 18.1 us)
Async XLA Ops:
  2.0 4.6 %collective-permute-start = (bf16[224,512]{1,0:T(8,128)(2,1)S(1)}, bf16[224,512]{1,0:T(8,128)(2,1)S(1)}, u32[]{:S(2)}, u32[]{:S(2)}) collective-permute-start(bf16[224,512]{1,0:T(8,128)(2,1)S(1)} %get-tuple-element.89), channel_id=1, source_target_pairs={{0,1},{1,0},{2,3},{3,2},{4,5},{5,4},{6,7},{7,6},{8,9},{9,8},{10,11... | collective-permute-start | bytes 688136 | tf_op jit(solution)/shard_map/ppermute | solution.py:22
  2.1 11.2 %collective-permute-start.1 = (bf16[96,512]{1,0:T(8,128)(2,1)S(1)}, bf16[96,512]{1,0:T(8,128)(2,1)S(1)}, u32[]{:S(2)}, u32[]{:S(2)}) collective-permute-start(bf16[96,512]{1,0:T(8,128)(2,1)S(1)} %get-tuple-element.90), channel_id=1, source_target_pairs={{1,2},{3,4},{5,6},{7,8},{9,10},{11,12},{13,14},{2,1},{4,3},{6,5},{... | collective-permute-start | bytes 294920 | tf_op jit(solution)/shard_map/ppermute | solution.py:28
  6.6 10.4 %collective-permute-start.9 = (bf16[2,32,512]{2,1,0:T(8,128)(2,1)S(1)}, bf16[2,32,512]{2,1,0:T(8,128)(2,1)S(1)}, u32[]{:S(2)}, u32[]{:S(2)}) collective-permute-start(bf16[2,32,512]{2,1,0:T(8,128)(2,1)S(1)} %get-tuple-element.100), channel_id=1, source_target_pairs={{0,14},{1,15},{2,12},{3,13},{4,10},{5,11},{6,8},{7,9},{8,6},{9,7},... | collective-permute-start | bytes 196616 | tf_op jit(solution)/shard_map/ppermute | solution.py:22
  9.0 9.4 %collective-permute-start.8 = (bf16[2,32,512]{2,1,0:T(8,128)(2,1)S(1)}, bf16[2,32,512]{2,1,0:T(8,128)(2,1)S(1)}, u32[]{:S(2)}, u32[]{:S(2)}) collective-permute-start(bf16[2,32,512]{2,1,0:T(8,128)(2,1)S(1)} %get-tuple-element.100), channel_id=1, source_target_pairs={{0,10},{1,11},{2,8},{3,9},{4,14},{5,15},{6,12},{7,13},{8,2},{9,3},... | collective-permute-start | bytes 196616 | tf_op jit(solution)/shard_map/ppermute | solution.py:22
  10.1 10.8 %collective-permute-start.5 = (bf16[2,32,512]{2,1,0:T(8,128)(2,1)S(1)}, bf16[2,32,512]{2,1,0:T(8,128)(2,1)S(1)}, u32[]{:S(2)}, u32[]{:S(2)}) collective-permute-start(bf16[2,32,512]{2,1,0:T(8,128)(2,1)S(1)} %get-tuple-element.99), channel_id=1, source_target_pairs={{0,12},{1,13},{2,14},{3,15},{4,8},{5,9},{6,10},{7,11},{8,4},{9,5},... | collective-permute-start | bytes 196616 | tf_op jit(solution)/shard_map/ppermute | solution.py:22
  12.3 10.3 %collective-permute-start.4 = (bf16[2,32,512]{2,1,0:T(8,128)(2,1)S(1)}, bf16[2,32,512]{2,1,0:T(8,128)(2,1)S(1)}, u32[]{:S(2)}, u32[]{:S(2)}) collective-permute-start(bf16[2,32,512]{2,1,0:T(8,128)(2,1)S(1)} %get-tuple-element.99), channel_id=1, source_target_pairs={{0,8},{1,9},{2,10},{3,11},{4,12},{5,13},{6,14},{7,15},{8,0},{9,1},... | collective-permute-start | bytes 196616 | tf_op jit(solution)/shard_map/ppermute | solution.py:22
  13.3 10.6 %collective-permute-start.7 = (bf16[2,2,32,512]{3,2,1,0:T(8,128)(2,1)S(1)}, bf16[2,2,32,512]{3,2,1,0:T(8,128)(2,1)S(1)}, u32[]{:S(2)}, u32[]{:S(2)}) collective-permute-start(bf16[2,2,32,512]{3,2,1,0:T(8,128)(2,1)S(1)} %get-tuple-element.96.full), channel_id=1, source_target_pairs={{0,6},{1,7},{2,4},{3,5},{4,2},{5,3},{6,0},{7,1},{8,14},{9,15},{10,... | collective-permute-start | bytes 393224 | tf_op jit(solution)/shard_map/ppermute | solution.py:22
  17.1 7.3 %collective-permute-start.3 = (bf16[2,2,32,512]{3,2,1,0:T(8,128)(2,1)S(1)}, bf16[2,2,32,512]{3,2,1,0:T(8,128)(2,1)S(1)}, u32[]{:S(2)}, u32[]{:S(2)}) collective-permute-start(bf16[2,2,32,512]{3,2,1,0:T(8,128)(2,1)S(1)} %get-tuple-element.98.refs_3_), channel_id=1, source_target_pairs={{0,4},{1,5},{2,6},{3,7},{4,0},{5,1},{6,2},{7,3},{8,12},{9,13},{10,... | collective-permute-start | bytes 393224 | tf_op jit(solution)/shard_map/ppermute | solution.py:22
  18.4 11.1 %collective-permute-start.2 = (bf16[384,512]{1,0:T(8,128)(2,1)S(1)}, bf16[384,512]{1,0:T(8,128)(2,1)S(1)}, u32[]{:S(2)}, u32[]{:S(2)}) collective-permute-start(bf16[384,512]{1,0:T(8,128)(2,1)S(1)} %get-tuple-element.97.mine), channel_id=1, source_target_pairs={{0,2},{1,3},{2,0},{3,1},{4,6},{5,7},{6,4},{7,5},{8,10},{9,11},{10,... | collective-permute-start | bytes 1179656 | tf_op jit(solution)/shard_map/ppermute | solution.py:22
  22.6 5.4 %collective-permute-start.6 = (bf16[2,2,32,512]{3,2,1,0:T(8,128)(2,1)S(1)}, bf16[2,2,32,512]{3,2,1,0:T(8,128)(2,1)S(1)}, u32[]{:S(2)}, u32[]{:S(2)}) collective-permute-start(bf16[2,2,32,512]{3,2,1,0:T(8,128)(2,1)S(1)} %shard_map.163.refs_5_), channel_id=1, source_target_pairs={{0,16},{16,0},{1,17},{17,1},{2,18},{18,2},{3,19},{19,3},{4,20},{20... | collective-permute-start | bytes 393224 | tf_op jit(solution)/shard_map/ppermute | solution.py:36
  35.9 4.7 %collective-permute-start.16 = (bf16[256,512]{1,0:T(8,128)(2,1)S(1)}, bf16[256,512]{1,0:T(8,128)(2,1)S(1)}, u32[]{:S(2)}, u32[]{:S(2)}) collective-permute-start(bf16[256,512]{1,0:T(8,128)(2,1)S(1)} %get-tuple-element.116), channel_id=1, source_target_pairs={{0,1},{1,0},{2,3},{3,2},{4,5},{5,4},{6,7},{7,6},{8,9},{9,8},{10,11... | collective-permute-start | bytes 786440 | tf_op jit(solution)/shard_map/ppermute | solution.py:22
  36.2 4.8 %collective-permute-start.15 = (bf16[128,512]{1,0:T(8,128)(2,1)S(1)}, bf16[128,512]{1,0:T(8,128)(2,1)S(1)}, u32[]{:S(2)}, u32[]{:S(2)}) collective-permute-start(bf16[128,512]{1,0:T(8,128)(2,1)S(1)} %get-tuple-element.111.after), channel_id=1, source_target_pairs={{0,2},{1,3},{2,0},{3,1},{4,6},{5,7},{6,4},{7,5},{8,10},{9,11},{10,... | collective-permute-start | bytes 393224 | tf_op jit(solution)/shard_map/ppermute | solution.py:22
  37.5 13.3 %collective-permute-start.13 = (bf16[128,512]{1,0:T(8,128)(2,1)S(1)}, bf16[128,512]{1,0:T(8,128)(2,1)S(1)}, u32[]{:S(2)}, u32[]{:S(2)}) collective-permute-start(bf16[128,512]{1,0:T(8,128)(2,1)S(1)} %get-tuple-element.112), channel_id=1, source_target_pairs={{0,14},{1,15},{2,12},{3,13},{4,10},{5,11},{6,8},{7,9},{8,6},{9,7},... | collective-permute-start | bytes 393224 | tf_op jit(solution)/shard_map/ppermute | solution.py:22
  40.6 13.6 %collective-permute-start.14 = (bf16[128,512]{1,0:T(8,128)(2,1)S(1)}, bf16[128,512]{1,0:T(8,128)(2,1)S(1)}, u32[]{:S(2)}, u32[]{:S(2)}) collective-permute-start(bf16[128,512]{1,0:T(8,128)(2,1)S(1)} %get-tuple-element.113), channel_id=1, source_target_pairs={{0,10},{1,11},{2,8},{3,9},{4,14},{5,15},{6,12},{7,13},{8,2},{9,3},... | collective-permute-start | bytes 393224 | tf_op jit(solution)/shard_map/ppermute | solution.py:22
  42.9 5.3 %collective-permute-start.17 = (f32[28,512]{1,0:T(8,128)S(1)}, f32[28,512]{1,0:T(8,128)S(1)}, u32[]{:S(2)}, u32[]{:S(2)}) collective-permute-start(f32[28,512]{1,0:T(8,128)S(1)} %get-tuple-element.124), channel_id=1, source_target_pairs={{0,1},{1,0},{2,3},{3,2},{4,5},{5,4},{6,7},{7,6},{8,9},{9,8},{10,11... | collective-permute-start | bytes 172040 | tf_op jit(solution)/shard_map/ppermute | solution.py:22
  44.2 14.9 %collective-permute-start.19 = (bf16[128,512]{1,0:T(8,128)(2,1)S(1)}, bf16[128,512]{1,0:T(8,128)(2,1)S(1)}, u32[]{:S(2)}, u32[]{:S(2)}) collective-permute-start(bf16[128,512]{1,0:T(8,128)(2,1)S(1)} %get-tuple-element.127), channel_id=1, source_target_pairs={{0,12},{1,13},{2,14},{3,15},{4,8},{5,9},{6,10},{7,11},{8,4},{9,5},... | collective-permute-start | bytes 393224 | tf_op jit(solution)/shard_map/ppermute | solution.py:22
  47.2 11.9 %collective-permute-start.20 = (bf16[128,512]{1,0:T(8,128)(2,1)S(1)}, bf16[128,512]{1,0:T(8,128)(2,1)S(1)}, u32[]{:S(2)}, u32[]{:S(2)}) collective-permute-start(bf16[128,512]{1,0:T(8,128)(2,1)S(1)} %get-tuple-element.130), channel_id=1, source_target_pairs={{0,6},{1,7},{2,4},{3,5},{4,2},{5,3},{6,0},{7,1},{8,14},{9,15},{10,... | collective-permute-start | bytes 393224 | tf_op jit(solution)/shard_map/ppermute | solution.py:22
  48.2 10.9 %collective-permute-start.21 = (bf16[96,512]{1,0:T(8,128)(2,1)S(1)}, bf16[96,512]{1,0:T(8,128)(2,1)S(1)}, u32[]{:S(2)}, u32[]{:S(2)}) collective-permute-start(bf16[96,512]{1,0:T(8,128)(2,1)S(1)} %get-tuple-element.131), channel_id=1, source_target_pairs={{1,2},{3,4},{5,6},{7,8},{9,10},{11,12},{13,14},{2,1},{4,3},{6,5},{... | collective-permute-start | bytes 294920 | tf_op jit(solution)/shard_map/ppermute | solution.py:28
  54.2 4.9 %collective-permute-start.18 = (f32[28,512]{1,0:T(8,128)S(1)}, f32[28,512]{1,0:T(8,128)S(1)}, u32[]{:S(2)}, u32[]{:S(2)}) collective-permute-start(f32[28,512]{1,0:T(8,128)S(1)} %add.6), channel_id=1, source_target_pairs={{0,2},{1,3},{2,0},{3,1},{4,6},{5,7},{6,4},{7,5},{8,10},{9,11},{10,... | collective-permute-start | bytes 172040 | tf_op jit(solution)/shard_map/ppermute | solution.py:22
  59.2 11.6 %collective-permute-start.22 = (bf16[160,512]{1,0:T(8,128)(2,1)S(1)}, bf16[160,512]{1,0:T(8,128)(2,1)S(1)}, u32[]{:S(2)}, u32[]{:S(2)}) collective-permute-start(bf16[160,512]{1,0:T(8,128)(2,1)S(1)} %get-tuple-element.137), channel_id=1, source_target_pairs={{0,8},{1,9},{2,10},{3,11},{4,12},{5,13},{6,14},{7,15},{8,0},{9,1},... | collective-permute-start | bytes 491528 | tf_op jit(solution)/shard_map/ppermute | solution.py:22
  59.3 11.5 %collective-permute-start.23 = (bf16[160,512]{1,0:T(8,128)(2,1)S(1)}, bf16[160,512]{1,0:T(8,128)(2,1)S(1)}, u32[]{:S(2)}, u32[]{:S(2)}) collective-permute-start(bf16[160,512]{1,0:T(8,128)(2,1)S(1)} %get-tuple-element.138), channel_id=1, source_target_pairs={{0,4},{1,5},{2,6},{3,7},{4,0},{5,1},{6,2},{7,3},{8,12},{9,13},{10,... | collective-permute-start | bytes 491528 | tf_op jit(solution)/shard_map/ppermute | solution.py:22
  61.9 8.2 %collective-permute-start.26 = (bf16[128,512]{1,0:T(8,128)(2,1)S(1)}, bf16[128,512]{1,0:T(8,128)(2,1)S(1)}, u32[]{:S(2)}, u32[]{:S(2)}) collective-permute-start(bf16[128,512]{1,0:T(8,128)(2,1)S(1)} %get-tuple-element.146), channel_id=1, source_target_pairs={{0,2},{1,3},{2,0},{3,1},{4,6},{5,7},{6,4},{7,5},{8,10},{9,11},{10,... | collective-permute-start | bytes 393224 | tf_op jit(solution)/shard_map/ppermute | solution.py:22
  62.1 8.7 %collective-permute-start.24 = (bf16[128,512]{1,0:T(8,128)(2,1)S(1)}, bf16[128,512]{1,0:T(8,128)(2,1)S(1)}, u32[]{:S(2)}, u32[]{:S(2)}) collective-permute-start(bf16[128,512]{1,0:T(8,128)(2,1)S(1)} %get-tuple-element.139), channel_id=1, source_target_pairs={{0,2},{1,3},{2,0},{3,1},{4,6},{5,7},{6,4},{7,5},{8,10},{9,11},{10,... | collective-permute-start | bytes 393224 | tf_op jit(solution)/shard_map/ppermute | solution.py:22
  66.1 4.8 %collective-permute-start.27 = (bf16[28,512]{1,0:T(8,128)(2,1)S(1)}, bf16[28,512]{1,0:T(8,128)(2,1)S(1)}, u32[]{:S(2)}, u32[]{:S(2)}) collective-permute-start(bf16[28,512]{1,0:T(8,128)(2,1)S(1)} %convert_element_type.3), channel_id=1, source_target_pairs={{0,12},{1,13},{2,14},{3,15},{4,8},{5,9},{6,10},{7,11},{8,4},{9,5},... | collective-permute-start | bytes 86024 | tf_op jit(solution)/shard_map/ppermute | solution.py:22
  (5 other events, 14.7 us)

commit v13 on v12

--- a/solution.py
+++ b/solution.py
@@ -598,8 +598,18 @@
     solo_part = swap(parts[-1], 2 * solo)
     first_parts[:2], sums = lax.optimization_barrier((first_parts[:2], sums))
     sums = sums + swap(sums, 2)
-    sums, mixed_leave, solo_part, first_parts, rim_got = lax.optimization_barrier(
-        (sums, mixed_leave, solo_part, first_parts, rim_got)
+    input_grad = run(
+        input_grad_body,
+        (shaped(features.shape),),
+        conv_grad,
+        inner_got,
+        rim_got,
+        taps,
+        cotan,
+        scratch=(padded,),
+    )[0]
+    sums, mixed_leave, solo_part, first_parts, input_grad = lax.optimization_barrier(
+        (sums, mixed_leave, solo_part, first_parts, input_grad)
     )
     solo_sums = swap(sums.astype(NARROW), 2 * solo)
     if copied:
@@ -618,16 +628,6 @@
         next_parts = [swap(flat[p].astype(NARROW), 2 * p) for p in next_turns[:-1]] + [flat[0]]
         sums_parts = [swap(sums.astype(NARROW), 2 * p) for p in next_turns[:-2]]
 
-    input_grad = run(
-        input_grad_body,
-        (shaped(features.shape),),
-        conv_grad,
-        inner_got,
-        rim_got,
-        taps,
-        cotan,
-        scratch=(padded,),
-    )[0]
     output = run(
         output_body,
         (shaped(features.shape),),

time: 75 us -> 76.3 us (1.017)
  waiting for transfers between devices: 18.8 us -> 22.7 us
  starting transfers between devices: 41.6 us -> 39.1 us
    ppermute x2, waiting for transfers between devices: 0.01 us -> 3.79 us  [swap_rim(): return lax.ppermute(value, 'row', pairs + [(j, i) for i, j in pairs])]
    ppermute x25, starting transfers between devices: 32 us -> 30.1 us  [swap(): return lax.ppermute(value, 'row', [(i, i ^ bit) for i in range(count)])]
  transfers between devices with their start and end apart: 29 -> 29, of which waited for: 12 -> 14; matrix products, arithmetic and copies ran while one was open for 0% -> 0% of each run, Pallas kernels for 12% -> 12%
where the time goes in v13:
time: 76.3 us; the launch traced here: 75.8 us
  starting transfers between devices  39.1 us (51%)
  waiting for transfers between devices  22.7 us (30%)
  Pallas kernels  13.1 us (17%)
  between operations  0.84 us (1%)
    ppermute x25, starting transfers between devices, swap(): return lax.ppermute(value, 'row', [(i, i ^ bit) for i in range(count)])  30.1 us
    ppermute x25, waiting for transfers between devices, swap(): return lax.ppermute(value, 'row', [(i, i ^ bit) for i in range(count)])  15.3 us
    pallas_call x17, Pallas kernels, run(): pl.pallas_call(body, out_shape=outs, **extra, scratch_shapes=scratch, com...  13.1 us
    ppermute x2, starting transfers between devices, swap_rim(): return lax.ppermute(value, 'row', pairs + [(j, i) for i, j in pairs])  6.45 us
    ppermute x2, waiting for transfers between devices, swap_rim(): return lax.ppermute(value, 'row', pairs + [(j, i) for i, j in pairs])  3.79 us
    ppermute x2, waiting for transfers between devices, swap_group(): return lax.ppermute(value, 'grp', [(0, 1), (1, 0)])  3.56 us
    ppermute x2, starting transfers between devices, swap_group(): return lax.ppermute(value, 'grp', [(0, 1), (1, 0)])  2.61 us
  transfers between devices with their start and end apart: 29, of which 14 were waited for; matrix products, arithmetic and copies ran while one was open for 0% of the time, Pallas kernels for 12%

profile of v13, /device:TPU:1, one launch (start us, length us, event | category | flops | bytes accessed | tf_op | source)
XLA Modules:
  0.0 75.8 jit_solution(4882071384477195652)
XLA Ops:
  0.6 1.3 %shard_map.160 = (bf16[2,2,32,512]{3,2,1,0:T(8,128)(2,1)S(1)}, bf16[224,512]{1,0:T(8,128)(2,1)S(1)}, bf16[96,512]{1,0:T(8,128)(2,1)S(1)}, bf16[128,512]{1,0:T(8,...) custom-call(f32[32,2048]{1,0:T(8,128)} %refs_0_.1, ...), custom_call_target="tpu_custom_call" | custom-call | tf_op jit(solution)/shard_map/pallas_call | solution.py:44
  2.1 4.5 %collective-permute-start.1 = (bf16[96,512]{1,0:T(8,128)(2,1)S(1)}, bf16[96,512]{1,0:T(8,128)(2,1)S(1)}, u32[]{:S(2)}, u32[]{:S(2)}) collective-permute-start(bf16[96,512]{1,0:T(8,128)(2,1)S(1)} %get-tuple-element.90), channel_id=1, source_target_pairs={{1,2},{3,4},{5,6},{7,8},{9,10},{11,12},{13,14},{2,1},{4,3},{6,5},{... | collective-permute-start | bytes 294920 | tf_op jit(solution)/shard_map/ppermute | solution.py:28
  6.6 2.4 %collective-permute-start.9 = (bf16[2,32,512]{2,1,0:T(8,128)(2,1)S(1)}, bf16[2,32,512]{2,1,0:T(8,128)(2,1)S(1)}, u32[]{:S(2)}, u32[]{:S(2)}) collective-permute-start(bf16[2,32,512]{2,1,0:T(8,128)(2,1)S(1)} %get-tuple-element.100), channel_id=1, source_target_pairs={{0,14},{1,15},{2,12},{3,13},{4,10},{5,11},{6,8},{7,9},{8,6},{9,7},... | collective-permute-start | bytes 196616 | tf_op jit(solution)/shard_map/ppermute | solution.py:22
  10.1 2.2 %collective-permute-start.5 = (bf16[2,32,512]{2,1,0:T(8,128)(2,1)S(1)}, bf16[2,32,512]{2,1,0:T(8,128)(2,1)S(1)}, u32[]{:S(2)}, u32[]{:S(2)}) collective-permute-start(bf16[2,32,512]{2,1,0:T(8,128)(2,1)S(1)} %get-tuple-element.99), channel_id=1, source_target_pairs={{0,12},{1,13},{2,14},{3,15},{4,8},{5,9},{6,10},{7,11},{8,4},{9,5},... | collective-permute-start | bytes 196616 | tf_op jit(solution)/shard_map/ppermute | solution.py:22
  13.3 1.3 %collective-permute-start.7 = (bf16[2,2,32,512]{3,2,1,0:T(8,128)(2,1)S(1)}, bf16[2,2,32,512]{3,2,1,0:T(8,128)(2,1)S(1)}, u32[]{:S(2)}, u32[]{:S(2)}) collective-permute-start(bf16[2,2,32,512]{3,2,1,0:T(8,128)(2,1)S(1)} %get-tuple-element.96.full), channel_id=1, source_target_pairs={{0,6},{1,7},{2,4},{3,5},{4,2},{5,3},{6,0},{7,1},{8,14},{9,15},{10,... | collective-permute-start | bytes 393224 | tf_op jit(solution)/shard_map/ppermute | solution.py:22
  14.6 2.4 %shard_map.162 = (f32[128,512]{1,0:T(8,128)S(1)}, f32[128,128]{1,0:T(8,128)S(1)}, bf16[384,512]{1,0:T(8,128)(2,1)S(1)}) custom-call(f32[4,32,512]{2,1,0:T(8,128)S(1)} %get-tuple-element.88.feats.refs_5_, bf16[224,512]{1,0:T(8,128)(2,1)S(1)} %collective-permute-done.other.core_got.refs_6_, bf16[96,512]{1,0:T(8,128)(2,1)S(1)} %collective-permute-done.1.outer.refs_7_, ...), custom_call_target="tpu_custom_call" | custom-call | tf_op jit(solution)/shard_map/pallas_call | solution.py:44
  18.4 2.4 %collective-permute-start.2 = (bf16[384,512]{1,0:T(8,128)(2,1)S(1)}, bf16[384,512]{1,0:T(8,128)(2,1)S(1)}, u32[]{:S(2)}, u32[]{:S(2)}) collective-permute-start(bf16[384,512]{1,0:T(8,128)(2,1)S(1)} %get-tuple-element.97.mine), channel_id=1, source_target_pairs={{0,2},{1,3},{2,0},{3,1},{4,6},{5,7},{6,4},{7,5},{8,10},{9,11},{10,... | collective-permute-start | bytes 1179656 | tf_op jit(solution)/shard_map/ppermute | solution.py:22
  20.9 1.3 %collective-permute-start.10 = (bf16[2,2,32,512]{3,2,1,0:T(8,128)(2,1)S(1)}, bf16[2,2,32,512]{3,2,1,0:T(8,128)(2,1)S(1)}, u32[]{:S(2)}, u32[]{:S(2)}) collective-permute-start(bf16[2,2,32,512]{3,2,1,0:T(8,128)(2,1)S(1)} %shard_map.164.refs_9_), channel_id=1, source_target_pairs={{0,16},{16,0},{1,17},{17,1},{2,18},{18,2},{3,19},{19,3},{4,20},{20... | collective-permute-start | bytes 393224 | tf_op jit(solution)/shard_map/ppermute | solution.py:36
  22.6 1.3 %collective-permute-start.6 = (bf16[2,2,32,512]{3,2,1,0:T(8,128)(2,1)S(1)}, bf16[2,2,32,512]{3,2,1,0:T(8,128)(2,1)S(1)}, u32[]{:S(2)}, u32[]{:S(2)}) collective-permute-start(bf16[2,2,32,512]{3,2,1,0:T(8,128)(2,1)S(1)} %shard_map.163.refs_5_), channel_id=1, source_target_pairs={{0,16},{16,0},{1,17},{17,1},{2,18},{18,2},{3,19},{19,3},{4,20},{20... | collective-permute-start | bytes 393224 | tf_op jit(solution)/shard_map/ppermute | solution.py:36
  25.1 2.9 %collective-permute-done.6.refs_1_.refs_6_ = bf16[2,2,32,512]{3,2,1,0:T(8,128)(2,1)S(1)} collective-permute-done((bf16[2,2,32,512]{3,2,1,0:T(8,128)(2,1)S(1)}, bf16[2,2,32,512]{3,2,1,0:T(8,128)(2,1)S(1)}, u32[]{:S(2)}, u32[]{:S(2)}) %collective-permute-start.6) | collective-permute-done | bytes 131104 | tf_op jit(solution)/shard_map/ppermute | solution.py:36
  28.0 1.6 %collective-permute-done.2.got = bf16[384,512]{1,0:T(8,128)(2,1)S(1)} collective-permute-done((bf16[384,512]{1,0:T(8,128)(2,1)S(1)}, bf16[384,512]{1,0:T(8,128)(2,1)S(1)}, u32[]{:S(2)}, u32[]{:S(2)}) %collective-permute-start.2) | collective-permute-done | bytes 393248 | tf_op jit(solution)/shard_map/ppermute | solution.py:22
  29.6 1.9 %collective-permute-start.11 = (bf16[2,256,512]{2,1,0:T(8,128)(2,1)S(1)}, bf16[2,256,512]{2,1,0:T(8,128)(2,1)S(1)}, u32[]{:S(2)}, u32[]{:S(2)}) collective-permute-start(bf16[2,256,512]{2,1,0:T(8,128)(2,1)S(1)} %get-tuple-element.101.refs_0_), channel_id=1, source_target_pairs={{0,1},{1,0},{2,3},{3,2},{4,5},{5,4},{6,7},{7,6},{8,9},{9,8},{10,11... | collective-permute-start | bytes 1572872 | tf_op jit(solution)/shard_map/ppermute | solution.py:22
  31.5 1.5 %collective-permute-done.11.refs_1_ = bf16[2,256,512]{2,1,0:T(8,128)(2,1)S(1)} collective-permute-done((bf16[2,256,512]{2,1,0:T(8,128)(2,1)S(1)}, bf16[2,256,512]{2,1,0:T(8,128)(2,1)S(1)}, u32[]{:S(2)}, u32[]{:S(2)}) %collective-permute-start.11) | collective-permute-done | bytes 524320 | tf_op jit(solution)/shard_map/ppermute | solution.py:22
  33.0 1.4 %shard_map.166 = (f32[256,512]{1,0:T(8,128)S(1)}, bf16[256,512]{1,0:T(8,128)(2,1)S(1)}, bf16[512,512]{1,0:T(8,128)(2,1)S(1)}, bf16[512,512]{1,0:T(8,128)(2,1)S(1...) custom-call(bf16[2,256,512]{2,1,0:T(8,128)(2,1)S(1)} %get-tuple-element.101.refs_0_, ...), custom_call_target="tpu_custom_call" | custom-call | tf_op jit(solution)/shard_map/pallas_call | solution.py:44
  37.5 3.1 %collective-permute-start.13 = (bf16[128,512]{1,0:T(8,128)(2,1)S(1)}, bf16[128,512]{1,0:T(8,128)(2,1)S(1)}, u32[]{:S(2)}, u32[]{:S(2)}) collective-permute-start(bf16[128,512]{1,0:T(8,128)(2,1)S(1)} %get-tuple-element.112), channel_id=1, source_target_pairs={{0,14},{1,15},{2,12},{3,13},{4,10},{5,11},{6,8},{7,9},{8,6},{9,7},... | collective-permute-start | bytes 393224 | tf_op jit(solution)/shard_map/ppermute | solution.py:22
  41.0 1.9 %shard_map.171 = (f32[128,512]{1,0:T(8,128)S(1)}, bf16[96,512]{1,0:T(8,128)(2,1)S(1)}, bf16[96,512]{1,0:T(8,128)(2,1)S(1)}, f32[28,512]{1,0:T(8,128)S(1)}, f32[28,512]{1,0:T(8,128)S(1)}) custom-call(f32[128,512]{1,0:T(8,128)S(1)} %get-tuple-element.114.refs_0_, bf16[128,512]{1,0:T(8,128)(2,1)S(1)} %collective-permute-done.15.refs_1_, ...), custom_call_target="tpu_custom_call" | custom-call | tf_op jit(solution)/shard_map/pallas_call | solution.py:44
  44.2 3.0 %collective-permute-start.19 = (bf16[128,512]{1,0:T(8,128)(2,1)S(1)}, bf16[128,512]{1,0:T(8,128)(2,1)S(1)}, u32[]{:S(2)}, u32[]{:S(2)}) collective-permute-start(bf16[128,512]{1,0:T(8,128)(2,1)S(1)} %get-tuple-element.127), channel_id=1, source_target_pairs={{0,12},{1,13},{2,14},{3,15},{4,8},{5,9},{6,10},{7,11},{8,4},{9,5},... | collective-permute-start | bytes 393224 | tf_op jit(solution)/shard_map/ppermute | solution.py:22
  48.8 2.0 %collective-permute-start.22 = (bf16[96,512]{1,0:T(8,128)(2,1)S(1)}, bf16[96,512]{1,0:T(8,128)(2,1)S(1)}, u32[]{:S(2)}, u32[]{:S(2)}) collective-permute-start(bf16[96,512]{1,0:T(8,128)(2,1)S(1)} %get-tuple-element.133), channel_id=1, source_target_pairs={{1,2},{3,4},{5,6},{7,8},{9,10},{11,12},{13,14},{2,1},{4,3},{6,5},{... | collective-permute-start | bytes 294920 | tf_op jit(solution)/shard_map/ppermute | solution.py:28
  50.8 3.4 %collective-permute-done.14.refs_1_ = bf16[128,512]{1,0:T(8,128)(2,1)S(1)} collective-permute-done((bf16[128,512]{1,0:T(8,128)(2,1)S(1)}, bf16[128,512]{1,0:T(8,128)(2,1)S(1)}, u32[]{:S(2)}, u32[]{:S(2)}) %collective-permute-start.14) | collective-permute-done | bytes 131104 | tf_op jit(solution)/shard_map/ppermute | solution.py:22
  54.7 3.8 %collective-permute-done.22.outer = bf16[96,512]{1,0:T(8,128)(2,1)S(1)} collective-permute-done((bf16[96,512]{1,0:T(8,128)(2,1)S(1)}, bf16[96,512]{1,0:T(8,128)(2,1)S(1)}, u32[]{:S(2)}, u32[]{:S(2)}) %collective-permute-start.22) | collective-permute-done | bytes 98336 | tf_op jit(solution)/shard_map/ppermute | solution.py:28
  58.5 2.9 %shard_map.172 = f32[4,32,512]{2,1,0:T(8,128)} custom-call(f32[128,512]{1,0:T(8,128)S(1)} %get-tuple-element.131.grad, bf16[96,512]{1,0:T(8,128)(2,1)S(1)} %collective-permute-done.21.inner, bf16[96,512]{1,0:T(8,128)(2,1)S(1)} %collective-permute-done.22.outer, f32[7,7,512]{2,1,0:T(8,128)S(1)} %get-tuple-element.91.kernel, ...), custom_call_target="tpu_custom_call" | custom-call | tf_op jit(solution)/shard_map/pallas_call | solution.py:44
  61.6 3.2 %collective-permute-start.24 = (bf16[160,512]{1,0:T(8,128)(2,1)S(1)}, bf16[160,512]{1,0:T(8,128)(2,1)S(1)}, u32[]{:S(2)}, u32[]{:S(2)}) collective-permute-start(bf16[160,512]{1,0:T(8,128)(2,1)S(1)} %get-tuple-element.141), channel_id=1, source_target_pairs={{0,4},{1,5},{2,6},{3,7},{4,0},{5,1},{6,2},{7,3},{8,12},{9,13},{10,... | collective-permute-start | bytes 491528 | tf_op jit(solution)/shard_map/ppermute | solution.py:22
  64.8 1.5 %collective-permute-start.25 = (bf16[128,512]{1,0:T(8,128)(2,1)S(1)}, bf16[128,512]{1,0:T(8,128)(2,1)S(1)}, u32[]{:S(2)}, u32[]{:S(2)}) collective-permute-start(bf16[128,512]{1,0:T(8,128)(2,1)S(1)} %get-tuple-element.142), channel_id=1, source_target_pairs={{0,2},{1,3},{2,0},{3,1},{4,6},{5,7},{6,4},{7,5},{8,10},{9,11},{10,... | collective-permute-start | bytes 393224 | tf_op jit(solution)/shard_map/ppermute | solution.py:22
  66.6 3.4 %collective-permute-done.26.got = bf16[128,512]{1,0:T(8,128)(2,1)S(1)} collective-permute-done((bf16[128,512]{1,0:T(8,128)(2,1)S(1)}, bf16[128,512]{1,0:T(8,128)(2,1)S(1)}, u32[]{:S(2)}, u32[]{:S(2)}) %collective-permute-start.26) | collective-permute-done | bytes 131104 | tf_op jit(solution)/shard_map/ppermute | solution.py:22
  (58 shorter events, 18.4 us)
Async XLA Ops:
  2.1 11.2 %collective-permute-start.1 = (bf16[96,512]{1,0:T(8,128)(2,1)S(1)}, bf16[96,512]{1,0:T(8,128)(2,1)S(1)}, u32[]{:S(2)}, u32[]{:S(2)}) collective-permute-start(bf16[96,512]{1,0:T(8,128)(2,1)S(1)} %get-tuple-element.90), channel_id=1, source_target_pairs={{1,2},{3,4},{5,6},{7,8},{9,10},{11,12},{13,14},{2,1},{4,3},{6,5},{... | collective-permute-start | bytes 294920 | tf_op jit(solution)/shard_map/ppermute | solution.py:28
  6.6 10.4 %collective-permute-start.9 = (bf16[2,32,512]{2,1,0:T(8,128)(2,1)S(1)}, bf16[2,32,512]{2,1,0:T(8,128)(2,1)S(1)}, u32[]{:S(2)}, u32[]{:S(2)}) collective-permute-start(bf16[2,32,512]{2,1,0:T(8,128)(2,1)S(1)} %get-tuple-element.100), channel_id=1, source_target_pairs={{0,14},{1,15},{2,12},{3,13},{4,10},{5,11},{6,8},{7,9},{8,6},{9,7},... | collective-permute-start | bytes 196616 | tf_op jit(solution)/shard_map/ppermute | solution.py:22
  9.0 9.4 %collective-permute-start.8 = (bf16[2,32,512]{2,1,0:T(8,128)(2,1)S(1)}, bf16[2,32,512]{2,1,0:T(8,128)(2,1)S(1)}, u32[]{:S(2)}, u32[]{:S(2)}) collective-permute-start(bf16[2,32,512]{2,1,0:T(8,128)(2,1)S(1)} %get-tuple-element.100), channel_id=1, source_target_pairs={{0,10},{1,11},{2,8},{3,9},{4,14},{5,15},{6,12},{7,13},{8,2},{9,3},... | collective-permute-start | bytes 196616 | tf_op jit(solution)/shard_map/ppermute | solution.py:22
  10.1 10.8 %collective-permute-start.5 = (bf16[2,32,512]{2,1,0:T(8,128)(2,1)S(1)}, bf16[2,32,512]{2,1,0:T(8,128)(2,1)S(1)}, u32[]{:S(2)}, u32[]{:S(2)}) collective-permute-start(bf16[2,32,512]{2,1,0:T(8,128)(2,1)S(1)} %get-tuple-element.99), channel_id=1, source_target_pairs={{0,12},{1,13},{2,14},{3,15},{4,8},{5,9},{6,10},{7,11},{8,4},{9,5},... | collective-permute-start | bytes 196616 | tf_op jit(solution)/shard_map/ppermute | solution.py:22
  12.3 10.3 %collective-permute-start.4 = (bf16[2,32,512]{2,1,0:T(8,128)(2,1)S(1)}, bf16[2,32,512]{2,1,0:T(8,128)(2,1)S(1)}, u32[]{:S(2)}, u32[]{:S(2)}) collective-permute-start(bf16[2,32,512]{2,1,0:T(8,128)(2,1)S(1)} %get-tuple-element.99), channel_id=1, source_target_pairs={{0,8},{1,9},{2,10},{3,11},{4,12},{5,13},{6,14},{7,15},{8,0},{9,1},... | collective-permute-start | bytes 196616 | tf_op jit(solution)/shard_map/ppermute | solution.py:22
  13.3 10.6 %collective-permute-start.7 = (bf16[2,2,32,512]{3,2,1,0:T(8,128)(2,1)S(1)}, bf16[2,2,32,512]{3,2,1,0:T(8,128)(2,1)S(1)}, u32[]{:S(2)}, u32[]{:S(2)}) collective-permute-start(bf16[2,2,32,512]{3,2,1,0:T(8,128)(2,1)S(1)} %get-tuple-element.96.full), channel_id=1, source_target_pairs={{0,6},{1,7},{2,4},{3,5},{4,2},{5,3},{6,0},{7,1},{8,14},{9,15},{10,... | collective-permute-start | bytes 393224 | tf_op jit(solution)/shard_map/ppermute | solution.py:22
  17.1 7.3 %collective-permute-start.3 = (bf16[2,2,32,512]{3,2,1,0:T(8,128)(2,1)S(1)}, bf16[2,2,32,512]{3,2,1,0:T(8,128)(2,1)S(1)}, u32[]{:S(2)}, u32[]{:S(2)}) collective-permute-start(bf16[2,2,32,512]{3,2,1,0:T(8,128)(2,1)S(1)} %get-tuple-element.98.refs_3_), channel_id=1, source_target_pairs={{0,4},{1,5},{2,6},{3,7},{4,0},{5,1},{6,2},{7,3},{8,12},{9,13},{10,... | collective-permute-start | bytes 393224 | tf_op jit(solution)/shard_map/ppermute | solution.py:22
  18.4 11.1 %collective-permute-start.2 = (bf16[384,512]{1,0:T(8,128)(2,1)S(1)}, bf16[384,512]{1,0:T(8,128)(2,1)S(1)}, u32[]{:S(2)}, u32[]{:S(2)}) collective-permute-start(bf16[384,512]{1,0:T(8,128)(2,1)S(1)} %get-tuple-element.97.mine), channel_id=1, source_target_pairs={{0,2},{1,3},{2,0},{3,1},{4,6},{5,7},{6,4},{7,5},{8,10},{9,11},{10,... | collective-permute-start | bytes 1179656 | tf_op jit(solution)/shard_map/ppermute | solution.py:22
  22.6 5.4 %collective-permute-start.6 = (bf16[2,2,32,512]{3,2,1,0:T(8,128)(2,1)S(1)}, bf16[2,2,32,512]{3,2,1,0:T(8,128)(2,1)S(1)}, u32[]{:S(2)}, u32[]{:S(2)}) collective-permute-start(bf16[2,2,32,512]{3,2,1,0:T(8,128)(2,1)S(1)} %shard_map.163.refs_5_), channel_id=1, source_target_pairs={{0,16},{16,0},{1,17},{17,1},{2,18},{18,2},{3,19},{19,3},{4,20},{20... | collective-permute-start | bytes 393224 | tf_op jit(solution)/shard_map/ppermute | solution.py:36
  35.9 4.7 %collective-permute-start.16 = (bf16[256,512]{1,0:T(8,128)(2,1)S(1)}, bf16[256,512]{1,0:T(8,128)(2,1)S(1)}, u32[]{:S(2)}, u32[]{:S(2)}) collective-permute-start(bf16[256,512]{1,0:T(8,128)(2,1)S(1)} %get-tuple-element.116), channel_id=1, source_target_pairs={{0,1},{1,0},{2,3},{3,2},{4,5},{5,4},{6,7},{7,6},{8,9},{9,8},{10,11... | collective-permute-start | bytes 786440 | tf_op jit(solution)/shard_map/ppermute | solution.py:22
  36.2 4.8 %collective-permute-start.15 = (bf16[128,512]{1,0:T(8,128)(2,1)S(1)}, bf16[128,512]{1,0:T(8,128)(2,1)S(1)}, u32[]{:S(2)}, u32[]{:S(2)}) collective-permute-start(bf16[128,512]{1,0:T(8,128)(2,1)S(1)} %get-tuple-element.111.after), channel_id=1, source_target_pairs={{0,2},{1,3},{2,0},{3,1},{4,6},{5,7},{6,4},{7,5},{8,10},{9,11},{10,... | collective-permute-start | bytes 393224 | tf_op jit(solution)/shard_map/ppermute | solution.py:22
  37.5 10.7 %collective-permute-start.13 = (bf16[128,512]{1,0:T(8,128)(2,1)S(1)}, bf16[128,512]{1,0:T(8,128)(2,1)S(1)}, u32[]{:S(2)}, u32[]{:S(2)}) collective-permute-start(bf16[128,512]{1,0:T(8,128)(2,1)S(1)} %get-tuple-element.112), channel_id=1, source_target_pairs={{0,14},{1,15},{2,12},{3,13},{4,10},{5,11},{6,8},{7,9},{8,6},{9,7},... | collective-permute-start | bytes 393224 | tf_op jit(solution)/shard_map/ppermute | solution.py:22
  40.6 13.6 %collective-permute-start.14 = (bf16[128,512]{1,0:T(8,128)(2,1)S(1)}, bf16[128,512]{1,0:T(8,128)(2,1)S(1)}, u32[]{:S(2)}, u32[]{:S(2)}) collective-permute-start(bf16[128,512]{1,0:T(8,128)(2,1)S(1)} %get-tuple-element.113), channel_id=1, source_target_pairs={{0,10},{1,11},{2,8},{3,9},{4,14},{5,15},{6,12},{7,13},{8,2},{9,3},... | collective-permute-start | bytes 393224 | tf_op jit(solution)/shard_map/ppermute | solution.py:22
  42.9 5.9 %collective-permute-start.17 = (f32[28,512]{1,0:T(8,128)S(1)}, f32[28,512]{1,0:T(8,128)S(1)}, u32[]{:S(2)}, u32[]{:S(2)}) collective-permute-start(f32[28,512]{1,0:T(8,128)S(1)} %get-tuple-element.124), channel_id=1, source_target_pairs={{0,1},{1,0},{2,3},{3,2},{4,5},{5,4},{6,7},{7,6},{8,9},{9,8},{10,11... | collective-permute-start | bytes 172040 | tf_op jit(solution)/shard_map/ppermute | solution.py:22
  44.2 17.2 %collective-permute-start.19 = (bf16[128,512]{1,0:T(8,128)(2,1)S(1)}, bf16[128,512]{1,0:T(8,128)(2,1)S(1)}, u32[]{:S(2)}, u32[]{:S(2)}) collective-permute-start(bf16[128,512]{1,0:T(8,128)(2,1)S(1)} %get-tuple-element.127), channel_id=1, source_target_pairs={{0,12},{1,13},{2,14},{3,15},{4,8},{5,9},{6,10},{7,11},{8,4},{9,5},... | collective-permute-start | bytes 393224 | tf_op jit(solution)/shard_map/ppermute | solution.py:22
  47.2 14.2 %collective-permute-start.20 = (bf16[128,512]{1,0:T(8,128)(2,1)S(1)}, bf16[128,512]{1,0:T(8,128)(2,1)S(1)}, u32[]{:S(2)}, u32[]{:S(2)}) collective-permute-start(bf16[128,512]{1,0:T(8,128)(2,1)S(1)} %get-tuple-element.130), channel_id=1, source_target_pairs={{0,6},{1,7},{2,4},{3,5},{4,2},{5,3},{6,0},{7,1},{8,14},{9,15},{10,... | collective-permute-start | bytes 393224 | tf_op jit(solution)/shard_map/ppermute | solution.py:22
  48.2 6.5 %collective-permute-start.21 = (bf16[96,512]{1,0:T(8,128)(2,1)S(1)}, bf16[96,512]{1,0:T(8,128)(2,1)S(1)}, u32[]{:S(2)}, u32[]{:S(2)}) collective-permute-start(bf16[96,512]{1,0:T(8,128)(2,1)S(1)} %get-tuple-element.132), channel_id=1, source_target_pairs={{0,1},{1,0},{2,3},{3,2},{4,5},{5,4},{6,7},{7,6},{8,9},{9,8},{10,11... | collective-permute-start | bytes 294920 | tf_op jit(solution)/shard_map/ppermute | solution.py:22
  48.8 9.7 %collective-permute-start.22 = (bf16[96,512]{1,0:T(8,128)(2,1)S(1)}, bf16[96,512]{1,0:T(8,128)(2,1)S(1)}, u32[]{:S(2)}, u32[]{:S(2)}) collective-permute-start(bf16[96,512]{1,0:T(8,128)(2,1)S(1)} %get-tuple-element.133), channel_id=1, source_target_pairs={{1,2},{3,4},{5,6},{7,8},{9,10},{11,12},{13,14},{2,1},{4,3},{6,5},{... | collective-permute-start | bytes 294920 | tf_op jit(solution)/shard_map/ppermute | solution.py:28
  54.2 7.2 %collective-permute-start.18 = (f32[28,512]{1,0:T(8,128)S(1)}, f32[28,512]{1,0:T(8,128)S(1)}, u32[]{:S(2)}, u32[]{:S(2)}) collective-permute-start(f32[28,512]{1,0:T(8,128)S(1)} %add.6), channel_id=1, source_target_pairs={{0,2},{1,3},{2,0},{3,1},{4,6},{5,7},{6,4},{7,5},{8,10},{9,11},{10,... | collective-permute-start | bytes 172040 | tf_op jit(solution)/shard_map/ppermute | solution.py:22
  61.5 10.5 %collective-permute-start.23 = (bf16[160,512]{1,0:T(8,128)(2,1)S(1)}, bf16[160,512]{1,0:T(8,128)(2,1)S(1)}, u32[]{:S(2)}, u32[]{:S(2)}) collective-permute-start(bf16[160,512]{1,0:T(8,128)(2,1)S(1)} %get-tuple-element.140), channel_id=1, source_target_pairs={{0,8},{1,9},{2,10},{3,11},{4,12},{5,13},{6,14},{7,15},{8,0},{9,1},... | collective-permute-start | bytes 491528 | tf_op jit(solution)/shard_map/ppermute | solution.py:22
  61.6 10.4 %collective-permute-start.24 = (bf16[160,512]{1,0:T(8,128)(2,1)S(1)}, bf16[160,512]{1,0:T(8,128)(2,1)S(1)}, u32[]{:S(2)}, u32[]{:S(2)}) collective-permute-start(bf16[160,512]{1,0:T(8,128)(2,1)S(1)} %get-tuple-element.141), channel_id=1, source_target_pairs={{0,4},{1,5},{2,6},{3,7},{4,0},{5,1},{6,2},{7,3},{8,12},{9,13},{10,... | collective-permute-start | bytes 491528 | tf_op jit(solution)/shard_map/ppermute | solution.py:22
  64.8 5.2 %collective-permute-start.26 = (bf16[128,512]{1,0:T(8,128)(2,1)S(1)}, bf16[128,512]{1,0:T(8,128)(2,1)S(1)}, u32[]{:S(2)}, u32[]{:S(2)}) collective-permute-start(bf16[128,512]{1,0:T(8,128)(2,1)S(1)} %get-tuple-element.146), channel_id=1, source_target_pairs={{0,2},{1,3},{2,0},{3,1},{4,6},{5,7},{6,4},{7,5},{8,10},{9,11},{10,... | collective-permute-start | bytes 393224 | tf_op jit(solution)/shard_map/ppermute | solution.py:22
  64.8 8.0 %collective-permute-start.25 = (bf16[128,512]{1,0:T(8,128)(2,1)S(1)}, bf16[128,512]{1,0:T(8,128)(2,1)S(1)}, u32[]{:S(2)}, u32[]{:S(2)}) collective-permute-start(bf16[128,512]{1,0:T(8,128)(2,1)S(1)} %get-tuple-element.142), channel_id=1, source_target_pairs={{0,2},{1,3},{2,0},{3,1},{4,6},{5,7},{6,4},{7,5},{8,10},{9,11},{10,... | collective-permute-start | bytes 393224 | tf_op jit(solution)/shard_map/ppermute | solution.py:22
  66.2 6.6 %collective-permute-start.27 = (bf16[28,512]{1,0:T(8,128)(2,1)S(1)}, bf16[28,512]{1,0:T(8,128)(2,1)S(1)}, u32[]{:S(2)}, u32[]{:S(2)}) collective-permute-start(bf16[28,512]{1,0:T(8,128)(2,1)S(1)} %convert_element_type.3), channel_id=1, source_target_pairs={{0,12},{1,13},{2,14},{3,15},{4,8},{5,9},{6,10},{7,11},{8,4},{9,5},... | collective-permute-start | bytes 86024 | tf_op jit(solution)/shard_map/ppermute | solution.py:22
  (5 other events, 16.0 us)

commit v14 on v12

--- a/solution.py
+++ b/solution.py
@@ -598,8 +598,8 @@
     solo_part = swap(parts[-1], 2 * solo)
     first_parts[:2], sums = lax.optimization_barrier((first_parts[:2], sums))
     sums = sums + swap(sums, 2)
-    sums, mixed_leave, solo_part, first_parts, rim_got = lax.optimization_barrier(
-        (sums, mixed_leave, solo_part, first_parts, rim_got)
+    sums, mixed_leave, solo_part, first_parts, rim_got, inner_got = lax.optimization_barrier(
+        (sums, mixed_leave, solo_part, first_parts, rim_got, inner_got)
     )
     solo_sums = swap(sums.astype(NARROW), 2 * solo)
     if copied:

time: 75 us -> 74.1 us (0.988)
  starting transfers between devices: 41.6 us -> 40 us
    ppermute x25, starting transfers between devices: 32 us -> 30.4 us  [swap(): return lax.ppermute(value, 'row', [(i, i ^ bit) for i in range(count)])]
  transfers between devices with their start and end apart: 29 -> 29, of which waited for: 12 -> 12; matrix products, arithmetic and copies ran while one was open for 0% -> 0% of each run, Pallas kernels for 12% -> 13%
where the time goes in v14:
time: 74.1 us; the launch traced here: 73.6 us
  starting transfers between devices  40 us (54%)
  waiting for transfers between devices  19.5 us (26%)
  Pallas kernels  13.1 us (18%)
  between operations  0.9 us (1%)
    ppermute x25, starting transfers between devices, swap(): return lax.ppermute(value, 'row', [(i, i ^ bit) for i in range(count)])  30.4 us
    ppermute x25, waiting for transfers between devices, swap(): return lax.ppermute(value, 'row', [(i, i ^ bit) for i in range(count)])  15.9 us
    pallas_call x17, Pallas kernels, run(): pl.pallas_call(body, out_shape=outs, **extra, scratch_shapes=scratch, com...  13.1 us
    ppermute x2, starting transfers between devices, swap_rim(): return lax.ppermute(value, 'row', pairs + [(j, i) for i, j in pairs])  7.06 us
    ppermute x2, waiting for transfers between devices, swap_group(): return lax.ppermute(value, 'grp', [(0, 1), (1, 0)])  3.56 us
    ppermute x2, starting transfers between devices, swap_group(): return lax.ppermute(value, 'grp', [(0, 1), (1, 0)])  2.61 us
  transfers between devices with their start and end apart: 29, of which 12 were waited for; matrix products, arithmetic and copies ran while one was open for 0% of the time, Pallas kernels for 13%

profile of v14, /device:TPU:1, one launch (start us, length us, event | category | flops | bytes accessed | tf_op | source)
XLA Modules:
  0.0 73.6 jit_solution(15667681441447176996)
XLA Ops:
  0.6 1.3 %shard_map.160 = (bf16[2,2,32,512]{3,2,1,0:T(8,128)(2,1)S(1)}, bf16[224,512]{1,0:T(8,128)(2,1)S(1)}, bf16[96,512]{1,0:T(8,128)(2,1)S(1)}, bf16[128,512]{1,0:T(8,...) custom-call(f32[32,2048]{1,0:T(8,128)} %refs_0_.1, ...), custom_call_target="tpu_custom_call" | custom-call | tf_op jit(solution)/shard_map/pallas_call | solution.py:44
  2.1 4.5 %collective-permute-start.1 = (bf16[96,512]{1,0:T(8,128)(2,1)S(1)}, bf16[96,512]{1,0:T(8,128)(2,1)S(1)}, u32[]{:S(2)}, u32[]{:S(2)}) collective-permute-start(bf16[96,512]{1,0:T(8,128)(2,1)S(1)} %get-tuple-element.91), channel_id=1, source_target_pairs={{1,2},{3,4},{5,6},{7,8},{9,10},{11,12},{13,14},{2,1},{4,3},{6,5},{... | collective-permute-start | bytes 294920 | tf_op jit(solution)/shard_map/ppermute | solution.py:28
  6.6 2.4 %collective-permute-start.9 = (bf16[2,32,512]{2,1,0:T(8,128)(2,1)S(1)}, bf16[2,32,512]{2,1,0:T(8,128)(2,1)S(1)}, u32[]{:S(2)}, u32[]{:S(2)}) collective-permute-start(bf16[2,32,512]{2,1,0:T(8,128)(2,1)S(1)} %get-tuple-element.101), channel_id=1, source_target_pairs={{0,14},{1,15},{2,12},{3,13},{4,10},{5,11},{6,8},{7,9},{8,6},{9,7},... | collective-permute-start | bytes 196616 | tf_op jit(solution)/shard_map/ppermute | solution.py:22
  10.1 2.2 %collective-permute-start.5 = (bf16[2,32,512]{2,1,0:T(8,128)(2,1)S(1)}, bf16[2,32,512]{2,1,0:T(8,128)(2,1)S(1)}, u32[]{:S(2)}, u32[]{:S(2)}) collective-permute-start(bf16[2,32,512]{2,1,0:T(8,128)(2,1)S(1)} %get-tuple-element.100), channel_id=1, source_target_pairs={{0,12},{1,13},{2,14},{3,15},{4,8},{5,9},{6,10},{7,11},{8,4},{9,5},... | collective-permute-start | bytes 196616 | tf_op jit(solution)/shard_map/ppermute | solution.py:22
  13.3 1.3 %collective-permute-start.7 = (bf16[2,2,32,512]{3,2,1,0:T(8,128)(2,1)S(1)}, bf16[2,2,32,512]{3,2,1,0:T(8,128)(2,1)S(1)}, u32[]{:S(2)}, u32[]{:S(2)}) collective-permute-start(bf16[2,2,32,512]{3,2,1,0:T(8,128)(2,1)S(1)} %get-tuple-element.97.full), channel_id=1, source_target_pairs={{0,6},{1,7},{2,4},{3,5},{4,2},{5,3},{6,0},{7,1},{8,14},{9,15},{10,... | collective-permute-start | bytes 393224 | tf_op jit(solution)/shard_map/ppermute | solution.py:22
  14.6 2.4 %shard_map.162 = (f32[128,512]{1,0:T(8,128)S(1)}, f32[128,128]{1,0:T(8,128)S(1)}, bf16[384,512]{1,0:T(8,128)(2,1)S(1)}) custom-call(f32[4,32,512]{2,1,0:T(8,128)S(1)} %get-tuple-element.89.feats.refs_5_, bf16[224,512]{1,0:T(8,128)(2,1)S(1)} %collective-permute-done.other.core_got.refs_6_, bf16[96,512]{1,0:T(8,128)(2,1)S(1)} %collective-permute-done.1.outer.refs_7_, ...), custom_call_target="tpu_custom_call" | custom-call | tf_op jit(solution)/shard_map/pallas_call | solution.py:44
  18.4 2.4 %collective-permute-start.2 = (bf16[384,512]{1,0:T(8,128)(2,1)S(1)}, bf16[384,512]{1,0:T(8,128)(2,1)S(1)}, u32[]{:S(2)}, u32[]{:S(2)}) collective-permute-start(bf16[384,512]{1,0:T(8,128)(2,1)S(1)} %get-tuple-element.98.mine), channel_id=1, source_target_pairs={{0,2},{1,3},{2,0},{3,1},{4,6},{5,7},{6,4},{7,5},{8,10},{9,11},{10,... | collective-permute-start | bytes 1179656 | tf_op jit(solution)/shard_map/ppermute | solution.py:22
  20.9 1.3 %collective-permute-start.10 = (bf16[2,2,32,512]{3,2,1,0:T(8,128)(2,1)S(1)}, bf16[2,2,32,512]{3,2,1,0:T(8,128)(2,1)S(1)}, u32[]{:S(2)}, u32[]{:S(2)}) collective-permute-start(bf16[2,2,32,512]{3,2,1,0:T(8,128)(2,1)S(1)} %shard_map.164.refs_9_), channel_id=1, source_target_pairs={{0,16},{16,0},{1,17},{17,1},{2,18},{18,2},{3,19},{19,3},{4,20},{20... | collective-permute-start | bytes 393224 | tf_op jit(solution)/shard_map/ppermute | solution.py:36
  22.6 1.3 %collective-permute-start.6 = (bf16[2,2,32,512]{3,2,1,0:T(8,128)(2,1)S(1)}, bf16[2,2,32,512]{3,2,1,0:T(8,128)(2,1)S(1)}, u32[]{:S(2)}, u32[]{:S(2)}) collective-permute-start(bf16[2,2,32,512]{3,2,1,0:T(8,128)(2,1)S(1)} %shard_map.163.refs_5_), channel_id=1, source_target_pairs={{0,16},{16,0},{1,17},{17,1},{2,18},{18,2},{3,19},{19,3},{4,20},{20... | collective-permute-start | bytes 393224 | tf_op jit(solution)/shard_map/ppermute | solution.py:36
  25.1 2.9 %collective-permute-done.6.refs_1_.refs_6_ = bf16[2,2,32,512]{3,2,1,0:T(8,128)(2,1)S(1)} collective-permute-done((bf16[2,2,32,512]{3,2,1,0:T(8,128)(2,1)S(1)}, bf16[2,2,32,512]{3,2,1,0:T(8,128)(2,1)S(1)}, u32[]{:S(2)}, u32[]{:S(2)}) %collective-permute-start.6) | collective-permute-done | bytes 131104 | tf_op jit(solution)/shard_map/ppermute | solution.py:36
  28.0 1.6 %collective-permute-done.2.got = bf16[384,512]{1,0:T(8,128)(2,1)S(1)} collective-permute-done((bf16[384,512]{1,0:T(8,128)(2,1)S(1)}, bf16[384,512]{1,0:T(8,128)(2,1)S(1)}, u32[]{:S(2)}, u32[]{:S(2)}) %collective-permute-start.2) | collective-permute-done | bytes 393248 | tf_op jit(solution)/shard_map/ppermute | solution.py:22
  29.6 1.9 %collective-permute-start.11 = (bf16[2,256,512]{2,1,0:T(8,128)(2,1)S(1)}, bf16[2,256,512]{2,1,0:T(8,128)(2,1)S(1)}, u32[]{:S(2)}, u32[]{:S(2)}) collective-permute-start(bf16[2,256,512]{2,1,0:T(8,128)(2,1)S(1)} %get-tuple-element.102.refs_0_), channel_id=1, source_target_pairs={{0,1},{1,0},{2,3},{3,2},{4,5},{5,4},{6,7},{7,6},{8,9},{9,8},{10,11... | collective-permute-start | bytes 1572872 | tf_op jit(solution)/shard_map/ppermute | solution.py:22
  31.5 1.5 %collective-permute-done.11.refs_1_ = bf16[2,256,512]{2,1,0:T(8,128)(2,1)S(1)} collective-permute-done((bf16[2,256,512]{2,1,0:T(8,128)(2,1)S(1)}, bf16[2,256,512]{2,1,0:T(8,128)(2,1)S(1)}, u32[]{:S(2)}, u32[]{:S(2)}) %collective-permute-start.11) | collective-permute-done | bytes 524320 | tf_op jit(solution)/shard_map/ppermute | solution.py:22
  33.0 1.4 %shard_map.166 = (f32[256,512]{1,0:T(8,128)S(1)}, bf16[256,512]{1,0:T(8,128)(2,1)S(1)}, bf16[512,512]{1,0:T(8,128)(2,1)S(1)}, bf16[512,512]{1,0:T(8,128)(2,1)S(1...) custom-call(bf16[2,256,512]{2,1,0:T(8,128)(2,1)S(1)} %get-tuple-element.102.refs_0_, ...), custom_call_target="tpu_custom_call" | custom-call | tf_op jit(solution)/shard_map/pallas_call | solution.py:44
  37.5 3.1 %collective-permute-start.13 = (bf16[128,512]{1,0:T(8,128)(2,1)S(1)}, bf16[128,512]{1,0:T(8,128)(2,1)S(1)}, u32[]{:S(2)}, u32[]{:S(2)}) collective-permute-start(bf16[128,512]{1,0:T(8,128)(2,1)S(1)} %get-tuple-element.113), channel_id=1, source_target_pairs={{0,14},{1,15},{2,12},{3,13},{4,10},{5,11},{6,8},{7,9},{8,6},{9,7},... | collective-permute-start | bytes 393224 | tf_op jit(solution)/shard_map/ppermute | solution.py:22
  41.0 1.9 %shard_map.171 = (f32[128,512]{1,0:T(8,128)S(1)}, bf16[96,512]{1,0:T(8,128)(2,1)S(1)}, bf16[96,512]{1,0:T(8,128)(2,1)S(1)}, f32[28,512]{1,0:T(8,128)S(1)}, f32[28,512]{1,0:T(8,128)S(1)}) custom-call(f32[128,512]{1,0:T(8,128)S(1)} %get-tuple-element.115.refs_0_, bf16[128,512]{1,0:T(8,128)(2,1)S(1)} %collective-permute-done.15.refs_1_, ...), custom_call_target="tpu_custom_call" | custom-call | tf_op jit(solution)/shard_map/pallas_call | solution.py:44
  44.2 3.0 %collective-permute-start.19 = (bf16[128,512]{1,0:T(8,128)(2,1)S(1)}, bf16[128,512]{1,0:T(8,128)(2,1)S(1)}, u32[]{:S(2)}, u32[]{:S(2)}) collective-permute-start(bf16[128,512]{1,0:T(8,128)(2,1)S(1)} %get-tuple-element.128), channel_id=1, source_target_pairs={{0,12},{1,13},{2,14},{3,15},{4,8},{5,9},{6,10},{7,11},{8,4},{9,5},... | collective-permute-start | bytes 393224 | tf_op jit(solution)/shard_map/ppermute | solution.py:22
  48.2 2.6 %collective-permute-start.21 = (bf16[96,512]{1,0:T(8,128)(2,1)S(1)}, bf16[96,512]{1,0:T(8,128)(2,1)S(1)}, u32[]{:S(2)}, u32[]{:S(2)}) collective-permute-start(bf16[96,512]{1,0:T(8,128)(2,1)S(1)} %get-tuple-element.132), channel_id=1, source_target_pairs={{1,2},{3,4},{5,6},{7,8},{9,10},{11,12},{13,14},{2,1},{4,3},{6,5},{... | collective-permute-start | bytes 294920 | tf_op jit(solution)/shard_map/ppermute | solution.py:28
  50.9 3.3 %collective-permute-done.14.refs_1_ = bf16[128,512]{1,0:T(8,128)(2,1)S(1)} collective-permute-done((bf16[128,512]{1,0:T(8,128)(2,1)S(1)}, bf16[128,512]{1,0:T(8,128)(2,1)S(1)}, u32[]{:S(2)}, u32[]{:S(2)}) %collective-permute-start.14) | collective-permute-done | bytes 131104 | tf_op jit(solution)/shard_map/ppermute | solution.py:22
  54.7 4.4 %collective-permute-done.18 = f32[28,512]{1,0:T(8,128)S(1)} collective-permute-done((f32[28,512]{1,0:T(8,128)S(1)}, f32[28,512]{1,0:T(8,128)S(1)}, u32[]{:S(2)}, u32[]{:S(2)}) %collective-permute-start.18) | collective-permute-done | bytes 57376 | tf_op jit(solution)/shard_map/ppermute | solution.py:22
  59.3 2.6 %collective-permute-start.24 = (bf16[160,512]{1,0:T(8,128)(2,1)S(1)}, bf16[160,512]{1,0:T(8,128)(2,1)S(1)}, u32[]{:S(2)}, u32[]{:S(2)}) collective-permute-start(bf16[160,512]{1,0:T(8,128)(2,1)S(1)} %get-tuple-element.140), channel_id=1, source_target_pairs={{0,4},{1,5},{2,6},{3,7},{4,0},{5,1},{6,2},{7,3},{8,12},{9,13},{10,... | collective-permute-start | bytes 491528 | tf_op jit(solution)/shard_map/ppermute | solution.py:22
  63.3 1.5 %collective-permute-start.27 = (bf16[28,512]{1,0:T(8,128)(2,1)S(1)}, bf16[28,512]{1,0:T(8,128)(2,1)S(1)}, u32[]{:S(2)}, u32[]{:S(2)}) collective-permute-start(bf16[28,512]{1,0:T(8,128)(2,1)S(1)} %convert_element_type.3), channel_id=1, source_target_pairs={{0,12},{1,13},{2,14},{3,15},{4,8},{5,9},{6,10},{7,11},{8,4},{9,5},... | collective-permute-start | bytes 86024 | tf_op jit(solution)/shard_map/ppermute | solution.py:22
  64.8 2.9 %shard_map.173 = f32[4,32,512]{2,1,0:T(8,128)} custom-call(f32[128,512]{1,0:T(8,128)S(1)} %get-tuple-element.143.grad, bf16[96,512]{1,0:T(8,128)(2,1)S(1)} %collective-permute-done.22.inner, bf16[96,512]{1,0:T(8,128)(2,1)S(1)} %collective-permute-done.21.outer, f32[7,7,512]{2,1,0:T(8,128)S(1)} %get-tuple-element.92.kernel, ...), custom_call_target="tpu_custom_call" | custom-call | tf_op jit(solution)/shard_map/pallas_call | solution.py:44
  68.4 1.7 %collective-permute-done.23 = bf16[160,512]{1,0:T(8,128)(2,1)S(1)} collective-permute-done((bf16[160,512]{1,0:T(8,128)(2,1)S(1)}, bf16[160,512]{1,0:T(8,128)(2,1)S(1)}, u32[]{:S(2)}, u32[]{:S(2)}) %collective-permute-start.23) | collective-permute-done | bytes 163872 | tf_op jit(solution)/shard_map/ppermute | solution.py:22
  (58 shorter events, 17.3 us)
Async XLA Ops:
  2.1 11.2 %collective-permute-start.1 = (bf16[96,512]{1,0:T(8,128)(2,1)S(1)}, bf16[96,512]{1,0:T(8,128)(2,1)S(1)}, u32[]{:S(2)}, u32[]{:S(2)}) collective-permute-start(bf16[96,512]{1,0:T(8,128)(2,1)S(1)} %get-tuple-element.91), channel_id=1, source_target_pairs={{1,2},{3,4},{5,6},{7,8},{9,10},{11,12},{13,14},{2,1},{4,3},{6,5},{... | collective-permute-start | bytes 294920 | tf_op jit(solution)/shard_map/ppermute | solution.py:28
  6.6 10.4 %collective-permute-start.9 = (bf16[2,32,512]{2,1,0:T(8,128)(2,1)S(1)}, bf16[2,32,512]{2,1,0:T(8,128)(2,1)S(1)}, u32[]{:S(2)}, u32[]{:S(2)}) collective-permute-start(bf16[2,32,512]{2,1,0:T(8,128)(2,1)S(1)} %get-tuple-element.101), channel_id=1, source_target_pairs={{0,14},{1,15},{2,12},{3,13},{4,10},{5,11},{6,8},{7,9},{8,6},{9,7},... | collective-permute-start | bytes 196616 | tf_op jit(solution)/shard_map/ppermute | solution.py:22
  9.0 9.4 %collective-permute-start.8 = (bf16[2,32,512]{2,1,0:T(8,128)(2,1)S(1)}, bf16[2,32,512]{2,1,0:T(8,128)(2,1)S(1)}, u32[]{:S(2)}, u32[]{:S(2)}) collective-permute-start(bf16[2,32,512]{2,1,0:T(8,128)(2,1)S(1)} %get-tuple-element.101), channel_id=1, source_target_pairs={{0,10},{1,11},{2,8},{3,9},{4,14},{5,15},{6,12},{7,13},{8,2},{9,3},... | collective-permute-start | bytes 196616 | tf_op jit(solution)/shard_map/ppermute | solution.py:22
  10.1 10.8 %collective-permute-start.5 = (bf16[2,32,512]{2,1,0:T(8,128)(2,1)S(1)}, bf16[2,32,512]{2,1,0:T(8,128)(2,1)S(1)}, u32[]{:S(2)}, u32[]{:S(2)}) collective-permute-start(bf16[2,32,512]{2,1,0:T(8,128)(2,1)S(1)} %get-tuple-element.100), channel_id=1, source_target_pairs={{0,12},{1,13},{2,14},{3,15},{4,8},{5,9},{6,10},{7,11},{8,4},{9,5},... | collective-permute-start | bytes 196616 | tf_op jit(solution)/shard_map/ppermute | solution.py:22
  12.3 10.3 %collective-permute-start.4 = (bf16[2,32,512]{2,1,0:T(8,128)(2,1)S(1)}, bf16[2,32,512]{2,1,0:T(8,128)(2,1)S(1)}, u32[]{:S(2)}, u32[]{:S(2)}) collective-permute-start(bf16[2,32,512]{2,1,0:T(8,128)(2,1)S(1)} %get-tuple-element.100), channel_id=1, source_target_pairs={{0,8},{1,9},{2,10},{3,11},{4,12},{5,13},{6,14},{7,15},{8,0},{9,1},... | collective-permute-start | bytes 196616 | tf_op jit(solution)/shard_map/ppermute | solution.py:22
  13.3 10.6 %collective-permute-start.7 = (bf16[2,2,32,512]{3,2,1,0:T(8,128)(2,1)S(1)}, bf16[2,2,32,512]{3,2,1,0:T(8,128)(2,1)S(1)}, u32[]{:S(2)}, u32[]{:S(2)}) collective-permute-start(bf16[2,2,32,512]{3,2,1,0:T(8,128)(2,1)S(1)} %get-tuple-element.97.full), channel_id=1, source_target_pairs={{0,6},{1,7},{2,4},{3,5},{4,2},{5,3},{6,0},{7,1},{8,14},{9,15},{10,... | collective-permute-start | bytes 393224 | tf_op jit(solution)/shard_map/ppermute | solution.py:22
  17.1 7.3 %collective-permute-start.3 = (bf16[2,2,32,512]{3,2,1,0:T(8,128)(2,1)S(1)}, bf16[2,2,32,512]{3,2,1,0:T(8,128)(2,1)S(1)}, u32[]{:S(2)}, u32[]{:S(2)}) collective-permute-start(bf16[2,2,32,512]{3,2,1,0:T(8,128)(2,1)S(1)} %get-tuple-element.99.refs_3_), channel_id=1, source_target_pairs={{0,4},{1,5},{2,6},{3,7},{4,0},{5,1},{6,2},{7,3},{8,12},{9,13},{10,... | collective-permute-start | bytes 393224 | tf_op jit(solution)/shard_map/ppermute | solution.py:22
  18.4 11.1 %collective-permute-start.2 = (bf16[384,512]{1,0:T(8,128)(2,1)S(1)}, bf16[384,512]{1,0:T(8,128)(2,1)S(1)}, u32[]{:S(2)}, u32[]{:S(2)}) collective-permute-start(bf16[384,512]{1,0:T(8,128)(2,1)S(1)} %get-tuple-element.98.mine), channel_id=1, source_target_pairs={{0,2},{1,3},{2,0},{3,1},{4,6},{5,7},{6,4},{7,5},{8,10},{9,11},{10,... | collective-permute-start | bytes 1179656 | tf_op jit(solution)/shard_map/ppermute | solution.py:22
  22.6 5.4 %collective-permute-start.6 = (bf16[2,2,32,512]{3,2,1,0:T(8,128)(2,1)S(1)}, bf16[2,2,32,512]{3,2,1,0:T(8,128)(2,1)S(1)}, u32[]{:S(2)}, u32[]{:S(2)}) collective-permute-start(bf16[2,2,32,512]{3,2,1,0:T(8,128)(2,1)S(1)} %shard_map.163.refs_5_), channel_id=1, source_target_pairs={{0,16},{16,0},{1,17},{17,1},{2,18},{18,2},{3,19},{19,3},{4,20},{20... | collective-permute-start | bytes 393224 | tf_op jit(solution)/shard_map/ppermute | solution.py:36
  35.9 4.7 %collective-permute-start.16 = (bf16[256,512]{1,0:T(8,128)(2,1)S(1)}, bf16[256,512]{1,0:T(8,128)(2,1)S(1)}, u32[]{:S(2)}, u32[]{:S(2)}) collective-permute-start(bf16[256,512]{1,0:T(8,128)(2,1)S(1)} %get-tuple-element.117), channel_id=1, source_target_pairs={{0,1},{1,0},{2,3},{3,2},{4,5},{5,4},{6,7},{7,6},{8,9},{9,8},{10,11... | collective-permute-start | bytes 786440 | tf_op jit(solution)/shard_map/ppermute | solution.py:22
  36.2 4.8 %collective-permute-start.15 = (bf16[128,512]{1,0:T(8,128)(2,1)S(1)}, bf16[128,512]{1,0:T(8,128)(2,1)S(1)}, u32[]{:S(2)}, u32[]{:S(2)}) collective-permute-start(bf16[128,512]{1,0:T(8,128)(2,1)S(1)} %get-tuple-element.112.after), channel_id=1, source_target_pairs={{0,2},{1,3},{2,0},{3,1},{4,6},{5,7},{6,4},{7,5},{8,10},{9,11},{10,... | collective-permute-start | bytes 393224 | tf_op jit(solution)/shard_map/ppermute | solution.py:22
  37.5 10.7 %collective-permute-start.13 = (bf16[128,512]{1,0:T(8,128)(2,1)S(1)}, bf16[128,512]{1,0:T(8,128)(2,1)S(1)}, u32[]{:S(2)}, u32[]{:S(2)}) collective-permute-start(bf16[128,512]{1,0:T(8,128)(2,1)S(1)} %get-tuple-element.113), channel_id=1, source_target_pairs={{0,14},{1,15},{2,12},{3,13},{4,10},{5,11},{6,8},{7,9},{8,6},{9,7},... | collective-permute-start | bytes 393224 | tf_op jit(solution)/shard_map/ppermute | solution.py:22
  40.6 13.6 %collective-permute-start.14 = (bf16[128,512]{1,0:T(8,128)(2,1)S(1)}, bf16[128,512]{1,0:T(8,128)(2,1)S(1)}, u32[]{:S(2)}, u32[]{:S(2)}) collective-permute-start(bf16[128,512]{1,0:T(8,128)(2,1)S(1)} %get-tuple-element.114), channel_id=1, source_target_pairs={{0,10},{1,11},{2,8},{3,9},{4,14},{5,15},{6,12},{7,13},{8,2},{9,3},... | collective-permute-start | bytes 393224 | tf_op jit(solution)/shard_map/ppermute | solution.py:22
  42.9 7.9 %collective-permute-start.17 = (f32[28,512]{1,0:T(8,128)S(1)}, f32[28,512]{1,0:T(8,128)S(1)}, u32[]{:S(2)}, u32[]{:S(2)}) collective-permute-start(f32[28,512]{1,0:T(8,128)S(1)} %get-tuple-element.125), channel_id=1, source_target_pairs={{0,1},{1,0},{2,3},{3,2},{4,5},{5,4},{6,7},{7,6},{8,9},{9,8},{10,11... | collective-permute-start | bytes 172040 | tf_op jit(solution)/shard_map/ppermute | solution.py:22
  44.2 14.9 %collective-permute-start.19 = (bf16[128,512]{1,0:T(8,128)(2,1)S(1)}, bf16[128,512]{1,0:T(8,128)(2,1)S(1)}, u32[]{:S(2)}, u32[]{:S(2)}) collective-permute-start(bf16[128,512]{1,0:T(8,128)(2,1)S(1)} %get-tuple-element.128), channel_id=1, source_target_pairs={{0,12},{1,13},{2,14},{3,15},{4,8},{5,9},{6,10},{7,11},{8,4},{9,5},... | collective-permute-start | bytes 393224 | tf_op jit(solution)/shard_map/ppermute | solution.py:22
  47.2 11.9 %collective-permute-start.20 = (bf16[128,512]{1,0:T(8,128)(2,1)S(1)}, bf16[128,512]{1,0:T(8,128)(2,1)S(1)}, u32[]{:S(2)}, u32[]{:S(2)}) collective-permute-start(bf16[128,512]{1,0:T(8,128)(2,1)S(1)} %get-tuple-element.131), channel_id=1, source_target_pairs={{0,6},{1,7},{2,4},{3,5},{4,2},{5,3},{6,0},{7,1},{8,14},{9,15},{10,... | collective-permute-start | bytes 393224 | tf_op jit(solution)/shard_map/ppermute | solution.py:22
  48.2 10.9 %collective-permute-start.21 = (bf16[96,512]{1,0:T(8,128)(2,1)S(1)}, bf16[96,512]{1,0:T(8,128)(2,1)S(1)}, u32[]{:S(2)}, u32[]{:S(2)}) collective-permute-start(bf16[96,512]{1,0:T(8,128)(2,1)S(1)} %get-tuple-element.132), channel_id=1, source_target_pairs={{1,2},{3,4},{5,6},{7,8},{9,10},{11,12},{13,14},{2,1},{4,3},{6,5},{... | collective-permute-start | bytes 294920 | tf_op jit(solution)/shard_map/ppermute | solution.py:28
  50.8 8.3 %collective-permute-start.22 = (bf16[96,512]{1,0:T(8,128)(2,1)S(1)}, bf16[96,512]{1,0:T(8,128)(2,1)S(1)}, u32[]{:S(2)}, u32[]{:S(2)}) collective-permute-start(bf16[96,512]{1,0:T(8,128)(2,1)S(1)} %get-tuple-element.133), channel_id=1, source_target_pairs={{0,1},{1,0},{2,3},{3,2},{4,5},{5,4},{6,7},{7,6},{8,9},{9,8},{10,11... | collective-permute-start | bytes 294920 | tf_op jit(solution)/shard_map/ppermute | solution.py:22
  54.2 4.9 %collective-permute-start.18 = (f32[28,512]{1,0:T(8,128)S(1)}, f32[28,512]{1,0:T(8,128)S(1)}, u32[]{:S(2)}, u32[]{:S(2)}) collective-permute-start(f32[28,512]{1,0:T(8,128)S(1)} %add.6), channel_id=1, source_target_pairs={{0,2},{1,3},{2,0},{3,1},{4,6},{5,7},{6,4},{7,5},{8,10},{9,11},{10,... | collective-permute-start | bytes 172040 | tf_op jit(solution)/shard_map/ppermute | solution.py:22
  59.2 10.9 %collective-permute-start.23 = (bf16[160,512]{1,0:T(8,128)(2,1)S(1)}, bf16[160,512]{1,0:T(8,128)(2,1)S(1)}, u32[]{:S(2)}, u32[]{:S(2)}) collective-permute-start(bf16[160,512]{1,0:T(8,128)(2,1)S(1)} %get-tuple-element.139), channel_id=1, source_target_pairs={{0,8},{1,9},{2,10},{3,11},{4,12},{5,13},{6,14},{7,15},{8,0},{9,1},... | collective-permute-start | bytes 491528 | tf_op jit(solution)/shard_map/ppermute | solution.py:22
  59.3 10.9 %collective-permute-start.24 = (bf16[160,512]{1,0:T(8,128)(2,1)S(1)}, bf16[160,512]{1,0:T(8,128)(2,1)S(1)}, u32[]{:S(2)}, u32[]{:S(2)}) collective-permute-start(bf16[160,512]{1,0:T(8,128)(2,1)S(1)} %get-tuple-element.140), channel_id=1, source_target_pairs={{0,4},{1,5},{2,6},{3,7},{4,0},{5,1},{6,2},{7,3},{8,12},{9,13},{10,... | collective-permute-start | bytes 491528 | tf_op jit(solution)/shard_map/ppermute | solution.py:22
  61.9 5.8 %collective-permute-start.26 = (bf16[128,512]{1,0:T(8,128)(2,1)S(1)}, bf16[128,512]{1,0:T(8,128)(2,1)S(1)}, u32[]{:S(2)}, u32[]{:S(2)}) collective-permute-start(bf16[128,512]{1,0:T(8,128)(2,1)S(1)} %get-tuple-element.148), channel_id=1, source_target_pairs={{0,2},{1,3},{2,0},{3,1},{4,6},{5,7},{6,4},{7,5},{8,10},{9,11},{10,... | collective-permute-start | bytes 393224 | tf_op jit(solution)/shard_map/ppermute | solution.py:22
  62.2 8.1 %collective-permute-start.25 = (bf16[128,512]{1,0:T(8,128)(2,1)S(1)}, bf16[128,512]{1,0:T(8,128)(2,1)S(1)}, u32[]{:S(2)}, u32[]{:S(2)}) collective-permute-start(bf16[128,512]{1,0:T(8,128)(2,1)S(1)} %get-tuple-element.141), channel_id=1, source_target_pairs={{0,2},{1,3},{2,0},{3,1},{4,6},{5,7},{6,4},{7,5},{8,10},{9,11},{10,... | collective-permute-start | bytes 393224 | tf_op jit(solution)/shard_map/ppermute | solution.py:22
  63.3 6.9 %collective-permute-start.27 = (bf16[28,512]{1,0:T(8,128)(2,1)S(1)}, bf16[28,512]{1,0:T(8,128)(2,1)S(1)}, u32[]{:S(2)}, u32[]{:S(2)}) collective-permute-start(bf16[28,512]{1,0:T(8,128)(2,1)S(1)} %convert_element_type.3), channel_id=1, source_target_pairs={{0,12},{1,13},{2,14},{3,15},{4,8},{5,9},{6,10},{7,11},{8,4},{9,5},... | collective-permute-start | bytes 86024 | tf_op jit(solution)/shard_map/ppermute | solution.py:22
  (5 other events, 16.3 us)
